TPU v7x, 512 devices: a whole 4x8x8 slice. The times are simulated.
512 devices in a mesh: leaf: 64 (over y, x, core), sep: 8 (over z).
Axes of the slice: x: 4, y: 8, z: 8, core: 2. Of those that a mesh axis runs over, the one named last changes fastest.
Arguments:
- rhs_root: float32 [16, 4096], P(None, ('leaf', 'sep')), may hold values from -6 to 6
- rhs_level1: float32 [16, 4096], P(None, ('leaf', 'sep')), may hold values from -6 to 6
- rhs_level2: float32 [16, 8192], P(None, ('leaf', 'sep')), may hold values from -6 to 6
- rhs_level3: float32 [16, 8192], P(None, ('leaf', 'sep')), may hold values from -6 to 6
- inv_root: float32 [4096, 4096], P(('leaf', 'sep')), may hold values from -1 to 2, as said below
- inv_level1: float32 [4096, 2048], P(('leaf', 'sep')), may hold values from -1 to 2, as said below
- inv_level2: float32 [8192, 2048], P(('leaf', 'sep')), may hold values from -1 to 2, as said below
- inv_level3: float32 [8192, 1024], P(('leaf', 'sep')), may hold values from -1 to 2, as said below
- cross_level1: float32 [4096, 4096], P(('leaf', 'sep')), may hold values from -0.046875 to 0.046875
- cross_level2: float32 [8192, 6144], P(('leaf', 'sep')), may hold values from -0.046875 to 0.046875
- cross_level3: float32 [8192, 8192], P(('leaf', 'sep')), may hold values from -0.0625 to 0.0625
- subtree_values: float32 [16, 16384], P(None, ('leaf', 'sep')), may hold values from -6 to 6
- coupling: float32 [16384, 2048], P(('leaf', 'sep')), may hold values from -0.1875 to 0.1875
- coupled_rows: int32 [16, 2048], replicated, may hold values from 0 to 9215, as said below
Outputs:
- x_root: float32 [16, 4096], P(None, ('leaf', 'sep'))
- x_level1: float32 [16, 4096], P(None, ('leaf', 'sep'))
- x_level2: float32 [16, 8192], P(None, ('leaf', 'sep'))
- x_level3: float32 [16, 8192], P(None, ('leaf', 'sep'))
- subtree_rhs: float32 [16, 16384], P(None, ('leaf', 'sep'))
Inputs may be any that keep to these rules, and one draw needn't show every extreme that they name: `coupled_rows`: each row holds 2048 distinct indices into its subtree's path rows in increasing order; the first is 0 and the last 9215. `inv_root`: lower triangular inside each separator's block of rows, with a positive diagonal. `inv_level1`: lower triangular inside each separator's block of rows, with a positive diagonal. `inv_level2`: lower triangular inside each separator's block of rows, with a positive diagonal. `inv_level3`: lower triangular inside each separator's block of rows, with a positive diagonal.
All inputs are finite; a program needn't handle non-finite values.
Results may differ from a plain program's by a relative error of at most 0.00016.
Values sent between devices are 32-bit elements; how exact they have to be, the bound alone decides.
No kernel may reach another device: no remote copies, remote signals or barrier semaphores. Data moves between devices by JAX's collectives and lax.ppermute only.
A program may use at most 128 MiB of HBM per device.

v0:
```python
import jax
import jax.numpy as jnp
from jax import lax
from jax.sharding import PartitionSpec as P

ROOT_ROWS = 4096
LEVEL1_ROWS = 2048
LEVEL2_ROWS = 2048
LEVEL3_ROWS = 1024
SUBTREES = 16


precise = lax.Precision.HIGHEST


def subtree_of():
    return lax.axis_index("leaf") // (lax.axis_size("leaf") // SUBTREES)


def owner_of(height):
    return subtree_of() // 2 ** (4 - height)


def shard_start(local_width):
    return (lax.axis_index("leaf") * lax.axis_size("sep") + lax.axis_index("sep")) * local_width


def whole_sum(operand):
    return lax.psum(operand, ("leaf", "sep"))


def solve_block(rhs_parts, inverses, crosses, values, coupling, coupled_rows):
    widths = [ROOT_ROWS, LEVEL1_ROWS, LEVEL2_ROWS, LEVEL3_ROWS]
    starts = [0, widths[0], widths[0] + widths[1], widths[0] + widths[1] + widths[2]]
    path_rows = starts[3] + widths[3]
    samples = values.shape[0]
    indices = lax.dynamic_index_in_dim(coupled_rows, subtree_of(), 0, keepdims=False)
    update = jnp.dot(values, coupling, precision=precise, preferred_element_type=jnp.float32)
    pending = jnp.zeros((samples, path_rows), jnp.float32).at[:, indices].add(update)
    solved = [None, None, None, None]
    for height in (3, 2, 1, 0):
        block_width = widths[height]
        local_width = rhs_parts[height].shape[1]
        own_pending = pending[:, starts[height] : starts[height] + block_width]
        level_width = block_width * 2**height
        operand = jnp.zeros((samples, level_width), jnp.float32)
        operand = lax.dynamic_update_slice_in_dim(
            operand, rhs_parts[height], shard_start(local_width), 1
        )
        corner = owner_of(height) * block_width
        moved = lax.dynamic_slice_in_dim(operand, corner, block_width, 1) - own_pending
        operand = lax.dynamic_update_slice_in_dim(operand, moved, corner, 1)
        target = lax.dynamic_slice_in_dim(whole_sum(operand), corner, block_width, 1)
        result = jnp.einsum("ns,rs->nr", target, inverses[height], precision=precise)
        solved[height] = result
        if height > 0:
            pending = pending.at[:, : starts[height]].add(
                jnp.dot(
                    result,
                    crosses[height - 1],
                    precision=precise,
                    preferred_element_type=jnp.float32,
                )
            )
    known_path = jnp.zeros((samples, path_rows), jnp.float32)
    answers = []
    for height in range(4):
        block_width = widths[height]
        local_width = rhs_parts[height].shape[1]
        residual = solved[height]
        if height > 0:
            residual = residual - jnp.einsum(
                "na,ra->nr", known_path[:, : starts[height]], crosses[height - 1], precision=precise
            )
        partial_value = jnp.dot(
            residual, inverses[height], precision=precise, preferred_element_type=jnp.float32
        )
        level_width = block_width * 2**height
        corner = owner_of(height) * block_width
        operand = jnp.zeros((samples, level_width), jnp.float32)
        operand = lax.dynamic_update_slice_in_dim(operand, partial_value, corner, 1)
        level_x = whole_sum(operand)
        own_rows = lax.dynamic_slice_in_dim(level_x, shard_start(local_width), local_width, 1)
        block_x = lax.dynamic_slice_in_dim(level_x, corner, block_width, 1)
        answers.append(own_rows)
        known_path = known_path.at[:, starts[height] : starts[height] + block_width].set(block_x)
    handed = values - jnp.einsum("nk,mk->nm", known_path[:, indices], coupling, precision=precise)
    return [answers[0], answers[1], answers[2], answers[3], handed]


def body(
    rhs_root,
    rhs_level1,
    rhs_level2,
    rhs_level3,
    inv_root,
    inv_level1,
    inv_level2,
    inv_level3,
    cross_level1,
    cross_level2,
    cross_level3,
    subtree_values,
    coupling,
    coupled_rows,
):
    rhs_parts = [rhs_root, rhs_level1, rhs_level2, rhs_level3]
    inverses = [inv_root, inv_level1, inv_level2, inv_level3]
    crosses = [cross_level1, cross_level2, cross_level3]
    outputs = solve_block(rhs_parts, inverses, crosses, subtree_values, coupling, coupled_rows)
    return (outputs[0], outputs[1], outputs[2], outputs[3], outputs[4])


def solution(mesh):
    in_specs = (
        P(None, ("leaf", "sep")),
        P(None, ("leaf", "sep")),
        P(None, ("leaf", "sep")),
        P(None, ("leaf", "sep")),
        P(("leaf", "sep"), None),
        P(("leaf", "sep"), None),
        P(("leaf", "sep"), None),
        P(("leaf", "sep"), None),
        P(("leaf", "sep"), None),
        P(("leaf", "sep"), None),
        P(("leaf", "sep"), None),
        P(None, ("leaf", "sep")),
        P(("leaf", "sep"), None),
        P(),
    )
    out_specs = (
        P(None, ("leaf", "sep")),
        P(None, ("leaf", "sep")),
        P(None, ("leaf", "sep")),
        P(None, ("leaf", "sep")),
        P(None, ("leaf", "sep")),
    )
    return jax.shard_map(body, mesh=mesh, in_specs=in_specs, out_specs=out_specs, check_vma=False)
```

profile of v0, /device:TPU:1, one launch (start us, length us, event | category | flops | bytes accessed | tf_op | source)
XLA Modules:
  0.0 2213.2 jit_solution(16149836239635392545)
XLA Ops:
  7.3 0.9 compare_select_fusion
  8.1 2.8 fusion.20
  10.9 13.8 scatter_custom_fusion
  24.7 1.1 slice.165
  25.8 0.2 copy.37
  26.0 0.3 dynamic_update_slice.33
  26.4 0.8 copy-done.2
  27.2 0.0 all-reduce.12.cloned.1.call-start
  27.2 4.5 slice.164
  31.8 3.0 copy.36
  34.9 0.3 dynamic_update_slice.35
  35.2 0.6 compare_reduce_fusion.2
  35.8 266.3 %all-reduce.10.cloned.1.call-done = f32[16,8192]{1,0:T(8,128)} async-done(((f32[16,8192]{1,0:T(8,128)}), f32[16,8192]{1,0:T(8,128)}) %all-reduce.10.cloned.1.call-update) | async-done | bytes 524304 | tf_op jit(solution)/shard_map/psum | solution.py:29
  302.2 1.0 fusion.15
  303.2 1.2 fusion
  304.5 0.8 copy-done.1
  305.4 0.1 copy.31
  305.5 0.3 dynamic_update_slice.37
  305.8 0.6 compare_reduce_fusion.3
  306.4 267.2 %all-reduce.12.cloned.1.call-done = f32[16,8192]{1,0:T(8,128)} async-done(((f32[16,8192]{1,0:T(8,128)}), f32[16,8192]{1,0:T(8,128)}) %all-reduce.12.cloned.1.call-update) | async-done | bytes 524304 | tf_op jit(solution)/shard_map/psum | solution.py:29
  573.7 1.1 fusion.13
  574.9 1.1 fusion.1
  576.0 0.7 copy-done.5
  576.8 0.1 copy.27
  576.9 0.3 dynamic_update_slice.32
  577.2 0.6 compare_reduce_fusion.4
  577.9 264.5 %all-reduce.14.cloned.1.call-done = f32[16,4096]{1,0:T(8,128)} async-done(((f32[16,4096]{1,0:T(8,128)}), f32[16,4096]{1,0:T(8,128)}) %all-reduce.14.cloned.1.call-update) | async-done | bytes 262160 | tf_op jit(solution)/shard_map/psum | solution.py:29
  842.4 1.1 fusion.11
  843.5 1.8 fusion.3
  845.3 0.0 all-reduce.18.cloned.1.call-start
  845.4 266.1 %all-reduce.16.cloned.1.call-done = f32[16,4096]{1,0:T(8,128)} async-done(((f32[16,4096]{1,0:T(8,128)}), f32[16,4096]{1,0:T(8,128)}) %all-reduce.16.cloned.1.call-update) | async-done | bytes 262160 | tf_op jit(solution)/shard_map/psum | solution.py:29
  1111.5 1.4 fusion.21
  1112.9 1.1 fusion.22
  1114.0 0.0 all-reduce.20.cloned.1.call-start
  1114.1 265.8 %all-reduce.18.cloned.1.call-done = f32[16,4096]{1,0:T(8,128)} async-done(((f32[16,4096]{1,0:T(8,128)}), f32[16,4096]{1,0:T(8,128)}) %all-reduce.18.cloned.1.call-update) | async-done | bytes 262160 | tf_op jit(solution)/shard_map/psum | solution.py:29
  1379.8 1.6 broadcast_select_fusion
  1381.5 0.4 convolution_subtract_fusion.3
  1381.9 0.3 convolution_dynamic-update-slice_fusion.1
  1382.2 0.7 copy-done.8
  1383.0 0.6 compare_reduce_fusion.1
  1383.7 265.3 %all-reduce.20.cloned.1.call-done = f32[16,4096]{1,0:T(8,128)} async-done(((f32[16,4096]{1,0:T(8,128)}), f32[16,4096]{1,0:T(8,128)}) %all-reduce.20.cloned.1.call-update) | async-done | bytes 262160 | tf_op jit(solution)/shard_map/psum | solution.py:29
  1649.0 1.6 select_dynamic-update-slice_fusion
  1650.6 0.6 convolution_subtract_fusion.2
  1651.2 0.3 convolution_dynamic-update-slice_fusion
  1651.5 0.8 copy-done.4
  1652.3 0.2 all-reduce.24.cloned.1.call-start
  1652.6 0.6 compare_reduce_fusion
  1653.2 266.4 %all-reduce.22.cloned.1.call-done = f32[16,8192]{1,0:T(8,128)} async-done(((f32[16,8192]{1,0:T(8,128)}), f32[16,8192]{1,0:T(8,128)}) %all-reduce.22.cloned.1.call-update) | async-done | bytes 524304 | tf_op jit(solution)/shard_map/psum | solution.py:29
  1919.6 1.6 fusion.8
  1921.2 0.8 convolution_subtract_fusion.1
  1922.0 0.1 broadcast.167
  1922.1 0.2 convolution_dynamic-update-slice_fusion.2
  1922.3 0.8 copy-done.3
  1923.1 0.8 constant_dynamic-slice_fusion.2
  1923.8 0.7 copy.33
  1924.5 0.8 constant_dynamic-slice_fusion.1
  1925.3 0.7 copy.34
  1925.9 1.4 constant_dynamic-slice_fusion
  1927.3 263.8 %all-reduce.24.cloned.1.call-done = f32[16,8192]{1,0:T(8,128)} async-done(((f32[16,8192]{1,0:T(8,128)}), f32[16,8192]{1,0:T(8,128)}) %all-reduce.24.cloned.1.call-update) | async-done | bytes 524304 | tf_op jit(solution)/shard_map/psum | solution.py:29
  2191.1 0.8 dynamic-slice_dynamic-update-slice_fusion
  2192.0 2.8 copy.32
  2194.8 7.8 gather_fusion
  2202.7 2.4 convolution_subtract_fusion
  2205.0 1.4 constant_dynamic-slice_fusion.3
  (55 shorter events, 0.7 us)
Async XLA Ops:
  7.2 296.0 %copy-start = (f32[16,8192]{1,0:T(8,128)S(1)}, f32[16,8192]{1,0:T(8,128)}, u32[]{:S(2)}) copy-start(f32[16,8192]{1,0:T(8,128)} %param.38) | copy-start | bytes 1572868
  7.2 18.9 copy-start.15
  7.2 295.0 %all-reduce.10.cloned.1.call-start = ((), (), s32[]{:S(2)}) async-start(), calls=%async_computation | async-start | bytes 1048576 | tf_op jit(solution)/shard_map/psum | solution.py:29
  26.4 0.8 copy-start.2
  27.2 546.5 %all-reduce.12.cloned.1.call-start = ((), (), s32[]{:S(2)}) async-start(), calls=%async_computation.1 | async-start | bytes 1048576 | tf_op jit(solution)/shard_map/psum | solution.py:29
  31.7 3.2 copy-start.16
  31.7 270.4 %copy-start.13 = (f32[16,1024]{1,0:T(8,128)S(1)}, f32[16,1024]{1,0:T(8,128)}, u32[]{:S(2)}) copy-start(f32[16,1024]{1,0:T(8,128)} %param.35) | copy-start | bytes 196612
  31.7 273.6 %copy-start.17 = (f32[16,8]{0,1:T(8,128)S(1)}, f32[16,8]{0,1:T(8,128)}, u32[]{:S(2)}) copy-start(f32[16,8]{0,1:T(8,128)} %param.29) | copy-start | bytes 1540
  31.7 541.9 %copy-start.11 = (f32[16,2048]{1,0:T(8,128)S(1)}, f32[16,2048]{1,0:T(8,128)}, u32[]{:S(2)}) copy-start(f32[16,2048]{1,0:T(8,128)} %param.34) | copy-start | bytes 393220
  31.7 543.1 %copy-start.6 = (f32[16,6144]{1,0:T(8,128)S(1)}, f32[16,6144]{1,0:T(8,128)}, u32[]{:S(2)}) copy-start(f32[16,6144]{1,0:T(8,128)} %param.37) | copy-start | bytes 1179652
  31.8 545.0 %copy-start.18 = (f32[16,8]{0,1:T(8,128)S(1)}, f32[16,8]{0,1:T(8,128)}, u32[]{:S(2)}) copy-start(f32[16,8]{0,1:T(8,128)} %param.28) | copy-start | bytes 1540
  31.8 810.6 %copy-start.12 = (f32[8,2048]{1,0:T(8,128)S(1)}, f32[8,2048]{1,0:T(8,128)}, u32[]{:S(2)}) copy-start(f32[8,2048]{1,0:T(8,128)} %param.33) | copy-start | bytes 196612
  31.8 811.7 %copy-start.10 = (f32[8,4096]{1,0:T(8,128)S(1)}, f32[8,4096]{1,0:T(8,128)}, u32[]{:S(2)}) copy-start(f32[8,4096]{1,0:T(8,128)} %param.36) | copy-start | bytes 393220
  34.8 1076.7 %copy-start.9 = (f32[8,4096]{1,0:T(8,128)S(1)}, f32[8,4096]{1,0:T(8,128)}, u32[]{:S(2)}) copy-start(f32[8,4096]{1,0:T(8,128)} %param.32) | copy-start | bytes 393220
  304.5 0.8 copy-start.1
  305.3 537.1 %all-reduce.14.cloned.1.call-start = ((), (), s32[]{:S(2)}) async-start(), calls=%async_computation.2 | async-start | bytes 524288 | tf_op jit(solution)/shard_map/psum | solution.py:29
  576.0 0.7 copy-start.5
  576.7 534.8 %all-reduce.16.cloned.1.call-start = ((), (), s32[]{:S(2)}) async-start(), calls=%async_computation.3 | async-start | bytes 524288 | tf_op jit(solution)/shard_map/psum | solution.py:29
  845.3 534.5 %all-reduce.18.cloned.1.call-start = ((), (), s32[]{:S(2)}) async-start(), calls=%async_computation.4 | async-start | bytes 524288 | tf_op jit(solution)/shard_map/psum | solution.py:29
  1114.0 535.0 %all-reduce.20.cloned.1.call-start = ((), (), s32[]{:S(2)}) async-start(), calls=%async_computation.5 | async-start | bytes 524288 | tf_op jit(solution)/shard_map/psum | solution.py:29
  1382.2 0.7 copy-start.8
  1383.0 536.7 %all-reduce.22.cloned.1.call-start = ((), (), s32[]{:S(2)}) async-start(), calls=%async_computation.6 | async-start | bytes 1048576 | tf_op jit(solution)/shard_map/psum | solution.py:29
  1651.5 0.8 copy-start.4
  1652.3 550.3 %copy-start.7 = (f32[32,2048]{1,0:T(8,128)S(1)}, f32[32,2048]{1,0:T(8,128)}, u32[]{:S(2)}) copy-start(f32[32,2048]{1,0:T(8,128)} %param.40) | copy-start | bytes 786436
  1652.3 550.3 %copy-start.14 = (f32[16,32]{1,0:T(8,128)S(1)}, f32[16,32]{1,0:T(8,128)}, u32[]{:S(2)}) copy-start(f32[16,32]{1,0:T(8,128)} %param.39) | copy-start | bytes 6148
  1652.3 538.8 %all-reduce.24.cloned.1.call-start = ((), (), s32[]{:S(2)}) async-start(), calls=%async_computation.7 | async-start | bytes 1048576 | tf_op jit(solution)/shard_map/psum | solution.py:29
  1922.3 0.8 copy-start.3
Sparse Core Ops, SparseCore 0:
  27.3 274.7 all-reduce.9
  307.9 265.6 all-reduce.11
  578.7 263.6 all-reduce.13
  848.0 263.4 all-reduce.15
  1116.4 263.4 all-reduce.17
  1385.5 263.4 all-reduce.19
  1654.0 265.6 all-reduce.21
  1925.4 265.6 all-reduce.23
where the time goes:
time: 2210 us
  waiting for transfers between devices  2130 us (96%)
  local copies, waits for them, and re-layouts  32.1 us (1%)
  other arithmetic  22.7 us (1%)
    psum x8, waiting for transfers between devices, whole_sum(): return lax.psum(operand, ('leaf', 'sep'))  2130 us
  transfers between devices with their start and end apart: 8, of which 8 were waited for; matrix products, arithmetic and copies ran while one was open for 1% of the time, Pallas kernels for 0%

commit v1 on v0

v1 whole, which is shorter than its diff:
```python
import jax
import jax.numpy as jnp
from jax import lax
from jax.sharding import Mesh, PartitionSpec as P

ROOT_ROWS = 4096
LEVEL1_ROWS = 2048
LEVEL2_ROWS = 2048
LEVEL3_ROWS = 1024
WIDTHS = (ROOT_ROWS, LEVEL1_ROWS, LEVEL2_ROWS, LEVEL3_ROWS)
Y, X, C = 8, 4, 2
XC = X * C
PAIR = 2

precise = lax.Precision.HIGHEST


def group_size(axes):
    size = 1
    for name in axes:
        size *= lax.axis_size(name)
    return size


def exchange(operand, axes):
    shape = operand.shape
    count = shape[0]
    elements = operand.size // count
    rows = elements // 128 if elements % 128 == 0 else 1
    flat = operand.reshape(count * rows, elements // rows)
    return lax.all_to_all(flat, axes, 0, 0, tiled=True).reshape(shape)


def sum_to_all(partial, axes):
    copies = jnp.broadcast_to(partial[None], (group_size(axes),) + partial.shape)
    return jnp.sum(exchange(copies, axes), axis=0)


def matmul_rows(vector, matrix):
    return jnp.einsum("sk,rk->sr", vector, matrix, precision=precise, preferred_element_type=jnp.float32)


def matmul_columns(vector, matrix):
    return jnp.einsum("sr,rk->sk", vector, matrix, precision=precise, preferred_element_type=jnp.float32)


def body(
    rhs_root,
    rhs_level1,
    rhs_level2,
    rhs_level3,
    inv_root,
    inv_level1,
    inv_level2,
    inv_level3,
    cross_level1,
    cross_level2,
    cross_level3,
    subtree_values,
    coupling,
    coupled_rows,
):
    widths = WIDTHS
    starts = (0, widths[0], widths[0] + widths[1], widths[0] + widths[1] + widths[2])
    path_rows = starts[3] + widths[3]
    ancestors = starts[3]
    depth = lax.axis_size("z")
    y = (lax.axis_index("y2") * 2 + lax.axis_index("y1")) * 2 + lax.axis_index("y0")
    x = lax.axis_index("x")
    c = lax.axis_index("c")
    z = lax.axis_index("z")
    all_y = ("y2", "y1", "y0")

    pack3 = jnp.concatenate([inv_level3, cross_level3], axis=1)
    pack2 = jnp.concatenate([inv_level2, cross_level2], axis=1)
    pack1 = jnp.concatenate([inv_level1, cross_level1, inv_root], axis=1)
    all3 = lax.all_gather(pack3, ("x", "c"), axis=0, tiled=True)
    all2 = lax.all_gather(pack2, ("x", "c"), axis=0, tiled=True)
    all1 = lax.all_gather(pack1, ("x", "c"), axis=0, tiled=True)
    all_coupling = lax.all_gather(coupling, ("x", "c"), axis=0, tiled=True)
    inv3, cross3 = all3[:, : widths[3]], all3[:, widths[3] :]
    inv2, cross2 = all2[:, : widths[2]], all2[:, widths[2] :]
    inv1 = all1[:, : widths[1]]
    cross1 = all1[:, widths[1] : widths[1] + widths[0]]
    inv0 = all1[:, widths[1] + widths[0] :]

    rhs_parts = [rhs_root, rhs_level1, rhs_level2, rhs_level3]
    locals_ = [part.shape[1] for part in rhs_parts]
    small = jnp.concatenate(rhs_parts + [subtree_values], axis=1)
    both_small = lax.all_gather(small, "c", axis=0, tiled=False)
    both_small = both_small.reshape(C, X, C, PAIR, small.shape[1])
    both_small = lax.dynamic_index_in_dim(both_small, c, 2, keepdims=False).reshape(C, X * PAIR, small.shape[1])
    both_coupling = lax.all_gather(coupling, "c", axis=0, tiled=True)
    values = both_small[:, :, sum(locals_) :]
    values = jnp.transpose(values, (1, 0, 2)).reshape(X * PAIR, -1)
    subtree = y * 2 + x // 2
    indices = lax.dynamic_index_in_dim(coupled_rows, subtree, 0, keepdims=False)
    update = matmul_columns(values, both_coupling)
    pending = jnp.zeros((X * PAIR, path_rows), jnp.float32).at[:, indices].add(
        -update, unique_indices=True, indices_are_sorted=True
    )
    offset = 0
    for height in range(4):
        width = locals_[height]
        planes = Y // 2**height
        for other in range(C):
            place = ((y % planes) * XC + x * C + other) * depth + z
            column = starts[height] + place * width
            own = lax.dynamic_slice_in_dim(pending, column, width, 1)
            own = own + both_small[other, :, offset : offset + width]
            pending = lax.dynamic_update_slice_in_dim(pending, own, column, 1)
        offset += width

    block = ancestors // depth
    upper = pending[:, :ancestors].reshape(X, PAIR, depth, block)
    upper = jnp.transpose(upper, (0, 2, 1, 3)).reshape(X, depth, -1)
    lower = jnp.broadcast_to(
        pending[:, ancestors:].reshape(X, 1, PAIR * widths[3]), (X, depth, PAIR * widths[3])
    )
    send = jnp.concatenate([lower, upper], axis=2).reshape(X * depth, -1)
    received = jnp.sum(exchange(send, ("x", "z")), axis=0)
    target3 = received[: PAIR * widths[3]].reshape(PAIR, widths[3])
    upper = received[PAIR * widths[3] :].reshape(PAIR, block)

    solved3 = matmul_rows(target3, inv3)
    rest = -matmul_columns(solved3, cross3)
    own = lax.dynamic_slice_in_dim(rest, z * block, block, 1) + upper
    rest = lax.dynamic_update_slice_in_dim(rest, own, z * block, 1)
    target2 = sum_to_all(rest[:, starts[2] : ancestors], ("y0", "z"))
    solved2 = matmul_rows(target2, inv2)
    rest = rest[:, : starts[2]] - matmul_columns(solved2, cross2)
    target1 = sum_to_all(rest[:, starts[1] :], ("y1", "y0", "z"))
    solved1 = matmul_rows(target1, inv1)
    rest = rest[:, : starts[1]] - matmul_columns(solved1, cross1)

    def sum_root(partial):
        block = widths[0] // depth
        cut = jnp.transpose(partial.reshape(PAIR, depth, block), (1, 0, 2))
        cut = jnp.broadcast_to(cut[None], (Y, depth, PAIR, block)).reshape(Y * depth, PAIR, block)
        mine = jnp.sum(exchange(cut, all_y + ("z",)), axis=0)
        whole = exchange(jnp.broadcast_to(mine[None], (depth, PAIR, block)), ("z",))
        return jnp.transpose(whole, (1, 0, 2)).reshape(PAIR, widths[0])

    target0 = sum_root(rest)
    solved0 = matmul_rows(target0, inv0)
    x0 = sum_root(matmul_columns(solved0, inv0))
    residual = solved1 - matmul_rows(x0, cross1)
    x1 = sum_to_all(matmul_columns(residual, inv1), ("y1", "y0", "z"))
    known = jnp.concatenate([x0, x1], axis=1)
    residual = solved2 - matmul_rows(known, cross2)
    x2 = sum_to_all(matmul_columns(residual, inv2), ("y0", "z"))
    known = jnp.concatenate([known, x2], axis=1)
    residual = solved3 - matmul_rows(known, cross3)
    x3 = sum_to_all(matmul_columns(residual, inv3), ("z",))
    known = jnp.concatenate([known, x3], axis=1)

    rows = coupling.shape[0]
    both_indices = lax.dynamic_slice_in_dim(coupled_rows, y * 2, 2, 0)
    halves = all_coupling.reshape(2, XC // 2 * rows, -1)
    handed = []
    for half in range(2):
        chosen = known[:, both_indices[half]]
        handed.append(matmul_rows(chosen, halves[half]).reshape(PAIR, XC // 2, rows))
    handed = jnp.concatenate(handed, axis=1)

    pieces = []
    for height, answer in enumerate((x0, x1, x2, x3)):
        planes = Y // 2**height
        cube = answer.reshape(PAIR, planes, XC, depth, locals_[height])
        cube = lax.dynamic_index_in_dim(cube, z, 3, keepdims=False)
        pieces.append(lax.dynamic_index_in_dim(cube, y % planes, 1, keepdims=False))
    pieces.append(handed)
    out = jnp.transpose(jnp.concatenate(pieces, axis=2), (1, 0, 2))
    out = exchange(out, ("x", "c")).reshape(XC * PAIR, -1)
    cuts = [0]
    for width in locals_:
        cuts.append(cuts[-1] + width)
    answers = [out[:, cuts[k] : cuts[k + 1]] for k in range(4)]
    return (answers[0], answers[1], answers[2], answers[3], subtree_values - out[:, cuts[4] :])


def solution(mesh):
    shape = (2, 2, 2, X, C, mesh.shape["sep"])
    fine = Mesh(mesh.devices.reshape(shape), ("y2", "y1", "y0", "x", "c", "z"))
    every = ("y2", "y1", "y0", "x", "c", "z")
    columns, rows = P(None, every), P(every, None)
    in_specs = (columns,) * 4 + (rows,) * 7 + (columns, rows, P())
    return jax.shard_map(body, mesh=fine, in_specs=in_specs, out_specs=(columns,) * 5, check_vma=False)
```

time: 2210 us -> 315 us (0.14)
  waiting for transfers between devices: 2130 us -> 52.2 us
  blocking collectives: 0 us -> 102 us
  starting transfers between devices: 0.51 us -> 29.5 us
  matrix products: 17.6 us -> 40.2 us
    psum x8 -> x0, waiting for transfers between devices: 2130 us -> none  [whole_sum(): return lax.psum(operand, ('leaf', 'sep'))]
    all_to_all x0 -> x6, blocking collectives: none -> 91.9 us  [exchange(): return lax.all_to_all(flat, axes, 0, 0, tiled=True).reshape(shape)]
    all_to_all x0 -> x5, waiting for transfers between devices: none -> 51.6 us  [exchange(): return lax.all_to_all(flat, axes, 0, 0, tiled=True).reshape(shape)]
    all_to_all x0 -> x5, starting transfers between devices: none -> 29.3 us  [exchange(): return lax.all_to_all(flat, axes, 0, 0, tiled=True).reshape(shape)]
    dot_general x16 -> x17, matrix products: 17.6 us -> 40.2 us  [the longest x9 25.9 us: matmul_rows(): jnp.einsum('sk,rk->sr', vector, matrix, precision=precise, preferred_elem...]
  transfers between devices with their start and end apart: 8 -> 9, of which waited for: 8 -> 5; matrix products, arithmetic and copies ran while one was open for 1% -> 22% of each run, Pallas kernels for 0% -> 0%
where the time goes in v1:
time: 315 us; the launch traced here: 313 us
  blocking collectives  102 us (32%)
  waiting for transfers between devices  52.2 us (17%)
  local copies, waits for them, and re-layouts  42.3 us (13%)
  matrix products  40.2 us (13%)
  other arithmetic  31.8 us (10%)
  starting transfers between devices  29.5 us (9%)
  between operations  14.3 us (5%)
    all_to_all x6, blocking collectives, exchange(): return lax.all_to_all(flat, axes, 0, 0, tiled=True).reshape(shape)  91.9 us
    all_to_all x5, waiting for transfers between devices, exchange(): return lax.all_to_all(flat, axes, 0, 0, tiled=True).reshape(shape)  51.6 us
    all_to_all x5, starting transfers between devices, exchange(): return lax.all_to_all(flat, axes, 0, 0, tiled=True).reshape(shape)  29.3 us
    dot_general x9, matrix products, matmul_rows(): jnp.einsum('sk,rk->sr', vector, matrix, precision=precise, preferred_elem...  25.9 us
    gather x2, local copies, waits for them, and re-layouts, body(): chosen = known[:, both_indices[half]]  17.8 us
    dot_general x8, matrix products, matmul_columns(): jnp.einsum('sr,rk->sk', vector, matrix, precision=precise, preferred_elem...  14.2 us
    scatter-add x1, other arithmetic, body(): jnp.zeros((X * PAIR, path_rows), jnp.float32).at[:, indices]  13.9 us
    dynamic_update_slice x8, other arithmetic, body(): pending = lax.dynamic_update_slice_in_dim(pending, own, column, 1)  10.2 us
  transfers between devices with their start and end apart: 9, of which 5 were waited for; matrix products, arithmetic and copies ran while one was open for 22% of the time, Pallas kernels for 0%

profile of v1, /device:TPU:1, one launch (start us, length us, event | category | flops | bytes accessed | tf_op | source)
XLA Modules:
  0.0 312.8 jit_solution(7719416996324022920)
XLA Ops:
  7.2 1.9 pad_maximum_fusion
  9.2 1.9 pad_maximum_fusion.1
  11.2 1.8 pad_maximum_fusion.2
  13.0 0.8 copy.101
  13.8 0.8 copy.102
  14.5 0.8 concatenate.32
  15.3 8.4 %all-gather = f32[32,80]{1,0:T(8,128)S(1)} all-gather(f32[16,80]{1,0:T(8,128)S(1)} %concatenate.32), channel_id=2, replica_groups=mesh['y2'=2,'y1'=2,'y0'=2,'x'=4,'c'=2,'z'=8] {'c'}, dimensions={0}, use_global_device_ids=true | all-gather | bytes 15360 | tf_op jit(solution)/shard_map/all_gather | solution.py:90
  24.0 2.2 all_gather.23
  27.4 1.0 compare_select_fusion.1
  28.4 13.9 %scatter_custom_fusion = f32[8,9216]{0,1:T(8,128)} fusion(s32[2048]{0:T(1024)S(1)} %bitcast.122, f32[2048,8]{1,0:T(8,128)S(1)} %copy.105, f32[]{:T(128)} %constant.210.clone.1), kind=kCustom, calls=%fused_computation.12 | custom fusion | flops 16384 | bytes 294916 | tf_op jit(solution)/shard_map/scatter-add | solution.py:99
  42.3 1.3 constant_dynamic-update-slice_fusion.3
  43.6 1.3 constant_dynamic-update-slice_fusion.2
  44.9 1.3 constant_dynamic-update-slice_fusion.1
  46.1 1.3 constant_dynamic-update-slice_fusion
  47.4 1.3 add_dynamic-update-slice_fusion.4
  48.7 1.3 add_dynamic-update-slice_fusion.3
  50.0 1.3 add_dynamic-update-slice_fusion.2
  51.3 1.3 add_dynamic-update-slice_fusion.1
  52.6 4.4 %slice.158 = f32[8,8192]{0,1:T(8,128)} slice(f32[8,9216]{0,1:T(8,128)} %add_dynamic-update-slice_fusion.1), slice={[0:8], [0:8192]} | slice | bytes 524288 | tf_op jit(solution)/shard_map/slice | solution.py:115
  57.0 1.1 slice.157
  58.0 2.8 copy.115
  61.3 0.9 copy.136
  62.1 7.6 %all-to-all-start = ((f32[32,32,128]{2,1,0:T(8,128)}), f32[32,32,128]{2,1,0:T(8,128)S(1)}, u32[]{:S(2)}, u32[]{:S(2)}) async-start(f32[32,32,128]{2,1,0:T(8,128)} %bitcast.45), calls=%async_computation | async-start | bytes 1048576 | tf_op jit(solution)/shard_map/all_to_all | solution.py:31
  69.7 14.1 %all-to-all-done = f32[32,32,128]{2,1,0:T(8,128)S(1)} async-done(((f32[32,32,128]{2,1,0:T(8,128)}), f32[32,32,128]{2,1,0:T(8,128)S(1)}, u32[]{:S(2)}, u32[]{:S(2)}) %all-to-all-start) | async-done | bytes 524320 | tf_op jit(solution)/shard_map/all_to_all | solution.py:31
  83.9 1.5 fusion.35
  85.4 4.3 %convolution_negate_fusion = f32[2,8192]{1,0:T(2,128)S(1)} fusion(f32[2,128]{1,0:T(2,128)S(1)} %fusion.35, f32[128,9216]{1,0:T(8,128)} %all-gather.6.cloned.1.call-done), kind=kOutput, calls=%fused_computation.3 | convolution fusion | flops 25182208 | bytes 4260864 | tf_op jit(solution)/shard_map/sr,rk->sk/dot_general | solution.py:44
  89.8 15.3 %all_to_all.79 = f32[16,32,128]{2,1,0:T(8,128)S(1)} all-to-all(f32[16,32,128]{2,1,0:T(8,128)S(1)} %broadcast_in_dim.38), channel_id=1, replica_groups=mesh['y2'=2,'y1'=2,'y0'=2,'x'=4,'c'=2,'z'=8] {'y0','z'}, dimensions={0} | all-to-all | bytes 524288 | tf_op jit(solution)/shard_map/all_to_all | solution.py:31
  105.1 2.1 fusion.27
  107.3 3.5 %convolution_subtract_fusion = f32[2,6144]{1,0:T(2,128)S(1)} fusion(f32[2,128]{1,0:T(2,128)S(1)} %fusion.27, f32[128,8192]{1,0:T(8,128)} %all-gather.8.cloned.1.call-done, f32[2,8192]{1,0:T(2,128)S(1)} %add_dynamic-update-slice_fusion), kind=kOutput, calls=%fused_computation.4 | convolution fusion | flops 18886656 | bytes 3245056 | tf_op jit(solution)/shard_map/sr,rk->sk/dot_general | solution.py:44
  110.8 24.0 %all_to_all.80 = f32[32,32,128]{2,1,0:T(8,128)S(1)} all-to-all(f32[32,32,128]{2,1,0:T(8,128)S(1)} %broadcast_in_dim.40), channel_id=1, replica_groups=mesh['y2'=2,'y1'=2,'y0'=2,'x'=4,'c'=2,'z'=8] {'y1','y0','z'}, dimensions={0} | all-to-all | bytes 1048576 | tf_op jit(solution)/shard_map/all_to_all | solution.py:31
  135.0 1.7 fusion.31
  136.7 1.8 convolution_subtract_fusion.1
  138.6 0.9 all_to_all.56
  139.5 10.8 %all-to-all-start.3 = ((f32[64,8,128]{2,1,0:T(8,128)}), f32[64,8,128]{2,1,0:T(8,128)S(1)}, u32[]{:S(2)}, u32[]{:S(2)}) async-start(f32[64,8,128]{2,1,0:T(8,128)} %all_to_all.56), calls=%async_computation.3 | async-start | bytes 524288 | tf_op jit(solution)/shard_map/all_to_all | solution.py:31
  150.9 12.6 %all-to-all-done.3 = f32[64,8,128]{2,1,0:T(8,128)S(1)} async-done(((f32[64,8,128]{2,1,0:T(8,128)}), f32[64,8,128]{2,1,0:T(8,128)S(1)}, u32[]{:S(2)}, u32[]{:S(2)}) %all-to-all-start.3) | async-done | bytes 262176 | tf_op jit(solution)/shard_map/all_to_all | solution.py:31
  163.6 10.3 %all_to_all.81 = f32[8,8,128]{2,1,0:T(8,128)S(1)} all-to-all(f32[8,8,128]{2,1,0:T(8,128)S(1)} %broadcast_in_dim.42), channel_id=1, replica_groups=mesh['y2'=2,'y1'=2,'y0'=2,'x'=4,'c'=2,'z'=8] {'z'}, dimensions={0} | all-to-all | bytes 65536 | tf_op jit(solution)/shard_map/all_to_all | solution.py:31
  173.9 2.2 fusion.21
  177.0 16.7 %all_to_all.82 = f32[64,8,128]{2,1,0:T(8,128)S(1)} all-to-all(f32[64,8,128]{2,1,0:T(8,128)S(1)} %all_to_all.59), channel_id=1, replica_groups=mesh['y2'=2,'y1'=2,'y0'=2,'x'=4,'c'=2,'z'=8] {'y2','y1','y0','z'}, dimensions={0} | all-to-all | bytes 524288 | tf_op jit(solution)/shard_map/all_to_all | solution.py:31
  193.8 9.5 %all_to_all.83 = f32[8,8,128]{2,1,0:T(8,128)S(1)} all-to-all(f32[8,8,128]{2,1,0:T(8,128)S(1)} %broadcast_in_dim.87), channel_id=1, replica_groups=mesh['y2'=2,'y1'=2,'y0'=2,'x'=4,'c'=2,'z'=8] {'z'}, dimensions={0} | all-to-all | bytes 65536 | tf_op jit(solution)/shard_map/all_to_all | solution.py:31
  203.4 0.9 convolution_subtract_fusion.2
  204.7 0.9 broadcast_in_dim.89
  205.5 3.9 %all-to-all-start.7 = ((f32[32,32,128]{2,1,0:T(8,128)}), f32[32,32,128]{2,1,0:T(8,128)S(1)}, u32[]{:S(2)}, u32[]{:S(2)}) async-start(f32[32,32,128]{2,1,0:T(8,128)} %broadcast_in_dim.89), calls=%async_computation.7 | async-start | bytes 1048576 | tf_op jit(solution)/shard_map/all_to_all | solution.py:31
  209.5 12.6 %all-to-all-done.7 = f32[32,32,128]{2,1,0:T(8,128)S(1)} async-done(((f32[32,32,128]{2,1,0:T(8,128)}), f32[32,32,128]{2,1,0:T(8,128)S(1)}, u32[]{:S(2)}, u32[]{:S(2)}) %all-to-all-start.7) | async-done | bytes 524320 | tf_op jit(solution)/shard_map/all_to_all | solution.py:31
  222.2 4.4 %fusion.9 = f32[2,128]{1,0:T(2,128)S(1)} fusion(f32[2,128]{1,0:T(2,128)S(1)} %fusion.27, f32[128,8192]{1,0:T(8,128)} %all-gather.8.cloned.1.call-done, f32[2,2048]{1,0:T(2,128)S(1)} %reduce_sum.90, f32[2,4096]{1,0:T(2,128)S(1)} %bitcast.102), kind=kOutput, calls=%fused_computation.16 | convolution fusion | flops 18886912 | bytes 3196928 | tf_op jit(solution)/shard_map/sk,rk->sr/dot_general | solution.py:40
  226.6 1.8 fusion.25
  228.5 0.7 broadcast_in_dim.91
  229.2 3.8 %all-to-all-start.8 = ((f32[16,32,128]{2,1,0:T(8,128)}), f32[16,32,128]{2,1,0:T(8,128)S(1)}, u32[]{:S(2)}, u32[]{:S(2)}) async-start(f32[16,32,128]{2,1,0:T(8,128)} %broadcast_in_dim.91), calls=%async_computation.8 | async-start | bytes 524288 | tf_op jit(solution)/shard_map/all_to_all | solution.py:31
  233.0 1.7 fusion.51
  235.2 5.3 %all-to-all-done.8 = f32[16,32,128]{2,1,0:T(8,128)S(1)} async-done(((f32[16,32,128]{2,1,0:T(8,128)}), f32[16,32,128]{2,1,0:T(8,128)S(1)}, u32[]{:S(2)}, u32[]{:S(2)}) %all-to-all-start.8) | async-done | bytes 262176 | tf_op jit(solution)/shard_map/all_to_all | solution.py:31
  240.5 5.1 %fusion.12 = f32[2,128]{1,0:T(2,128)S(1)} fusion(f32[2,128]{1,0:T(2,128)S(1)} %fusion.35, f32[128,9216]{1,0:T(8,128)} %all-gather.6.cloned.1.call-done, f32[2,2048]{1,0:T(2,128)S(1)} %reduce_sum.92, f32[2,2048]{1,0:T(2,128)S(1)} %reduce_sum.90, f32[2,4096]{1,0:T(2,128)S(1)} %bitcast.104), kind=kOutput, calls=%fused_computation.18 | convolution fusion | flops 25198848 | bytes 4261888 | tf_op jit(solution)/shard_map/sk,rk->sr/dot_general | solution.py:40
  245.6 1.4 fusion.33
  247.0 0.6 broadcast_in_dim.93
  247.7 3.3 %all-to-all-start.9 = ((f32[8,16,128]{2,1,0:T(8,128)}), f32[8,16,128]{2,1,0:T(8,128)S(1)}, u32[]{:S(2)}, u32[]{:S(2)}) async-start(f32[8,16,128]{2,1,0:T(8,128)} %broadcast_in_dim.93), calls=%async_computation.9 | async-start | bytes 131072 | tf_op jit(solution)/shard_map/all_to_all | solution.py:31
  251.2 7.0 %all-to-all-done.9 = f32[8,16,128]{2,1,0:T(8,128)S(1)} async-done(((f32[8,16,128]{2,1,0:T(8,128)}), f32[8,16,128]{2,1,0:T(8,128)S(1)}, u32[]{:S(2)}, u32[]{:S(2)}) %all-to-all-start.9) | async-done | bytes 65568 | tf_op jit(solution)/shard_map/all_to_all | solution.py:31
  258.3 2.9 copy.121
  261.2 10.0 %gather_fusion = f32[2048,2]{1,0:T(8,128)} fusion(f32[2,9216]{0,1:T(8,128)} %copy.121, s32[2048]{0:T(1024)S(1)} %broadcast_clamp_fusion.1), kind=kCustom, calls=%fused_computation | custom fusion | bytes 40960 | tf_op jit(solution)/shard_map/gather | solution.py:162
  271.2 7.8 %gather_fusion.1 = f32[2048,2]{1,0:T(8,128)S(1)} fusion(f32[2,9216]{0,1:T(8,128)} %copy.121, s32[2048]{0:T(1024)S(1)} %broadcast_clamp_fusion), kind=kCustom, calls=%fused_computation.1 | custom fusion | bytes 40960 | tf_op jit(solution)/shard_map/gather | solution.py:162
  279.0 4.6 %fusion.17 = f32[2,4,32]{2,0,1:T(2,128)S(1)} fusion(f32[4,32,2048]{2,1,0:T(8,128)S(1)} %bitcast.100, f32[2048,2]{1,0:T(8,128)} %gather_fusion), kind=kOutput, calls=%fused_computation.21 | convolution fusion | flops 6291456 | bytes 1065984 | tf_op jit(solution)/shard_map/sk,rk->sr/dot_general | solution.py:40
  283.6 3.4 %fusion.15 = f32[2,4,32]{2,0,1:T(2,128)S(1)} fusion(f32[4,32,2048]{2,1,0:T(8,128)S(1)} %bitcast.99, f32[2048,2]{1,0:T(8,128)S(1)} %gather_fusion.1), kind=kOutput, calls=%fused_computation.19 | convolution fusion | flops 6291456 | bytes 1065984 | tf_op jit(solution)/shard_map/sk,rk->sr/dot_general | solution.py:40
  287.2 16.1 %all_to_all.84 = f32[8,1,160]{2,1,0:T(1,128)S(1)} all-to-all(f32[8,1,160]{2,1,0:T(1,128)S(1)} %all_to_all.67), channel_id=1, replica_groups=mesh['y2'=2,'y1'=2,'y0'=2,'x'=4,'c'=2,'z'=8] {'x','c'}, dimensions={0} | all-to-all | bytes 10240 | tf_op jit(solution)/shard_map/all_to_all | solution.py:31
  303.6 0.7 fusion.53
  304.2 0.7 slice_subtract_fusion
  304.9 0.7 copy.128
  305.6 0.7 copy.129
  (98 shorter events, 6.0 us)
Async XLA Ops:
  7.2 16.8 %copy-start.1 = (f32[32,2048]{1,0:T(8,128)S(1)}, f32[32,2048]{1,0:T(8,128)}, u32[]{:S(2)}) copy-start(f32[32,2048]{1,0:T(8,128)} %param.26) | copy-start | bytes 786436
  7.2 76.7 %all-gather.6.cloned.1.call-start = ((), (), s32[]{:S(2)}) async-start(), calls=%async_computation.11 | async-start | bytes 5308416 | tf_op jit(solution)/shard_map/all_gather | solution.py:77
  9.2 95.9 %all-gather.8.cloned.1.call-start = ((), (), s32[]{:S(2)}) async-start(), calls=%async_computation.12 | async-start | bytes 4718592 | tf_op jit(solution)/shard_map/all_gather | solution.py:78
  11.1 123.8 %all-gather.10.cloned.1.call-start = ((), (), s32[]{:S(2)}) async-start(), calls=%async_computation.13 | async-start | bytes 2949120 | tf_op jit(solution)/shard_map/all_gather | solution.py:79
  62.1 21.6 %all-to-all-start = ((f32[32,32,128]{2,1,0:T(8,128)}), f32[32,32,128]{2,1,0:T(8,128)S(1)}, u32[]{:S(2)}, u32[]{:S(2)}) async-start(f32[32,32,128]{2,1,0:T(8,128)} %bitcast.45), calls=%async_computation | async-start | bytes 1048576 | tf_op jit(solution)/shard_map/all_to_all | solution.py:31
  134.9 41.1 %copy-start = (f32[64,10240]{1,0:T(8,128)S(1)}, f32[64,10240]{1,0:T(8,128)}, u32[]{:S(2)}) copy-start(f32[64,10240]{1,0:T(8,128)} %all-gather.10.cloned.1.call-done) | copy-start | bytes 7864324
  139.5 24.0 %all-to-all-start.3 = ((f32[64,8,128]{2,1,0:T(8,128)}), f32[64,8,128]{2,1,0:T(8,128)S(1)}, u32[]{:S(2)}, u32[]{:S(2)}) async-start(f32[64,8,128]{2,1,0:T(8,128)} %all_to_all.56), calls=%async_computation.3 | async-start | bytes 524288 | tf_op jit(solution)/shard_map/all_to_all | solution.py:31
  150.3 82.7 %all-gather.12.cloned.1.call-start = ((), (), s32[]{:S(2)}) async-start(), calls=%async_computation.14 | async-start | bytes 2359296 | tf_op jit(solution)/shard_map/all_gather | solution.py:80
  205.5 16.6 %all-to-all-start.7 = ((f32[32,32,128]{2,1,0:T(8,128)}), f32[32,32,128]{2,1,0:T(8,128)S(1)}, u32[]{:S(2)}, u32[]{:S(2)}) async-start(f32[32,32,128]{2,1,0:T(8,128)} %broadcast_in_dim.89), calls=%async_computation.7 | async-start | bytes 1048576 | tf_op jit(solution)/shard_map/all_to_all | solution.py:31
  229.2 11.3 %all-to-all-start.8 = ((f32[16,32,128]{2,1,0:T(8,128)}), f32[16,32,128]{2,1,0:T(8,128)S(1)}, u32[]{:S(2)}, u32[]{:S(2)}) async-start(f32[16,32,128]{2,1,0:T(8,128)} %broadcast_in_dim.91), calls=%async_computation.8 | async-start | bytes 524288 | tf_op jit(solution)/shard_map/all_to_all | solution.py:31
  247.7 10.5 %all-to-all-start.9 = ((f32[8,16,128]{2,1,0:T(8,128)}), f32[8,16,128]{2,1,0:T(8,128)S(1)}, u32[]{:S(2)}, u32[]{:S(2)}) async-start(f32[8,16,128]{2,1,0:T(8,128)} %broadcast_in_dim.93), calls=%async_computation.9 | async-start | bytes 131072 | tf_op jit(solution)/shard_map/all_to_all | solution.py:31
  258.3 45.9 %copy-start.2 = (f32[16,32]{1,0:T(8,128)S(1)}, f32[16,32]{1,0:T(8,128)}, u32[]{:S(2)}) copy-start(f32[16,32]{1,0:T(8,128)} %param.25) | copy-start | bytes 6148
Sparse Core Ops, SparseCore 0:
  10.1 45.5 all-gather.5
  57.9 41.7 all-gather.7
  101.8 30.8 all-gather.9
  153.0 30.7 all-gather.11

commit v2 on v0

v2 whole, which is shorter than its diff:
```python
import functools

import jax
import jax.numpy as jnp
from jax import lax
from jax.experimental import pallas as pl
from jax.experimental.pallas import tpu as pltpu
from jax.sharding import Mesh, PartitionSpec as P

ROOT_ROWS = 4096
LEVEL1_ROWS = 2048
LEVEL2_ROWS = 2048
LEVEL3_ROWS = 1024
WIDTHS = (ROOT_ROWS, LEVEL1_ROWS, LEVEL2_ROWS, LEVEL3_ROWS)
Y, X, C = 8, 4, 2
XC = X * C
PAIR = 2
LANES = 128
LIMIT = 48 * 2**20
ALL_Y = ("y2", "y1", "y0")
INTERPRET = False


def call(kernel, out_shape, **options):
    limit = options.pop("limit", LIMIT)
    return pl.pallas_call(
        kernel,
        out_shape=out_shape,
        compiler_params=pltpu.CompilerParams(vmem_limit_bytes=limit),
        interpret=INTERPRET,
        **options,
    )


def f32(*shape):
    return jax.ShapeDtypeStruct(shape, jnp.float32)


def exchange(operand, axes):
    flat = operand.reshape(-1, LANES)
    return lax.all_to_all(flat, axes, 0, 0, tiled=True).reshape(operand.shape)


def split3(value):
    high = value.astype(jnp.bfloat16)
    rest = value - high.astype(jnp.float32)
    middle = rest.astype(jnp.bfloat16)
    low = (rest - middle.astype(jnp.float32)).astype(jnp.bfloat16)
    return high, middle, low


def one_hot(index_row, block):
    shape = (LANES, index_row.shape[1])
    rows = lax.broadcasted_iota(jnp.int32, shape, 0) + block * LANES
    return jnp.where(rows == index_row, 1.0, 0.0).astype(jnp.bfloat16)


NT = (((1,), (1,)), ((), ()))
NN = (((1,), (0,)), ((), ()))


def row_dot(matrix, column, vector, first, blocks):
    rows = matrix.shape[0]
    sums = [jnp.zeros((rows, LANES), jnp.float32) for _ in range(PAIR)]
    for block in range(blocks):
        tile = matrix[:, column + block * LANES : column + (block + 1) * LANES]
        for s in range(PAIR):
            at = (first + block) * PAIR + s
            sums[s] = sums[s] + tile * vector[at : at + 1, :]
    return [jnp.sum(value, axis=1, keepdims=True) for value in sums]


def column_dot(matrix, column, blocks, factors, total, fresh):
    rows = matrix.shape[0]
    wide = [jnp.broadcast_to(value, (rows, LANES)) for value in factors]
    for block in range(blocks):
        tile = matrix[:, column + block * LANES : column + (block + 1) * LANES]
        for s in range(PAIR):
            part = jnp.sum((tile * wide[s]).reshape(rows // 8, 8, LANES), axis=0)
            at = block * PAIR + s
            total[at] = jnp.where(fresh, part, total[at] + part)


def forward_kernel(steps, blocks, upper, skip_from, keep, copies, scalars, received, matrix, rest_in, solved, send, rest, vector, total):
    step = pl.program_id(0)

    @pl.when(step == 0)
    def _():
        vector[...] = jnp.sum(received[...], axis=0)

    values = row_dot(matrix, 0, vector, 0, blocks)
    rows = matrix.shape[0]
    for s in range(PAIR):
        solved[s] = jnp.broadcast_to(values[s], (rows, LANES))
    column_dot(matrix, blocks * LANES, upper, values, total, step == 0)

    @pl.when(step == steps - 1)
    def _():
        whole = -jnp.sum(total[...], axis=1)
        if skip_from:
            rest[...] = whole
            size = 2 * upper // skip_from
            at = pl.multiple_of(scalars[0] * size, 8)
            rest[pl.ds(at, size), :] = rest[pl.ds(at, size), :] + vector[2 * blocks :, :]
            whole = rest[...]
        else:
            whole = whole + rest_in[0 : 2 * upper, :]
            rest[...] = whole
        for copy in range(copies):
            send[copy] = whole[2 * keep :, :]


def forward(received, matrix, rest_in, scalars, blocks, keep, copies, first):
    rows, width = matrix.shape
    upper = width // LANES - blocks
    steps = 4
    chunk = rows // steps
    kernel = functools.partial(forward_kernel, steps, blocks, upper, first, keep, copies)
    whole = lambda array: pl.BlockSpec(array.shape, lambda i: (0,) * array.ndim)
    send_rows = 2 * (upper - keep)
    return call(
        kernel,
        (f32(PAIR, rows, LANES), f32(copies, send_rows, LANES), f32(2 * upper, LANES)),
        grid=(steps,),
        in_specs=[
            pl.BlockSpec(memory_space=pltpu.SMEM),
            whole(received),
            pl.BlockSpec((chunk, width), lambda i: (i, 0)),
            whole(rest_in),
        ],
        out_specs=(
            pl.BlockSpec((PAIR, chunk, LANES), lambda i: (0, i, 0)),
            pl.BlockSpec((copies, send_rows, LANES), lambda i: (0, 0, 0)),
            pl.BlockSpec((2 * upper, LANES), lambda i: (0, 0)),
        ),
        scratch_shapes=[pltpu.VMEM(received.shape[1:], jnp.float32), pltpu.VMEM((2 * upper, 8, LANES), jnp.float32)],
    )(scalars, received, matrix, rest_in)


def backward_kernel(steps, blocks, upper, known_blocks, copies, received, matrix, solved, *refs):
    known, (send, newest, total) = refs[: len(known_blocks)], refs[len(known_blocks) :]
    step = pl.program_id(0)

    @pl.when(step == 0)
    def _():
        newest[...] = jnp.sum(received[...], axis=0)

    values = [solved[s][:, 0:1] for s in range(PAIR)]
    column = blocks * LANES
    for ref, count in list(zip(known, known_blocks)) + [(newest, upper - sum(known_blocks))]:
        part = row_dot(matrix, column, ref, 0, count)
        values = [values[s] - part[s] for s in range(PAIR)]
        column += count * LANES
    column_dot(matrix, 0, blocks, values, total, step == 0)

    @pl.when(step == steps - 1)
    def _():
        whole = jnp.sum(total[...], axis=1)
        for copy in range(copies):
            send[copy] = whole


def backward(received, matrix, solved, known, blocks, copies):
    rows, width = matrix.shape
    upper = width // LANES - blocks
    steps = 4
    chunk = rows // steps
    counts = [array.shape[0] // PAIR for array in known]
    kernel = functools.partial(backward_kernel, steps, blocks, upper, counts, copies)
    whole = lambda array: pl.BlockSpec(array.shape, lambda i: (0,) * array.ndim)
    return call(
        kernel,
        (f32(copies, 2 * blocks, LANES), f32(*received.shape[1:])),
        grid=(steps,),
        in_specs=[
            whole(received),
            pl.BlockSpec((chunk, width), lambda i: (i, 0)),
            pl.BlockSpec((PAIR, chunk, LANES), lambda i: (0, i, 0)),
        ]
        + [whole(array) for array in known],
        out_specs=(
            pl.BlockSpec((copies, 2 * blocks, LANES), lambda i: (0, 0, 0)),
            pl.BlockSpec(received.shape[1:], lambda i: (0, 0)),
        ),
        scratch_shapes=[pltpu.VMEM((2 * blocks, 8, LANES), jnp.float32)],
    )(received, matrix, solved, *known)


def root_kernel(steps, blocks, copies, vector, matrix, send, total):
    step = pl.program_id(0)
    values = row_dot(matrix, 0, vector, 0, blocks)
    column_dot(matrix, 0, blocks, values, total, step == 0)

    @pl.when(step == steps - 1)
    def _():
        whole = jnp.sum(total[...], axis=1)
        for copy in range(copies):
            send[copy] = whole


def root(vector, matrix, copies):
    rows, width = matrix.shape
    blocks = width // LANES
    steps = 2
    chunk = rows // steps
    return call(
        functools.partial(root_kernel, steps, blocks, copies),
        f32(copies, 2 * blocks, LANES),
        grid=(steps,),
        in_specs=[pl.BlockSpec(vector.shape, lambda i: (0, 0)), pl.BlockSpec((chunk, width), lambda i: (i, 0))],
        out_specs=pl.BlockSpec((copies, 2 * blocks, LANES), lambda i: (0, 0, 0)),
        scratch_shapes=[pltpu.VMEM((2 * blocks, 8, LANES), jnp.float32)],
    )(vector, matrix)


def sum_kernel(copies, received, send):
    whole = jnp.sum(received[...], axis=0)
    for copy in range(copies):
        send[copy] = whole


def sum_and_copy(received, copies):
    return call(functools.partial(sum_kernel, copies), f32(copies, *received.shape[1:]))(received)


def first_kernel(columns, depth, scalars, small, coupling, index, send, terms, path):
    z, core, x = scalars[0], scalars[1], scalars[2]
    upper = sum(WIDTHS[:3]) // LANES
    count = upper + WIDTHS[3] // LANES
    rows = coupling.shape[1]
    half = pl.multiple_of(core * 8, 8)
    parts = [small[other, pl.ds(half, 8), :] for other in range(C)]
    update = None
    for other in range(C):
        product = lax.dot_general(
            parts[other][:, :rows], coupling[other], NN, precision=lax.Precision.HIGHEST, preferred_element_type=jnp.float32
        )
        update = product if update is None else update + product
    pieces = split3(update)
    terms[:, columns:] = jnp.zeros((32, terms.shape[1] - columns), jnp.bfloat16)
    terms[:, :columns] = jnp.concatenate([*pieces, jnp.zeros_like(pieces[0])], axis=0)

    def expand(block, carry):
        at = pl.multiple_of(scalars[8 + block] * LANES, LANES)
        selector = one_hot(index[0:1, pl.ds(at, 2 * LANES)], block)
        out = lax.dot_general(terms[:, pl.ds(at, 2 * LANES)], selector, NT, preferred_element_type=jnp.float32)
        path[block] = -(out[0:8] + out[8:16] + out[16:24])
        return carry

    lax.fori_loop(0, count, expand, 0, unroll=4)

    lane = lax.broadcasted_iota(jnp.int32, (8, LANES), 1)
    start = 0
    source = rows
    for height in range(4):
        width = 8 if height < 2 else 16
        for other in range(C):
            offset = z * width
            block = start
            if height < 3:
                block = block + scalars[3 + height] * (XC * depth * width // LANES)
            if width == 8:
                offset = offset + other * 64
                block = block + x
            else:
                block = block + x * 2 + other
            moved = pltpu.roll(parts[other], lax.rem(offset - source + LANES, LANES), 1)
            kept = jnp.where((lane >= offset) & (lane < offset + width), moved, 0.0)
            path[block] = path[block] + kept
        start += WIDTHS[height] // LANES
        source += width

    lower = WIDTHS[3] // LANES
    mine = upper // depth
    for block in range(upper):
        value = path[block]
        for dest in range(X):
            at = 2 * lower + 2 * (block % mine)
            send[dest * depth + block // mine, at : at + 2, :] = value[2 * dest : 2 * dest + 2, :]
    for dest in range(X):
        value = jnp.concatenate([path[upper + block][2 * dest : 2 * dest + 2, :] for block in range(lower)], axis=0)
        for other in range(depth):
            send[dest * depth + other, 0 : 2 * lower, :] = value


def first(small, coupling, index, scalars, depth):
    columns = coupling.shape[2]
    upper = sum(WIDTHS[:3]) // LANES
    lower = WIDTHS[3] // LANES
    vmem = pl.BlockSpec(memory_space=pltpu.VMEM)
    return call(
        functools.partial(first_kernel, columns, depth),
        f32(X * depth, 2 * (lower + upper // depth), LANES),
        in_specs=[pl.BlockSpec(memory_space=pltpu.SMEM), vmem, vmem, vmem],
        scratch_shapes=[
            pltpu.VMEM((32, columns + 2 * LANES), jnp.bfloat16),
            pltpu.VMEM((upper + lower, 8, LANES), jnp.float32),
        ],
    )(scalars, small, coupling, index)


def last_kernel(columns, counts, scalars, received, x0, x1, x2, coupling, index, send, x3, terms, chosen):
    x3[...] = jnp.sum(received[...], axis=0)
    blocks = sum(counts)
    at = 0
    for ref, count in zip((x0, x1, x2, x3), counts):
        pieces = split3(ref[...].reshape(count, PAIR, LANES))
        stacked = jnp.concatenate([*pieces, jnp.zeros_like(pieces[0])], axis=1)
        terms[at : at + count] = stacked.astype(jnp.float32)
        at += count
    chosen[...] = jnp.zeros_like(chosen)
    for half in range(2):

        def pick(block, carry):
            at = pl.multiple_of(scalars[8 + half * blocks + block] * LANES, LANES)
            selector = one_hot(index[half : half + 1, pl.ds(at, 2 * LANES)], block)
            out = lax.dot_general(
                terms[block].astype(jnp.bfloat16), selector, NN, preferred_element_type=jnp.float32
            )
            chosen[half, :, pl.ds(at, 2 * LANES)] = chosen[half, :, pl.ds(at, 2 * LANES)] + out
            return carry

        lax.fori_loop(0, blocks, pick, 0, unroll=4)
    rows = coupling.shape[0] // 2
    handed = []
    for half in range(2):
        value = chosen[half, 0:2, :columns] + chosen[half, 2:4, :columns] + chosen[half, 4:6, :columns]
        handed.append(
            lax.dot_general(
                value,
                coupling[half * rows : (half + 1) * rows, :],
                NT,
                precision=lax.Precision.HIGHEST,
                preferred_element_type=jnp.float32,
            )
        )
    send[...] = jnp.zeros_like(send)
    for dest in range(XC):
        core, x = dest // X, dest % X
        for level, ref in enumerate((x0, x1, x2, x3)):
            block = x if level < 2 else x * 2 + core
            if level < 3:
                block = block + scalars[level] * (counts[level] // (Y // 2**level))
            send[dest, 2 * level : 2 * level + 2, :] = ref[pl.ds(block * 2, 2), :]
        send[dest, 8:10, :] = handed[x // 2]


def last(received, known, coupling, index, scalars):
    columns = coupling.shape[1]
    counts = [width // LANES for width in WIDTHS]
    vmem = pl.BlockSpec(memory_space=pltpu.VMEM)
    return call(
        functools.partial(last_kernel, columns, counts),
        f32(XC, 16, LANES),
        in_specs=[pl.BlockSpec(memory_space=pltpu.SMEM)] + [vmem] * 6,
        scratch_shapes=[
            pltpu.VMEM(received.shape[1:], jnp.float32),
            pltpu.VMEM((sum(counts), 8, LANES), jnp.float32),
            pltpu.VMEM((2, 8, columns + 2 * LANES), jnp.float32),
        ],
    )(scalars, received, *known, coupling, index)


def finish_kernel(scalars, received, values, out0, out1, out2, out3, handed):
    z, core = scalars[0], scalars[1]
    offsets = (core * 64 + z * 8, core * 64 + z * 8, z * 16, z * 16, scalars[2] * values.shape[1])
    for level, ref in enumerate((out0, out1, out2, out3, handed)):
        value = jnp.concatenate([received[source, 2 * level : 2 * level + 2, :] for source in range(XC)], axis=0)
        moved = pltpu.roll(value, lax.rem(LANES - offsets[level], LANES), 1)[:, : ref.shape[1]]
        ref[...] = values[...] - moved if level == 4 else moved


def finish(received, values, scalars, widths):
    vmem = pl.BlockSpec(memory_space=pltpu.VMEM)
    shapes = tuple(f32(XC * PAIR, width) for width in widths) + (f32(*values.shape),)
    return call(
        finish_kernel, shapes, in_specs=[pl.BlockSpec(memory_space=pltpu.SMEM), vmem, vmem]
    )(scalars, received, values)


def body(
    rhs_root,
    rhs_level1,
    rhs_level2,
    rhs_level3,
    inv_root,
    inv_level1,
    inv_level2,
    inv_level3,
    cross_level1,
    cross_level2,
    cross_level3,
    subtree_values,
    coupling,
    coupled_rows,
):
    depth = lax.axis_size("z")
    y = (lax.axis_index("y2") * 2 + lax.axis_index("y1")) * 2 + lax.axis_index("y0")
    x, c, z = lax.axis_index("x"), lax.axis_index("c"), lax.axis_index("z")
    counts = [width // LANES for width in WIDTHS]
    blocks = sum(counts)

    def gathered(parts):
        whole = parts[0] if len(parts) == 1 else jnp.concatenate(parts, axis=1)
        return lax.all_gather(whole, ("x", "c"), axis=0, tiled=True)

    matrix3 = gathered([inv_level3, cross_level3])
    matrix2 = gathered([inv_level2, cross_level2])
    matrix1 = gathered([inv_level1, cross_level1])
    matrix0 = gathered([inv_root])
    all_coupling = gathered([coupling])

    rhs_parts = [rhs_root, rhs_level1, rhs_level2, rhs_level3]
    small = jnp.concatenate([subtree_values] + rhs_parts, axis=1)
    small = jnp.pad(small, ((0, 0), (0, LANES - small.shape[1])))
    both_small = lax.all_gather(small, "c", axis=0, tiled=False)
    both_coupling = lax.all_gather(coupling, "c", axis=0, tiled=False)

    both_indices = lax.dynamic_slice_in_dim(coupled_rows, y * 2, 2, 0)
    edges = jnp.arange(blocks, dtype=jnp.int32) * LANES
    windows = jnp.sum((both_indices[:, None, :] < edges[None, :, None]).astype(jnp.int32), axis=2) // LANES
    both_indices = jnp.pad(both_indices, ((0, 0), (0, 2 * LANES)), constant_values=-1)
    own_windows = lax.dynamic_index_in_dim(windows, x // 2, 0, keepdims=False)
    own_indices = lax.dynamic_slice_in_dim(both_indices, x // 2, 1, 0)

    def scalars(head, *tails):
        head = jnp.stack([jnp.asarray(value, jnp.int32) for value in head] + [jnp.int32(0)] * (8 - len(head)))
        return jnp.concatenate([head, *tails])

    places = scalars([z, c, x, y, y % 4, y % 2], own_windows)
    send = first(both_small, both_coupling, own_indices, places, depth)
    received = exchange(send, ("x", "z"))
    solved3, send, rest = forward(
        received, matrix3, jnp.zeros((8, LANES), jnp.float32), places, counts[3], counts[0] + counts[1], 2 * depth, depth
    )
    received = exchange(send, ("y0", "z"))
    solved2, send, rest = forward(received, matrix2, rest, places, counts[2], counts[0], 4 * depth, 0)
    received = exchange(send, ("y1", "y0", "z"))
    solved1, send, rest = forward(received, matrix1, rest, places, counts[1], 0, Y, 0)

    def sum_root(copies):
        received = exchange(copies.reshape(Y * depth, -1, LANES), ALL_Y + ("z",))
        return exchange(sum_and_copy(received, depth), ("z",))

    target = sum_root(send).reshape(-1, LANES)
    received = sum_root(root(target, matrix0, Y)).reshape(1, -1, LANES)
    send, x0 = backward(received, matrix1, solved1, [], counts[1], 4 * depth)
    received = exchange(send, ("y1", "y0", "z"))
    send, x1 = backward(received, matrix2, solved2, [x0], counts[2], 2 * depth)
    received = exchange(send, ("y0", "z"))
    send, x2 = backward(received, matrix3, solved3, [x0, x1], counts[3], depth)
    received = exchange(send, ("z",))
    heads = scalars([y, y % 4, y % 2], windows.reshape(-1))
    send = last(received, [x0, x1, x2], all_coupling, both_indices, heads)
    received = exchange(send, ("c", "x"))
    ends = scalars([z, c, (x % 2) * 2 + c])
    return finish(received, subtree_values, ends, [part.shape[1] for part in rhs_parts])


def solution(mesh):
    shape = (2, 2, 2, X, C, mesh.shape["sep"])
    fine = Mesh(mesh.devices.reshape(shape), ("y2", "y1", "y0", "x", "c", "z"))
    every = ("y2", "y1", "y0", "x", "c", "z")
    columns, rows = P(None, every), P(every, None)
    in_specs = (columns,) * 4 + (rows,) * 7 + (columns, rows, P())
    return jax.shard_map(body, mesh=fine, in_specs=in_specs, out_specs=(columns,) * 5, check_vma=False)
```

time: 2210 us -> 285 us (0.13)
  waiting for transfers between devices: 2130 us -> 82.5 us
  blocking collectives: 0 us -> 101 us
  starting transfers between devices: 0.51 us -> 40.7 us
  Pallas kernels: 0 us -> 28.6 us
    psum x8 -> x0, waiting for transfers between devices: 2130 us -> none  [whole_sum(): return lax.psum(operand, ('leaf', 'sep'))]
    all_to_all x0 -> x5, blocking collectives: none -> 90.3 us  [exchange(): return lax.all_to_all(flat, axes, 0, 0, tiled=True).reshape(operand.shape)]
    all_gather x0 -> x5, waiting for transfers between devices: none -> 55.2 us  [gathered(): return lax.all_gather(whole, ('x', 'c'), axis=0, tiled=True)]
    all_to_all x0 -> x6, starting transfers between devices: none -> 40.5 us  [exchange(): return lax.all_to_all(flat, axes, 0, 0, tiled=True).reshape(operand.shape)]
    pallas_call x0 -> x12, Pallas kernels: none -> 28.6 us  [the longest x1 8.96 us: last(): call(functools.partial(last_kernel, columns, counts), f32(XC, 16, LANES),...]
    all_to_all x0 -> x6, waiting for transfers between devices: none -> 26.2 us  [exchange(): return lax.all_to_all(flat, axes, 0, 0, tiled=True).reshape(operand.shape)]
  transfers between devices with their start and end apart: 8 -> 11, of which waited for: 8 -> 7; matrix products, arithmetic and copies ran while one was open for 1% -> 1% of each run, Pallas kernels for 0% -> 6%
where the time goes in v2:
time: 285 us; the launch traced here: 284 us
  blocking collectives  101 us (35%)
  waiting for transfers between devices  82.5 us (29%)
  starting transfers between devices  40.7 us (14%)
  Pallas kernels  28.6 us (10%)
  between operations  14.1 us (5%)
  local copies, waits for them, and re-layouts  13.1 us (5%)
  other arithmetic  3.85 us (1%)
    all_to_all x5, blocking collectives, exchange(): return lax.all_to_all(flat, axes, 0, 0, tiled=True).reshape(operand.shape)  90.3 us
    all_gather x5, waiting for transfers between devices, gathered(): return lax.all_gather(whole, ('x', 'c'), axis=0, tiled=True)  55.2 us
    all_to_all x6, starting transfers between devices, exchange(): return lax.all_to_all(flat, axes, 0, 0, tiled=True).reshape(operand.shape)  40.5 us
    all_to_all x6, waiting for transfers between devices, exchange(): return lax.all_to_all(flat, axes, 0, 0, tiled=True).reshape(operand.shape)  26.2 us
    unnamed x40, local copies, waits for them, and re-layouts  11.3 us
    pallas_call x1, Pallas kernels, last(): call(functools.partial(last_kernel, columns, counts), f32(XC, 16, LANES),...  8.96 us
    all_gather x1, blocking collectives, body(): both_small = lax.all_gather(small, 'c', axis=0, tiled=False)  8.37 us
    pallas_call x3, Pallas kernels, forward(): call(kernel, (f32(PAIR, rows, LANES), f32(copies, send_rows, LANES), f32(...  7.09 us
  transfers between devices with their start and end apart: 11, of which 7 were waited for; matrix products, arithmetic and copies ran while one was open for 1% of the time, Pallas kernels for 6%

profile of v2, /device:TPU:1, one launch (start us, length us, event | category | flops | bytes accessed | tf_op | source)
XLA Modules:
  0.0 283.7 jit_solution(9243660863218344808)
XLA Ops:
  7.2 0.0 copy-start
  7.2 0.0 all-gather.8.cloned.1.call-start
  7.3 2.0 pad_maximum_fusion
  9.3 0.0 copy-start.16
  9.3 0.0 all-gather.8.cloned.1.call-update
  9.3 0.0 all-gather.10.cloned.1.call-start
  9.4 0.9 pad_maximum_fusion.1
  10.2 0.0 all-gather.10.cloned.1.call-update
  10.3 0.0 all-gather.12.cloned.1.call-start
  10.3 0.7 pad_maximum_fusion.2
  11.0 0.0 all-gather.12.cloned.1.call-update
  11.1 0.0 all-gather.14.cloned.1.call-start
  11.1 0.5 all-gather.14.cloned.1.call-update
  11.7 0.3 convert_reduce_fusion
  12.1 0.1 copy.23
  12.2 0.1 copy.24
  12.2 0.1 concatenate.20
  12.3 8.4 %all-gather = f32[32,128]{1,0:T(8,128)S(1)} all-gather(f32[16,128]{1,0:T(8,128)S(1)} %pad.8), channel_id=2, replica_groups=mesh['y2'=2,'y1'=2,'y0'=2,'x'=4,'c'=2,'z'=8] {'c'}, dimensions={0}, use_global_device_ids=true | all-gather | bytes 24576 | tf_op jit(solution)/shard_map/all_gather | solution.py:416
  20.7 0.1 concatenate.19.scalars
  20.8 2.2 all-gather.1
  23.0 4.8 %shard_map.173 = f32[32,32,128]{2,1,0:T(8,128)S(1)} custom-call(s32[80]{0:T(128)S(1)} %concatenate.19.scalars, f32[2,16,128]{2,1,0:T(8,128)S(1)} %bitcast.20, f32[2,32,2048]{2,1,0:T(8,128)S(1)} %bitcast.15, s32[1,2304]{1,0:T(1,128)S(1)} %constant_dynamic-slice_fusion.index), custom_call_target="tpu_custom_call" | custom-call | tf_op jit(solution)/shard_map/pallas_call | solution.py:291
  27.8 21.4 %all_to_all.74.received = f32[32,32,128]{2,1,0:T(8,128)S(1)} all-to-all(f32[32,32,128]{2,1,0:T(8,128)S(1)} %shard_map.173), channel_id=1, replica_groups=mesh['y2'=2,'y1'=2,'y0'=2,'x'=4,'c'=2,'z'=8] {'x','z'}, dimensions={0} | all-to-all | bytes 1048576 | tf_op jit(solution)/shard_map/all_to_all | solution.py:41
  49.2 12.2 %all-gather.8.cloned.1.call-done.matrix = f32[128,9216]{1,0:T(8,128)} async-done(((f32[16,9216]{1,0:T(8,128)}), f32[128,9216]{1,0:T(8,128)}) %all-gather.8.cloned.1.call-update) | async-done | bytes 4718608 | tf_op jit(solution)/shard_map/all_gather | solution.py:405
  61.4 2.3 copy-done.1
  63.7 2.6 shard_map.174
  66.3 8.1 %all-to-all-start.1 = ((f32[16,32,128]{2,1,0:T(8,128)}), f32[16,32,128]{2,1,0:T(8,128)S(1)}, u32[]{:S(2)}, u32[]{:S(2)}) async-start(f32[16,32,128]{2,1,0:T(8,128)} %get-tuple-element.19), calls=%async_computation.1 | async-start | bytes 524288 | tf_op jit(solution)/shard_map/all_to_all | solution.py:41
  74.4 26.6 %all-gather.10.cloned.1.call-done.matrix = f32[128,8192]{1,0:T(8,128)} async-done(((f32[16,8192]{1,0:T(8,128)}), f32[128,8192]{1,0:T(8,128)}) %all-gather.10.cloned.1.call-update) | async-done | bytes 4194320 | tf_op jit(solution)/shard_map/all_gather | solution.py:405
  101.0 2.2 copy-done.3
  103.2 2.5 shard_map.175
  105.7 10.3 %all-to-all-start.2 = ((f32[32,32,128]{2,1,0:T(8,128)}), f32[32,32,128]{2,1,0:T(8,128)S(1)}, u32[]{:S(2)}, u32[]{:S(2)}) async-start(f32[32,32,128]{2,1,0:T(8,128)} %get-tuple-element.21), calls=%async_computation.2 | async-start | bytes 1048576 | tf_op jit(solution)/shard_map/all_to_all | solution.py:41
  116.0 0.0 all-gather.16.cloned.1.call-start
  116.0 0.5 all-gather.16.cloned.1.call-update
  116.6 16.4 %all-gather.12.cloned.1.call-done.matrix = f32[64,6144]{1,0:T(8,128)} async-done(((f32[8,6144]{1,0:T(8,128)}), f32[64,6144]{1,0:T(8,128)}) %all-gather.12.cloned.1.call-update) | async-done | bytes 1572880 | tf_op jit(solution)/shard_map/all_gather | solution.py:405
  133.0 1.4 copy-done.5
  134.4 2.0 shard_map.176
  136.4 26.2 %all_to_all.75.received = f32[64,8,128]{2,1,0:T(8,128)S(1)} all-to-all(f32[64,8,128]{2,1,0:T(8,128)S(1)} %bitcast.17), channel_id=1, replica_groups=mesh['y2'=2,'y1'=2,'y0'=2,'x'=4,'c'=2,'z'=8] {'y2','y1','y0','z'}, dimensions={0} | all-to-all | bytes 524288 | tf_op jit(solution)/shard_map/all_to_all | solution.py:41
  162.5 0.7 shard_map.177
  163.2 3.6 %all-to-all-start.4 = ((f32[8,8,128]{2,1,0:T(8,128)}), f32[8,8,128]{2,1,0:T(8,128)S(1)}, u32[]{:S(2)}, u32[]{:S(2)}) async-start(f32[8,8,128]{2,1,0:T(8,128)} %shard_map.177), calls=%async_computation.4 | async-start | bytes 65536 | tf_op jit(solution)/shard_map/all_to_all | solution.py:41
  166.8 0.0 all-gather.14.cloned.1.call-done.matrix
  166.9 6.9 %all-to-all-done.4 = f32[8,8,128]{2,1,0:T(8,128)S(1)} async-done(((f32[8,8,128]{2,1,0:T(8,128)}), f32[8,8,128]{2,1,0:T(8,128)S(1)}, u32[]{:S(2)}, u32[]{:S(2)}) %all-to-all-start.4) | async-done | bytes 32800 | tf_op jit(solution)/shard_map/all_to_all | solution.py:41
  173.7 1.2 copy-done.8
  174.9 0.5 shard_map.178
  175.5 17.5 %all_to_all.76.received = f32[64,8,128]{2,1,0:T(8,128)S(1)} all-to-all(f32[64,8,128]{2,1,0:T(8,128)S(1)} %bitcast.16), channel_id=1, replica_groups=mesh['y2'=2,'y1'=2,'y0'=2,'x'=4,'c'=2,'z'=8] {'y2','y1','y0','z'}, dimensions={0} | all-to-all | bytes 524288 | tf_op jit(solution)/shard_map/all_to_all | solution.py:41
  193.0 0.1 shard_map.179
  193.1 9.5 %all_to_all.77 = f32[8,8,128]{2,1,0:T(8,128)S(1)} all-to-all(f32[8,8,128]{2,1,0:T(8,128)S(1)} %shard_map.179), channel_id=1, replica_groups=mesh['y2'=2,'y1'=2,'y0'=2,'x'=4,'c'=2,'z'=8] {'z'}, dimensions={0} | all-to-all | bytes 65536 | tf_op jit(solution)/shard_map/all_to_all | solution.py:41
  202.6 1.1 shard_map.180
  203.7 15.7 %all_to_all.78.received = f32[32,32,128]{2,1,0:T(8,128)S(1)} all-to-all(f32[32,32,128]{2,1,0:T(8,128)S(1)} %get-tuple-element.25), channel_id=1, replica_groups=mesh['y2'=2,'y1'=2,'y0'=2,'x'=4,'c'=2,'z'=8] {'y1','y0','z'}, dimensions={0} | all-to-all | bytes 1048576 | tf_op jit(solution)/shard_map/all_to_all | solution.py:41
  219.4 2.1 shard_map.181
  221.5 3.5 %all-to-all-start.8 = ((f32[16,32,128]{2,1,0:T(8,128)}), f32[16,32,128]{2,1,0:T(8,128)S(1)}, u32[]{:S(2)}, u32[]{:S(2)}) async-start(f32[16,32,128]{2,1,0:T(8,128)} %get-tuple-element.28), calls=%async_computation.8 | async-start | bytes 524288 | tf_op jit(solution)/shard_map/all_to_all | solution.py:41
  225.0 0.1 reduce_sum.12
  225.1 7.4 %all-to-all-done.8.received = f32[16,32,128]{2,1,0:T(8,128)S(1)} async-done(((f32[16,32,128]{2,1,0:T(8,128)}), f32[16,32,128]{2,1,0:T(8,128)S(1)}, u32[]{:S(2)}, u32[]{:S(2)}) %all-to-all-start.8) | async-done | bytes 262176 | tf_op jit(solution)/shard_map/all_to_all | solution.py:41
  232.6 2.3 copy-done.2
  234.9 2.1 shard_map.182
  237.0 3.3 %all-to-all-start.9 = ((f32[8,16,128]{2,1,0:T(8,128)}), f32[8,16,128]{2,1,0:T(8,128)S(1)}, u32[]{:S(2)}, u32[]{:S(2)}) async-start(f32[8,16,128]{2,1,0:T(8,128)} %get-tuple-element.31), calls=%async_computation.9 | async-start | bytes 131072 | tf_op jit(solution)/shard_map/all_to_all | solution.py:41
  240.4 0.1 concatenate.18.scalars
  240.4 7.0 %all-to-all-done.9.received = f32[8,16,128]{2,1,0:T(8,128)S(1)} async-done(((f32[8,16,128]{2,1,0:T(8,128)}), f32[8,16,128]{2,1,0:T(8,128)S(1)}, u32[]{:S(2)}, u32[]{:S(2)}) %all-to-all-start.9) | async-done | bytes 65568 | tf_op jit(solution)/shard_map/all_to_all | solution.py:41
  247.5 1.6 copy-done.7
  249.1 9.0 %shard_map.183 = f32[8,16,128]{2,1,0:T(8,128)} custom-call(s32[152]{0:T(256)S(1)} %concatenate.18.scalars, f32[8,16,128]{2,1,0:T(8,128)S(1)} %all-to-all-done.9.received, f32[64,128]{1,0:T(8,128)S(1)} %get-tuple-element.27.refs_0_.x0, f32[32,128]{1,0:T(8,128)S(1)} %get-tuple-element.30.refs_1_.x1, f32[32,128]{1,0:T(8,128)S(1)} %get-tuple-element.32.x2, ...), custom_call_target="tpu_custom_call" | custom-call | tf_op jit(solution)/shard_map/pallas_call | solution.py:352
  258.0 11.7 %all-to-all-start.10 = ((f32[8,16,128]{2,1,0:T(8,128)}), f32[8,16,128]{2,1,0:T(8,128)S(1)}, u32[]{:S(2)}, u32[]{:S(2)}) async-start(f32[8,16,128]{2,1,0:T(8,128)} %shard_map.183), calls=%async_computation.10 | async-start | bytes 131072 | tf_op jit(solution)/shard_map/all_to_all | solution.py:41
  269.7 0.1 stack.32.scalars
  269.8 4.9 %all-to-all-done.10.received = f32[8,16,128]{2,1,0:T(8,128)S(1)} async-done(((f32[8,16,128]{2,1,0:T(8,128)}), f32[8,16,128]{2,1,0:T(8,128)S(1)}, u32[]{:S(2)}, u32[]{:S(2)}) %all-to-all-start.10) | async-done | bytes 65568 | tf_op jit(solution)/shard_map/all_to_all | solution.py:41
  274.7 1.2 shard_map.184
  275.9 0.7 copy.25
  276.5 0.7 copy.26
  (44 shorter events, 0.2 us)
Async XLA Ops:
  7.2 4.5 %copy-start = (s32[16,2048]{1,0:T(8,128)S(1)}, s32[16,2048]{1,0:T(8,128)}, u32[]{:S(2)}) copy-start(s32[16,2048]{1,0:T(8,128)} %param.27) | copy-start | bytes 393220
  7.2 2.2 copy-start.11
  7.2 2.2 copy-start.13
  7.2 54.1 %all-gather.8.cloned.1.call-start = ((), (), s32[]{:S(2)}) async-start(), calls=%async_computation.11 | async-start | bytes 5308416 | tf_op jit(solution)/shard_map/all_gather | solution.py:405
  7.2 3.1 %copy-start.12 = (f32[8,4096]{1,0:T(8,128)S(1)}, f32[8,4096]{1,0:T(8,128)}, u32[]{:S(2)}) copy-start(f32[8,4096]{1,0:T(8,128)} %param.22) | copy-start | bytes 393220
  7.3 3.1 %copy-start.14 = (f32[8,2048]{1,0:T(8,128)S(1)}, f32[8,2048]{1,0:T(8,128)}, u32[]{:S(2)}) copy-start(f32[8,2048]{1,0:T(8,128)} %param.19) | copy-start | bytes 196612
  9.2 2.8 copy-start.17
  9.2 2.9 %copy-start.18 = (f32[16,8]{0,1:T(8,128)S(1)}, f32[16,8]{0,1:T(8,128)}, u32[]{:S(2)}) copy-start(f32[16,8]{0,1:T(8,128)} %param.15) | copy-start | bytes 1540
  9.2 3.0 %copy-start.9 = (f32[16,32]{1,0:T(8,128)S(1)}, f32[16,32]{1,0:T(8,128)}, u32[]{:S(2)}) copy-start(f32[16,32]{1,0:T(8,128)} %values.1) | copy-start | bytes 6148
  9.2 3.0 %copy-start.15 = (f32[16,16]{1,0:T(8,128)S(1)}, f32[16,16]{1,0:T(8,128)}, u32[]{:S(2)}) copy-start(f32[16,16]{1,0:T(8,128)} %param.16) | copy-start | bytes 3076
  9.3 3.0 %copy-start.16 = (f32[16,16]{1,0:T(8,128)S(1)}, f32[16,16]{1,0:T(8,128)}, u32[]{:S(2)}) copy-start(f32[16,16]{1,0:T(8,128)} %param.17) | copy-start | bytes 3076
  9.3 11.5 %copy-start.10 = (f32[32,2048]{1,0:T(8,128)S(1)}, f32[32,2048]{1,0:T(8,128)}, u32[]{:S(2)}) copy-start(f32[32,2048]{1,0:T(8,128)} %param.26) | copy-start | bytes 786436
  9.3 91.7 %all-gather.10.cloned.1.call-start = ((), (), s32[]{:S(2)}) async-start(), calls=%async_computation.12 | async-start | bytes 4718592 | tf_op jit(solution)/shard_map/all_gather | solution.py:405
  10.3 122.7 %all-gather.12.cloned.1.call-start = ((), (), s32[]{:S(2)}) async-start(), calls=%async_computation.13 | async-start | bytes 1769472 | tf_op jit(solution)/shard_map/all_gather | solution.py:405
  11.1 155.8 %all-gather.14.cloned.1.call-start = ((), (), s32[]{:S(2)}) async-start(), calls=%async_computation.14 | async-start | bytes 1179648 | tf_op jit(solution)/shard_map/all_gather | solution.py:405
  61.3 2.3 copy-start.1
  66.3 34.7 %all-to-all-start.1 = ((f32[16,32,128]{2,1,0:T(8,128)}), f32[16,32,128]{2,1,0:T(8,128)S(1)}, u32[]{:S(2)}, u32[]{:S(2)}) async-start(f32[16,32,128]{2,1,0:T(8,128)} %get-tuple-element.19), calls=%async_computation.1 | async-start | bytes 524288 | tf_op jit(solution)/shard_map/all_to_all | solution.py:41
  101.0 2.2 copy-start.3
  105.7 27.3 %all-to-all-start.2 = ((f32[32,32,128]{2,1,0:T(8,128)}), f32[32,32,128]{2,1,0:T(8,128)S(1)}, u32[]{:S(2)}, u32[]{:S(2)}) async-start(f32[32,32,128]{2,1,0:T(8,128)} %get-tuple-element.21), calls=%async_computation.2 | async-start | bytes 1048576 | tf_op jit(solution)/shard_map/all_to_all | solution.py:41
  116.0 124.5 %all-gather.16.cloned.1.call-start = ((), (), s32[]{:S(2)}) async-start(), calls=%async_computation.15 | async-start | bytes 2359296 | tf_op jit(solution)/shard_map/all_gather | solution.py:405
  133.0 1.4 copy-start.5
  136.4 66.2 %copy-start.6 = (f32[64,6144]{1,0:T(8,128)S(1)}, f32[64,6144]{1,0:T(8,128)}, u32[]{:S(2)}) copy-start(f32[64,6144]{1,0:T(8,128)} %all-gather.12.cloned.1.call-done.matrix) | copy-start | bytes 4718596
  163.2 10.5 %all-to-all-start.4 = ((f32[8,8,128]{2,1,0:T(8,128)}), f32[8,8,128]{2,1,0:T(8,128)S(1)}, u32[]{:S(2)}, u32[]{:S(2)}) async-start(f32[8,8,128]{2,1,0:T(8,128)} %shard_map.177), calls=%async_computation.4 | async-start | bytes 65536 | tf_op jit(solution)/shard_map/all_to_all | solution.py:41
  173.7 1.2 copy-start.8
  174.9 44.4 %copy-start.4 = (f32[128,8192]{1,0:T(8,128)S(1)}, f32[128,8192]{1,0:T(8,128)}, u32[]{:S(2)}) copy-start(f32[128,8192]{1,0:T(8,128)} %all-gather.10.cloned.1.call-done.matrix) | copy-start | bytes 12582916
  221.5 11.1 %all-to-all-start.8 = ((f32[16,32,128]{2,1,0:T(8,128)}), f32[16,32,128]{2,1,0:T(8,128)S(1)}, u32[]{:S(2)}, u32[]{:S(2)}) async-start(f32[16,32,128]{2,1,0:T(8,128)} %get-tuple-element.28), calls=%async_computation.8 | async-start | bytes 524288 | tf_op jit(solution)/shard_map/all_to_all | solution.py:41
  232.6 2.3 copy-start.2
  237.0 10.5 %all-to-all-start.9 = ((f32[8,16,128]{2,1,0:T(8,128)}), f32[8,16,128]{2,1,0:T(8,128)S(1)}, u32[]{:S(2)}, u32[]{:S(2)}) async-start(f32[8,16,128]{2,1,0:T(8,128)} %get-tuple-element.31), calls=%async_computation.9 | async-start | bytes 131072 | tf_op jit(solution)/shard_map/all_to_all | solution.py:41
  247.5 1.6 copy-start.7
  258.0 16.6 %all-to-all-start.10 = ((f32[8,16,128]{2,1,0:T(8,128)}), f32[8,16,128]{2,1,0:T(8,128)S(1)}, u32[]{:S(2)}, u32[]{:S(2)}) async-start(f32[8,16,128]{2,1,0:T(8,128)} %shard_map.183), calls=%async_computation.10 | async-start | bytes 131072 | tf_op jit(solution)/shard_map/all_to_all | solution.py:41
Sparse Core Ops, SparseCore 0:
  10.2 51.1 all-gather.7
  63.5 37.4 all-gather.9
  103.1 29.8 all-gather.11
  135.0 28.6 all-gather.13
  165.7 30.3 all-gather.15

commit v3 on v2

v3 whole, which is shorter than its diff:
```python
import functools

import jax
import jax.numpy as jnp
from jax import lax
from jax.experimental import pallas as pl
from jax.experimental.pallas import tpu as pltpu
from jax.sharding import Mesh, PartitionSpec as P

ROOT_ROWS = 4096
LEVEL1_ROWS = 2048
LEVEL2_ROWS = 2048
LEVEL3_ROWS = 1024
WIDTHS = (ROOT_ROWS, LEVEL1_ROWS, LEVEL2_ROWS, LEVEL3_ROWS)
Y, X, C = 8, 4, 2
XC = X * C
PAIR = 2
LANES = 128
CHUNK = 32
HBM = pl.BlockSpec(memory_space=pltpu.HBM)
LIMIT = 16 * 2**20
WHOLE = 50 * 2**20
ALL_Y = ("y2", "y1", "y0")
INTERPRET = False
VMEM = pl.BlockSpec(memory_space=pltpu.VMEM)
SMEM = pl.BlockSpec(memory_space=pltpu.SMEM)


def call(kernel, out_shape, **options):
    limit = options.pop("limit", LIMIT)
    return pl.pallas_call(
        kernel,
        out_shape=out_shape,
        compiler_params=pltpu.CompilerParams(vmem_limit_bytes=limit),
        interpret=INTERPRET,
        **options,
    )


def cost(elements):
    return pl.CostEstimate(flops=8 * elements, bytes_accessed=4 * elements, transcendentals=0)


def f32(*shape):
    return jax.ShapeDtypeStruct(shape, jnp.float32)


def exchange(operand, axes):
    flat = operand.reshape(-1, LANES)
    return lax.all_to_all(flat, axes, 0, 0, tiled=True).reshape(operand.shape)


def split3(value):
    high = value.astype(jnp.bfloat16)
    rest = value - high.astype(jnp.float32)
    middle = rest.astype(jnp.bfloat16)
    low = (rest - middle.astype(jnp.float32)).astype(jnp.bfloat16)
    return high, middle, low


def one_hot(index_row, block):
    shape = (LANES, index_row.shape[1])
    rows = lax.broadcasted_iota(jnp.int32, shape, 0) + block * LANES
    return jnp.where(rows == index_row, 1.0, 0.0).astype(jnp.bfloat16)


NT = (((1,), (1,)), ((), ()))
NN = (((1,), (0,)), ((), ()))


def row_dot(matrix, rows, column, vector, first, blocks):
    sums = [jnp.zeros((CHUNK, LANES), jnp.float32) for _ in range(PAIR)]
    for block in range(blocks):
        tile = matrix[rows, column + block * LANES : column + (block + 1) * LANES]
        for s in range(PAIR):
            at = (first + block) * PAIR + s
            sums[s] = sums[s] + tile * vector[at : at + 1, :]
    return [jnp.sum(value, axis=1, keepdims=True) for value in sums]


def column_dot(matrix, rows, column, blocks, factors, total):
    wide = [jnp.broadcast_to(value, (CHUNK, LANES)) for value in factors]
    for block in range(blocks):
        tile = matrix[rows, column + block * LANES : column + (block + 1) * LANES]
        for s in range(PAIR):
            part = jnp.sum((tile * wide[s]).reshape(CHUNK // 8, 8, LANES), axis=0)
            at = block * PAIR + s
            total[at] = total[at] + part


def chunk_copies(matrices, buffer, ready):
    copies = []
    for number, matrix in enumerate(matrices):
        count = matrix.shape[0] // CHUNK
        for chunk in range(count):
            place = number * count + chunk
            columns = pl.ds(0, buffer.shape[1])
            source = matrix.at[pl.ds(chunk * CHUNK, CHUNK), columns]
            copies.append(pltpu.make_async_copy(source, buffer.at[pl.ds(place * CHUNK, CHUNK), columns], ready.at[place]))
    for copy in copies:
        copy.start()
    return copies


def each_chunk(copies, step):
    for place, copy in enumerate(copies):
        copy.wait()
        step(pl.ds(place * CHUNK, CHUNK))


def chunk_buffers(matrices, width):
    rows = 2 * matrices[0].shape[0]
    return [pltpu.VMEM((rows, width), jnp.float32), pltpu.SemaphoreType.DMA((rows // CHUNK,))]


def forward_kernel(blocks, upper, depth, keep, scalars, received, own, other, rest_in, solved, send, rest, vector, total, buffer, ready):
    copies = chunk_copies((own, other), buffer, ready)
    vector[...] = jnp.sum(received[...], axis=0)
    total[...] = jnp.zeros_like(total)

    def step(rows):
        values = row_dot(buffer, rows, 0, vector, 0, blocks)
        for s in range(PAIR):
            solved[s, rows, :] = jnp.broadcast_to(values[s], (CHUNK, LANES))
        column_dot(buffer, rows, blocks * LANES, upper, values, total)

    each_chunk(copies, step)
    whole = -jnp.sum(total[...], axis=1)
    if depth:
        rest[...] = whole
        size = 2 * upper // depth
        at = pl.multiple_of(scalars[0] * size, 8)
        rest[pl.ds(at, size), :] = rest[pl.ds(at, size), :] + vector[2 * blocks :, :]
        whole = rest[...]
    else:
        whole = whole + rest_in[0 : 2 * upper, :]
        rest[...] = whole
    for copy in range(send.shape[0]):
        send[copy] = whole[2 * keep :, :]


def forward(received, matrices, rest_in, scalars, blocks, upper, keep, copies, depth):
    rows = matrices[0].shape[0]
    width = upper * LANES + blocks * LANES
    return call(
        functools.partial(forward_kernel, blocks, upper, depth, keep),
        (f32(PAIR, 2 * rows, LANES), f32(copies, 2 * (upper - keep), LANES), f32(2 * upper, LANES)),
        in_specs=[SMEM, VMEM, HBM, HBM, VMEM],
        out_specs=(VMEM,) * 3,
        scratch_shapes=[pltpu.VMEM(received.shape[1:], jnp.float32), pltpu.VMEM((2 * upper, 8, LANES), jnp.float32)]
        + chunk_buffers(matrices, width),
        cost_estimate=cost(2 * rows * width),
        limit=WHOLE,
    )(scalars, received, *matrices, rest_in)


def backward_kernel(blocks, known_blocks, received, own, other, solved, *refs):
    known, (send, newest, total, buffer, ready) = refs[: len(known_blocks) - 1], refs[len(known_blocks) - 1 :]
    copies = chunk_copies((own, other), buffer, ready)
    newest[...] = jnp.sum(received[...], axis=0)
    total[...] = jnp.zeros_like(total)

    def step(rows):
        values = [solved[s, rows, 0:1] for s in range(PAIR)]
        column = blocks * LANES
        for ref, count in zip((*known, newest), known_blocks):
            part = row_dot(buffer, rows, column, ref, 0, count)
            values = [values[s] - part[s] for s in range(PAIR)]
            column += count * LANES
        column_dot(buffer, rows, 0, blocks, values, total)

    each_chunk(copies, step)
    whole = jnp.sum(total[...], axis=1)
    for copy in range(send.shape[0]):
        send[copy] = whole


def backward(received, matrices, solved, known, blocks, copies):
    rows = matrices[0].shape[0]
    counts = [array.shape[0] // PAIR for array in known] + [received.shape[1] // PAIR]
    width = (blocks + sum(counts)) * LANES
    return call(
        functools.partial(backward_kernel, blocks, counts),
        (f32(copies, 2 * blocks, LANES), f32(*received.shape[1:])),
        in_specs=[VMEM, HBM, HBM, VMEM] + [VMEM] * len(known),
        out_specs=(VMEM,) * 2,
        scratch_shapes=[pltpu.VMEM((2 * blocks, 8, LANES), jnp.float32)] + chunk_buffers(matrices, width),
        cost_estimate=cost(2 * rows * width),
        limit=WHOLE,
    )(received, *matrices, solved, *known)


def root_kernel(column, blocks, vector, own, other, send, total, buffer, ready):
    copies = chunk_copies((own.at[:, column:], other.at[:, column:]), buffer, ready)
    total[...] = jnp.zeros_like(total)

    def step(rows):
        values = row_dot(buffer, rows, 0, vector, 0, blocks)
        column_dot(buffer, rows, 0, blocks, values, total)

    each_chunk(copies, step)
    whole = jnp.sum(total[...], axis=1)
    for copy in range(send.shape[0]):
        send[copy] = whole


def root(vector, matrices, column, copies):
    rows = matrices[0].shape[0]
    blocks = vector.shape[0] // PAIR
    return call(
        functools.partial(root_kernel, column, blocks),
        f32(copies, 2 * blocks, LANES),
        in_specs=[VMEM, HBM, HBM],
        out_specs=VMEM,
        scratch_shapes=[pltpu.VMEM((2 * blocks, 8, LANES), jnp.float32)] + chunk_buffers(matrices, blocks * LANES),
        cost_estimate=cost(2 * rows * blocks * LANES),
        limit=WHOLE,
    )(vector, *matrices)


def sum_kernel(copies, received, send):
    whole = jnp.sum(received[...], axis=0)
    for copy in range(copies):
        send[copy] = whole


def sum_and_copy(received, copies):
    return call(functools.partial(sum_kernel, copies), f32(copies, *received.shape[1:]))(received)


def first_kernel(depth, scalars, small, coupling, index, send, terms, path):
    z, core, x = scalars[0], scalars[1], scalars[2]
    upper = sum(WIDTHS[:3]) // LANES
    count = upper + WIDTHS[3] // LANES
    rows, columns = coupling.shape[1:]
    half = pl.multiple_of(core * 8, 8)
    parts = [small[other, pl.ds(half, 8), :] for other in range(C)]
    update = None
    for other in range(C):
        product = lax.dot_general(
            parts[other][:, :rows], coupling[other], NN, precision=lax.Precision.HIGHEST, preferred_element_type=jnp.float32
        )
        update = product if update is None else update + product
    pieces = split3(update)
    terms[:, columns:] = jnp.zeros((32, terms.shape[1] - columns), jnp.bfloat16)
    terms[:, :columns] = jnp.concatenate([*pieces, jnp.zeros_like(pieces[0])], axis=0)

    def expand(block, carry):
        at = pl.multiple_of(scalars[8 + block] * LANES, LANES)
        selector = one_hot(index[0:1, pl.ds(at, 2 * LANES)], block)
        out = lax.dot_general(terms[:, pl.ds(at, 2 * LANES)], selector, NT, preferred_element_type=jnp.float32)
        path[block] = -(out[0:8] + out[8:16] + out[16:24])
        return carry

    lax.fori_loop(0, count, expand, 0, unroll=4)

    lane = lax.broadcasted_iota(jnp.int32, (8, LANES), 1)
    start = 0
    source = rows
    for height in range(4):
        width = 8 if height < 2 else 16
        for other in range(C):
            offset = z * width
            block = start
            if height < 3:
                block = block + scalars[3 + height] * (XC * depth * width // LANES)
            if width == 8:
                offset = offset + other * 64
                block = block + x
            else:
                block = block + x * 2 + other
            moved = pltpu.roll(parts[other], lax.rem(offset - source + LANES, LANES), 1)
            kept = jnp.where((lane >= offset) & (lane < offset + width), moved, 0.0)
            path[block] = path[block] + kept
        start += WIDTHS[height] // LANES
        source += width

    lower = WIDTHS[3] // LANES
    mine = upper // depth
    for block in range(upper):
        value = path[block]
        for dest in range(X):
            at = 2 * lower + 2 * (block % mine)
            send[dest * depth + block // mine, at : at + 2, :] = value[2 * dest : 2 * dest + 2, :]
    for dest in range(X):
        value = jnp.concatenate([path[upper + block][2 * dest : 2 * dest + 2, :] for block in range(lower)], axis=0)
        for other in range(depth):
            send[dest * depth + other, 0 : 2 * lower, :] = value


def first(small, coupling, index, scalars, depth):
    columns = coupling.shape[2]
    upper = sum(WIDTHS[:3]) // LANES
    lower = WIDTHS[3] // LANES
    return call(
        functools.partial(first_kernel, depth),
        f32(X * depth, 2 * (lower + upper // depth), LANES),
        in_specs=[SMEM, VMEM, VMEM, VMEM],
        scratch_shapes=[
            pltpu.VMEM((32, columns + 2 * LANES), jnp.bfloat16),
            pltpu.VMEM((upper + lower, 8, LANES), jnp.float32),
        ],
    )(scalars, small, coupling, index)


def pick(scalars, index, terms, first_block, blocks, chosen):
    total = sum(WIDTHS) // LANES

    def one(block, carry):
        for half in range(2):
            at = pl.multiple_of(scalars[8 + half * total + first_block + block] * LANES, LANES)
            selector = one_hot(index[half : half + 1, pl.ds(at, 2 * LANES)], first_block + block)
            out = lax.dot_general(
                terms[block].astype(jnp.bfloat16), selector, NN, preferred_element_type=jnp.float32
            )
            chosen[half, :, pl.ds(at, 2 * LANES)] = chosen[half, :, pl.ds(at, 2 * LANES)] + out
        return carry

    lax.fori_loop(0, blocks, one, 0, unroll=4)


def store_terms(ref, terms):
    blocks = ref.shape[0] // PAIR
    pieces = split3(ref[...].reshape(blocks, PAIR, LANES))
    terms[...] = jnp.concatenate([*pieces, jnp.zeros_like(pieces[0])], axis=1).astype(jnp.float32)


def pick_kernel(first_block, scalars, x, index, chosen, terms):
    store_terms(x, terms)
    chosen[...] = jnp.zeros_like(chosen)
    pick(scalars, index, terms, first_block, x.shape[0] // PAIR, chosen)


def picked(x, index, scalars, first_block):
    blocks = x.shape[0] // PAIR
    return call(
        functools.partial(pick_kernel, first_block),
        f32(2, 8, index.shape[1]),
        in_specs=[SMEM, VMEM, VMEM],
        out_specs=VMEM,
        scratch_shapes=[pltpu.VMEM((blocks, 8, LANES), jnp.float32)],
        cost_estimate=cost(blocks * 2 * LANES * LANES),
    )(scalars, x, index)


def last_kernel(columns, counts, scalars, received, x0, x1, x2, coupling, index, chosen0, chosen1, chosen2, send, x3, terms, chosen, buffer, ready):
    copy = pltpu.make_async_copy(coupling, buffer, ready)
    copy.start()
    x3[...] = jnp.sum(received[...], axis=0)
    store_terms(x3, terms)
    chosen[...] = chosen0[...] + chosen1[...] + chosen2[...]
    pick(scalars, index, terms, sum(counts[:3]), counts[3], chosen)
    rows = coupling.shape[0] // 2
    copy.wait()
    handed = []
    for half in range(2):
        value = chosen[half, 0:2, :columns] + chosen[half, 2:4, :columns] + chosen[half, 4:6, :columns]
        handed.append(
            lax.dot_general(
                value,
                buffer[half * rows : (half + 1) * rows, :],
                NT,
                precision=lax.Precision.HIGHEST,
                preferred_element_type=jnp.float32,
            )
        )
    send[...] = jnp.zeros_like(send)
    for dest in range(XC):
        core, x = dest // X, dest % X
        for level, ref in enumerate((x0, x1, x2, x3)):
            block = x if level < 2 else x * 2 + core
            if level < 3:
                block = block + scalars[level] * (counts[level] // (Y // 2**level))
            send[dest, 2 * level : 2 * level + 2, :] = ref[pl.ds(block * 2, 2), :]
        send[dest, 8:10, :] = handed[x // 2]


def last(received, known, chosen, coupling, index, scalars):
    columns = coupling.shape[1]
    counts = [width // LANES for width in WIDTHS]
    return call(
        functools.partial(last_kernel, columns, counts),
        f32(XC, 16, LANES),
        in_specs=[SMEM] + [VMEM] * 4 + [HBM] + [VMEM] * 4,
        out_specs=VMEM,
        scratch_shapes=[
            pltpu.VMEM(received.shape[1:], jnp.float32),
            pltpu.VMEM((counts[3], 8, LANES), jnp.float32),
            pltpu.VMEM((2, 8, columns + 2 * LANES), jnp.float32),
            pltpu.VMEM(coupling.shape, jnp.float32),
            pltpu.SemaphoreType.DMA,
        ],
        limit=WHOLE,
    )(scalars, received, *known, coupling, index, *chosen)


def finish_kernel(scalars, received, values, out0, out1, out2, out3, handed):
    z, core = scalars[0], scalars[1]
    offsets = (core * 64 + z * 8, core * 64 + z * 8, z * 16, z * 16, scalars[2] * values.shape[1])
    for level, ref in enumerate((out0, out1, out2, out3, handed)):
        value = jnp.concatenate([received[source, 2 * level : 2 * level + 2, :] for source in range(XC)], axis=0)
        moved = pltpu.roll(value, lax.rem(LANES - offsets[level], LANES), 1)[:, : ref.shape[1]]
        ref[...] = values[...] - moved if level == 4 else moved


def finish(received, values, scalars, widths):
    shapes = tuple(f32(XC * PAIR, width) for width in widths) + (f32(*values.shape),)
    return call(
        finish_kernel, shapes, in_specs=[SMEM, VMEM, VMEM]
    )(scalars, received, values)


def body(
    rhs_root,
    rhs_level1,
    rhs_level2,
    rhs_level3,
    inv_root,
    inv_level1,
    inv_level2,
    inv_level3,
    cross_level1,
    cross_level2,
    cross_level3,
    subtree_values,
    coupling,
    coupled_rows,
):
    depth = lax.axis_size("z")
    y = (lax.axis_index("y2") * 2 + lax.axis_index("y1")) * 2 + lax.axis_index("y0")
    x, c, z = lax.axis_index("x"), lax.axis_index("c"), lax.axis_index("z")
    counts = [width // LANES for width in WIDTHS]
    blocks = sum(counts)

    rhs_parts = [rhs_root, rhs_level1, rhs_level2, rhs_level3]
    small = jnp.concatenate([subtree_values] + rhs_parts, axis=1)
    small = jnp.pad(small, ((0, 0), (0, LANES - small.shape[1])))
    both_small = lax.all_gather(small, "c", axis=0, tiled=False)
    both_coupling = lax.all_gather(coupling, "c", axis=0, tiled=False)

    def gathered(parts):
        return lax.all_gather(jnp.concatenate(parts, axis=1), "x", axis=0, tiled=True)

    def swap(after, own):
        after, own = lax.optimization_barrier((after, own))
        return after, (own, lax.ppermute(own, "c", [(0, 1), (1, 0)]))

    own3 = gathered([inv_level3, cross_level3])
    own2 = gathered([inv_level2, cross_level2])
    own1 = gathered([inv_level1, cross_level1, inv_root])
    all_coupling = lax.all_gather(coupling, ("x", "c"), axis=0, tiled=True)

    both_indices = lax.dynamic_slice_in_dim(coupled_rows, y * 2, 2, 0)
    edges = jnp.arange(blocks, dtype=jnp.int32) * LANES
    windows = jnp.sum((both_indices[:, None, :] < edges[None, :, None]).astype(jnp.int32), axis=2) // LANES
    both_indices = jnp.pad(both_indices, ((0, 0), (0, 2 * LANES)), constant_values=-1)
    own_windows = lax.dynamic_index_in_dim(windows, x // 2, 0, keepdims=False)
    own_indices = lax.dynamic_slice_in_dim(both_indices, x // 2, 1, 0)

    def scalars(head, *tails):
        head = jnp.stack([jnp.asarray(value, jnp.int32) for value in head] + [jnp.int32(0)] * (8 - len(head)))
        return jnp.concatenate([head, *tails])

    places = scalars([z, c, x, y, y % 4, y % 2], own_windows)
    send = first(both_small, both_coupling, own_indices, places, depth)
    received, matrix3 = swap(exchange(send, ("x", "z")), own3)
    solved3, send, rest = forward(
        received, matrix3, jnp.zeros((8, LANES), jnp.float32), places, counts[3], sum(counts[:3]), counts[0] + counts[1], 2 * depth, depth
    )
    send, matrix2 = swap(send, own2)
    received = exchange(send, ("y0", "z"))
    solved2, send, rest = forward(received, matrix2, rest, places, counts[2], counts[0] + counts[1], counts[0], 4 * depth, 0)
    send, matrix1 = swap(send, own1)
    received = exchange(send, ("y1", "y0", "z"))
    solved1, send, rest = forward(received, matrix1, rest, places, counts[1], counts[0], 0, Y, 0)

    def sum_root(copies):
        received = exchange(copies.reshape(Y * depth, -1, LANES), ALL_Y + ("z",))
        return exchange(sum_and_copy(received, depth), ("z",))

    target = sum_root(send).reshape(-1, LANES)
    received = sum_root(root(target, matrix1, WIDTHS[1] + WIDTHS[0], Y)).reshape(1, -1, LANES)
    heads = scalars([y, y % 4, y % 2], windows.reshape(-1))
    send, x0 = backward(received, matrix1, solved1, [], counts[1], 4 * depth)
    received = exchange(send, ("y1", "y0", "z"))
    received, chosen0 = lax.optimization_barrier((received, picked(x0, both_indices, heads, 0)))
    send, x1 = backward(received, matrix2, solved2, [x0], counts[2], 2 * depth)
    received = exchange(send, ("y0", "z"))
    received, chosen1 = lax.optimization_barrier((received, picked(x1, both_indices, heads, counts[0])))
    send, x2 = backward(received, matrix3, solved3, [x0, x1], counts[3], depth)
    received = exchange(send, ("z",))
    chosen2 = picked(x2, both_indices, heads, counts[0] + counts[1])
    send = last(received, [x0, x1, x2], [chosen0, chosen1, chosen2], all_coupling, both_indices, heads)
    received = exchange(send, ("c", "x"))
    ends = scalars([z, c, (x % 2) * 2 + c])
    return finish(received, subtree_values, ends, [part.shape[1] for part in rhs_parts])


def solution(mesh):
    shape = (2, 2, 2, X, C, mesh.shape["sep"])
    fine = Mesh(mesh.devices.reshape(shape), ("y2", "y1", "y0", "x", "c", "z"))
    every = ("y2", "y1", "y0", "x", "c", "z")
    columns, rows = P(None, every), P(every, None)
    in_specs = (columns,) * 4 + (rows,) * 7 + (columns, rows, P())
    return jax.shard_map(body, mesh=fine, in_specs=in_specs, out_specs=(columns,) * 5, check_vma=False)
```

time: 285 us -> 303 us (1.063)
  waiting for transfers between devices: 82.5 us -> 101 us
  blocking collectives: 101 us -> 83.3 us
  starting transfers between devices: 40.7 us -> 50.4 us
    all_to_all x6, waiting for transfers between devices: 26.2 us -> 55.5 us  [exchange(): return lax.all_to_all(flat, axes, 0, 0, tiled=True).reshape(operand.shape)]
    all_to_all x5, blocking collectives: 90.3 us -> 72.8 us  [exchange(): return lax.all_to_all(flat, axes, 0, 0, tiled=True).reshape(operand.shape)]
    all_gather x5 -> x4, waiting for transfers between devices: 55.2 us -> 40.4 us  [the longest x3 40.4 us: gathered(): lax.all_gather(jnp.concatenate(parts, axis=1), 'x', axis=0, tiled=True)]
    ppermute x0 -> x3, starting transfers between devices: none -> 9.03 us  [swap(): return (after, (own, lax.ppermute(own, 'c', [(0, 1), (1, 0)])))]
    pallas_call x9 -> x12, Pallas kernels: 18.9 us -> 27.2 us  [the longest x3 7.52 us: backward(): call(functools.partial(backward_kernel, blocks, counts), (f32(copies, 2 *...]
    pallas_call x1, Pallas kernels: 8.96 us -> 3.48 us  [last(): call(functools.partial(last_kernel, columns, counts), f32(XC, 16, LANES),...]
    ppermute x0 -> x3, waiting for transfers between devices: none -> 4.36 us  [swap(): return (after, (own, lax.ppermute(own, 'c', [(0, 1), (1, 0)])))]
    unnamed x40 -> x38, local copies, waits for them, and re-layouts: 11.3 us -> 13.2 us
  transfers between devices with their start and end apart: 11 -> 13, of which waited for: 7 -> 10; matrix products, arithmetic and copies ran while one was open for 1% -> 2% of each run, Pallas kernels for 6% -> 9%
where the time goes in v3:
time: 303 us; the launch traced here: 301 us
  waiting for transfers between devices  101 us (33%)
  blocking collectives  83.3 us (27%)
  starting transfers between devices  50.4 us (17%)
  Pallas kernels  30.8 us (10%)
  local copies, waits for them, and re-layouts  15.7 us (5%)
  between operations  15.5 us (5%)
  other arithmetic  4.73 us (2%)
    all_to_all x5, blocking collectives, exchange(): return lax.all_to_all(flat, axes, 0, 0, tiled=True).reshape(operand.shape)  72.8 us
    all_to_all x6, waiting for transfers between devices, exchange(): return lax.all_to_all(flat, axes, 0, 0, tiled=True).reshape(operand.shape)  55.5 us
    all_to_all x6, starting transfers between devices, exchange(): return lax.all_to_all(flat, axes, 0, 0, tiled=True).reshape(operand.shape)  41.2 us
    all_gather x3, waiting for transfers between devices, gathered(): lax.all_gather(jnp.concatenate(parts, axis=1), 'x', axis=0, tiled=True)  40.4 us
    unnamed x38, local copies, waits for them, and re-layouts  13.2 us
    ppermute x3, starting transfers between devices, swap(): return (after, (own, lax.ppermute(own, 'c', [(0, 1), (1, 0)])))  9.03 us
    all_gather x1, blocking collectives, body(): both_small = lax.all_gather(small, 'c', axis=0, tiled=False)  8.36 us
    pallas_call x3, Pallas kernels, backward(): call(functools.partial(backward_kernel, blocks, counts), (f32(copies, 2 *...  7.52 us
  transfers between devices with their start and end apart: 13, of which 10 were waited for; matrix products, arithmetic and copies ran while one was open for 2% of the time, Pallas kernels for 9%

profile of v3, /device:TPU:1, one launch (start us, length us, event | category | flops | bytes accessed | tf_op | source)
XLA Modules:
  0.0 301.3 jit_solution(12772807171666756413)
XLA Ops:
  8.1 2.0 pad_maximum_fusion
  10.1 0.8 copy.23
  10.9 0.8 copy.24
  11.7 0.8 concatenate.20
  12.5 0.3 convert_reduce_fusion
  12.8 0.1 concatenate.19.scalars
  12.9 8.4 %all-gather = f32[32,128]{1,0:T(8,128)S(1)} all-gather(f32[16,128]{1,0:T(8,128)S(1)} %pad.8), channel_id=2, replica_groups=mesh['y2'=2,'y1'=2,'y0'=2,'x'=4,'c'=2,'z'=8] {'c'}, dimensions={0}, use_global_device_ids=true | all-gather | bytes 24576 | tf_op jit(solution)/shard_map/all_gather | solution.py:438
  21.3 2.2 all-gather.1
  23.5 5.6 %shard_map.173 = f32[32,32,128]{2,1,0:T(8,128)} custom-call(s32[80]{0:T(128)S(1)} %concatenate.19.scalars, f32[2,16,128]{2,1,0:T(8,128)S(1)} %bitcast.20, f32[2,32,2048]{2,1,0:T(8,128)S(1)} %bitcast.15, s32[1,2304]{1,0:T(1,128)S(1)} %constant_dynamic-slice_fusion.index), custom_call_target="tpu_custom_call" | custom-call | tf_op jit(solution)/shard_map/pallas_call | solution.py:295
  29.1 7.5 %all-to-all-start = ((f32[32,32,128]{2,1,0:T(8,128)}), f32[32,32,128]{2,1,0:T(8,128)S(1)}, u32[]{:S(2)}, u32[]{:S(2)}) async-start(f32[32,32,128]{2,1,0:T(8,128)} %shard_map.173), calls=%async_computation | async-start | bytes 1048576 | tf_op jit(solution)/shard_map/all_to_all | solution.py:50
  36.7 0.8 pad_maximum_fusion.1
  37.6 13.1 %all-to-all-done.received = f32[32,32,128]{2,1,0:T(8,128)S(1)} async-done(((f32[32,32,128]{2,1,0:T(8,128)}), f32[32,32,128]{2,1,0:T(8,128)S(1)}, u32[]{:S(2)}, u32[]{:S(2)}) %all-to-all-start) | async-done | bytes 524320 | tf_op jit(solution)/shard_map/all_to_all | solution.py:50
  50.7 9.7 %all-gather.7.cloned.1.call-done.own = f32[64,9216]{1,0:T(8,128)} async-done(((f32[16,9216]{1,0:T(8,128)}), f32[64,9216]{1,0:T(8,128)}) %all-gather.7.cloned.1.call-update) | async-done | bytes 2359312 | tf_op jit(solution)/shard_map/all_gather | solution.py:442
  60.4 2.6 collective-permute-start
  63.0 4.3 %collective-permute-done.other = f32[64,9216]{1,0:T(8,128)S(1)} collective-permute-done((f32[64,9216]{1,0:T(8,128)}, f32[64,9216]{1,0:T(8,128)S(1)}, u32[]{:S(2)}, u32[]{:S(2)}) %collective-permute-start) | collective-permute-done | bytes 2359328 | tf_op jit(solution)/shard_map/ppermute | solution.py:446
  67.4 1.4 copy-done.11
  68.8 1.7 copy-done.2
  70.5 3.1 %shard_map.174 = (f32[2,128,128]{2,1,0:T(8,128)S(1)}, f32[16,32,128]{2,1,0:T(8,128)S(1)}, f32[128,128]{1,0:T(8,128)S(1)}) custom-call(s32[80]{0:T(128)S(1)} %concatenate.19.scalars, f32[32,32,128]{2,1,0:T(8,128)S(1)} %all-to-all-done.received, f32[64,9216]{1,0:T(8,128)S(1)} %copy-done.2, f32[64,9216]{1,0:T(8,128)} %copy-done.11, ...), custom_call_target="tpu_custom_call" | custom-call | flops 9437184 | bytes 4718592 | tf_op jit(solution)/shard_map/pallas_call | solution.py:145
  73.5 25.3 %all-gather.9.cloned.1.call-done.own = f32[64,8192]{1,0:T(8,128)} async-done(((f32[16,8192]{1,0:T(8,128)}), f32[64,8192]{1,0:T(8,128)}) %all-gather.9.cloned.1.call-update) | async-done | bytes 2097168 | tf_op jit(solution)/shard_map/all_gather | solution.py:442
  98.8 2.6 collective-permute-start.1
  101.4 1.6 pad_maximum_fusion.2
  103.1 16.4 %all_to_all.74.received = f32[16,32,128]{2,1,0:T(8,128)S(1)} all-to-all(f32[16,32,128]{2,1,0:T(8,128)S(1)} %get-tuple-element.32), channel_id=1, replica_groups=mesh['y2'=2,'y1'=2,'y0'=2,'x'=4,'c'=2,'z'=8] {'y0','z'}, dimensions={0} | all-to-all | bytes 524288 | tf_op jit(solution)/shard_map/all_to_all | solution.py:50
  119.5 1.3 copy-done.12
  120.9 1.6 copy-done.4
  122.5 2.6 shard_map.175
  125.1 0.8 copy-done.7
  125.9 0.6 copy-done.8
  126.6 5.3 %all-gather.11.cloned.1.call-done.own = f32[32,10240]{1,0:T(8,128)} async-done(((f32[8,10240]{1,0:T(8,128)}), f32[32,10240]{1,0:T(8,128)}) %all-gather.11.cloned.1.call-update) | async-done | bytes 1310736 | tf_op jit(solution)/shard_map/all_gather | solution.py:442
  131.9 3.9 %collective-permute-start.2 = (f32[32,10240]{1,0:T(8,128)}, f32[32,10240]{1,0:T(8,128)S(1)}, u32[]{:S(2)}, u32[]{:S(2)}) collective-permute-start(f32[32,10240]{1,0:T(8,128)} %all-gather.11.cloned.1.call-done.own), channel_id=1, source_target_pairs={{0,8},{8,0},{1,9},{9,1},{2,10},{10,2},{3,11},{11,3},{4,12},{12,4},... | collective-permute-start | bytes 3932168 | tf_op jit(solution)/shard_map/ppermute | solution.py:446
  135.8 10.3 %all-to-all-start.2 = ((f32[32,32,128]{2,1,0:T(8,128)}), f32[32,32,128]{2,1,0:T(8,128)S(1)}, u32[]{:S(2)}, u32[]{:S(2)}) async-start(f32[32,32,128]{2,1,0:T(8,128)} %copy-done.7), calls=%async_computation.2 | async-start | bytes 1048576 | tf_op jit(solution)/shard_map/all_to_all | solution.py:50
  146.1 0.5 all-gather.13.cloned.1.call-update
  146.6 15.1 %all-to-all-done.2.received = f32[32,32,128]{2,1,0:T(8,128)S(1)} async-done(((f32[32,32,128]{2,1,0:T(8,128)}), f32[32,32,128]{2,1,0:T(8,128)S(1)}, u32[]{:S(2)}, u32[]{:S(2)}) %all-to-all-start.2) | async-done | bytes 524320 | tf_op jit(solution)/shard_map/all_to_all | solution.py:50
  161.8 1.7 shard_map.176
  163.5 20.2 %all_to_all.75.received = f32[64,8,128]{2,1,0:T(8,128)S(1)} all-to-all(f32[64,8,128]{2,1,0:T(8,128)S(1)} %bitcast.17), channel_id=1, replica_groups=mesh['y2'=2,'y1'=2,'y0'=2,'x'=4,'c'=2,'z'=8] {'y2','y1','y0','z'}, dimensions={0} | all-to-all | bytes 524288 | tf_op jit(solution)/shard_map/all_to_all | solution.py:50
  183.7 0.1 shard_map.177
  183.7 10.2 %all_to_all.76 = f32[8,8,128]{2,1,0:T(8,128)S(1)} all-to-all(f32[8,8,128]{2,1,0:T(8,128)S(1)} %shard_map.177), channel_id=1, replica_groups=mesh['y2'=2,'y1'=2,'y0'=2,'x'=4,'c'=2,'z'=8] {'z'}, dimensions={0} | all-to-all | bytes 65536 | tf_op jit(solution)/shard_map/all_to_all | solution.py:50
  193.9 0.6 shard_map.178
  194.5 16.5 %all_to_all.77.received = f32[64,8,128]{2,1,0:T(8,128)S(1)} all-to-all(f32[64,8,128]{2,1,0:T(8,128)S(1)} %bitcast.16), channel_id=1, replica_groups=mesh['y2'=2,'y1'=2,'y0'=2,'x'=4,'c'=2,'z'=8] {'y2','y1','y0','z'}, dimensions={0} | all-to-all | bytes 524288 | tf_op jit(solution)/shard_map/all_to_all | solution.py:50
  211.0 0.1 shard_map.179
  211.1 9.5 %all_to_all.78 = f32[8,8,128]{2,1,0:T(8,128)S(1)} all-to-all(f32[8,8,128]{2,1,0:T(8,128)S(1)} %shard_map.179), channel_id=1, replica_groups=mesh['y2'=2,'y1'=2,'y0'=2,'x'=4,'c'=2,'z'=8] {'z'}, dimensions={0} | all-to-all | bytes 65536 | tf_op jit(solution)/shard_map/all_to_all | solution.py:50
  220.6 1.5 shard_map.180
  222.1 3.9 %all-to-all-start.7 = ((f32[32,32,128]{2,1,0:T(8,128)}), f32[32,32,128]{2,1,0:T(8,128)S(1)}, u32[]{:S(2)}, u32[]{:S(2)}) async-start(f32[32,32,128]{2,1,0:T(8,128)} %get-tuple-element.41), calls=%async_computation.7 | async-start | bytes 1048576 | tf_op jit(solution)/shard_map/all_to_all | solution.py:50
  226.0 0.1 reduce_sum.12
  226.1 0.1 concatenate.18.scalars
  226.2 2.2 shard_map.181.chosen0
  228.4 10.5 %all-to-all-done.7.received = f32[32,32,128]{2,1,0:T(8,128)S(1)} async-done(((f32[32,32,128]{2,1,0:T(8,128)}), f32[32,32,128]{2,1,0:T(8,128)S(1)}, u32[]{:S(2)}, u32[]{:S(2)}) %all-to-all-start.7) | async-done | bytes 524320 | tf_op jit(solution)/shard_map/all_to_all | solution.py:50
  238.8 1.6 copy-done.5
  240.4 0.9 copy-done.9
  241.3 2.9 shard_map.182
  244.2 3.7 %all-to-all-start.8 = ((f32[16,32,128]{2,1,0:T(8,128)}), f32[16,32,128]{2,1,0:T(8,128)S(1)}, u32[]{:S(2)}, u32[]{:S(2)}) async-start(f32[16,32,128]{2,1,0:T(8,128)} %get-tuple-element.45), calls=%async_computation.8 | async-start | bytes 524288 | tf_op jit(solution)/shard_map/all_to_all | solution.py:50
  248.0 1.4 shard_map.183.chosen1
  249.3 6.2 %all-to-all-done.8.received = f32[16,32,128]{2,1,0:T(8,128)S(1)} async-done(((f32[16,32,128]{2,1,0:T(8,128)}), f32[16,32,128]{2,1,0:T(8,128)S(1)}, u32[]{:S(2)}, u32[]{:S(2)}) %all-to-all-start.8) | async-done | bytes 262176 | tf_op jit(solution)/shard_map/all_to_all | solution.py:50
  255.5 3.1 %shard_map.184 = (f32[8,16,128]{2,1,0:T(8,128)}, f32[32,128]{1,0:T(8,128)S(1)}) custom-call(f32[16,32,128]{2,1,0:T(8,128)S(1)} %all-to-all-done.8.received, f32[64,9216]{1,0:T(8,128)S(1)} %copy-done.3, f32[64,9216]{1,0:T(8,128)} %copy-done.11, f32[2,128,128]{2,1,0:T(8,128)S(1)} %get-tuple-element.48.solved, f32[64,128]{1,0:T(8,128)S(1)} %get-tuple-element.42.x.refs_0_.x0, ...), custom_call_target="tpu_custom_call" | custom-call | flops 9437184 | bytes 4718592 | tf_op jit(solution)/shard_map/pallas_call | solution.py:182
  258.6 3.4 %all-to-all-start.9 = ((f32[8,16,128]{2,1,0:T(8,128)}), f32[8,16,128]{2,1,0:T(8,128)S(1)}, u32[]{:S(2)}, u32[]{:S(2)}) async-start(f32[8,16,128]{2,1,0:T(8,128)} %get-tuple-element.49), calls=%async_computation.9 | async-start | bytes 131072 | tf_op jit(solution)/shard_map/all_to_all | solution.py:50
  262.0 1.4 shard_map.185.chosen2
  263.4 5.8 %all-to-all-done.9.received = f32[8,16,128]{2,1,0:T(8,128)S(1)} async-done(((f32[8,16,128]{2,1,0:T(8,128)}), f32[8,16,128]{2,1,0:T(8,128)S(1)}, u32[]{:S(2)}, u32[]{:S(2)}) %all-to-all-start.9) | async-done | bytes 65568 | tf_op jit(solution)/shard_map/all_to_all | solution.py:50
  269.1 1.6 copy-done.6
  270.7 3.5 %shard_map.186 = f32[8,16,128]{2,1,0:T(8,128)} custom-call(s32[152]{0:T(256)S(1)} %concatenate.18.scalars, f32[8,16,128]{2,1,0:T(8,128)S(1)} %all-to-all-done.9.received, f32[64,128]{1,0:T(8,128)S(1)} %get-tuple-element.42.x.refs_0_.x0, f32[32,128]{1,0:T(8,128)S(1)} %get-tuple-element.46.x.refs_1_.x1, f32[32,128]{1,0:T(8,128)S(1)} %get-tuple-element.50.x.x2, ...), custom_call_target="tpu_custom_call" | custom-call | tf_op jit(solution)/shard_map/pallas_call | solution.py:381
  274.2 12.5 %all-to-all-start.10 = ((f32[8,16,128]{2,1,0:T(8,128)}), f32[8,16,128]{2,1,0:T(8,128)S(1)}, u32[]{:S(2)}, u32[]{:S(2)}) async-start(f32[8,16,128]{2,1,0:T(8,128)} %shard_map.186), calls=%async_computation.10 | async-start | bytes 131072 | tf_op jit(solution)/shard_map/all_to_all | solution.py:50
  286.7 0.1 stack.32.scalars
  286.8 4.9 %all-to-all-done.10.received = f32[8,16,128]{2,1,0:T(8,128)S(1)} async-done(((f32[8,16,128]{2,1,0:T(8,128)}), f32[8,16,128]{2,1,0:T(8,128)S(1)}, u32[]{:S(2)}, u32[]{:S(2)}) %all-to-all-start.10) | async-done | bytes 65568 | tf_op jit(solution)/shard_map/all_to_all | solution.py:50
  291.7 1.2 shard_map.187
  292.9 0.7 copy.25
  293.6 0.7 copy.26
  (48 shorter events, 0.4 us)
Async XLA Ops:
  8.0 4.5 %copy-start = (s32[16,2048]{1,0:T(8,128)S(1)}, s32[16,2048]{1,0:T(8,128)}, u32[]{:S(2)}) copy-start(s32[16,2048]{1,0:T(8,128)} %param.27) | copy-start | bytes 393220
  8.0 13.3 %copy-start.13 = (f32[32,2048]{1,0:T(8,128)S(1)}, f32[32,2048]{1,0:T(8,128)}, u32[]{:S(2)}) copy-start(f32[32,2048]{1,0:T(8,128)} %param.26) | copy-start | bytes 786436
  8.0 52.4 %all-gather.7.cloned.1.call-start = ((), (), s32[]{:S(2)}) async-start(), calls=%async_computation.11 | async-start | bytes 2949120 | tf_op jit(solution)/shard_map/all_gather | solution.py:442
  10.0 26.6 %copy-start.14 = (f32[16,6144]{1,0:T(8,128)S(1)}, f32[16,6144]{1,0:T(8,128)}, u32[]{:S(2)}) copy-start(f32[16,6144]{1,0:T(8,128)} %param.23) | copy-start | bytes 1179652
  10.0 26.7 %copy-start.16 = (f32[16,2048]{1,0:T(8,128)S(1)}, f32[16,2048]{1,0:T(8,128)}, u32[]{:S(2)}) copy-start(f32[16,2048]{1,0:T(8,128)} %param.20) | copy-start | bytes 393220
  29.1 21.6 %all-to-all-start = ((f32[32,32,128]{2,1,0:T(8,128)}), f32[32,32,128]{2,1,0:T(8,128)S(1)}, u32[]{:S(2)}, u32[]{:S(2)}) async-start(f32[32,32,128]{2,1,0:T(8,128)} %shard_map.173), calls=%async_computation | async-start | bytes 1048576 | tf_op jit(solution)/shard_map/all_to_all | solution.py:50
  36.6 62.2 %all-gather.9.cloned.1.call-start = ((), (), s32[]{:S(2)}) async-start(), calls=%async_computation.12 | async-start | bytes 2621440 | tf_op jit(solution)/shard_map/all_gather | solution.py:442
  37.6 94.3 %all-gather.11.cloned.1.call-start = ((), (), s32[]{:S(2)}) async-start(), calls=%async_computation.13 | async-start | bytes 1638400 | tf_op jit(solution)/shard_map/all_gather | solution.py:442
  60.4 6.9 %collective-permute-start = (f32[64,9216]{1,0:T(8,128)}, f32[64,9216]{1,0:T(8,128)S(1)}, u32[]{:S(2)}, u32[]{:S(2)}) collective-permute-start(f32[64,9216]{1,0:T(8,128)} %all-gather.7.cloned.1.call-done.own), channel_id=1, source_target_pairs={{0,8},{8,0},{1,9},{9,1},{2,10},{10,2},{3,11},{11,3},{4,12},{12,4},... | collective-permute-start | bytes 7077896 | tf_op jit(solution)/shard_map/ppermute | solution.py:446
  67.4 1.4 copy-start.11
  68.8 1.7 copy-start.2
  70.5 31.0 %copy-start.15 = (f32[8,4096]{1,0:T(8,128)S(1)}, f32[8,4096]{1,0:T(8,128)}, u32[]{:S(2)}) copy-start(f32[8,4096]{1,0:T(8,128)} %param.18) | copy-start | bytes 393220
  70.5 31.0 %copy-start.17 = (f32[8,2048]{1,0:T(8,128)S(1)}, f32[8,2048]{1,0:T(8,128)}, u32[]{:S(2)}) copy-start(f32[8,2048]{1,0:T(8,128)} %param.19) | copy-start | bytes 196612
  98.8 20.7 %collective-permute-start.1 = (f32[64,8192]{1,0:T(8,128)}, f32[64,8192]{1,0:T(8,128)S(1)}, u32[]{:S(2)}, u32[]{:S(2)}) collective-permute-start(f32[64,8192]{1,0:T(8,128)} %all-gather.9.cloned.1.call-done.own), channel_id=1, source_target_pairs={{0,8},{8,0},{1,9},{9,1},{2,10},{10,2},{3,11},{11,3},{4,12},{12,4},... | collective-permute-start | bytes 6291464 | tf_op jit(solution)/shard_map/ppermute | solution.py:446
  119.5 1.3 copy-start.12
  120.9 1.6 copy-start.4
  125.1 0.8 copy-start.7
  125.9 0.6 copy-start.8
  131.9 29.9 %copy-start.1 = (f32[32,10240]{1,0:T(8,128)S(1)}, f32[32,10240]{1,0:T(8,128)}, u32[]{:S(2)}) copy-start(f32[32,10240]{1,0:T(8,128)} %all-gather.11.cloned.1.call-done.own) | copy-start | bytes 3932164
  131.9 29.9 %collective-permute-start.2 = (f32[32,10240]{1,0:T(8,128)}, f32[32,10240]{1,0:T(8,128)S(1)}, u32[]{:S(2)}, u32[]{:S(2)}) collective-permute-start(f32[32,10240]{1,0:T(8,128)} %all-gather.11.cloned.1.call-done.own), channel_id=1, source_target_pairs={{0,8},{8,0},{1,9},{9,1},{2,10},{10,2},{3,11},{11,3},{4,12},{12,4},... | collective-permute-start | bytes 3932168 | tf_op jit(solution)/shard_map/ppermute | solution.py:446
  135.8 26.0 %all-to-all-start.2 = ((f32[32,32,128]{2,1,0:T(8,128)}), f32[32,32,128]{2,1,0:T(8,128)S(1)}, u32[]{:S(2)}, u32[]{:S(2)}) async-start(f32[32,32,128]{2,1,0:T(8,128)} %copy-done.7), calls=%async_computation.2 | async-start | bytes 1048576 | tf_op jit(solution)/shard_map/all_to_all | solution.py:50
  146.0 117.3 %all-gather.13.cloned.1.call-start = ((), (), s32[]{:S(2)}) async-start(), calls=%async_computation.14 | async-start | bytes 2359296 | tf_op jit(solution)/shard_map/all_gather | solution.py:451
  222.1 16.7 %all-to-all-start.7 = ((f32[32,32,128]{2,1,0:T(8,128)}), f32[32,32,128]{2,1,0:T(8,128)S(1)}, u32[]{:S(2)}, u32[]{:S(2)}) async-start(f32[32,32,128]{2,1,0:T(8,128)} %get-tuple-element.41), calls=%async_computation.7 | async-start | bytes 1048576 | tf_op jit(solution)/shard_map/all_to_all | solution.py:50
  238.8 1.6 copy-start.5
  240.4 0.9 copy-start.9
  241.3 14.2 %copy-start.3 = (f32[64,9216]{1,0:T(8,128)S(1)}, f32[64,9216]{1,0:T(8,128)}, u32[]{:S(2)}) copy-start(f32[64,9216]{1,0:T(8,128)} %all-gather.7.cloned.1.call-done.own) | copy-start | bytes 7077892
  244.2 11.3 %all-to-all-start.8 = ((f32[16,32,128]{2,1,0:T(8,128)}), f32[16,32,128]{2,1,0:T(8,128)S(1)}, u32[]{:S(2)}, u32[]{:S(2)}) async-start(f32[16,32,128]{2,1,0:T(8,128)} %get-tuple-element.45), calls=%async_computation.8 | async-start | bytes 524288 | tf_op jit(solution)/shard_map/all_to_all | solution.py:50
  258.6 33.1 %copy-start.10 = (f32[16,32]{1,0:T(8,128)S(1)}, f32[16,32]{1,0:T(8,128)}, u32[]{:S(2)}) copy-start(f32[16,32]{1,0:T(8,128)} %values.1) | copy-start | bytes 6148
  258.6 10.5 %all-to-all-start.9 = ((f32[8,16,128]{2,1,0:T(8,128)}), f32[8,16,128]{2,1,0:T(8,128)S(1)}, u32[]{:S(2)}, u32[]{:S(2)}) async-start(f32[8,16,128]{2,1,0:T(8,128)} %get-tuple-element.49), calls=%async_computation.9 | async-start | bytes 131072 | tf_op jit(solution)/shard_map/all_to_all | solution.py:50
  269.1 1.6 copy-start.6
  274.2 17.5 %all-to-all-start.10 = ((f32[8,16,128]{2,1,0:T(8,128)}), f32[8,16,128]{2,1,0:T(8,128)S(1)}, u32[]{:S(2)}, u32[]{:S(2)}) async-start(f32[8,16,128]{2,1,0:T(8,128)} %shard_map.186), calls=%async_computation.10 | async-start | bytes 131072 | tf_op jit(solution)/shard_map/all_to_all | solution.py:50
Sparse Core Ops, SparseCore 0:
  11.0 49.4 all-gather.6
  62.5 36.2 all-gather.8
  103.2 28.5 all-gather.10
Sparse Core Ops, SparseCore 1:
  148.7 28.8 all-gather.12

commit v4 on v3

--- a/solution.py
+++ b/solution.py
@@ -19,7 +19,7 @@
 CHUNK = 32
 HBM = pl.BlockSpec(memory_space=pltpu.HBM)
 LIMIT = 16 * 2**20
-WHOLE = 50 * 2**20
+WHOLE = 58 * 2**20
 ALL_Y = ("y2", "y1", "y0")
 INTERPRET = False
 VMEM = pl.BlockSpec(memory_space=pltpu.VMEM)
@@ -108,14 +108,17 @@
         step(pl.ds(place * CHUNK, CHUNK))
 
 
-def chunk_buffers(matrices, width):
-    rows = 2 * matrices[0].shape[0]
+def chunk_buffers(rows, width):
     return [pltpu.VMEM((rows, width), jnp.float32), pltpu.SemaphoreType.DMA((rows // CHUNK,))]
 
 
-def forward_kernel(blocks, upper, depth, keep, scalars, received, own, other, rest_in, solved, send, rest, vector, total, buffer, ready):
-    copies = chunk_copies((own, other), buffer, ready)
-    vector[...] = jnp.sum(received[...], axis=0)
+def forward_kernel(blocks, upper, keep, extra, scalars, received, matrix, rest_in, solved, send, rest, vector, total, buffer, ready):
+    copies = chunk_copies((matrix,), buffer, ready)
+    if extra:
+        for source in range(blocks):
+            vector[2 * source : 2 * source + 2, :] = received[source, 0:2, :]
+    else:
+        vector[...] = jnp.sum(received[...], axis=0)
     total[...] = jnp.zeros_like(total)
 
     def step(rows):
@@ -126,11 +129,11 @@
 
     each_chunk(copies, step)
     whole = -jnp.sum(total[...], axis=1)
-    if depth:
+    if extra:
         rest[...] = whole
-        size = 2 * upper // depth
-        at = pl.multiple_of(scalars[0] * size, 8)
-        rest[pl.ds(at, size), :] = rest[pl.ds(at, size), :] + vector[2 * blocks :, :]
+        for row in range(extra):
+            at = pl.ds(scalars[6] * extra + row, 1)
+            rest[at, :] = rest[at, :] + rest_in[2 + row : 3 + row, :]
         whole = rest[...]
     else:
         whole = whole + rest_in[0 : 2 * upper, :]
@@ -139,29 +142,94 @@
         send[copy] = whole[2 * keep :, :]
 
 
-def forward(received, matrices, rest_in, scalars, blocks, upper, keep, copies, depth):
-    rows = matrices[0].shape[0]
+def forward(received, matrix, rest_in, scalars, blocks, upper, keep, copies, extra):
+    rows = matrix.shape[0]
     width = upper * LANES + blocks * LANES
     return call(
-        functools.partial(forward_kernel, blocks, upper, depth, keep),
-        (f32(PAIR, 2 * rows, LANES), f32(copies, 2 * (upper - keep), LANES), f32(2 * upper, LANES)),
-        in_specs=[SMEM, VMEM, HBM, HBM, VMEM],
+        functools.partial(forward_kernel, blocks, upper, keep, extra),
+        (f32(PAIR, rows, LANES), f32(copies, 2 * (upper - keep), LANES), f32(2 * upper, LANES)),
+        in_specs=[SMEM, VMEM, HBM, VMEM],
         out_specs=(VMEM,) * 3,
-        scratch_shapes=[pltpu.VMEM(received.shape[1:], jnp.float32), pltpu.VMEM((2 * upper, 8, LANES), jnp.float32)]
-        + chunk_buffers(matrices, width),
+        scratch_shapes=[pltpu.VMEM((2 * blocks, LANES), jnp.float32), pltpu.VMEM((2 * upper, 8, LANES), jnp.float32)]
+        + chunk_buffers(rows, width),
+        cost_estimate=cost(rows * width),
+        limit=WHOLE,
+    )(scalars, received, matrix, rest_in)
+
+
+def lowest_kernel(blocks, upper, received, own, other, path, send, total, buffer, ready):
+    rows = own.shape[0]
+    copies = []
+    for number, matrix in enumerate((own, other)):
+        copies.append(pltpu.make_async_copy(matrix, buffer.at[pl.ds(number * rows, rows), :], ready.at[number]))
+    for copy in copies:
+        copy.start()
+    for copy in copies:
+        copy.wait()
+    samples = range(received.shape[1])
+    sums = [jnp.zeros((2 * rows, LANES), jnp.float32) for _ in samples]
+    for block in range(blocks):
+        tile = buffer[:, block * LANES : (block + 1) * LANES]
+        for s in samples:
+            sums[s] = sums[s] + tile * received[block, s : s + 1, :]
+    wide = [jnp.broadcast_to(jnp.sum(value, axis=1, keepdims=True), (2 * rows, LANES)) for value in sums]
+    for s in samples:
+        total[s] = wide[s]
+
+    def one(block, carry):
+        at = pl.multiple_of((blocks + block) * LANES, LANES)
+        tile = buffer[:, pl.ds(at, LANES)]
+        parts = [jnp.sum(tile * total[s], axis=0, keepdims=True) for s in samples]
+        path_block = path[block] - jnp.concatenate(parts, axis=0)
+        send_block(block, path_block)
+        return carry
+
+    groups = send.shape[0] // X
+    share = (upper - groups) // groups
+
+    def send_block(block, value):
+        low = block >= upper - groups
+        place = jnp.where(low, block - (upper - groups), block // share)
+        row = jnp.where(low, 0, 2 + 2 * lax.rem(block, share))
+        depth = groups // 2
+        for x in range(X):
+            dest = (place // depth) * (X * depth) + x * depth + lax.rem(place, depth)
+            send[dest, pl.ds(row, 2), :] = value[2 * x : 2 * x + 2, :]
+
+    lax.fori_loop(0, upper, one, 0, unroll=4)
+
+
+def lowest(received, own, other, path, blocks, upper, groups):
+    rows, width = own.shape
+    return call(
+        functools.partial(lowest_kernel, blocks, upper),
+        f32(X * groups, 8, LANES),
+        in_specs=[VMEM, HBM, HBM, VMEM],
+        out_specs=VMEM,
+        scratch_shapes=[
+            pltpu.VMEM((received.shape[1], 2 * rows, LANES), jnp.float32),
+            pltpu.VMEM((2 * rows, width), jnp.float32),
+            pltpu.SemaphoreType.DMA((2,)),
+        ],
         cost_estimate=cost(2 * rows * width),
-        limit=WHOLE,
-    )(scalars, received, *matrices, rest_in)
-
-
-def backward_kernel(blocks, known_blocks, received, own, other, solved, *refs):
-    known, (send, newest, total, buffer, ready) = refs[: len(known_blocks) - 1], refs[len(known_blocks) - 1 :]
-    copies = chunk_copies((own, other), buffer, ready)
+    )(received, own, other, path)
+
+
+def backward_kernel(blocks, known_blocks, scalars, received, matrix, solved, *refs):
+    known, (send, newest, total, vector, buffer, ready) = refs[: len(known_blocks) - 1], refs[len(known_blocks) - 1 :]
+    copies = chunk_copies((matrix,), buffer, ready)
     newest[...] = jnp.sum(received[...], axis=0)
     total[...] = jnp.zeros_like(total)
+    again = solved.shape[2] == LANES and solved.shape[0] == blocks
+    if again:
+        for block in range(blocks):
+            vector[2 * block : 2 * block + 2, :] = solved[block, pl.ds(scalars[2] * 2, 2), :]
 
     def step(rows):
-        values = [solved[s, rows, 0:1] for s in range(PAIR)]
+        if again:
+            values = row_dot(buffer, rows, 0, vector, 0, blocks)
+        else:
+            values = [solved[s, rows, 0:1] for s in range(PAIR)]
         column = blocks * LANES
         for ref, count in zip((*known, newest), known_blocks):
             part = row_dot(buffer, rows, column, ref, 0, count)
@@ -175,23 +243,24 @@
         send[copy] = whole
 
 
-def backward(received, matrices, solved, known, blocks, copies):
-    rows = matrices[0].shape[0]
+def backward(received, matrix, solved, known, scalars, blocks, copies):
+    rows = matrix.shape[0]
     counts = [array.shape[0] // PAIR for array in known] + [received.shape[1] // PAIR]
     width = (blocks + sum(counts)) * LANES
     return call(
         functools.partial(backward_kernel, blocks, counts),
         (f32(copies, 2 * blocks, LANES), f32(*received.shape[1:])),
-        in_specs=[VMEM, HBM, HBM, VMEM] + [VMEM] * len(known),
+        in_specs=[SMEM, VMEM, HBM, VMEM] + [VMEM] * len(known),
         out_specs=(VMEM,) * 2,
-        scratch_shapes=[pltpu.VMEM((2 * blocks, 8, LANES), jnp.float32)] + chunk_buffers(matrices, width),
-        cost_estimate=cost(2 * rows * width),
+        scratch_shapes=[pltpu.VMEM((2 * blocks, 8, LANES), jnp.float32), pltpu.VMEM((2 * blocks, LANES), jnp.float32)]
+        + chunk_buffers(rows, width),
+        cost_estimate=cost(rows * width),
         limit=WHOLE,
-    )(received, *matrices, solved, *known)
-
-
-def root_kernel(column, blocks, vector, own, other, send, total, buffer, ready):
-    copies = chunk_copies((own.at[:, column:], other.at[:, column:]), buffer, ready)
+    )(scalars, received, matrix, solved, *known)
+
+
+def root_kernel(column, blocks, vector, matrix, send, total, buffer, ready):
+    copies = chunk_copies((matrix.at[:, column:],), buffer, ready)
     total[...] = jnp.zeros_like(total)
 
     def step(rows):
@@ -204,18 +273,18 @@
         send[copy] = whole
 
 
-def root(vector, matrices, column, copies):
-    rows = matrices[0].shape[0]
+def root(vector, matrix, column, copies):
+    rows = matrix.shape[0]
     blocks = vector.shape[0] // PAIR
     return call(
         functools.partial(root_kernel, column, blocks),
         f32(copies, 2 * blocks, LANES),
-        in_specs=[VMEM, HBM, HBM],
+        in_specs=[VMEM, HBM],
         out_specs=VMEM,
-        scratch_shapes=[pltpu.VMEM((2 * blocks, 8, LANES), jnp.float32)] + chunk_buffers(matrices, blocks * LANES),
-        cost_estimate=cost(2 * rows * blocks * LANES),
+        scratch_shapes=[pltpu.VMEM((2 * blocks, 8, LANES), jnp.float32)] + chunk_buffers(rows, blocks * LANES),
+        cost_estimate=cost(rows * blocks * LANES),
         limit=WHOLE,
-    )(vector, *matrices)
+    )(vector, matrix)
 
 
 def sum_kernel(copies, received, send):
@@ -228,7 +297,7 @@
     return call(functools.partial(sum_kernel, copies), f32(copies, *received.shape[1:]))(received)
 
 
-def first_kernel(depth, scalars, small, coupling, index, send, terms, path):
+def first_kernel(depth, scalars, small, coupling, index, send, path, terms):
     z, core, x = scalars[0], scalars[1], scalars[2]
     upper = sum(WIDTHS[:3]) // LANES
     count = upper + WIDTHS[3] // LANES
@@ -275,17 +344,9 @@
         start += WIDTHS[height] // LANES
         source += width
 
-    lower = WIDTHS[3] // LANES
-    mine = upper // depth
-    for block in range(upper):
-        value = path[block]
-        for dest in range(X):
-            at = 2 * lower + 2 * (block % mine)
-            send[dest * depth + block // mine, at : at + 2, :] = value[2 * dest : 2 * dest + 2, :]
     for dest in range(X):
-        value = jnp.concatenate([path[upper + block][2 * dest : 2 * dest + 2, :] for block in range(lower)], axis=0)
         for other in range(depth):
-            send[dest * depth + other, 0 : 2 * lower, :] = value
+            send[dest * depth + other] = path[upper + other]
 
 
 def first(small, coupling, index, scalars, depth):
@@ -294,12 +355,10 @@
     lower = WIDTHS[3] // LANES
     return call(
         functools.partial(first_kernel, depth),
-        f32(X * depth, 2 * (lower + upper // depth), LANES),
+        (f32(X * depth, 8, LANES), f32(upper + lower, 8, LANES)),
         in_specs=[SMEM, VMEM, VMEM, VMEM],
-        scratch_shapes=[
-            pltpu.VMEM((32, columns + 2 * LANES), jnp.bfloat16),
-            pltpu.VMEM((upper + lower, 8, LANES), jnp.float32),
-        ],
+        out_specs=(VMEM, VMEM),
+        scratch_shapes=[pltpu.VMEM((32, columns + 2 * LANES), jnp.bfloat16)],
     )(scalars, small, coupling, index)
 
 
@@ -399,15 +458,20 @@
     offsets = (core * 64 + z * 8, core * 64 + z * 8, z * 16, z * 16, scalars[2] * values.shape[1])
     for level, ref in enumerate((out0, out1, out2, out3, handed)):
         value = jnp.concatenate([received[source, 2 * level : 2 * level + 2, :] for source in range(XC)], axis=0)
-        moved = pltpu.roll(value, lax.rem(LANES - offsets[level], LANES), 1)[:, : ref.shape[1]]
-        ref[...] = values[...] - moved if level == 4 else moved
+        moved = pltpu.roll(value, lax.rem(LANES - offsets[level], LANES), 1)
+        if level < 2:
+            ref[...] = jnp.transpose(moved)[: ref.shape[0], :]
+        elif level < 4:
+            ref[...] = moved[:, : ref.shape[1]]
+        else:
+            ref[...] = values[...] - moved[:, : ref.shape[1]]
 
 
 def finish(received, values, scalars, widths):
-    shapes = tuple(f32(XC * PAIR, width) for width in widths) + (f32(*values.shape),)
-    return call(
-        finish_kernel, shapes, in_specs=[SMEM, VMEM, VMEM]
-    )(scalars, received, values)
+    samples = XC * PAIR
+    shapes = [f32(width, samples) for width in widths[:2]] + [f32(samples, width) for width in widths[2:]]
+    outs = call(finish_kernel, (*shapes, f32(*values.shape)), in_specs=[SMEM, VMEM, VMEM])(scalars, received, values)
+    return outs[0].T, outs[1].T, *outs[2:]
 
 
 def body(
@@ -438,17 +502,11 @@
     both_small = lax.all_gather(small, "c", axis=0, tiled=False)
     both_coupling = lax.all_gather(coupling, "c", axis=0, tiled=False)
 
-    def gathered(parts):
-        return lax.all_gather(jnp.concatenate(parts, axis=1), "x", axis=0, tiled=True)
-
-    def swap(after, own):
-        after, own = lax.optimization_barrier((after, own))
-        return after, (own, lax.ppermute(own, "c", [(0, 1), (1, 0)]))
-
-    own3 = gathered([inv_level3, cross_level3])
-    own2 = gathered([inv_level2, cross_level2])
-    own1 = gathered([inv_level1, cross_level1, inv_root])
-    all_coupling = lax.all_gather(coupling, ("x", "c"), axis=0, tiled=True)
+    def gathered(whole):
+        return lax.all_gather(whole, ("x", "c"), axis=0, tiled=True)
+
+    matrix2 = gathered(jnp.concatenate([inv_level2, cross_level2], axis=1))
+    matrix1 = gathered(jnp.concatenate([inv_level1, cross_level1, inv_root], axis=1))
 
     both_indices = lax.dynamic_slice_in_dim(coupled_rows, y * 2, 2, 0)
     edges = jnp.arange(blocks, dtype=jnp.int32) * LANES
@@ -461,16 +519,22 @@
         head = jnp.stack([jnp.asarray(value, jnp.int32) for value in head] + [jnp.int32(0)] * (8 - len(head)))
         return jnp.concatenate([head, *tails])
 
-    places = scalars([z, c, x, y, y % 4, y % 2], own_windows)
-    send = first(both_small, both_coupling, own_indices, places, depth)
-    received, matrix3 = swap(exchange(send, ("x", "z")), own3)
-    solved3, send, rest = forward(
-        received, matrix3, jnp.zeros((8, LANES), jnp.float32), places, counts[3], sum(counts[:3]), counts[0] + counts[1], 2 * depth, depth
+    places = scalars([z, c, x, y, y % 4, y % 2, (y % 2) * depth + z], own_windows)
+    send, path = first(both_small, both_coupling, own_indices, places, depth)
+    send, inv_level3, cross_level3, coupling = lax.optimization_barrier((send, inv_level3, cross_level3, coupling))
+    own3 = jnp.concatenate([inv_level3, cross_level3], axis=1)
+    received, other3 = lax.optimization_barrier(
+        (exchange(send, ("x", "z")), lax.ppermute(own3, "c", [(0, 1), (1, 0)]))
     )
-    send, matrix2 = swap(send, own2)
-    received = exchange(send, ("y0", "z"))
-    solved2, send, rest = forward(received, matrix2, rest, places, counts[2], counts[0] + counts[1], counts[0], 4 * depth, 0)
-    send, matrix1 = swap(send, own1)
+    target3 = exchange(sum_and_copy(received, depth), ("z",))
+    send = lowest(target3, own3, other3, path, counts[3], sum(counts[:3]), 2 * depth)
+    send, own3, coupling = lax.optimization_barrier((send, own3, coupling))
+    matrix3 = gathered(own3)
+    all_coupling = gathered(coupling)
+    received = sum_and_copy(exchange(send, ("y0", "x", "z")), 2 * depth)
+    solved2, send, rest = forward(
+        exchange(received, ("y0", "z")), matrix2, received[0], places, counts[2], counts[0] + counts[1], counts[0], 4 * depth, 6
+    )
     received = exchange(send, ("y1", "y0", "z"))
     solved1, send, rest = forward(received, matrix1, rest, places, counts[1], counts[0], 0, Y, 0)
 
@@ -481,13 +545,13 @@
     target = sum_root(send).reshape(-1, LANES)
     received = sum_root(root(target, matrix1, WIDTHS[1] + WIDTHS[0], Y)).reshape(1, -1, LANES)
     heads = scalars([y, y % 4, y % 2], windows.reshape(-1))
-    send, x0 = backward(received, matrix1, solved1, [], counts[1], 4 * depth)
+    send, x0 = backward(received, matrix1, solved1, [], places, counts[1], 4 * depth)
     received = exchange(send, ("y1", "y0", "z"))
     received, chosen0 = lax.optimization_barrier((received, picked(x0, both_indices, heads, 0)))
-    send, x1 = backward(received, matrix2, solved2, [x0], counts[2], 2 * depth)
+    send, x1 = backward(received, matrix2, solved2, [x0], places, counts[2], 2 * depth)
     received = exchange(send, ("y0", "z"))
     received, chosen1 = lax.optimization_barrier((received, picked(x1, both_indices, heads, counts[0])))
-    send, x2 = backward(received, matrix3, solved3, [x0, x1], counts[3], depth)
+    send, x2 = backward(received, matrix3, target3, [x0, x1], places, counts[3], depth)
     received = exchange(send, ("z",))
     chosen2 = picked(x2, both_indices, heads, counts[0] + counts[1])
     send = last(received, [x0, x1, x2], [chosen0, chosen1, chosen2], all_coupling, both_indices, heads)

time: 303 us -> 261 us (0.86)
  waiting for transfers between devices: 101 us -> 40.9 us
  blocking collectives: 83.3 us -> 113 us
  starting transfers between devices: 50.4 us -> 36.3 us
  Pallas kernels: 30.8 us -> 41.1 us
  local copies, waits for them, and re-layouts: 15.7 us -> 9.73 us
    all_gather x4, waiting for transfers between devices: 40.4 us -> 0.02 us  [gathered(): return lax.all_gather(whole, ('x', 'c'), axis=0, tiled=True)]
    all_to_all x5 -> x7, blocking collectives: 72.8 us -> 102 us  [exchange(): return lax.all_to_all(flat, axes, 0, 0, tiled=True).reshape(operand.shape)]
    all_to_all x6, waiting for transfers between devices: 55.5 us -> 40.3 us  [exchange(): return lax.all_to_all(flat, axes, 0, 0, tiled=True).reshape(operand.shape)]
    all_to_all x6, starting transfers between devices: 41.2 us -> 33.9 us  [exchange(): return lax.all_to_all(flat, axes, 0, 0, tiled=True).reshape(operand.shape)]
    ppermute x3 -> x1, starting transfers between devices: 9.03 us -> 2.23 us  [body(): lax.ppermute(own3, 'c', [(0, 1), (1, 0)])]
    unnamed x38 -> x53, local copies, waits for them, and re-layouts: 13.2 us -> 7.95 us
    pallas_call x3, Pallas kernels: 7.52 us -> 12 us  [backward(): call(functools.partial(backward_kernel, blocks, counts), (f32(copies, 2 *...]
    ppermute x3 -> x1, waiting for transfers between devices: 4.36 us -> 0.01 us  [body(): lax.ppermute(own3, 'c', [(0, 1), (1, 0)])]
  transfers between devices with their start and end apart: 13 -> 11, of which waited for: 10 -> 6; matrix products, arithmetic and copies ran while one was open for 2% -> 2% of each run, Pallas kernels for 9% -> 13%
where the time goes in v4:
time: 261 us; the launch traced here: 259 us
  blocking collectives  113 us (43%)
  Pallas kernels  41.1 us (16%)
  waiting for transfers between devices  40.9 us (16%)
  starting transfers between devices  36.3 us (14%)
  between operations  14.2 us (5%)
  local copies, waits for them, and re-layouts  9.73 us (4%)
  other arithmetic  4.05 us (2%)
    all_to_all x7, blocking collectives, exchange(): return lax.all_to_all(flat, axes, 0, 0, tiled=True).reshape(operand.shape)  102 us
    all_to_all x6, waiting for transfers between devices, exchange(): return lax.all_to_all(flat, axes, 0, 0, tiled=True).reshape(operand.shape)  40.3 us
    all_to_all x6, starting transfers between devices, exchange(): return lax.all_to_all(flat, axes, 0, 0, tiled=True).reshape(operand.shape)  33.9 us
    pallas_call x3, Pallas kernels, backward(): call(functools.partial(backward_kernel, blocks, counts), (f32(copies, 2 *...  12 us
    all_gather x1, blocking collectives, body(): both_small = lax.all_gather(small, 'c', axis=0, tiled=False)  8.36 us
    unnamed x53, local copies, waits for them, and re-layouts  7.95 us
    pallas_call x2, Pallas kernels, forward(): call(functools.partial(forward_kernel, blocks, upper, keep, extra), (f32(...  7.65 us
  transfers between devices with their start and end apart: 11, of which 6 were waited for; matrix products, arithmetic and copies ran while one was open for 2% of the time, Pallas kernels for 13%

profile of v4, /device:TPU:1, one launch (start us, length us, event | category | flops | bytes accessed | tf_op | source)
XLA Modules:
  0.0 259.0 jit_solution(5751692773281635789)
XLA Ops:
  7.3 2.0 pad_maximum_fusion
  9.4 0.0 all-gather.9.cloned.1.call-start
  9.4 1.7 pad_maximum_fusion.1
  11.2 0.0 all-gather.11.cloned.1.call-start
  11.3 0.1 copy.21
  11.3 0.1 copy.22
  11.4 0.1 concatenate.20
  11.5 0.3 convert_reduce_fusion
  11.9 0.1 concatenate.19.scalars
  11.9 8.4 %all-gather = f32[32,128]{1,0:T(8,128)S(1)} all-gather(f32[16,128]{1,0:T(8,128)S(1)} %pad.8), channel_id=2, replica_groups=mesh['y2'=2,'y1'=2,'y0'=2,'x'=4,'c'=2,'z'=8] {'c'}, dimensions={0}, use_global_device_ids=true | all-gather | bytes 24576 | tf_op jit(solution)/shard_map/all_gather | solution.py:502
  20.3 2.2 all-gather.1
  22.5 4.7 %shard_map.173 = (f32[32,8,128]{2,1,0:T(8,128)S(1)}, f32[72,8,128]{2,1,0:T(8,128)S(1)}) custom-call(s32[80]{0:T(128)S(1)} %concatenate.19.scalars, f32[2,16,128]{2,1,0:T(8,128)S(1)} %bitcast.21, f32[2,32,2048]{2,1,0:T(8,128)S(1)} %bitcast.20, s32[1,2304]{1,0:T(1,128)S(1)} %constant_dynamic-slice_fusion.index), custom_call_target="tpu_custom_call" | custom-call | tf_op jit(solution)/shard_map/pallas_call | solution.py:356
  27.3 2.2 collective-permute-start
  29.6 16.5 %all_to_all.86.received = f32[32,8,128]{2,1,0:T(8,128)S(1)} all-to-all(f32[32,8,128]{2,1,0:T(8,128)S(1)} %get-tuple-element.37), channel_id=1, replica_groups=mesh['y2'=2,'y1'=2,'y0'=2,'x'=4,'c'=2,'z'=8] {'x','z'}, dimensions={0} | all-to-all | bytes 262144 | tf_op jit(solution)/shard_map/all_to_all | solution.py:50
  46.1 10.0 %all_to_all.87.received.solved = f32[8,8,128]{2,1,0:T(8,128)S(1)} all-to-all(f32[8,8,128]{2,1,0:T(8,128)S(1)} %shard_map.174), channel_id=1, replica_groups=mesh['y2'=2,'y1'=2,'y0'=2,'x'=4,'c'=2,'z'=8] {'z'}, dimensions={0} | all-to-all | bytes 65536 | tf_op jit(solution)/shard_map/all_to_all | solution.py:50
  56.1 1.6 shard_map.175
  57.7 15.3 %all_to_all.88.received = f32[64,8,128]{2,1,0:T(8,128)S(1)} all-to-all(f32[64,8,128]{2,1,0:T(8,128)S(1)} %shard_map.175), channel_id=1, replica_groups=mesh['y2'=2,'y1'=2,'y0'=2,'x'=4,'c'=2,'z'=8] {'y0','x','z'}, dimensions={0} | all-to-all | bytes 524288 | tf_op jit(solution)/shard_map/all_to_all | solution.py:50
  73.0 0.7 shard_map.176
  73.7 3.5 %all-to-all-start.3 = ((f32[16,8,128]{2,1,0:T(8,128)}), f32[16,8,128]{2,1,0:T(8,128)S(1)}, u32[]{:S(2)}, u32[]{:S(2)}) async-start(f32[16,8,128]{2,1,0:T(8,128)} %shard_map.176), calls=%async_computation.3 | async-start | bytes 131072 | tf_op jit(solution)/shard_map/all_to_all | solution.py:50
  77.2 1.3 slice_bitcast_fusion.rest_in
  78.4 6.0 %all-to-all-done.3.received = f32[16,8,128]{2,1,0:T(8,128)S(1)} async-done(((f32[16,8,128]{2,1,0:T(8,128)}), f32[16,8,128]{2,1,0:T(8,128)S(1)}, u32[]{:S(2)}, u32[]{:S(2)}) %all-to-all-start.3) | async-done | bytes 65568 | tf_op jit(solution)/shard_map/all_to_all | solution.py:50
  84.5 0.6 copy-done.19
  85.1 4.2 %shard_map.177 = (f32[2,128,128]{2,1,0:T(8,128)}, f32[32,32,128]{2,1,0:T(8,128)}, f32[96,128]{1,0:T(8,128)}) custom-call(s32[80]{0:T(128)} %copy-done.12, f32[16,8,128]{2,1,0:T(8,128)} %copy-done.19, f32[128,8192]{1,0:T(8,128)} %all-gather.7.cloned.1.call-done.matrix, f32[8,128]{1,0:T(8,128)} %slice_bitcast_fusion.rest_in), custom_call_target="tpu_custom_call" | custom-call | flops 8388608 | bytes 4194304 | tf_op jit(solution)/shard_map/pallas_call | solution.py:148
  89.4 5.1 %all-to-all-start.4 = ((f32[32,32,128]{2,1,0:T(8,128)}), f32[32,32,128]{2,1,0:T(8,128)S(1)}, u32[]{:S(2)}, u32[]{:S(2)}) async-start(f32[32,32,128]{2,1,0:T(8,128)} %get-tuple-element.45), calls=%async_computation.4 | async-start | bytes 1048576 | tf_op jit(solution)/shard_map/all_to_all | solution.py:50
  94.5 0.0 all-gather.13.cloned.1.call-start
  94.5 0.5 all-gather.13.cloned.1.call-update
  95.1 11.9 %all-to-all-done.4.received = f32[32,32,128]{2,1,0:T(8,128)S(1)} async-done(((f32[32,32,128]{2,1,0:T(8,128)}), f32[32,32,128]{2,1,0:T(8,128)S(1)}, u32[]{:S(2)}, u32[]{:S(2)}) %all-to-all-start.4) | async-done | bytes 524320 | tf_op jit(solution)/shard_map/all_to_all | solution.py:50
  107.0 0.8 copy-done.14
  107.7 3.4 %shard_map.178 = (f32[2,64,128]{2,1,0:T(8,128)}, f32[8,64,128]{2,1,0:T(8,128)}, f32[64,128]{1,0:T(8,128)}) custom-call(s32[80]{0:T(128)} %copy-done.12, f32[32,32,128]{2,1,0:T(8,128)} %copy-done.14, f32[64,10240]{1,0:T(8,128)} %all-gather.9.cloned.1.call-done.matrix, f32[96,128]{1,0:T(8,128)} %get-tuple-element.46.rest_in), custom_call_target="tpu_custom_call" | custom-call | flops 3145728 | bytes 1572864 | tf_op jit(solution)/shard_map/pallas_call | solution.py:148
  111.2 23.3 %all_to_all.89.received = f32[64,8,128]{2,1,0:T(8,128)S(1)} all-to-all(f32[64,8,128]{2,1,0:T(8,128)} %bitcast.23), channel_id=1, replica_groups=mesh['y2'=2,'y1'=2,'y0'=2,'x'=4,'c'=2,'z'=8] {'y2','y1','y0','z'}, dimensions={0} | all-to-all | bytes 524288 | tf_op jit(solution)/shard_map/all_to_all | solution.py:50
  134.5 0.1 shard_map.179
  134.6 9.9 %all_to_all.90 = f32[8,8,128]{2,1,0:T(8,128)} all-to-all(f32[8,8,128]{2,1,0:T(8,128)S(1)} %shard_map.179), channel_id=1, replica_groups=mesh['y2'=2,'y1'=2,'y0'=2,'x'=4,'c'=2,'z'=8] {'z'}, dimensions={0} | all-to-all | bytes 65536 | tf_op jit(solution)/shard_map/all_to_all | solution.py:50
  144.5 3.0 %shard_map.180 = f32[8,64,128]{2,1,0:T(8,128)} custom-call(f32[64,128]{1,0:T(8,128)} %bitcast.25, f32[64,10240]{1,0:T(8,128)} %all-gather.9.cloned.1.call-done.matrix), custom_call_target="tpu_custom_call" | custom-call | flops 2097152 | bytes 1048576 | tf_op jit(solution)/shard_map/pallas_call | solution.py:279
  147.5 17.3 %all_to_all.91.received = f32[64,8,128]{2,1,0:T(8,128)S(1)} all-to-all(f32[64,8,128]{2,1,0:T(8,128)} %bitcast.22), channel_id=1, replica_groups=mesh['y2'=2,'y1'=2,'y0'=2,'x'=4,'c'=2,'z'=8] {'y2','y1','y0','z'}, dimensions={0} | all-to-all | bytes 524288 | tf_op jit(solution)/shard_map/all_to_all | solution.py:50
  164.8 0.1 shard_map.181
  164.9 9.9 %all_to_all.92 = f32[8,8,128]{2,1,0:T(8,128)} all-to-all(f32[8,8,128]{2,1,0:T(8,128)S(1)} %shard_map.181), channel_id=1, replica_groups=mesh['y2'=2,'y1'=2,'y0'=2,'x'=4,'c'=2,'z'=8] {'z'}, dimensions={0} | all-to-all | bytes 65536 | tf_op jit(solution)/shard_map/all_to_all | solution.py:50
  174.8 3.4 %shard_map.182 = (f32[32,32,128]{2,1,0:T(8,128)}, f32[64,128]{1,0:T(8,128)}) custom-call(s32[80]{0:T(128)} %copy-done.12, f32[1,64,128]{2,1,0:T(8,128)} %bitcast.24, f32[64,10240]{1,0:T(8,128)} %all-gather.9.cloned.1.call-done.matrix, f32[2,64,128]{2,1,0:T(8,128)} %get-tuple-element.48.solved), custom_call_target="tpu_custom_call" | custom-call | flops 3145728 | bytes 1572864 | tf_op jit(solution)/shard_map/pallas_call | solution.py:250
  178.2 3.9 %all-to-all-start.9 = ((f32[32,32,128]{2,1,0:T(8,128)}), f32[32,32,128]{2,1,0:T(8,128)S(1)}, u32[]{:S(2)}, u32[]{:S(2)}) async-start(f32[32,32,128]{2,1,0:T(8,128)} %get-tuple-element.49), calls=%async_computation.9 | async-start | bytes 1048576 | tf_op jit(solution)/shard_map/all_to_all | solution.py:50
  182.1 0.1 reduce_sum.12
  182.2 0.1 concatenate.18.scalars
  182.3 0.8 copy-done.5
  183.1 2.2 shard_map.183.chosen0
  185.2 0.7 copy-done.2
  185.9 8.4 %all-to-all-done.9.received = f32[32,32,128]{2,1,0:T(8,128)S(1)} async-done(((f32[32,32,128]{2,1,0:T(8,128)}), f32[32,32,128]{2,1,0:T(8,128)S(1)}, u32[]{:S(2)}, u32[]{:S(2)}) %all-to-all-start.9) | async-done | bytes 524320 | tf_op jit(solution)/shard_map/all_to_all | solution.py:50
  194.3 0.8 copy-done.13
  195.1 4.4 %shard_map.184 = (f32[16,32,128]{2,1,0:T(8,128)}, f32[32,128]{1,0:T(8,128)}) custom-call(s32[80]{0:T(128)} %copy-done.12, f32[32,32,128]{2,1,0:T(8,128)} %copy-done.13, f32[128,8192]{1,0:T(8,128)} %all-gather.7.cloned.1.call-done.matrix, f32[2,128,128]{2,1,0:T(8,128)} %get-tuple-element.52.solved, f32[64,128]{1,0:T(8,128)} %get-tuple-element.50.x.refs_0_.x0), custom_call_target="tpu_custom_call" | custom-call | flops 8388608 | bytes 4194304 | tf_op jit(solution)/shard_map/pallas_call | solution.py:250
  199.5 3.5 %all-to-all-start.10 = ((f32[16,32,128]{2,1,0:T(8,128)}), f32[16,32,128]{2,1,0:T(8,128)S(1)}, u32[]{:S(2)}, u32[]{:S(2)}) async-start(f32[16,32,128]{2,1,0:T(8,128)} %get-tuple-element.53), calls=%async_computation.10 | async-start | bytes 524288 | tf_op jit(solution)/shard_map/all_to_all | solution.py:50
  203.0 0.7 copy-done.8
  203.7 1.4 shard_map.185.chosen1
  205.1 0.7 copy-done.3
  205.7 4.8 %all-to-all-done.10.received = f32[16,32,128]{2,1,0:T(8,128)S(1)} async-done(((f32[16,32,128]{2,1,0:T(8,128)}), f32[16,32,128]{2,1,0:T(8,128)S(1)}, u32[]{:S(2)}, u32[]{:S(2)}) %all-to-all-start.10) | async-done | bytes 262176 | tf_op jit(solution)/shard_map/all_to_all | solution.py:50
  210.5 0.7 copy-done.16
  211.3 4.2 %shard_map.186 = (f32[8,16,128]{2,1,0:T(8,128)}, f32[32,128]{1,0:T(8,128)}) custom-call(s32[80]{0:T(128)} %copy-done.12, f32[16,32,128]{2,1,0:T(8,128)} %copy-done.16, f32[128,9216]{1,0:T(8,128)} %all-gather.11.cloned.1.call-done.matrix, f32[8,8,128]{2,1,0:T(8,128)} %copy-done.7, f32[64,128]{1,0:T(8,128)} %get-tuple-element.50.x.refs_0_.x0, ...), custom_call_target="tpu_custom_call" | custom-call | flops 9437184 | bytes 4718592 | tf_op jit(solution)/shard_map/pallas_call | solution.py:250
  215.5 3.4 %all-to-all-start.11 = ((f32[8,16,128]{2,1,0:T(8,128)}), f32[8,16,128]{2,1,0:T(8,128)S(1)}, u32[]{:S(2)}, u32[]{:S(2)}) async-start(f32[8,16,128]{2,1,0:T(8,128)} %get-tuple-element.57), calls=%async_computation.11 | async-start | bytes 131072 | tf_op jit(solution)/shard_map/all_to_all | solution.py:50
  218.9 0.7 copy-done.9
  219.6 1.4 shard_map.187.chosen2
  221.0 0.7 copy-done.4
  221.6 4.4 %all-to-all-done.11.received = f32[8,16,128]{2,1,0:T(8,128)S(1)} async-done(((f32[8,16,128]{2,1,0:T(8,128)}), f32[8,16,128]{2,1,0:T(8,128)S(1)}, u32[]{:S(2)}, u32[]{:S(2)}) %all-to-all-start.11) | async-done | bytes 65568 | tf_op jit(solution)/shard_map/all_to_all | solution.py:50
  226.0 0.6 copy-done.18
  226.6 5.1 %shard_map.188 = f32[8,16,128]{2,1,0:T(8,128)} custom-call(s32[152]{0:T(256)} %copy-done.11, f32[8,16,128]{2,1,0:T(8,128)} %copy-done.18, f32[64,128]{1,0:T(8,128)} %get-tuple-element.50.x.refs_0_.x0, f32[32,128]{1,0:T(8,128)} %get-tuple-element.54.x.refs_1_.x1, f32[32,128]{1,0:T(8,128)} %get-tuple-element.58.x.x2, ...), custom_call_target="tpu_custom_call" | custom-call | tf_op jit(solution)/shard_map/pallas_call | solution.py:440
  231.8 14.5 %all-to-all-start.12 = ((f32[8,16,128]{2,1,0:T(8,128)}), f32[8,16,128]{2,1,0:T(8,128)S(1)}, u32[]{:S(2)}, u32[]{:S(2)}) async-start(f32[8,16,128]{2,1,0:T(8,128)} %shard_map.188), calls=%async_computation.12 | async-start | bytes 131072 | tf_op jit(solution)/shard_map/all_to_all | solution.py:50
  246.3 0.1 stack.35.scalars
  246.4 4.9 %all-to-all-done.12.received = f32[8,16,128]{2,1,0:T(8,128)S(1)} async-done(((f32[8,16,128]{2,1,0:T(8,128)}), f32[8,16,128]{2,1,0:T(8,128)S(1)}, u32[]{:S(2)}, u32[]{:S(2)}) %all-to-all-start.12) | async-done | bytes 65568 | tf_op jit(solution)/shard_map/all_to_all | solution.py:50
  251.2 1.3 shard_map.189
  (60 shorter events, 0.4 us)
Async XLA Ops:
  7.2 4.3 %copy-start = (s32[16,2048]{1,0:T(8,128)S(1)}, s32[16,2048]{1,0:T(8,128)}, u32[]{:S(2)}) copy-start(s32[16,2048]{1,0:T(8,128)} %param.27) | copy-start | bytes 393220
  7.2 4.1 %copy-start.23 = (f32[16,8]{0,1:T(8,128)S(1)}, f32[16,8]{0,1:T(8,128)}, u32[]{:S(2)}) copy-start(f32[16,8]{0,1:T(8,128)} %param.14) | copy-start | bytes 1540
  7.2 4.1 %copy-start.24 = (f32[16,8]{0,1:T(8,128)S(1)}, f32[16,8]{0,1:T(8,128)}, u32[]{:S(2)}) copy-start(f32[16,8]{0,1:T(8,128)} %param.15) | copy-start | bytes 1540
  7.2 4.2 %copy-start.10 = (f32[16,32]{1,0:T(8,128)S(1)}, f32[16,32]{1,0:T(8,128)}, u32[]{:S(2)}) copy-start(f32[16,32]{1,0:T(8,128)} %values.1) | copy-start | bytes 6148
  7.2 4.2 %copy-start.21 = (f32[16,16]{1,0:T(8,128)S(1)}, f32[16,16]{1,0:T(8,128)}, u32[]{:S(2)}) copy-start(f32[16,16]{1,0:T(8,128)} %param.16) | copy-start | bytes 3076
  7.2 4.2 %copy-start.22 = (f32[16,16]{1,0:T(8,128)S(1)}, f32[16,16]{1,0:T(8,128)}, u32[]{:S(2)}) copy-start(f32[16,16]{1,0:T(8,128)} %param.17) | copy-start | bytes 3076
  7.2 13.1 %copy-start.15 = (f32[32,2048]{1,0:T(8,128)S(1)}, f32[32,2048]{1,0:T(8,128)}, u32[]{:S(2)}) copy-start(f32[32,2048]{1,0:T(8,128)} %param.26) | copy-start | bytes 786436
  7.2 20.0 %copy-start.20 = (f32[16,1024]{1,0:T(8,128)S(1)}, f32[16,1024]{1,0:T(8,128)}, u32[]{:S(2)}) copy-start(f32[16,1024]{1,0:T(8,128)} %param.21) | copy-start | bytes 196612
  7.3 20.0 %copy-start.17 = (f32[16,8192]{1,0:T(8,128)S(1)}, f32[16,8192]{1,0:T(8,128)}, u32[]{:S(2)}) copy-start(f32[16,8192]{1,0:T(8,128)} %param.24) | copy-start | bytes 1572868
  7.3 77.2 %all-gather.7.cloned.1.call-start = ((), (), s32[]{:S(2)}) async-start(), calls=%async_computation.13 | async-start | bytes 4718592 | tf_op jit(solution)/shard_map/all_gather | solution.py:506
  9.4 85.7 %all-gather.9.cloned.1.call-start = ((), (), s32[]{:S(2)}) async-start(), calls=%async_computation.14 | async-start | bytes 2949120 | tf_op jit(solution)/shard_map/all_gather | solution.py:506
  11.2 199.4 %all-gather.11.cloned.1.call-start = ((), (), s32[]{:S(2)}) async-start(), calls=%async_computation.15 | async-start | bytes 5308416 | tf_op jit(solution)/shard_map/all_gather | solution.py:506
  11.9 45.7 %copy-start.12 = (s32[80]{0:T(128)}, s32[80]{0:T(128)S(1)}, u32[]{:S(2)}) copy-start(s32[80]{0:T(128)S(1)} %concatenate.19.scalars) | copy-start | bytes 964
  27.3 30.3 %copy-start.1 = (f32[16,9216]{1,0:T(8,128)}, f32[16,9216]{1,0:T(8,128)S(1)}, u32[]{:S(2)}) copy-start(f32[16,9216]{1,0:T(8,128)S(1)} %constant_dynamic-update-slice_fusion.own) | copy-start | bytes 1769476
  27.3 18.7 %collective-permute-start = (f32[16,9216]{1,0:T(8,128)S(1)}, f32[16,9216]{1,0:T(8,128)S(1)}, u32[]{:S(2)}, u32[]{:S(2)}) collective-permute-start(f32[16,9216]{1,0:T(8,128)S(1)} %constant_dynamic-update-slice_fusion.own), channel_id=1, source_target_pairs={{0,8},{8,0},{1,9},{9,1},{2,10},{10,2},{3,11},{11,3},{4,12},{12,4},... | collective-permute-start | bytes 1769480 | tf_op jit(solution)/shard_map/ppermute | solution.py:527
  56.1 33.3 %copy-start.7 = (f32[8,8,128]{2,1,0:T(8,128)}, f32[8,8,128]{2,1,0:T(8,128)S(1)}, u32[]{:S(2)}) copy-start(f32[8,8,128]{2,1,0:T(8,128)S(1)} %all_to_all.87.received.solved) | copy-start | bytes 98308
  73.7 10.8 %all-to-all-start.3 = ((f32[16,8,128]{2,1,0:T(8,128)}), f32[16,8,128]{2,1,0:T(8,128)S(1)}, u32[]{:S(2)}, u32[]{:S(2)}) async-start(f32[16,8,128]{2,1,0:T(8,128)} %shard_map.176), calls=%async_computation.3 | async-start | bytes 131072 | tf_op jit(solution)/shard_map/all_to_all | solution.py:50
  84.5 0.6 copy-start.19
  89.4 17.6 %all-to-all-start.4 = ((f32[32,32,128]{2,1,0:T(8,128)}), f32[32,32,128]{2,1,0:T(8,128)S(1)}, u32[]{:S(2)}, u32[]{:S(2)}) async-start(f32[32,32,128]{2,1,0:T(8,128)} %get-tuple-element.45), calls=%async_computation.4 | async-start | bytes 1048576 | tf_op jit(solution)/shard_map/all_to_all | solution.py:50
  94.5 127.2 %all-gather.13.cloned.1.call-start = ((), (), s32[]{:S(2)}) async-start(), calls=%async_computation.16 | async-start | bytes 2359296 | tf_op jit(solution)/shard_map/all_gather | solution.py:506
  106.9 0.8 copy-start.14
  178.2 16.1 %all-to-all-start.9 = ((f32[32,32,128]{2,1,0:T(8,128)}), f32[32,32,128]{2,1,0:T(8,128)S(1)}, u32[]{:S(2)}, u32[]{:S(2)}) async-start(f32[32,32,128]{2,1,0:T(8,128)} %get-tuple-element.49), calls=%async_computation.9 | async-start | bytes 1048576 | tf_op jit(solution)/shard_map/all_to_all | solution.py:50
  182.2 36.7 %copy-start.6 = (s32[2,2304]{1,0:T(2,128)}, s32[2,2304]{1,0:T(2,128)S(1)}, u32[]{:S(2)}) copy-start(s32[2,2304]{1,0:T(2,128)S(1)} %pad.9.index) | copy-start | bytes 55300
  182.3 36.6 %copy-start.11 = (s32[152]{0:T(256)}, s32[152]{0:T(256)S(1)}, u32[]{:S(2)}) copy-start(s32[152]{0:T(256)S(1)} %concatenate.18.scalars) | copy-start | bytes 1828
  182.3 0.8 copy-start.5
  185.2 0.7 copy-start.2
  194.3 0.8 copy-start.13
  199.5 11.1 %all-to-all-start.10 = ((f32[16,32,128]{2,1,0:T(8,128)}), f32[16,32,128]{2,1,0:T(8,128)S(1)}, u32[]{:S(2)}, u32[]{:S(2)}) async-start(f32[16,32,128]{2,1,0:T(8,128)} %get-tuple-element.53), calls=%async_computation.10 | async-start | bytes 524288 | tf_op jit(solution)/shard_map/all_to_all | solution.py:50
  203.0 0.7 copy-start.8
  205.1 0.7 copy-start.3
  210.5 0.7 copy-start.16
  215.5 10.5 %all-to-all-start.11 = ((f32[8,16,128]{2,1,0:T(8,128)}), f32[8,16,128]{2,1,0:T(8,128)S(1)}, u32[]{:S(2)}, u32[]{:S(2)}) async-start(f32[8,16,128]{2,1,0:T(8,128)} %get-tuple-element.57), calls=%async_computation.11 | async-start | bytes 131072 | tf_op jit(solution)/shard_map/all_to_all | solution.py:50
  218.9 0.7 copy-start.9
  221.0 0.7 copy-start.4
  226.0 0.6 copy-start.18
  231.8 19.5 %all-to-all-start.12 = ((f32[8,16,128]{2,1,0:T(8,128)}), f32[8,16,128]{2,1,0:T(8,128)S(1)}, u32[]{:S(2)}, u32[]{:S(2)}) async-start(f32[8,16,128]{2,1,0:T(8,128)} %shard_map.188), calls=%async_computation.12 | async-start | bytes 131072 | tf_op jit(solution)/shard_map/all_to_all | solution.py:50
Sparse Core Ops, SparseCore 0:
  10.3 44.7 all-gather.6
  57.1 31.4 all-gather.8
  90.8 40.1 all-gather.10
  133.0 30.5 all-gather.12

commit v5 on v4

--- a/solution.py
+++ b/solution.py
@@ -19,7 +19,7 @@
 CHUNK = 32
 HBM = pl.BlockSpec(memory_space=pltpu.HBM)
 LIMIT = 16 * 2**20
-WHOLE = 58 * 2**20
+WHOLE = 50 * 2**20
 ALL_Y = ("y2", "y1", "y0")
 INTERPRET = False
 VMEM = pl.BlockSpec(memory_space=pltpu.VMEM)
@@ -88,32 +88,30 @@
             total[at] = total[at] + part
 
 
-def chunk_copies(matrices, buffer, ready):
+def chunk_copies(matrix, buffer, ready):
     copies = []
-    for number, matrix in enumerate(matrices):
-        count = matrix.shape[0] // CHUNK
-        for chunk in range(count):
-            place = number * count + chunk
-            columns = pl.ds(0, buffer.shape[1])
-            source = matrix.at[pl.ds(chunk * CHUNK, CHUNK), columns]
-            copies.append(pltpu.make_async_copy(source, buffer.at[pl.ds(place * CHUNK, CHUNK), columns], ready.at[place]))
+    for place in range(matrix.shape[0] // 8):
+        rows, columns = pl.ds(place * 8, 8), pl.ds(0, buffer.shape[1])
+        copies.append(pltpu.make_async_copy(matrix.at[rows, columns], buffer.at[rows, columns], ready.at[place]))
     for copy in copies:
         copy.start()
     return copies
 
 
 def each_chunk(copies, step):
-    for place, copy in enumerate(copies):
-        copy.wait()
-        step(pl.ds(place * CHUNK, CHUNK))
+    share = CHUNK // 8
+    for chunk in range(len(copies) // share):
+        for copy in copies[chunk * share : (chunk + 1) * share]:
+            copy.wait()
+        step(pl.ds(chunk * CHUNK, CHUNK))
 
 
 def chunk_buffers(rows, width):
-    return [pltpu.VMEM((rows, width), jnp.float32), pltpu.SemaphoreType.DMA((rows // CHUNK,))]
+    return [pltpu.VMEM((rows, width), jnp.float32), pltpu.SemaphoreType.DMA((rows // 8,))]
 
 
 def forward_kernel(blocks, upper, keep, extra, scalars, received, matrix, rest_in, solved, send, rest, vector, total, buffer, ready):
-    copies = chunk_copies((matrix,), buffer, ready)
+    copies = chunk_copies(matrix, buffer, ready)
     if extra:
         for source in range(blocks):
             vector[2 * source : 2 * source + 2, :] = received[source, 0:2, :]
@@ -159,11 +157,7 @@
 
 def lowest_kernel(blocks, upper, received, own, other, path, send, total, buffer, ready):
     rows = own.shape[0]
-    copies = []
-    for number, matrix in enumerate((own, other)):
-        copies.append(pltpu.make_async_copy(matrix, buffer.at[pl.ds(number * rows, rows), :], ready.at[number]))
-    for copy in copies:
-        copy.start()
+    copies = chunk_copies(own, buffer.at[0:rows, :], ready.at[0]) + chunk_copies(other, buffer.at[rows:, :], ready.at[1])
     for copy in copies:
         copy.wait()
     samples = range(received.shape[1])
@@ -209,7 +203,7 @@
         scratch_shapes=[
             pltpu.VMEM((received.shape[1], 2 * rows, LANES), jnp.float32),
             pltpu.VMEM((2 * rows, width), jnp.float32),
-            pltpu.SemaphoreType.DMA((2,)),
+            pltpu.SemaphoreType.DMA((2, rows // 8)),
         ],
         cost_estimate=cost(2 * rows * width),
     )(received, own, other, path)
@@ -217,7 +211,7 @@
 
 def backward_kernel(blocks, known_blocks, scalars, received, matrix, solved, *refs):
     known, (send, newest, total, vector, buffer, ready) = refs[: len(known_blocks) - 1], refs[len(known_blocks) - 1 :]
-    copies = chunk_copies((matrix,), buffer, ready)
+    copies = chunk_copies(matrix, buffer, ready)
     newest[...] = jnp.sum(received[...], axis=0)
     total[...] = jnp.zeros_like(total)
     again = solved.shape[2] == LANES and solved.shape[0] == blocks
@@ -260,7 +254,7 @@
 
 
 def root_kernel(column, blocks, vector, matrix, send, total, buffer, ready):
-    copies = chunk_copies((matrix.at[:, column:],), buffer, ready)
+    copies = chunk_copies(matrix.at[:, column:], buffer, ready)
     total[...] = jnp.zeros_like(total)
 
     def step(rows):
@@ -297,38 +291,27 @@
     return call(functools.partial(sum_kernel, copies), f32(copies, *received.shape[1:]))(received)
 
 
-def first_kernel(depth, scalars, small, coupling, index, send, path, terms):
-    z, core, x = scalars[0], scalars[1], scalars[2]
-    upper = sum(WIDTHS[:3]) // LANES
-    count = upper + WIDTHS[3] // LANES
-    rows, columns = coupling.shape[1:]
-    half = pl.multiple_of(core * 8, 8)
-    parts = [small[other, pl.ds(half, 8), :] for other in range(C)]
-    update = None
-    for other in range(C):
-        product = lax.dot_general(
-            parts[other][:, :rows], coupling[other], NN, precision=lax.Precision.HIGHEST, preferred_element_type=jnp.float32
-        )
-        update = product if update is None else update + product
-    pieces = split3(update)
-    terms[:, columns:] = jnp.zeros((32, terms.shape[1] - columns), jnp.bfloat16)
-    terms[:, :columns] = jnp.concatenate([*pieces, jnp.zeros_like(pieces[0])], axis=0)
-
-    def expand(block, carry):
-        at = pl.multiple_of(scalars[8 + block] * LANES, LANES)
-        selector = one_hot(index[0:1, pl.ds(at, 2 * LANES)], block)
+def expand(scalars, terms, index, first_block, path):
+    def one(block, carry):
+        at = pl.multiple_of(scalars[8 + first_block + block] * LANES, LANES)
+        selector = one_hot(index[0:1, pl.ds(at, 2 * LANES)], first_block + block)
         out = lax.dot_general(terms[:, pl.ds(at, 2 * LANES)], selector, NT, preferred_element_type=jnp.float32)
         path[block] = -(out[0:8] + out[8:16] + out[16:24])
         return carry
 
-    lax.fori_loop(0, count, expand, 0, unroll=4)
-
+    lax.fori_loop(0, path.shape[0], one, 0, unroll=4)
+
+
+def add_own(scalars, small, source, depth, heights, path):
+    z, core, x = scalars[0], scalars[1], scalars[2]
+    half = pl.multiple_of(core * 8, 8)
     lane = lax.broadcasted_iota(jnp.int32, (8, LANES), 1)
     start = 0
-    source = rows
     for height in range(4):
         width = 8 if height < 2 else 16
         for other in range(C):
+            if height not in heights:
+                continue
             offset = z * width
             block = start
             if height < 3:
@@ -338,28 +321,60 @@
                 block = block + x
             else:
                 block = block + x * 2 + other
-            moved = pltpu.roll(parts[other], lax.rem(offset - source + LANES, LANES), 1)
-            kept = jnp.where((lane >= offset) & (lane < offset + width), moved, 0.0)
-            path[block] = path[block] + kept
-        start += WIDTHS[height] // LANES
+            moved = pltpu.roll(small[other, pl.ds(half, 8), :], lax.rem(offset - source + LANES, LANES), 1)
+            path[block] = path[block] + jnp.where((lane >= offset) & (lane < offset + width), moved, 0.0)
+        start += WIDTHS[height] // LANES if height in heights else 0
         source += width
 
+
+def first_kernel(depth, scalars, small, coupling, index, send, terms, path):
+    rows, columns = coupling.shape[1:]
+    half = pl.multiple_of(scalars[1] * 8, 8)
+    update = None
+    for other in range(C):
+        product = lax.dot_general(
+            small[other, pl.ds(half, 8), :][:, :rows],
+            coupling[other],
+            NN,
+            precision=lax.Precision.HIGHEST,
+            preferred_element_type=jnp.float32,
+        )
+        update = product if update is None else update + product
+    pieces = split3(update)
+    terms[:, columns:] = jnp.zeros((32, terms.shape[1] - columns), jnp.bfloat16)
+    terms[:, :columns] = jnp.concatenate([*pieces, jnp.zeros_like(pieces[0])], axis=0)
+    expand(scalars, terms, index, sum(WIDTHS[:3]) // LANES, path)
+    add_own(scalars, small, rows, depth, (3,), path)
     for dest in range(X):
         for other in range(depth):
-            send[dest * depth + other] = path[upper + other]
+            send[dest * depth + other] = path[other]
 
 
 def first(small, coupling, index, scalars, depth):
     columns = coupling.shape[2]
-    upper = sum(WIDTHS[:3]) // LANES
-    lower = WIDTHS[3] // LANES
     return call(
         functools.partial(first_kernel, depth),
-        (f32(X * depth, 8, LANES), f32(upper + lower, 8, LANES)),
+        (f32(X * depth, 8, LANES), jax.ShapeDtypeStruct((32, columns + 2 * LANES), jnp.bfloat16)),
         in_specs=[SMEM, VMEM, VMEM, VMEM],
         out_specs=(VMEM, VMEM),
-        scratch_shapes=[pltpu.VMEM((32, columns + 2 * LANES), jnp.bfloat16)],
+        scratch_shapes=[pltpu.VMEM((WIDTHS[3] // LANES, 8, LANES), jnp.float32)],
     )(scalars, small, coupling, index)
+
+
+def upper_kernel(depth, rows, scalars, small, terms, index, path):
+    expand(scalars, terms, index, 0, path)
+    add_own(scalars, small, rows, depth, (0, 1, 2), path)
+
+
+def upper_path(small, terms, index, scalars, depth, rows):
+    blocks = sum(WIDTHS[:3]) // LANES
+    return call(
+        functools.partial(upper_kernel, depth, rows),
+        f32(blocks, 8, LANES),
+        in_specs=[SMEM, VMEM, VMEM, VMEM],
+        out_specs=VMEM,
+        cost_estimate=cost(blocks * LANES * LANES),
+    )(scalars, small, terms, index)
 
 
 def pick(scalars, index, terms, first_block, blocks, chosen):
@@ -403,14 +418,14 @@
 
 
 def last_kernel(columns, counts, scalars, received, x0, x1, x2, coupling, index, chosen0, chosen1, chosen2, send, x3, terms, chosen, buffer, ready):
-    copy = pltpu.make_async_copy(coupling, buffer, ready)
-    copy.start()
+    copies = chunk_copies(coupling, buffer, ready)
     x3[...] = jnp.sum(received[...], axis=0)
     store_terms(x3, terms)
     chosen[...] = chosen0[...] + chosen1[...] + chosen2[...]
     pick(scalars, index, terms, sum(counts[:3]), counts[3], chosen)
     rows = coupling.shape[0] // 2
-    copy.wait()
+    for copy in copies:
+        copy.wait()
     handed = []
     for half in range(2):
         value = chosen[half, 0:2, :columns] + chosen[half, 2:4, :columns] + chosen[half, 4:6, :columns]
@@ -446,8 +461,7 @@
             pltpu.VMEM(received.shape[1:], jnp.float32),
             pltpu.VMEM((counts[3], 8, LANES), jnp.float32),
             pltpu.VMEM((2, 8, columns + 2 * LANES), jnp.float32),
-            pltpu.VMEM(coupling.shape, jnp.float32),
-            pltpu.SemaphoreType.DMA,
+            *chunk_buffers(*coupling.shape),
         ],
         limit=WHOLE,
     )(scalars, received, *known, coupling, index, *chosen)
@@ -505,9 +519,6 @@
     def gathered(whole):
         return lax.all_gather(whole, ("x", "c"), axis=0, tiled=True)
 
-    matrix2 = gathered(jnp.concatenate([inv_level2, cross_level2], axis=1))
-    matrix1 = gathered(jnp.concatenate([inv_level1, cross_level1, inv_root], axis=1))
-
     both_indices = lax.dynamic_slice_in_dim(coupled_rows, y * 2, 2, 0)
     edges = jnp.arange(blocks, dtype=jnp.int32) * LANES
     windows = jnp.sum((both_indices[:, None, :] < edges[None, :, None]).astype(jnp.int32), axis=2) // LANES
@@ -520,12 +531,24 @@
         return jnp.concatenate([head, *tails])
 
     places = scalars([z, c, x, y, y % 4, y % 2, (y % 2) * depth + z], own_windows)
-    send, path = first(both_small, both_coupling, own_indices, places, depth)
-    send, inv_level3, cross_level3, coupling = lax.optimization_barrier((send, inv_level3, cross_level3, coupling))
+    both_small, inv_level2, cross_level2 = lax.optimization_barrier((both_small, inv_level2, cross_level2))
+    matrix2 = gathered(jnp.concatenate([inv_level2, cross_level2], axis=1))
+    send, terms = first(both_small, both_coupling, own_indices, places, depth)
+    parts = (inv_level3, cross_level3, coupling, terms)
+    send, (inv_level3, cross_level3, coupling, terms) = lax.optimization_barrier((send, parts))
     own3 = jnp.concatenate([inv_level3, cross_level3], axis=1)
-    received, other3 = lax.optimization_barrier(
-        (exchange(send, ("x", "z")), lax.ppermute(own3, "c", [(0, 1), (1, 0)]))
+    path = upper_path(both_small, terms, own_indices, places, depth, coupling.shape[0])
+    received, other3, path, inv_root, inv_level1, cross_level1 = lax.optimization_barrier(
+        (
+            exchange(send, ("x", "z")),
+            lax.ppermute(own3, "c", [(0, 1), (1, 0)]),
+            path,
+            inv_root,
+            inv_level1,
+            cross_level1,
+        )
     )
+    matrix1 = gathered(jnp.concatenate([inv_level1, cross_level1, inv_root], axis=1))
     target3 = exchange(sum_and_copy(received, depth), ("z",))
     send = lowest(target3, own3, other3, path, counts[3], sum(counts[:3]), 2 * depth)
     send, own3, coupling = lax.optimization_barrier((send, own3, coupling))

time: 261 us -> 257 us (0.985)
  blocking collectives: 113 us -> 94.2 us
  waiting for transfers between devices: 40.9 us -> 51.2 us
  starting transfers between devices: 36.3 us -> 43.9 us
  local copies, waits for them, and re-layouts: 9.73 us -> 6.89 us
    all_to_all x7 -> x6, blocking collectives: 102 us -> 83.4 us  [exchange(): return lax.all_to_all(flat, axes, 0, 0, tiled=True).reshape(operand.shape)]
    all_to_all x6 -> x7, waiting for transfers between devices: 40.3 us -> 50.6 us  [exchange(): return lax.all_to_all(flat, axes, 0, 0, tiled=True).reshape(operand.shape)]
    all_to_all x6 -> x7, starting transfers between devices: 33.9 us -> 41.5 us  [exchange(): return lax.all_to_all(flat, axes, 0, 0, tiled=True).reshape(operand.shape)]
    unnamed x53 -> x25, local copies, waits for them, and re-layouts: 7.95 us -> 4.97 us
    pallas_call x1 -> x2, Pallas kernels: 4.75 us -> 6.05 us  [the longest x1 3.91 us: upper_path(): call(functools.partial(upper_kernel, depth, rows), f32(blocks, 8, LANES),...]
  transfers between devices with their start and end apart: 11 -> 12, of which waited for: 6 -> 7; matrix products, arithmetic and copies ran while one was open for 2% -> 1% of each run, Pallas kernels for 13% -> 14%
where the time goes in v5:
time: 257 us; the launch traced here: 256 us
  blocking collectives  94.2 us (37%)
  waiting for transfers between devices  51.2 us (20%)
  starting transfers between devices  43.9 us (17%)
  Pallas kernels  42.4 us (16%)
  between operations  14.1 us (5%)
  local copies, waits for them, and re-layouts  6.89 us (3%)
  other arithmetic  2.94 us (1%)
    all_to_all x6, blocking collectives, exchange(): return lax.all_to_all(flat, axes, 0, 0, tiled=True).reshape(operand.shape)  83.4 us
    all_to_all x7, waiting for transfers between devices, exchange(): return lax.all_to_all(flat, axes, 0, 0, tiled=True).reshape(operand.shape)  50.6 us
    all_to_all x7, starting transfers between devices, exchange(): return lax.all_to_all(flat, axes, 0, 0, tiled=True).reshape(operand.shape)  41.5 us
    pallas_call x3, Pallas kernels, backward(): call(functools.partial(backward_kernel, blocks, counts), (f32(copies, 2 *...  11.7 us
    all_gather x1, blocking collectives, body(): both_small = lax.all_gather(small, 'c', axis=0, tiled=False)  8.37 us
    pallas_call x2, Pallas kernels, forward(): call(functools.partial(forward_kernel, blocks, upper, keep, extra), (f32(...  7.76 us
    pallas_call x1, Pallas kernels, last(): call(functools.partial(last_kernel, columns, counts), f32(XC, 16, LANES),...  6.38 us
  transfers between devices with their start and end apart: 12, of which 7 were waited for; matrix products, arithmetic and copies ran while one was open for 1% of the time, Pallas kernels for 14%

profile of v5, /device:TPU:1, one launch (start us, length us, event | category | flops | bytes accessed | tf_op | source)
XLA Modules:
  0.0 255.6 jit_solution(13729755646270741744)
XLA Ops:
  7.2 0.0 copy-start
  7.2 0.0 all-gather.7.cloned.1.call-start
  7.2 0.8 copy.21
  8.1 0.8 copy.22
  8.8 0.8 concatenate.20
  9.7 8.4 %all-gather = f32[32,128]{1,0:T(8,128)S(1)} all-gather(f32[16,128]{1,0:T(8,128)S(1)} %pad.8), channel_id=2, replica_groups=mesh['y2'=2,'y1'=2,'y0'=2,'x'=4,'c'=2,'z'=8] {'c'}, dimensions={0}, use_global_device_ids=true | all-gather | bytes 24576 | tf_op jit(solution)/shard_map/all_gather | solution.py:516
  18.0 1.9 pad_maximum_fusion
  19.9 0.0 all-gather.7.cloned.1.call-update
  20.0 0.3 convert_reduce_fusion
  20.3 0.1 concatenate.19.scalars
  20.4 2.4 all-gather.1
  22.8 2.1 shard_map.173
  25.0 2.2 collective-permute-start
  27.3 7.5 %all-to-all-start = ((f32[32,8,128]{2,1,0:T(8,128)}), f32[32,8,128]{2,1,0:T(8,128)S(1)}, u32[]{:S(2)}, u32[]{:S(2)}) async-start(f32[32,8,128]{2,1,0:T(8,128)} %get-tuple-element.47), calls=%async_computation | async-start | bytes 262144 | tf_op jit(solution)/shard_map/all_to_all | solution.py:50
  34.8 0.0 all-gather.9.cloned.1.call-start
  34.8 3.9 %shard_map.174.path = f32[64,8,128]{2,1,0:T(8,128)S(1)} custom-call(s32[80]{0:T(128)S(1)} %concatenate.19.scalars, f32[2,16,128]{2,1,0:T(8,128)S(1)} %bitcast.24, bf16[32,2304]{1,0:T(8,128)(2,1)S(1)} %get-tuple-element.50.terms, s32[1,2304]{1,0:T(1,128)S(1)} %constant_dynamic-slice_fusion.index), custom_call_target="tpu_custom_call" | custom-call | flops 8388608 | bytes 4194304 | tf_op jit(solution)/shard_map/pallas_call | solution.py:371
  38.8 5.2 %all-to-all-done.received = f32[32,8,128]{2,1,0:T(8,128)S(1)} async-done(((f32[32,8,128]{2,1,0:T(8,128)}), f32[32,8,128]{2,1,0:T(8,128)S(1)}, u32[]{:S(2)}, u32[]{:S(2)}) %all-to-all-start) | async-done | bytes 131104 | tf_op jit(solution)/shard_map/all_to_all | solution.py:50
  44.0 0.8 pad_maximum_fusion.1
  44.7 0.0 all-gather.9.cloned.1.call-update
  44.8 0.0 all-gather.11.cloned.1.call-start
  44.9 10.0 %all_to_all.86.received.solved = f32[8,8,128]{2,1,0:T(8,128)S(1)} all-to-all(f32[8,8,128]{2,1,0:T(8,128)S(1)} %shard_map.175), channel_id=1, replica_groups=mesh['y2'=2,'y1'=2,'y0'=2,'x'=4,'c'=2,'z'=8] {'z'}, dimensions={0} | all-to-all | bytes 65536 | tf_op jit(solution)/shard_map/all_to_all | solution.py:50
  54.8 1.5 shard_map.176
  56.4 0.0 all-gather.11.cloned.1.call-update
  56.4 15.3 %all_to_all.87.received = f32[64,8,128]{2,1,0:T(8,128)S(1)} all-to-all(f32[64,8,128]{2,1,0:T(8,128)S(1)} %shard_map.176), channel_id=1, replica_groups=mesh['y2'=2,'y1'=2,'y0'=2,'x'=4,'c'=2,'z'=8] {'y0','x','z'}, dimensions={0} | all-to-all | bytes 524288 | tf_op jit(solution)/shard_map/all_to_all | solution.py:50
  71.7 0.7 shard_map.177
  72.4 3.5 %all-to-all-start.3 = ((f32[16,8,128]{2,1,0:T(8,128)}), f32[16,8,128]{2,1,0:T(8,128)S(1)}, u32[]{:S(2)}, u32[]{:S(2)}) async-start(f32[16,8,128]{2,1,0:T(8,128)} %shard_map.177), calls=%async_computation.3 | async-start | bytes 131072 | tf_op jit(solution)/shard_map/all_to_all | solution.py:50
  75.9 0.7 slice_bitcast_fusion.rest_in
  76.6 6.6 %all-to-all-done.3.received = f32[16,8,128]{2,1,0:T(8,128)S(1)} async-done(((f32[16,8,128]{2,1,0:T(8,128)}), f32[16,8,128]{2,1,0:T(8,128)S(1)}, u32[]{:S(2)}, u32[]{:S(2)}) %all-to-all-start.3) | async-done | bytes 65568 | tf_op jit(solution)/shard_map/all_to_all | solution.py:50
  83.2 4.0 %shard_map.178 = (f32[2,128,128]{2,1,0:T(8,128)S(1)}, f32[32,32,128]{2,1,0:T(8,128)}, f32[96,128]{1,0:T(8,128)S(1)}) custom-call(s32[80]{0:T(128)S(1)} %concatenate.19.scalars, f32[16,8,128]{2,1,0:T(8,128)S(1)} %all-to-all-done.3.received, f32[128,8192]{1,0:T(8,128)} %all-gather.7.cloned.1.call-done.matrix, f32[8,128]{1,0:T(8,128)S(1)} %slice_bitcast_fusion.rest_in), custom_call_target="tpu_custom_call" | custom-call | flops 8388608 | bytes 4194304 | tf_op jit(solution)/shard_map/pallas_call | solution.py:146
  87.3 5.1 %all-to-all-start.4 = ((f32[32,32,128]{2,1,0:T(8,128)}), f32[32,32,128]{2,1,0:T(8,128)S(1)}, u32[]{:S(2)}, u32[]{:S(2)}) async-start(f32[32,32,128]{2,1,0:T(8,128)} %get-tuple-element.58), calls=%async_computation.4 | async-start | bytes 1048576 | tf_op jit(solution)/shard_map/all_to_all | solution.py:50
  92.3 0.0 all-gather.13.cloned.1.call-start
  92.4 0.5 all-gather.13.cloned.1.call-update
  92.9 0.0 all-gather.9.cloned.1.call-done.matrix
  92.9 12.1 %all-to-all-done.4.received = f32[32,32,128]{2,1,0:T(8,128)S(1)} async-done(((f32[32,32,128]{2,1,0:T(8,128)}), f32[32,32,128]{2,1,0:T(8,128)S(1)}, u32[]{:S(2)}, u32[]{:S(2)}) %all-to-all-start.4) | async-done | bytes 524320 | tf_op jit(solution)/shard_map/all_to_all | solution.py:50
  105.0 1.7 copy-done.1
  106.8 3.7 %shard_map.179 = (f32[2,64,128]{2,1,0:T(8,128)S(1)}, f32[8,64,128]{2,1,0:T(8,128)S(1)}, f32[64,128]{1,0:T(8,128)}) custom-call(s32[80]{0:T(128)S(1)} %concatenate.19.scalars, f32[32,32,128]{2,1,0:T(8,128)S(1)} %all-to-all-done.4.received, f32[64,10240]{1,0:T(8,128)S(1)} %copy-done.1, f32[96,128]{1,0:T(8,128)S(1)} %get-tuple-element.62.rest_in), custom_call_target="tpu_custom_call" | custom-call | flops 3145728 | bytes 1572864 | tf_op jit(solution)/shard_map/pallas_call | solution.py:146
  110.5 22.9 %all_to_all.88.received = f32[64,8,128]{2,1,0:T(8,128)S(1)} all-to-all(f32[64,8,128]{2,1,0:T(8,128)S(1)} %bitcast.22), channel_id=1, replica_groups=mesh['y2'=2,'y1'=2,'y0'=2,'x'=4,'c'=2,'z'=8] {'y2','y1','y0','z'}, dimensions={0} | all-to-all | bytes 524288 | tf_op jit(solution)/shard_map/all_to_all | solution.py:50
  133.5 0.1 shard_map.180
  133.5 9.5 %all_to_all.89 = f32[8,8,128]{2,1,0:T(8,128)S(1)} all-to-all(f32[8,8,128]{2,1,0:T(8,128)S(1)} %shard_map.180), channel_id=1, replica_groups=mesh['y2'=2,'y1'=2,'y0'=2,'x'=4,'c'=2,'z'=8] {'z'}, dimensions={0} | all-to-all | bytes 65536 | tf_op jit(solution)/shard_map/all_to_all | solution.py:50
  143.0 1.9 shard_map.181
  144.9 16.4 %all_to_all.90.received = f32[64,8,128]{2,1,0:T(8,128)S(1)} all-to-all(f32[64,8,128]{2,1,0:T(8,128)S(1)} %bitcast.21), channel_id=1, replica_groups=mesh['y2'=2,'y1'=2,'y0'=2,'x'=4,'c'=2,'z'=8] {'y2','y1','y0','z'}, dimensions={0} | all-to-all | bytes 524288 | tf_op jit(solution)/shard_map/all_to_all | solution.py:50
  161.3 0.1 shard_map.182
  161.3 9.4 %all_to_all.91 = f32[8,8,128]{2,1,0:T(8,128)S(1)} all-to-all(f32[8,8,128]{2,1,0:T(8,128)S(1)} %shard_map.182), channel_id=1, replica_groups=mesh['y2'=2,'y1'=2,'y0'=2,'x'=4,'c'=2,'z'=8] {'z'}, dimensions={0} | all-to-all | bytes 65536 | tf_op jit(solution)/shard_map/all_to_all | solution.py:50
  170.7 4.0 %shard_map.183 = (f32[32,32,128]{2,1,0:T(8,128)}, f32[64,128]{1,0:T(8,128)S(1)}) custom-call(s32[80]{0:T(128)S(1)} %concatenate.19.scalars, f32[1,64,128]{2,1,0:T(8,128)S(1)} %bitcast.25, f32[64,10240]{1,0:T(8,128)S(1)} %copy-done.2, f32[2,64,128]{2,1,0:T(8,128)S(1)} %get-tuple-element.64.solved), custom_call_target="tpu_custom_call" | custom-call | flops 3145728 | bytes 1572864 | tf_op jit(solution)/shard_map/pallas_call | solution.py:244
  174.8 3.9 %all-to-all-start.9 = ((f32[32,32,128]{2,1,0:T(8,128)}), f32[32,32,128]{2,1,0:T(8,128)S(1)}, u32[]{:S(2)}, u32[]{:S(2)}) async-start(f32[32,32,128]{2,1,0:T(8,128)} %get-tuple-element.65), calls=%async_computation.9 | async-start | bytes 1048576 | tf_op jit(solution)/shard_map/all_to_all | solution.py:50
  178.7 0.1 reduce_sum.12
  178.8 0.1 concatenate.18.scalars
  178.9 2.2 shard_map.184.chosen0
  181.1 9.8 %all-to-all-done.9.received = f32[32,32,128]{2,1,0:T(8,128)S(1)} async-done(((f32[32,32,128]{2,1,0:T(8,128)}), f32[32,32,128]{2,1,0:T(8,128)S(1)}, u32[]{:S(2)}, u32[]{:S(2)}) %all-to-all-start.9) | async-done | bytes 524320 | tf_op jit(solution)/shard_map/all_to_all | solution.py:50
  190.9 3.8 %shard_map.185 = (f32[16,32,128]{2,1,0:T(8,128)}, f32[32,128]{1,0:T(8,128)S(1)}) custom-call(s32[80]{0:T(128)S(1)} %concatenate.19.scalars, f32[32,32,128]{2,1,0:T(8,128)S(1)} %all-to-all-done.9.received, f32[128,8192]{1,0:T(8,128)} %all-gather.7.cloned.1.call-done.matrix, f32[2,128,128]{2,1,0:T(8,128)S(1)} %get-tuple-element.68.solved, ...), custom_call_target="tpu_custom_call" | custom-call | flops 8388608 | bytes 4194304 | tf_op jit(solution)/shard_map/pallas_call | solution.py:244
  194.7 3.7 %all-to-all-start.10 = ((f32[16,32,128]{2,1,0:T(8,128)}), f32[16,32,128]{2,1,0:T(8,128)S(1)}, u32[]{:S(2)}, u32[]{:S(2)}) async-start(f32[16,32,128]{2,1,0:T(8,128)} %get-tuple-element.69), calls=%async_computation.10 | async-start | bytes 524288 | tf_op jit(solution)/shard_map/all_to_all | solution.py:50
  198.5 1.4 shard_map.186.chosen1
  199.8 6.2 %all-to-all-done.10.received = f32[16,32,128]{2,1,0:T(8,128)S(1)} async-done(((f32[16,32,128]{2,1,0:T(8,128)}), f32[16,32,128]{2,1,0:T(8,128)S(1)}, u32[]{:S(2)}, u32[]{:S(2)}) %all-to-all-start.10) | async-done | bytes 262176 | tf_op jit(solution)/shard_map/all_to_all | solution.py:50
  206.0 3.9 %shard_map.187 = (f32[8,16,128]{2,1,0:T(8,128)}, f32[32,128]{1,0:T(8,128)S(1)}) custom-call(s32[80]{0:T(128)S(1)} %concatenate.19.scalars, f32[16,32,128]{2,1,0:T(8,128)S(1)} %all-to-all-done.10.received, f32[128,9216]{1,0:T(8,128)} %all-gather.11.cloned.1.call-done.matrix, f32[8,8,128]{2,1,0:T(8,128)S(1)} %all_to_all.86.received.solved, ...), custom_call_target="tpu_custom_call" | custom-call | flops 9437184 | bytes 4718592 | tf_op jit(solution)/shard_map/pallas_call | solution.py:244
  209.9 3.4 %all-to-all-start.11 = ((f32[8,16,128]{2,1,0:T(8,128)}), f32[8,16,128]{2,1,0:T(8,128)S(1)}, u32[]{:S(2)}, u32[]{:S(2)}) async-start(f32[8,16,128]{2,1,0:T(8,128)} %get-tuple-element.73), calls=%async_computation.11 | async-start | bytes 131072 | tf_op jit(solution)/shard_map/all_to_all | solution.py:50
  213.3 1.4 shard_map.188.chosen2
  214.6 0.0 all-gather.13.cloned.1.call-done.coupling
  214.6 5.8 %all-to-all-done.11.received = f32[8,16,128]{2,1,0:T(8,128)S(1)} async-done(((f32[8,16,128]{2,1,0:T(8,128)}), f32[8,16,128]{2,1,0:T(8,128)S(1)}, u32[]{:S(2)}, u32[]{:S(2)}) %all-to-all-start.11) | async-done | bytes 65568 | tf_op jit(solution)/shard_map/all_to_all | solution.py:50
  220.4 1.6 copy-done.4
  222.0 6.4 %shard_map.189 = f32[8,16,128]{2,1,0:T(8,128)} custom-call(s32[152]{0:T(256)S(1)} %concatenate.18.scalars, f32[8,16,128]{2,1,0:T(8,128)S(1)} %all-to-all-done.11.received, f32[64,128]{1,0:T(8,128)S(1)} %get-tuple-element.66.x.refs_0_.x0, f32[32,128]{1,0:T(8,128)S(1)} %get-tuple-element.70.x.refs_1_.x1, f32[32,128]{1,0:T(8,128)S(1)} %get-tuple-element.74.x.x2, ...), custom_call_target="tpu_custom_call" | custom-call | tf_op jit(solution)/shard_map/pallas_call | solution.py:455
  228.4 14.4 %all-to-all-start.12 = ((f32[8,16,128]{2,1,0:T(8,128)}), f32[8,16,128]{2,1,0:T(8,128)S(1)}, u32[]{:S(2)}, u32[]{:S(2)}) async-start(f32[8,16,128]{2,1,0:T(8,128)} %shard_map.189), calls=%async_computation.12 | async-start | bytes 131072 | tf_op jit(solution)/shard_map/all_to_all | solution.py:50
  242.8 0.1 stack.35.scalars
  242.9 4.9 %all-to-all-done.12.received = f32[8,16,128]{2,1,0:T(8,128)S(1)} async-done(((f32[8,16,128]{2,1,0:T(8,128)}), f32[8,16,128]{2,1,0:T(8,128)S(1)}, u32[]{:S(2)}, u32[]{:S(2)}) %all-to-all-start.12) | async-done | bytes 65568 | tf_op jit(solution)/shard_map/all_to_all | solution.py:50
  247.8 1.3 shard_map.190
  (34 shorter events, 0.2 us)
Async XLA Ops:
  7.2 12.8 %copy-start = (s32[16,2048]{1,0:T(8,128)S(1)}, s32[16,2048]{1,0:T(8,128)}, u32[]{:S(2)}) copy-start(s32[16,2048]{1,0:T(8,128)} %param.27) | copy-start | bytes 393220
  7.2 17.8 %copy-start.10 = (f32[16,1024]{1,0:T(8,128)S(1)}, f32[16,1024]{1,0:T(8,128)}, u32[]{:S(2)}) copy-start(f32[16,1024]{1,0:T(8,128)} %param.21) | copy-start | bytes 196612
  7.2 17.8 %copy-start.6 = (f32[16,8192]{1,0:T(8,128)S(1)}, f32[16,8192]{1,0:T(8,128)}, u32[]{:S(2)}) copy-start(f32[16,8192]{1,0:T(8,128)} %param.24) | copy-start | bytes 1572868
  7.2 76.0 %all-gather.7.cloned.1.call-start = ((), (), s32[]{:S(2)}) async-start(), calls=%async_computation.13 | async-start | bytes 4718592 | tf_op jit(solution)/shard_map/all_gather | solution.py:520
  19.9 24.1 %copy-start.7 = (f32[8,4096]{1,0:T(8,128)S(1)}, f32[8,4096]{1,0:T(8,128)}, u32[]{:S(2)}) copy-start(f32[8,4096]{1,0:T(8,128)} %param.18) | copy-start | bytes 393220
  19.9 24.1 %copy-start.8 = (f32[8,4096]{1,0:T(8,128)S(1)}, f32[8,4096]{1,0:T(8,128)}, u32[]{:S(2)}) copy-start(f32[8,4096]{1,0:T(8,128)} %param.22) | copy-start | bytes 393220
  19.9 24.1 %copy-start.9 = (f32[8,2048]{1,0:T(8,128)S(1)}, f32[8,2048]{1,0:T(8,128)}, u32[]{:S(2)}) copy-start(f32[8,2048]{1,0:T(8,128)} %param.19) | copy-start | bytes 196612
  25.0 31.4 %copy-start.3 = (f32[16,9216]{1,0:T(8,128)}, f32[16,9216]{1,0:T(8,128)S(1)}, u32[]{:S(2)}) copy-start(f32[16,9216]{1,0:T(8,128)S(1)} %constant_dynamic-update-slice_fusion.own) | copy-start | bytes 1769476
  25.0 18.9 %collective-permute-start = (f32[16,9216]{1,0:T(8,128)S(1)}, f32[16,9216]{1,0:T(8,128)S(1)}, u32[]{:S(2)}, u32[]{:S(2)}) collective-permute-start(f32[16,9216]{1,0:T(8,128)S(1)} %constant_dynamic-update-slice_fusion.own), channel_id=1, source_target_pairs={{0,8},{8,0},{1,9},{9,1},{2,10},{10,2},{3,11},{11,3},{4,12},{12,4},... | collective-permute-start | bytes 1769480 | tf_op jit(solution)/shard_map/ppermute | solution.py:544
  27.3 16.7 %all-to-all-start = ((f32[32,8,128]{2,1,0:T(8,128)}), f32[32,8,128]{2,1,0:T(8,128)S(1)}, u32[]{:S(2)}, u32[]{:S(2)}) async-start(f32[32,8,128]{2,1,0:T(8,128)} %get-tuple-element.47), calls=%async_computation | async-start | bytes 262144 | tf_op jit(solution)/shard_map/all_to_all | solution.py:50
  34.8 58.1 %all-gather.9.cloned.1.call-start = ((), (), s32[]{:S(2)}) async-start(), calls=%async_computation.14 | async-start | bytes 2949120 | tf_op jit(solution)/shard_map/all_gather | solution.py:520
  44.8 161.2 %all-gather.11.cloned.1.call-start = ((), (), s32[]{:S(2)}) async-start(), calls=%async_computation.15 | async-start | bytes 5308416 | tf_op jit(solution)/shard_map/all_gather | solution.py:520
  72.4 10.8 %all-to-all-start.3 = ((f32[16,8,128]{2,1,0:T(8,128)}), f32[16,8,128]{2,1,0:T(8,128)S(1)}, u32[]{:S(2)}, u32[]{:S(2)}) async-start(f32[16,8,128]{2,1,0:T(8,128)} %shard_map.177), calls=%async_computation.3 | async-start | bytes 131072 | tf_op jit(solution)/shard_map/all_to_all | solution.py:50
  87.3 17.8 %all-to-all-start.4 = ((f32[32,32,128]{2,1,0:T(8,128)}), f32[32,32,128]{2,1,0:T(8,128)S(1)}, u32[]{:S(2)}, u32[]{:S(2)}) async-start(f32[32,32,128]{2,1,0:T(8,128)} %get-tuple-element.58), calls=%async_computation.4 | async-start | bytes 1048576 | tf_op jit(solution)/shard_map/all_to_all | solution.py:50
  92.3 122.3 %all-gather.13.cloned.1.call-start = ((), (), s32[]{:S(2)}) async-start(), calls=%async_computation.16 | async-start | bytes 2359296 | tf_op jit(solution)/shard_map/all_gather | solution.py:520
  105.0 1.7 copy-start.1
  106.8 36.2 %copy-start.2 = (f32[64,10240]{1,0:T(8,128)S(1)}, f32[64,10240]{1,0:T(8,128)}, u32[]{:S(2)}) copy-start(f32[64,10240]{1,0:T(8,128)} %all-gather.9.cloned.1.call-done.matrix) | copy-start | bytes 7864324
  174.8 16.1 %all-to-all-start.9 = ((f32[32,32,128]{2,1,0:T(8,128)}), f32[32,32,128]{2,1,0:T(8,128)S(1)}, u32[]{:S(2)}, u32[]{:S(2)}) async-start(f32[32,32,128]{2,1,0:T(8,128)} %get-tuple-element.65), calls=%async_computation.9 | async-start | bytes 1048576 | tf_op jit(solution)/shard_map/all_to_all | solution.py:50
  194.7 11.3 %all-to-all-start.10 = ((f32[16,32,128]{2,1,0:T(8,128)}), f32[16,32,128]{2,1,0:T(8,128)S(1)}, u32[]{:S(2)}, u32[]{:S(2)}) async-start(f32[16,32,128]{2,1,0:T(8,128)} %get-tuple-element.69), calls=%async_computation.10 | async-start | bytes 524288 | tf_op jit(solution)/shard_map/all_to_all | solution.py:50
  209.9 37.9 %copy-start.5 = (f32[16,32]{1,0:T(8,128)S(1)}, f32[16,32]{1,0:T(8,128)}, u32[]{:S(2)}) copy-start(f32[16,32]{1,0:T(8,128)} %values.1) | copy-start | bytes 6148
  209.9 10.5 %all-to-all-start.11 = ((f32[8,16,128]{2,1,0:T(8,128)}), f32[8,16,128]{2,1,0:T(8,128)S(1)}, u32[]{:S(2)}, u32[]{:S(2)}) async-start(f32[8,16,128]{2,1,0:T(8,128)} %get-tuple-element.73), calls=%async_computation.11 | async-start | bytes 131072 | tf_op jit(solution)/shard_map/all_to_all | solution.py:50
  220.4 1.6 copy-start.4
  228.4 19.4 %all-to-all-start.12 = ((f32[8,16,128]{2,1,0:T(8,128)}), f32[8,16,128]{2,1,0:T(8,128)S(1)}, u32[]{:S(2)}, u32[]{:S(2)}) async-start(f32[8,16,128]{2,1,0:T(8,128)} %shard_map.189), calls=%async_computation.12 | async-start | bytes 131072 | tf_op jit(solution)/shard_map/all_to_all | solution.py:50
Sparse Core Ops, SparseCore 0:
  20.0 38.1 all-gather.6
  60.4 31.3 all-gather.8
  93.9 40.2 all-gather.10
  136.2 30.5 all-gather.12

commit v6 on v5

--- a/solution.py
+++ b/solution.py
@@ -19,7 +19,8 @@
 CHUNK = 32
 HBM = pl.BlockSpec(memory_space=pltpu.HBM)
 LIMIT = 16 * 2**20
-WHOLE = 50 * 2**20
+STREAM = 50 * 2**20
+WHOLE = 57 * 2**20
 ALL_Y = ("y2", "y1", "y0")
 INTERPRET = False
 VMEM = pl.BlockSpec(memory_space=pltpu.VMEM)
@@ -69,13 +70,14 @@
 
 
 def row_dot(matrix, rows, column, vector, first, blocks):
-    sums = [jnp.zeros((CHUNK, LANES), jnp.float32) for _ in range(PAIR)]
+    sums = [[None, None] for _ in range(PAIR)]
     for block in range(blocks):
         tile = matrix[rows, column + block * LANES : column + (block + 1) * LANES]
         for s in range(PAIR):
             at = (first + block) * PAIR + s
-            sums[s] = sums[s] + tile * vector[at : at + 1, :]
-    return [jnp.sum(value, axis=1, keepdims=True) for value in sums]
+            part, old = tile * vector[at : at + 1, :], sums[s][block % 2]
+            sums[s][block % 2] = part if old is None else old + part
+    return [jnp.sum(value[0] + value[1], axis=1, keepdims=True) for value in sums]
 
 
 def column_dot(matrix, rows, column, blocks, factors, total):
@@ -93,25 +95,62 @@
     for place in range(matrix.shape[0] // 8):
         rows, columns = pl.ds(place * 8, 8), pl.ds(0, buffer.shape[1])
         copies.append(pltpu.make_async_copy(matrix.at[rows, columns], buffer.at[rows, columns], ready.at[place]))
+    return copies
+
+
+def begin(matrix, stream):
+    if not stream:
+        return matrix, None
+    buffer, ready = stream
+    copies = chunk_copies(matrix, buffer, ready)
+    start_chunk(copies, 0)
+    start_chunk(copies, 1)
+    return buffer, copies
+
+
+def start_chunk(copies, chunk):
+    share = CHUNK // 8
+    for copy in copies[chunk * share : (chunk + 1) * share]:
+        copy.start()
+
+
+def each_chunk(matrix, copies, step):
+    share = CHUNK // 8
+    for chunk in range(matrix.shape[0] // CHUNK):
+        if copies:
+            for copy in copies[chunk * share : (chunk + 1) * share]:
+                copy.wait()
+            start_chunk(copies, chunk + 2)
+        step(pl.ds(chunk * CHUNK, CHUNK))
+
+
+def stream_buffers(matrix, width, streamed):
+    rows = matrix.shape[0]
+    return [pltpu.VMEM((rows, width), jnp.float32), pltpu.SemaphoreType.DMA((rows // 8,))] if streamed else []
+
+
+def fetch_kernel(matrix, out, ready):
+    copies = chunk_copies(matrix, out, ready)
     for copy in copies:
         copy.start()
-    return copies
-
-
-def each_chunk(copies, step):
-    share = CHUNK // 8
-    for chunk in range(len(copies) // share):
-        for copy in copies[chunk * share : (chunk + 1) * share]:
-            copy.wait()
-        step(pl.ds(chunk * CHUNK, CHUNK))
-
-
-def chunk_buffers(rows, width):
-    return [pltpu.VMEM((rows, width), jnp.float32), pltpu.SemaphoreType.DMA((rows // 8,))]
-
-
-def forward_kernel(blocks, upper, keep, extra, scalars, received, matrix, rest_in, solved, send, rest, vector, total, buffer, ready):
-    copies = chunk_copies(matrix, buffer, ready)
+    for copy in copies:
+        copy.wait()
+
+
+def fetched(matrix):
+    rows, width = matrix.shape
+    return call(
+        fetch_kernel,
+        f32(rows, width),
+        in_specs=[HBM],
+        out_specs=VMEM,
+        scratch_shapes=[pltpu.SemaphoreType.DMA((rows // 8,))],
+        cost_estimate=cost(2 * rows * width),
+    )(matrix)
+
+
+def forward_kernel(blocks, upper, keep, extra, scalars, received, matrix, rest_in, solved, send, rest, vector, total, *stream):
+    matrix, copies = begin(matrix, stream)
     if extra:
         for source in range(blocks):
             vector[2 * source : 2 * source + 2, :] = received[source, 0:2, :]
@@ -120,12 +159,12 @@
     total[...] = jnp.zeros_like(total)
 
     def step(rows):
-        values = row_dot(buffer, rows, 0, vector, 0, blocks)
+        values = row_dot(matrix, rows, 0, vector, 0, blocks)
         for s in range(PAIR):
             solved[s, rows, :] = jnp.broadcast_to(values[s], (CHUNK, LANES))
-        column_dot(buffer, rows, blocks * LANES, upper, values, total)
-
-    each_chunk(copies, step)
+        column_dot(matrix, rows, blocks * LANES, upper, values, total)
+
+    each_chunk(matrix, copies, step)
     whole = -jnp.sum(total[...], axis=1)
     if extra:
         rest[...] = whole
@@ -140,24 +179,26 @@
         send[copy] = whole[2 * keep :, :]
 
 
-def forward(received, matrix, rest_in, scalars, blocks, upper, keep, copies, extra):
+def forward(received, matrix, rest_in, scalars, blocks, upper, keep, copies, extra, streamed):
     rows = matrix.shape[0]
     width = upper * LANES + blocks * LANES
     return call(
         functools.partial(forward_kernel, blocks, upper, keep, extra),
         (f32(PAIR, rows, LANES), f32(copies, 2 * (upper - keep), LANES), f32(2 * upper, LANES)),
-        in_specs=[SMEM, VMEM, HBM, VMEM],
+        in_specs=[SMEM, VMEM, HBM if streamed else VMEM, VMEM],
         out_specs=(VMEM,) * 3,
         scratch_shapes=[pltpu.VMEM((2 * blocks, LANES), jnp.float32), pltpu.VMEM((2 * upper, 8, LANES), jnp.float32)]
-        + chunk_buffers(rows, width),
+        + stream_buffers(matrix, width, streamed),
+        limit=STREAM if streamed else LIMIT,
         cost_estimate=cost(rows * width),
-        limit=WHOLE,
     )(scalars, received, matrix, rest_in)
 
 
 def lowest_kernel(blocks, upper, received, own, other, path, send, total, buffer, ready):
     rows = own.shape[0]
     copies = chunk_copies(own, buffer.at[0:rows, :], ready.at[0]) + chunk_copies(other, buffer.at[rows:, :], ready.at[1])
+    for copy in copies:
+        copy.start()
     for copy in copies:
         copy.wait()
     samples = range(received.shape[1])
@@ -210,8 +251,8 @@
 
 
 def backward_kernel(blocks, known_blocks, scalars, received, matrix, solved, *refs):
-    known, (send, newest, total, vector, buffer, ready) = refs[: len(known_blocks) - 1], refs[len(known_blocks) - 1 :]
-    copies = chunk_copies(matrix, buffer, ready)
+    known, (send, newest, total, vector, *stream) = refs[: len(known_blocks) - 1], refs[len(known_blocks) - 1 :]
+    matrix, copies = begin(matrix, stream)
     newest[...] = jnp.sum(received[...], axis=0)
     total[...] = jnp.zeros_like(total)
     again = solved.shape[2] == LANES and solved.shape[0] == blocks
@@ -221,47 +262,47 @@
 
     def step(rows):
         if again:
-            values = row_dot(buffer, rows, 0, vector, 0, blocks)
+            values = row_dot(matrix, rows, 0, vector, 0, blocks)
         else:
             values = [solved[s, rows, 0:1] for s in range(PAIR)]
         column = blocks * LANES
         for ref, count in zip((*known, newest), known_blocks):
-            part = row_dot(buffer, rows, column, ref, 0, count)
+            part = row_dot(matrix, rows, column, ref, 0, count)
             values = [values[s] - part[s] for s in range(PAIR)]
             column += count * LANES
-        column_dot(buffer, rows, 0, blocks, values, total)
-
-    each_chunk(copies, step)
+        column_dot(matrix, rows, 0, blocks, values, total)
+
+    each_chunk(matrix, copies, step)
     whole = jnp.sum(total[...], axis=1)
     for copy in range(send.shape[0]):
         send[copy] = whole
 
 
-def backward(received, matrix, solved, known, scalars, blocks, copies):
+def backward(received, matrix, solved, known, scalars, blocks, copies, streamed):
     rows = matrix.shape[0]
     counts = [array.shape[0] // PAIR for array in known] + [received.shape[1] // PAIR]
     width = (blocks + sum(counts)) * LANES
     return call(
         functools.partial(backward_kernel, blocks, counts),
         (f32(copies, 2 * blocks, LANES), f32(*received.shape[1:])),
-        in_specs=[SMEM, VMEM, HBM, VMEM] + [VMEM] * len(known),
+        in_specs=[SMEM, VMEM, HBM if streamed else VMEM] + [VMEM] * (1 + len(known)),
         out_specs=(VMEM,) * 2,
         scratch_shapes=[pltpu.VMEM((2 * blocks, 8, LANES), jnp.float32), pltpu.VMEM((2 * blocks, LANES), jnp.float32)]
-        + chunk_buffers(rows, width),
+        + stream_buffers(matrix, width, streamed),
+        limit=STREAM if streamed else LIMIT,
         cost_estimate=cost(rows * width),
-        limit=WHOLE,
     )(scalars, received, matrix, solved, *known)
 
 
-def root_kernel(column, blocks, vector, matrix, send, total, buffer, ready):
-    copies = chunk_copies(matrix.at[:, column:], buffer, ready)
+def root_kernel(column, blocks, vector, matrix, send, total):
     total[...] = jnp.zeros_like(total)
 
     def step(rows):
-        values = row_dot(buffer, rows, 0, vector, 0, blocks)
-        column_dot(buffer, rows, 0, blocks, values, total)
-
-    each_chunk(copies, step)
+        values = row_dot(matrix, rows, column, vector, 0, blocks)
+        column_dot(matrix, rows, column, blocks, values, total)
+
+    for chunk in range(matrix.shape[0] // CHUNK):
+        step(pl.ds(chunk * CHUNK, CHUNK))
     whole = jnp.sum(total[...], axis=1)
     for copy in range(send.shape[0]):
         send[copy] = whole
@@ -273,11 +314,10 @@
     return call(
         functools.partial(root_kernel, column, blocks),
         f32(copies, 2 * blocks, LANES),
-        in_specs=[VMEM, HBM],
+        in_specs=[VMEM, VMEM],
         out_specs=VMEM,
-        scratch_shapes=[pltpu.VMEM((2 * blocks, 8, LANES), jnp.float32)] + chunk_buffers(rows, blocks * LANES),
+        scratch_shapes=[pltpu.VMEM((2 * blocks, 8, LANES), jnp.float32)],
         cost_estimate=cost(rows * blocks * LANES),
-        limit=WHOLE,
     )(vector, matrix)
 
 
@@ -302,11 +342,11 @@
     lax.fori_loop(0, path.shape[0], one, 0, unroll=4)
 
 
-def add_own(scalars, small, source, depth, heights, path):
+def add_own(scalars, both, depth, heights, path):
     z, core, x = scalars[0], scalars[1], scalars[2]
     half = pl.multiple_of(core * 8, 8)
     lane = lax.broadcasted_iota(jnp.int32, (8, LANES), 1)
-    start = 0
+    start = source = 0
     for height in range(4):
         width = 8 if height < 2 else 16
         for other in range(C):
@@ -321,60 +361,89 @@
                 block = block + x
             else:
                 block = block + x * 2 + other
-            moved = pltpu.roll(small[other, pl.ds(half, 8), :], lax.rem(offset - source + LANES, LANES), 1)
+            small = both[other, pl.ds(half, 8), both.shape[2] - LANES :]
+            moved = pltpu.roll(small, lax.rem(offset - source + LANES, LANES), 1)
             path[block] = path[block] + jnp.where((lane >= offset) & (lane < offset + width), moved, 0.0)
         start += WIDTHS[height] // LANES if height in heights else 0
         source += width
 
 
-def first_kernel(depth, scalars, small, coupling, index, send, terms, path):
-    rows, columns = coupling.shape[1:]
+def product_kernel(values, coupling, rhs0, rhs1, rhs2, rhs3, out):
+    columns = coupling.shape[1]
+    out[:, :columns] = lax.dot_general(
+        values[...], coupling[...], NN, precision=lax.Precision.HIGHEST, preferred_element_type=jnp.float32
+    )
+    parts = [jnp.transpose(rhs0[...]), jnp.transpose(rhs1[...]), rhs2[...], rhs3[...]]
+    filled = sum(part.shape[1] for part in parts)
+    parts.append(jnp.zeros((out.shape[0], LANES - filled), jnp.float32))
+    out[:, columns:] = jnp.concatenate(parts, axis=1)
+
+
+def own_product(values, coupling, rhs_parts):
+    rhs0, rhs1, rhs2, rhs3 = rhs_parts
+    shape = f32(values.shape[0], coupling.shape[1] + LANES)
+    return call(product_kernel, shape, in_specs=[VMEM] * 6, out_specs=VMEM, limit=WHOLE)(values, coupling, rhs0.T, rhs1.T, rhs2, rhs3)
+
+
+def first_kernel(depth, groups, scalars, both, index, *refs):
+    count = sum(groups)
+    parts, (send, terms, *packs), (path, ready) = refs[:count], refs[count:-2], refs[-2:]
+    copies = []
+    for pack, size in zip(packs, groups):
+        column = 0
+        for part in parts[:size]:
+            width = part.shape[1]
+            for row in range(0, part.shape[0], 8):
+                target = pack.at[pl.ds(row, 8), pl.ds(column, width)]
+                copies.append(pltpu.make_async_copy(part.at[pl.ds(row, 8), :], target, ready.at[len(copies)]))
+            column += width
+        parts = parts[size:]
+    for copy in copies:
+        copy.start()
+    columns = both.shape[2] - LANES
     half = pl.multiple_of(scalars[1] * 8, 8)
-    update = None
-    for other in range(C):
-        product = lax.dot_general(
-            small[other, pl.ds(half, 8), :][:, :rows],
-            coupling[other],
-            NN,
-            precision=lax.Precision.HIGHEST,
-            preferred_element_type=jnp.float32,
-        )
-        update = product if update is None else update + product
-    pieces = split3(update)
+    pieces = split3(both[0, pl.ds(half, 8), :columns] + both[1, pl.ds(half, 8), :columns])
     terms[:, columns:] = jnp.zeros((32, terms.shape[1] - columns), jnp.bfloat16)
     terms[:, :columns] = jnp.concatenate([*pieces, jnp.zeros_like(pieces[0])], axis=0)
     expand(scalars, terms, index, sum(WIDTHS[:3]) // LANES, path)
-    add_own(scalars, small, rows, depth, (3,), path)
+    add_own(scalars, both, depth, (3,), path)
     for dest in range(X):
         for other in range(depth):
             send[dest * depth + other] = path[other]
-
-
-def first(small, coupling, index, scalars, depth):
-    columns = coupling.shape[2]
-    return call(
-        functools.partial(first_kernel, depth),
-        (f32(X * depth, 8, LANES), jax.ShapeDtypeStruct((32, columns + 2 * LANES), jnp.bfloat16)),
-        in_specs=[SMEM, VMEM, VMEM, VMEM],
-        out_specs=(VMEM, VMEM),
-        scratch_shapes=[pltpu.VMEM((WIDTHS[3] // LANES, 8, LANES), jnp.float32)],
-    )(scalars, small, coupling, index)
-
-
-def upper_kernel(depth, rows, scalars, small, terms, index, path):
+    for copy in copies:
+        copy.wait()
+
+
+def first(both, index, scalars, depth, groups):
+    columns = both.shape[2] - LANES
+    parts = [part for group in groups for part in group]
+    packs = [f32(group[0].shape[0], sum(part.shape[1] for part in group)) for group in groups]
+    count = sum(part.shape[0] // 8 for part in parts)
+    outs = call(
+        functools.partial(first_kernel, depth, [len(group) for group in groups]),
+        (f32(X * depth, 8, LANES), jax.ShapeDtypeStruct((32, columns + 2 * LANES), jnp.bfloat16), *packs),
+        in_specs=[SMEM, VMEM, VMEM] + [HBM] * len(parts),
+        out_specs=(VMEM, VMEM) + (HBM,) * len(packs),
+        scratch_shapes=[pltpu.VMEM((WIDTHS[3] // LANES, 8, LANES), jnp.float32), pltpu.SemaphoreType.DMA((count,))],
+        limit=WHOLE,
+    )(scalars, both, index, *parts)
+    return outs[0], outs[1], outs[2:]
+
+
+def upper_kernel(depth, scalars, both, terms, index, path):
     expand(scalars, terms, index, 0, path)
-    add_own(scalars, small, rows, depth, (0, 1, 2), path)
-
-
-def upper_path(small, terms, index, scalars, depth, rows):
+    add_own(scalars, both, depth, (0, 1, 2), path)
+
+
+def upper_path(both, terms, index, scalars, depth):
     blocks = sum(WIDTHS[:3]) // LANES
     return call(
-        functools.partial(upper_kernel, depth, rows),
+        functools.partial(upper_kernel, depth),
         f32(blocks, 8, LANES),
         in_specs=[SMEM, VMEM, VMEM, VMEM],
         out_specs=VMEM,
         cost_estimate=cost(blocks * LANES * LANES),
-    )(scalars, small, terms, index)
+    )(scalars, both, terms, index)
 
 
 def pick(scalars, index, terms, first_block, blocks, chosen):
@@ -417,22 +486,19 @@
     )(scalars, x, index)
 
 
-def last_kernel(columns, counts, scalars, received, x0, x1, x2, coupling, index, chosen0, chosen1, chosen2, send, x3, terms, chosen, buffer, ready):
-    copies = chunk_copies(coupling, buffer, ready)
+def last_kernel(columns, counts, scalars, received, x0, x1, x2, coupling, index, chosen0, chosen1, chosen2, send, x3, terms, chosen):
     x3[...] = jnp.sum(received[...], axis=0)
     store_terms(x3, terms)
     chosen[...] = chosen0[...] + chosen1[...] + chosen2[...]
     pick(scalars, index, terms, sum(counts[:3]), counts[3], chosen)
     rows = coupling.shape[0] // 2
-    for copy in copies:
-        copy.wait()
     handed = []
     for half in range(2):
         value = chosen[half, 0:2, :columns] + chosen[half, 2:4, :columns] + chosen[half, 4:6, :columns]
         handed.append(
             lax.dot_general(
                 value,
-                buffer[half * rows : (half + 1) * rows, :],
+                coupling[half * rows : (half + 1) * rows, :],
                 NT,
                 precision=lax.Precision.HIGHEST,
                 preferred_element_type=jnp.float32,
@@ -455,15 +521,13 @@
     return call(
         functools.partial(last_kernel, columns, counts),
         f32(XC, 16, LANES),
-        in_specs=[SMEM] + [VMEM] * 4 + [HBM] + [VMEM] * 4,
+        in_specs=[SMEM] + [VMEM] * 9,
         out_specs=VMEM,
         scratch_shapes=[
             pltpu.VMEM(received.shape[1:], jnp.float32),
             pltpu.VMEM((counts[3], 8, LANES), jnp.float32),
             pltpu.VMEM((2, 8, columns + 2 * LANES), jnp.float32),
-            *chunk_buffers(*coupling.shape),
         ],
-        limit=WHOLE,
     )(scalars, received, *known, coupling, index, *chosen)
 
 
@@ -511,10 +575,7 @@
     blocks = sum(counts)
 
     rhs_parts = [rhs_root, rhs_level1, rhs_level2, rhs_level3]
-    small = jnp.concatenate([subtree_values] + rhs_parts, axis=1)
-    small = jnp.pad(small, ((0, 0), (0, LANES - small.shape[1])))
-    both_small = lax.all_gather(small, "c", axis=0, tiled=False)
-    both_coupling = lax.all_gather(coupling, "c", axis=0, tiled=False)
+    both = lax.all_gather(own_product(subtree_values, coupling, rhs_parts), "c", axis=0, tiled=False)
 
     def gathered(whole):
         return lax.all_gather(whole, ("x", "c"), axis=0, tiled=True)
@@ -531,35 +592,26 @@
         return jnp.concatenate([head, *tails])
 
     places = scalars([z, c, x, y, y % 4, y % 2, (y % 2) * depth + z], own_windows)
-    both_small, inv_level2, cross_level2 = lax.optimization_barrier((both_small, inv_level2, cross_level2))
-    matrix2 = gathered(jnp.concatenate([inv_level2, cross_level2], axis=1))
-    send, terms = first(both_small, both_coupling, own_indices, places, depth)
-    parts = (inv_level3, cross_level3, coupling, terms)
-    send, (inv_level3, cross_level3, coupling, terms) = lax.optimization_barrier((send, parts))
-    own3 = jnp.concatenate([inv_level3, cross_level3], axis=1)
-    path = upper_path(both_small, terms, own_indices, places, depth, coupling.shape[0])
-    received, other3, path, inv_root, inv_level1, cross_level1 = lax.optimization_barrier(
-        (
-            exchange(send, ("x", "z")),
-            lax.ppermute(own3, "c", [(0, 1), (1, 0)]),
-            path,
-            inv_root,
-            inv_level1,
-            cross_level1,
-        )
+    groups = ((inv_level3, cross_level3), (inv_level2, cross_level2), (inv_level1, cross_level1, inv_root))
+    send, terms, (own3, pack2, pack1) = first(both, own_indices, places, depth, groups)
+    matrix2 = gathered(pack2)
+    matrix1 = gathered(pack1)
+    path = upper_path(both, terms, own_indices, places, depth)
+    received, other3, path = lax.optimization_barrier(
+        (exchange(send, ("x", "z")), lax.ppermute(own3, "c", [(0, 1), (1, 0)]), path)
     )
-    matrix1 = gathered(jnp.concatenate([inv_level1, cross_level1, inv_root], axis=1))
     target3 = exchange(sum_and_copy(received, depth), ("z",))
     send = lowest(target3, own3, other3, path, counts[3], sum(counts[:3]), 2 * depth)
     send, own3, coupling = lax.optimization_barrier((send, own3, coupling))
     matrix3 = gathered(own3)
     all_coupling = gathered(coupling)
     received = sum_and_copy(exchange(send, ("y0", "x", "z")), 2 * depth)
+    target2 = exchange(received, ("y0", "z"))
     solved2, send, rest = forward(
-        exchange(received, ("y0", "z")), matrix2, received[0], places, counts[2], counts[0] + counts[1], counts[0], 4 * depth, 6
+        target2, matrix2, received[0], places, counts[2], counts[0] + counts[1], counts[0], 4 * depth, 6, True
     )
-    received = exchange(send, ("y1", "y0", "z"))
-    solved1, send, rest = forward(received, matrix1, rest, places, counts[1], counts[0], 0, Y, 0)
+    received, matrix1 = lax.optimization_barrier((exchange(send, ("y1", "y0", "z")), fetched(matrix1)))
+    solved1, send, rest = forward(received, matrix1, rest, places, counts[1], counts[0], 0, Y, 0, False)
 
     def sum_root(copies):
         received = exchange(copies.reshape(Y * depth, -1, LANES), ALL_Y + ("z",))
@@ -568,13 +620,15 @@
     target = sum_root(send).reshape(-1, LANES)
     received = sum_root(root(target, matrix1, WIDTHS[1] + WIDTHS[0], Y)).reshape(1, -1, LANES)
     heads = scalars([y, y % 4, y % 2], windows.reshape(-1))
-    send, x0 = backward(received, matrix1, solved1, [], places, counts[1], 4 * depth)
+    send, x0 = backward(received, matrix1, solved1, [], places, counts[1], 4 * depth, False)
     received = exchange(send, ("y1", "y0", "z"))
     received, chosen0 = lax.optimization_barrier((received, picked(x0, both_indices, heads, 0)))
-    send, x1 = backward(received, matrix2, solved2, [x0], places, counts[2], 2 * depth)
+    send, x1 = backward(received, matrix2, solved2, [x0], places, counts[2], 2 * depth, True)
     received = exchange(send, ("y0", "z"))
-    received, chosen1 = lax.optimization_barrier((received, picked(x1, both_indices, heads, counts[0])))
-    send, x2 = backward(received, matrix3, target3, [x0, x1], places, counts[3], depth)
+    received, chosen1, all_coupling = lax.optimization_barrier(
+        (received, picked(x1, both_indices, heads, counts[0]), fetched(all_coupling))
+    )
+    send, x2 = backward(received, matrix3, target3, [x0, x1], places, counts[3], depth, True)
     received = exchange(send, ("z",))
     chosen2 = picked(x2, both_indices, heads, counts[0] + counts[1])
     send = last(received, [x0, x1, x2], [chosen0, chosen1, chosen2], all_coupling, both_indices, heads)

time: 257 us -> 292 us (1.14)
  Pallas kernels: 42.4 us -> 85.4 us
  waiting for transfers between devices: 51.2 us -> 44.3 us
    pallas_call x2 -> x5, Pallas kernels: 6.05 us -> 56.3 us  [the longest x1 46.5 us: first(): call(functools.partial(first_kernel, depth, [len(group) for group in grou...]
    all_to_all x7, waiting for transfers between devices: 50.6 us -> 41 us  [exchange(): return lax.all_to_all(flat, axes, 0, 0, tiled=True).reshape(operand.shape)]
    pallas_call x1, Pallas kernels: 6.38 us -> 3.34 us  [last(): call(functools.partial(last_kernel, columns, counts), f32(XC, 16, LANES),...]
    all_gather x2 -> x1, blocking collectives: 10.8 us -> 10.3 us  [body(): lax.all_gather(own_product(subtree_values, coupling, rhs_parts), 'c', axi...]
  transfers between devices with their start and end apart: 12 -> 12, of which waited for: 7 -> 8; matrix products, arithmetic and copies ran while one was open for 1% -> 0% of each run, Pallas kernels for 14% -> 10%
where the time goes in v6:
time: 292 us; the launch traced here: 290 us
  blocking collectives  94.1 us (32%)
  Pallas kernels  85.4 us (29%)
  waiting for transfers between devices  44.3 us (15%)
  starting transfers between devices  44.2 us (15%)
  between operations  14.1 us (5%)
  local copies, waits for them, and re-layouts  7.86 us (3%)
    all_to_all x6, blocking collectives, exchange(): return lax.all_to_all(flat, axes, 0, 0, tiled=True).reshape(operand.shape)  83.9 us
    pallas_call x1, Pallas kernels, first(): call(functools.partial(first_kernel, depth, [len(group) for group in grou...  46.5 us
    all_to_all x7, starting transfers between devices, exchange(): return lax.all_to_all(flat, axes, 0, 0, tiled=True).reshape(operand.shape)  42 us
    all_to_all x7, waiting for transfers between devices, exchange(): return lax.all_to_all(flat, axes, 0, 0, tiled=True).reshape(operand.shape)  41 us
    pallas_call x3, Pallas kernels, backward(): call(functools.partial(backward_kernel, blocks, counts), (f32(copies, 2 *...  10.7 us
    all_gather x1, blocking collectives, body(): lax.all_gather(own_product(subtree_values, coupling, rhs_parts), 'c', axi...  10.3 us
    pallas_call x2, Pallas kernels, forward(): call(functools.partial(forward_kernel, blocks, upper, keep, extra), (f32(...  6.17 us
  transfers between devices with their start and end apart: 12, of which 8 were waited for; matrix products, arithmetic and copies ran while one was open for 0% of the time, Pallas kernels for 10%

profile of v6, /device:TPU:1, one launch (start us, length us, event | category | flops | bytes accessed | tf_op | source)
XLA Modules:
  0.0 290.3 jit_solution(3884066815244936095)
XLA Ops:
  7.2 0.0 all-gather.6.cloned.1.call-start
  7.3 0.8 copy-done
  8.1 0.6 constant_dynamic-slice_fusion.index
  8.7 0.3 convert_reduce_fusion
  9.0 1.9 shard_map.173
  10.9 10.3 %all-gather = f32[32,2176]{1,0:T(8,128)} all-gather(f32[16,2176]{1,0:T(8,128)} %shard_map.173), channel_id=2, replica_groups=mesh['y2'=2,'y1'=2,'y0'=2,'x'=4,'c'=2,'z'=8] {'c'}, dimensions={0}, use_global_device_ids=true | all-gather | bytes 417792 | tf_op jit(solution)/shard_map/all_gather | solution.py:578
  21.2 0.6 concatenate.7.scalars
  21.8 46.5 %shard_map.174 = (f32[32,8,128]{2,1,0:T(8,128)}, bf16[32,2304]{1,0:T(8,128)(2,1)}, f32[16,9216]{1,0:T(8,128)}, f32[16,8192]{1,0:T(8,128)}, f32[8,10240]{1,0:T(8,128)}) custom-call(s32[80]{0:T(128)} %concatenate.7.scalars, f32[2,16,2176]{2,1,0:T(8,128)} %bitcast.21, s32[1,2304]{1,0:T(1,128)} %constant_dynamic-slice_fusion.index, f32[16,1024]{1,0:T(8,128)} %refs_0_.1, ...), custom_call_target="tpu_custom_call" | custom-call | tf_op jit(solution)/shard_map/pallas_call | solution.py:422
  68.4 0.0 all-gather.6.cloned.1.call-update
  68.4 0.0 all-gather.8.cloned.1.call-start
  68.4 0.7 all-gather.8.cloned.1.call-update
  69.2 2.1 collective-permute-start
  71.2 7.5 %all-to-all-start = ((f32[32,8,128]{2,1,0:T(8,128)}), f32[32,8,128]{2,1,0:T(8,128)S(1)}, u32[]{:S(2)}, u32[]{:S(2)}) async-start(f32[32,8,128]{2,1,0:T(8,128)} %get-tuple-element.39), calls=%async_computation | async-start | bytes 262144 | tf_op jit(solution)/shard_map/all_to_all | solution.py:51
  78.7 0.0 all-gather.10.cloned.1.call-start
  78.8 0.9 copy-done.5
  79.7 3.9 %shard_map.175.path = f32[64,8,128]{2,1,0:T(8,128)S(1)} custom-call(s32[80]{0:T(128)S(1)} %copy-done.8, f32[2,16,2176]{2,1,0:T(8,128)S(1)} %bitcast.22, bf16[32,2304]{1,0:T(8,128)(2,1)S(1)} %copy-done.5, s32[1,2304]{1,0:T(1,128)S(1)} %copy-done.6), custom_call_target="tpu_custom_call" | custom-call | flops 8388608 | bytes 4194304 | tf_op jit(solution)/shard_map/pallas_call | solution.py:440
  83.6 4.3 %all-to-all-done.received = f32[32,8,128]{2,1,0:T(8,128)S(1)} async-done(((f32[32,8,128]{2,1,0:T(8,128)}), f32[32,8,128]{2,1,0:T(8,128)S(1)}, u32[]{:S(2)}, u32[]{:S(2)}) %all-to-all-start) | async-done | bytes 131104 | tf_op jit(solution)/shard_map/all_to_all | solution.py:51
  87.9 9.9 %all_to_all.86.received.solved = f32[8,8,128]{2,1,0:T(8,128)S(1)} all-to-all(f32[8,8,128]{2,1,0:T(8,128)S(1)} %shard_map.176), channel_id=1, replica_groups=mesh['y2'=2,'y1'=2,'y0'=2,'x'=4,'c'=2,'z'=8] {'z'}, dimensions={0} | all-to-all | bytes 65536 | tf_op jit(solution)/shard_map/all_to_all | solution.py:51
  97.9 1.5 shard_map.177
  99.4 0.0 all-gather.10.cloned.1.call-update
  99.4 0.0 all-gather.12.cloned.1.call-start
  99.5 0.5 all-gather.12.cloned.1.call-update
  100.0 15.9 %all_to_all.87.received = f32[64,8,128]{2,1,0:T(8,128)S(1)} all-to-all(f32[64,8,128]{2,1,0:T(8,128)S(1)} %shard_map.177), channel_id=1, replica_groups=mesh['y2'=2,'y1'=2,'y0'=2,'x'=4,'c'=2,'z'=8] {'y0','x','z'}, dimensions={0} | all-to-all | bytes 524288 | tf_op jit(solution)/shard_map/all_to_all | solution.py:51
  115.9 0.7 shard_map.178
  116.6 3.5 %all-to-all-start.3 = ((f32[16,8,128]{2,1,0:T(8,128)}), f32[16,8,128]{2,1,0:T(8,128)S(1)}, u32[]{:S(2)}, u32[]{:S(2)}) async-start(f32[16,8,128]{2,1,0:T(8,128)} %shard_map.178), calls=%async_computation.3 | async-start | bytes 131072 | tf_op jit(solution)/shard_map/all_to_all | solution.py:51
  120.1 0.7 slice_bitcast_fusion.rest_in
  120.8 6.6 %all-to-all-done.3.received = f32[16,8,128]{2,1,0:T(8,128)S(1)} async-done(((f32[16,8,128]{2,1,0:T(8,128)}), f32[16,8,128]{2,1,0:T(8,128)S(1)}, u32[]{:S(2)}, u32[]{:S(2)}) %all-to-all-start.3) | async-done | bytes 65568 | tf_op jit(solution)/shard_map/all_to_all | solution.py:51
  127.4 4.7 %shard_map.179 = (f32[2,128,128]{2,1,0:T(8,128)S(1)}, f32[32,32,128]{2,1,0:T(8,128)}, f32[96,128]{1,0:T(8,128)S(1)}) custom-call(s32[80]{0:T(128)S(1)} %copy-done.8, f32[16,8,128]{2,1,0:T(8,128)S(1)} %all-to-all-done.3.received, f32[128,8192]{1,0:T(8,128)} %all-gather.6.cloned.1.call-done.matrix, f32[8,128]{1,0:T(8,128)S(1)} %slice_bitcast_fusion.rest_in), custom_call_target="tpu_custom_call" | custom-call | flops 8388608 | bytes 4194304 | tf_op jit(solution)/shard_map/pallas_call | solution.py:185
  132.1 4.8 %all-to-all-start.4 = ((f32[32,32,128]{2,1,0:T(8,128)}), f32[32,32,128]{2,1,0:T(8,128)S(1)}, u32[]{:S(2)}, u32[]{:S(2)}) async-start(f32[32,32,128]{2,1,0:T(8,128)} %get-tuple-element.47), calls=%async_computation.4 | async-start | bytes 1048576 | tf_op jit(solution)/shard_map/all_to_all | solution.py:51
  136.8 2.0 all-gather.8.cloned.1.call-done.matrix
  138.9 1.7 copy-done.1
  140.6 0.9 shard_map.180.matrix
  141.5 8.0 %all-to-all-done.4.received = f32[32,32,128]{2,1,0:T(8,128)S(1)} async-done(((f32[32,32,128]{2,1,0:T(8,128)}), f32[32,32,128]{2,1,0:T(8,128)S(1)}, u32[]{:S(2)}, u32[]{:S(2)}) %all-to-all-start.4) | async-done | bytes 524320 | tf_op jit(solution)/shard_map/all_to_all | solution.py:51
  149.5 0.6 copy-done.9
  150.2 1.5 shard_map.181
  151.7 22.8 %all_to_all.88.received = f32[64,8,128]{2,1,0:T(8,128)S(1)} all-to-all(f32[64,8,128]{2,1,0:T(8,128)S(1)} %bitcast.24), channel_id=1, replica_groups=mesh['y2'=2,'y1'=2,'y0'=2,'x'=4,'c'=2,'z'=8] {'y2','y1','y0','z'}, dimensions={0} | all-to-all | bytes 524288 | tf_op jit(solution)/shard_map/all_to_all | solution.py:51
  174.5 0.1 shard_map.182
  174.6 9.5 %all_to_all.89 = f32[8,8,128]{2,1,0:T(8,128)S(1)} all-to-all(f32[8,8,128]{2,1,0:T(8,128)S(1)} %shard_map.182), channel_id=1, replica_groups=mesh['y2'=2,'y1'=2,'y0'=2,'x'=4,'c'=2,'z'=8] {'z'}, dimensions={0} | all-to-all | bytes 65536 | tf_op jit(solution)/shard_map/all_to_all | solution.py:51
  184.0 0.4 shard_map.183
  184.4 16.4 %all_to_all.90.received = f32[64,8,128]{2,1,0:T(8,128)S(1)} all-to-all(f32[64,8,128]{2,1,0:T(8,128)S(1)} %bitcast.23), channel_id=1, replica_groups=mesh['y2'=2,'y1'=2,'y0'=2,'x'=4,'c'=2,'z'=8] {'y2','y1','y0','z'}, dimensions={0} | all-to-all | bytes 524288 | tf_op jit(solution)/shard_map/all_to_all | solution.py:51
  200.8 0.1 shard_map.184
  200.9 9.4 %all_to_all.91 = f32[8,8,128]{2,1,0:T(8,128)S(1)} all-to-all(f32[8,8,128]{2,1,0:T(8,128)S(1)} %shard_map.184), channel_id=1, replica_groups=mesh['y2'=2,'y1'=2,'y0'=2,'x'=4,'c'=2,'z'=8] {'z'}, dimensions={0} | all-to-all | bytes 65536 | tf_op jit(solution)/shard_map/all_to_all | solution.py:51
  210.3 1.8 shard_map.185
  212.1 3.9 %all-to-all-start.9 = ((f32[32,32,128]{2,1,0:T(8,128)}), f32[32,32,128]{2,1,0:T(8,128)S(1)}, u32[]{:S(2)}, u32[]{:S(2)}) async-start(f32[32,32,128]{2,1,0:T(8,128)} %get-tuple-element.54), calls=%async_computation.9 | async-start | bytes 1048576 | tf_op jit(solution)/shard_map/all_to_all | solution.py:51
  216.0 0.1 reduce_sum.12
  216.1 0.1 concatenate.6.scalars
  216.2 2.2 shard_map.186.chosen0
  218.3 9.8 %all-to-all-done.9.received = f32[32,32,128]{2,1,0:T(8,128)S(1)} async-done(((f32[32,32,128]{2,1,0:T(8,128)}), f32[32,32,128]{2,1,0:T(8,128)S(1)}, u32[]{:S(2)}, u32[]{:S(2)}) %all-to-all-start.9) | async-done | bytes 524320 | tf_op jit(solution)/shard_map/all_to_all | solution.py:51
  228.2 4.5 %shard_map.187 = (f32[16,32,128]{2,1,0:T(8,128)}, f32[32,128]{1,0:T(8,128)S(1)}) custom-call(s32[80]{0:T(128)S(1)} %copy-done.10, f32[32,32,128]{2,1,0:T(8,128)S(1)} %all-to-all-done.9.received, f32[128,8192]{1,0:T(8,128)} %all-gather.6.cloned.1.call-done.matrix, f32[2,128,128]{2,1,0:T(8,128)S(1)} %get-tuple-element.57.solved, ...), custom_call_target="tpu_custom_call" | custom-call | flops 8388608 | bytes 4194304 | tf_op jit(solution)/shard_map/pallas_call | solution.py:285
  232.6 3.7 %all-to-all-start.10 = ((f32[16,32,128]{2,1,0:T(8,128)}), f32[16,32,128]{2,1,0:T(8,128)S(1)}, u32[]{:S(2)}, u32[]{:S(2)}) async-start(f32[16,32,128]{2,1,0:T(8,128)} %get-tuple-element.58), calls=%async_computation.10 | async-start | bytes 524288 | tf_op jit(solution)/shard_map/all_to_all | solution.py:51
  236.4 0.0 all-gather.10.cloned.1.call-done.matrix
  236.4 1.6 copy-done.4
  238.0 3.0 %shard_map.189.coupling = f32[256,2048]{1,0:T(8,128)S(1)} custom-call(f32[256,2048]{1,0:T(8,128)S(1)} %copy-done.4), custom_call_target="tpu_custom_call" | custom-call | flops 8388608 | bytes 4194304 | tf_op jit(solution)/shard_map/pallas_call | solution.py:142
  241.0 1.4 shard_map.188.chosen1
  242.4 1.5 all-to-all-done.10.received
  243.9 4.5 %shard_map.190 = (f32[8,16,128]{2,1,0:T(8,128)}, f32[32,128]{1,0:T(8,128)S(1)}) custom-call(s32[80]{0:T(128)S(1)} %copy-done.10, f32[16,32,128]{2,1,0:T(8,128)S(1)} %all-to-all-done.10.received, f32[128,9216]{1,0:T(8,128)} %all-gather.12.cloned.1.call-done.matrix, f32[8,8,128]{2,1,0:T(8,128)S(1)} %all_to_all.86.received.solved, ...), custom_call_target="tpu_custom_call" | custom-call | flops 9437184 | bytes 4718592 | tf_op jit(solution)/shard_map/pallas_call | solution.py:285
  248.4 4.8 %all-to-all-start.11 = ((f32[8,16,128]{2,1,0:T(8,128)}), f32[8,16,128]{2,1,0:T(8,128)S(1)}, u32[]{:S(2)}, u32[]{:S(2)}) async-start(f32[8,16,128]{2,1,0:T(8,128)} %get-tuple-element.63), calls=%async_computation.11 | async-start | bytes 131072 | tf_op jit(solution)/shard_map/all_to_all | solution.py:51
  253.2 1.4 shard_map.191.chosen2
  254.5 5.9 %all-to-all-done.11.received = f32[8,16,128]{2,1,0:T(8,128)S(1)} async-done(((f32[8,16,128]{2,1,0:T(8,128)}), f32[8,16,128]{2,1,0:T(8,128)S(1)}, u32[]{:S(2)}, u32[]{:S(2)}) %all-to-all-start.11) | async-done | bytes 65568 | tf_op jit(solution)/shard_map/all_to_all | solution.py:51
  260.4 3.3 %shard_map.192 = f32[8,16,128]{2,1,0:T(8,128)} custom-call(s32[152]{0:T(256)S(1)} %concatenate.6.scalars, f32[8,16,128]{2,1,0:T(8,128)S(1)} %all-to-all-done.11.received, f32[64,128]{1,0:T(8,128)S(1)} %get-tuple-element.55.x.refs_0_.x0, f32[32,128]{1,0:T(8,128)S(1)} %get-tuple-element.59.x.refs_1_.x1, f32[32,128]{1,0:T(8,128)S(1)} %get-tuple-element.64.x.x2, ...), custom_call_target="tpu_custom_call" | custom-call | tf_op jit(solution)/shard_map/pallas_call | solution.py:521
  263.7 13.8 %all-to-all-start.12 = ((f32[8,16,128]{2,1,0:T(8,128)}), f32[8,16,128]{2,1,0:T(8,128)S(1)}, u32[]{:S(2)}, u32[]{:S(2)}) async-start(f32[8,16,128]{2,1,0:T(8,128)} %shard_map.192), calls=%async_computation.12 | async-start | bytes 131072 | tf_op jit(solution)/shard_map/all_to_all | solution.py:51
  277.5 0.1 stack.35.scalars
  277.6 4.9 %all-to-all-done.12.received = f32[8,16,128]{2,1,0:T(8,128)S(1)} async-done(((f32[8,16,128]{2,1,0:T(8,128)}), f32[8,16,128]{2,1,0:T(8,128)S(1)}, u32[]{:S(2)}, u32[]{:S(2)}) %all-to-all-start.12) | async-done | bytes 65568 | tf_op jit(solution)/shard_map/all_to_all | solution.py:51
  282.5 1.3 shard_map.193
  (28 shorter events, 0.1 us)
Async XLA Ops:
  7.2 0.9 copy-start
  7.2 120.2 %all-gather.6.cloned.1.call-start = ((), (), s32[]{:S(2)}) async-start(), calls=%async_computation.13 | async-start | bytes 4718592 | tf_op jit(solution)/shard_map/all_gather | solution.py:581
  8.7 70.1 %copy-start.6 = (s32[1,2304]{1,0:T(1,128)S(1)}, s32[1,2304]{1,0:T(1,128)}, u32[]{:S(2)}) copy-start(s32[1,2304]{1,0:T(1,128)} %constant_dynamic-slice_fusion.index) | copy-start | bytes 27652
  21.2 57.6 %copy-start.2 = (f32[32,2176]{1,0:T(8,128)S(1)}, f32[32,2176]{1,0:T(8,128)}, u32[]{:S(2)}) copy-start(f32[32,2176]{1,0:T(8,128)} %all-gather) | copy-start | bytes 835588
  21.8 57.0 %copy-start.8 = (s32[80]{0:T(128)S(1)}, s32[80]{0:T(128)}, u32[]{:S(2)}) copy-start(s32[80]{0:T(128)} %concatenate.7.scalars) | copy-start | bytes 964
  68.4 29.5 %copy-start.3 = (f32[16,9216]{1,0:T(8,128)S(1)}, f32[16,9216]{1,0:T(8,128)}, u32[]{:S(2)}) copy-start(f32[16,9216]{1,0:T(8,128)} %get-tuple-element.62.own) | copy-start | bytes 1769476
  68.4 70.5 %all-gather.8.cloned.1.call-start = ((), (), s32[]{:S(2)}) async-start(), calls=%async_computation.14 | async-start | bytes 2949120 | tf_op jit(solution)/shard_map/all_gather | solution.py:581
  69.2 18.8 %collective-permute-start = (f32[16,9216]{1,0:T(8,128)}, f32[16,9216]{1,0:T(8,128)S(1)}, u32[]{:S(2)}, u32[]{:S(2)}) collective-permute-start(f32[16,9216]{1,0:T(8,128)} %get-tuple-element.62.own), channel_id=1, source_target_pairs={{0,8},{8,0},{1,9},{9,1},{2,10},{10,2},{3,11},{11,3},{4,12},{12,4},... | collective-permute-start | bytes 1769480 | tf_op jit(solution)/shard_map/ppermute | solution.py:601
  71.2 16.7 %all-to-all-start = ((f32[32,8,128]{2,1,0:T(8,128)}), f32[32,8,128]{2,1,0:T(8,128)S(1)}, u32[]{:S(2)}, u32[]{:S(2)}) async-start(f32[32,8,128]{2,1,0:T(8,128)} %get-tuple-element.39), calls=%async_computation | async-start | bytes 262144 | tf_op jit(solution)/shard_map/all_to_all | solution.py:51
  78.7 157.6 %all-gather.10.cloned.1.call-start = ((), (), s32[]{:S(2)}) async-start(), calls=%async_computation.15 | async-start | bytes 2359296 | tf_op jit(solution)/shard_map/all_gather | solution.py:581
  78.8 0.9 copy-start.5
  99.4 144.5 %all-gather.12.cloned.1.call-start = ((), (), s32[]{:S(2)}) async-start(), calls=%async_computation.16 | async-start | bytes 5308416 | tf_op jit(solution)/shard_map/all_gather | solution.py:581
  116.6 10.8 %all-to-all-start.3 = ((f32[16,8,128]{2,1,0:T(8,128)}), f32[16,8,128]{2,1,0:T(8,128)S(1)}, u32[]{:S(2)}, u32[]{:S(2)}) async-start(f32[16,8,128]{2,1,0:T(8,128)} %shard_map.178), calls=%async_computation.3 | async-start | bytes 131072 | tf_op jit(solution)/shard_map/all_to_all | solution.py:51
  132.1 17.5 %all-to-all-start.4 = ((f32[32,32,128]{2,1,0:T(8,128)}), f32[32,32,128]{2,1,0:T(8,128)S(1)}, u32[]{:S(2)}, u32[]{:S(2)}) async-start(f32[32,32,128]{2,1,0:T(8,128)} %get-tuple-element.47), calls=%async_computation.4 | async-start | bytes 1048576 | tf_op jit(solution)/shard_map/all_to_all | solution.py:51
  138.9 1.7 copy-start.1
  149.5 0.6 copy-start.9
  174.5 35.8 %copy-start.10 = (s32[80]{0:T(128)S(1)}, s32[80]{0:T(128)}, u32[]{:S(2)}) copy-start(s32[80]{0:T(128)} %concatenate.7.scalars) | copy-start | bytes 964
  212.1 16.1 %all-to-all-start.9 = ((f32[32,32,128]{2,1,0:T(8,128)}), f32[32,32,128]{2,1,0:T(8,128)S(1)}, u32[]{:S(2)}, u32[]{:S(2)}) async-start(f32[32,32,128]{2,1,0:T(8,128)} %get-tuple-element.54), calls=%async_computation.9 | async-start | bytes 1048576 | tf_op jit(solution)/shard_map/all_to_all | solution.py:51
  232.6 11.3 %all-to-all-start.10 = ((f32[16,32,128]{2,1,0:T(8,128)}), f32[16,32,128]{2,1,0:T(8,128)S(1)}, u32[]{:S(2)}, u32[]{:S(2)}) async-start(f32[16,32,128]{2,1,0:T(8,128)} %get-tuple-element.58), calls=%async_computation.10 | async-start | bytes 524288 | tf_op jit(solution)/shard_map/all_to_all | solution.py:51
  236.4 1.6 copy-start.4
  248.4 34.1 %copy-start.7 = (f32[16,32]{1,0:T(8,128)S(1)}, f32[16,32]{1,0:T(8,128)}, u32[]{:S(2)}) copy-start(f32[16,32]{1,0:T(8,128)} %values.3) | copy-start | bytes 6148
  248.4 12.0 %all-to-all-start.11 = ((f32[8,16,128]{2,1,0:T(8,128)}), f32[8,16,128]{2,1,0:T(8,128)S(1)}, u32[]{:S(2)}, u32[]{:S(2)}) async-start(f32[8,16,128]{2,1,0:T(8,128)} %get-tuple-element.63), calls=%async_computation.11 | async-start | bytes 131072 | tf_op jit(solution)/shard_map/all_to_all | solution.py:51
  263.7 18.8 %all-to-all-start.12 = ((f32[8,16,128]{2,1,0:T(8,128)}), f32[8,16,128]{2,1,0:T(8,128)S(1)}, u32[]{:S(2)}, u32[]{:S(2)}) async-start(f32[8,16,128]{2,1,0:T(8,128)} %shard_map.192), calls=%async_computation.12 | async-start | bytes 131072 | tf_op jit(solution)/shard_map/all_to_all | solution.py:51
Sparse Core Ops, SparseCore 0:
  68.5 37.2 all-gather.5
  107.9 30.8 all-gather.7
  141.1 31.0 all-gather.9
  174.1 39.9 all-gather.11

commit v7 on v6

--- a/solution.py
+++ b/solution.py
@@ -98,47 +98,46 @@
     return copies
 
 
-def begin(matrix, stream):
+def begin(matrices, stream):
     if not stream:
-        return matrix, None
+        return matrices, None
     buffer, ready = stream
-    copies = chunk_copies(matrix, buffer, ready)
-    start_chunk(copies, 0)
-    start_chunk(copies, 1)
-    return buffer, copies
-
-
-def start_chunk(copies, chunk):
+    copies = chunk_copies(matrices[-1].at[pl.ds(matrices[-1].shape[0] - buffer.shape[0], buffer.shape[0]), :], buffer, ready)
+    for copy in copies:
+        copy.start()
+    return (*matrices[:-1], buffer), copies
+
+
+def each_chunk(matrices, copies, step):
     share = CHUNK // 8
-    for copy in copies[chunk * share : (chunk + 1) * share]:
+    base = 0
+    for matrix in matrices:
+        streamed = copies and matrix is matrices[-1]
+        for chunk in range(matrix.shape[0] // CHUNK):
+            if streamed:
+                for copy in copies[chunk * share : (chunk + 1) * share]:
+                    copy.wait()
+            step(matrix, pl.ds(chunk * CHUNK, CHUNK), pl.ds(base + chunk * CHUNK, CHUNK))
+        base += matrix.shape[0]
+
+
+def stream_buffers(matrices, width):
+    if len(matrices) == 1:
+        return []
+    rows = matrices[1].shape[0] - matrices[0].shape[0]
+    return [pltpu.VMEM((rows, width), jnp.float32), pltpu.SemaphoreType.DMA((rows // 8,))]
+
+
+def fetch_kernel(matrix, out, ready):
+    copies = chunk_copies(matrix.at[pl.ds(0, out.shape[0]), :], out, ready)
+    for copy in copies:
         copy.start()
-
-
-def each_chunk(matrix, copies, step):
-    share = CHUNK // 8
-    for chunk in range(matrix.shape[0] // CHUNK):
-        if copies:
-            for copy in copies[chunk * share : (chunk + 1) * share]:
-                copy.wait()
-            start_chunk(copies, chunk + 2)
-        step(pl.ds(chunk * CHUNK, CHUNK))
-
-
-def stream_buffers(matrix, width, streamed):
-    rows = matrix.shape[0]
-    return [pltpu.VMEM((rows, width), jnp.float32), pltpu.SemaphoreType.DMA((rows // 8,))] if streamed else []
-
-
-def fetch_kernel(matrix, out, ready):
-    copies = chunk_copies(matrix, out, ready)
-    for copy in copies:
-        copy.start()
     for copy in copies:
         copy.wait()
 
 
-def fetched(matrix):
-    rows, width = matrix.shape
+def fetched(matrix, part=1):
+    rows, width = matrix.shape[0] // part, matrix.shape[1]
     return call(
         fetch_kernel,
         f32(rows, width),
@@ -149,8 +148,9 @@
     )(matrix)
 
 
-def forward_kernel(blocks, upper, keep, extra, scalars, received, matrix, rest_in, solved, send, rest, vector, total, *stream):
-    matrix, copies = begin(matrix, stream)
+def forward_kernel(blocks, upper, keep, extra, count, scalars, received, rest_in, *refs):
+    matrices, (solved, send, rest, vector, total, *stream) = refs[:count], refs[count:]
+    matrices, copies = begin(matrices, stream)
     if extra:
         for source in range(blocks):
             vector[2 * source : 2 * source + 2, :] = received[source, 0:2, :]
@@ -158,13 +158,13 @@
         vector[...] = jnp.sum(received[...], axis=0)
     total[...] = jnp.zeros_like(total)
 
-    def step(rows):
+    def step(matrix, rows, place):
         values = row_dot(matrix, rows, 0, vector, 0, blocks)
         for s in range(PAIR):
-            solved[s, rows, :] = jnp.broadcast_to(values[s], (CHUNK, LANES))
+            solved[s, place, :] = jnp.broadcast_to(values[s], (CHUNK, LANES))
         column_dot(matrix, rows, blocks * LANES, upper, values, total)
 
-    each_chunk(matrix, copies, step)
+    each_chunk(matrices, copies, step)
     whole = -jnp.sum(total[...], axis=1)
     if extra:
         rest[...] = whole
@@ -179,19 +179,20 @@
         send[copy] = whole[2 * keep :, :]
 
 
-def forward(received, matrix, rest_in, scalars, blocks, upper, keep, copies, extra, streamed):
-    rows = matrix.shape[0]
+def forward(received, matrices, rest_in, scalars, blocks, upper, keep, copies, extra):
+    rows = matrices[-1].shape[0]
+    streamed = len(matrices) > 1
     width = upper * LANES + blocks * LANES
     return call(
-        functools.partial(forward_kernel, blocks, upper, keep, extra),
+        functools.partial(forward_kernel, blocks, upper, keep, extra, len(matrices)),
         (f32(PAIR, rows, LANES), f32(copies, 2 * (upper - keep), LANES), f32(2 * upper, LANES)),
-        in_specs=[SMEM, VMEM, HBM if streamed else VMEM, VMEM],
+        in_specs=[SMEM, VMEM, VMEM] + ([VMEM, HBM] if streamed else [VMEM]),
         out_specs=(VMEM,) * 3,
         scratch_shapes=[pltpu.VMEM((2 * blocks, LANES), jnp.float32), pltpu.VMEM((2 * upper, 8, LANES), jnp.float32)]
-        + stream_buffers(matrix, width, streamed),
+        + stream_buffers(matrices, width),
         limit=STREAM if streamed else LIMIT,
         cost_estimate=cost(rows * width),
-    )(scalars, received, matrix, rest_in)
+    )(scalars, received, rest_in, *matrices)
 
 
 def lowest_kernel(blocks, upper, received, own, other, path, send, total, buffer, ready):
@@ -250,9 +251,10 @@
     )(received, own, other, path)
 
 
-def backward_kernel(blocks, known_blocks, scalars, received, matrix, solved, *refs):
+def backward_kernel(blocks, known_blocks, number, scalars, received, solved, *refs):
+    matrices, refs = refs[:number], refs[number:]
     known, (send, newest, total, vector, *stream) = refs[: len(known_blocks) - 1], refs[len(known_blocks) - 1 :]
-    matrix, copies = begin(matrix, stream)
+    matrices, copies = begin(matrices, stream)
     newest[...] = jnp.sum(received[...], axis=0)
     total[...] = jnp.zeros_like(total)
     again = solved.shape[2] == LANES and solved.shape[0] == blocks
@@ -260,11 +262,11 @@
         for block in range(blocks):
             vector[2 * block : 2 * block + 2, :] = solved[block, pl.ds(scalars[2] * 2, 2), :]
 
-    def step(rows):
+    def step(matrix, rows, place):
         if again:
             values = row_dot(matrix, rows, 0, vector, 0, blocks)
         else:
-            values = [solved[s, rows, 0:1] for s in range(PAIR)]
+            values = [solved[s, place, 0:1] for s in range(PAIR)]
         column = blocks * LANES
         for ref, count in zip((*known, newest), known_blocks):
             part = row_dot(matrix, rows, column, ref, 0, count)
@@ -272,26 +274,27 @@
             column += count * LANES
         column_dot(matrix, rows, 0, blocks, values, total)
 
-    each_chunk(matrix, copies, step)
+    each_chunk(matrices, copies, step)
     whole = jnp.sum(total[...], axis=1)
     for copy in range(send.shape[0]):
         send[copy] = whole
 
 
-def backward(received, matrix, solved, known, scalars, blocks, copies, streamed):
-    rows = matrix.shape[0]
+def backward(received, matrices, solved, known, scalars, blocks, copies):
+    rows = matrices[-1].shape[0]
+    streamed = len(matrices) > 1
     counts = [array.shape[0] // PAIR for array in known] + [received.shape[1] // PAIR]
     width = (blocks + sum(counts)) * LANES
     return call(
-        functools.partial(backward_kernel, blocks, counts),
+        functools.partial(backward_kernel, blocks, counts, len(matrices)),
         (f32(copies, 2 * blocks, LANES), f32(*received.shape[1:])),
-        in_specs=[SMEM, VMEM, HBM if streamed else VMEM] + [VMEM] * (1 + len(known)),
+        in_specs=[SMEM, VMEM, VMEM] + ([VMEM, HBM] if streamed else [VMEM]) + [VMEM] * len(known),
         out_specs=(VMEM,) * 2,
         scratch_shapes=[pltpu.VMEM((2 * blocks, 8, LANES), jnp.float32), pltpu.VMEM((2 * blocks, LANES), jnp.float32)]
-        + stream_buffers(matrix, width, streamed),
+        + stream_buffers(matrices, width),
         limit=STREAM if streamed else LIMIT,
         cost_estimate=cost(rows * width),
-    )(scalars, received, matrix, solved, *known)
+    )(scalars, received, solved, *matrices, *known)
 
 
 def root_kernel(column, blocks, vector, matrix, send, total):
@@ -387,9 +390,9 @@
 
 def first_kernel(depth, groups, scalars, both, index, *refs):
     count = sum(groups)
-    parts, (send, terms, *packs), (path, ready) = refs[:count], refs[count:-2], refs[-2:]
+    parts, (send, terms, *packs), (path, ready, done, *stages) = refs[:count], refs[count : -3 - len(groups)], refs[-3 - len(groups) :]
     copies = []
-    for pack, size in zip(packs, groups):
+    for pack, size in zip(stages, groups):
         column = 0
         for part in parts[:size]:
             width = part.shape[1]
@@ -405,6 +408,15 @@
     pieces = split3(both[0, pl.ds(half, 8), :columns] + both[1, pl.ds(half, 8), :columns])
     terms[:, columns:] = jnp.zeros((32, terms.shape[1] - columns), jnp.bfloat16)
     terms[:, :columns] = jnp.concatenate([*pieces, jnp.zeros_like(pieces[0])], axis=0)
+    for copy in copies:
+        copy.wait()
+    copies = []
+    for stage, pack in zip(stages, packs):
+        for row in range(0, pack.shape[0], 8):
+            rows = pl.ds(row, 8)
+            copies.append(pltpu.make_async_copy(stage.at[rows, :], pack.at[rows, :], done.at[len(copies)]))
+    for copy in copies:
+        copy.start()
     expand(scalars, terms, index, sum(WIDTHS[:3]) // LANES, path)
     add_own(scalars, both, depth, (3,), path)
     for dest in range(X):
@@ -424,7 +436,12 @@
         (f32(X * depth, 8, LANES), jax.ShapeDtypeStruct((32, columns + 2 * LANES), jnp.bfloat16), *packs),
         in_specs=[SMEM, VMEM, VMEM] + [HBM] * len(parts),
         out_specs=(VMEM, VMEM) + (HBM,) * len(packs),
-        scratch_shapes=[pltpu.VMEM((WIDTHS[3] // LANES, 8, LANES), jnp.float32), pltpu.SemaphoreType.DMA((count,))],
+        scratch_shapes=[
+            pltpu.VMEM((WIDTHS[3] // LANES, 8, LANES), jnp.float32),
+            pltpu.SemaphoreType.DMA((count,)),
+            pltpu.SemaphoreType.DMA((sum(pack.shape[0] // 8 for pack in packs),)),
+        ]
+        + [pltpu.VMEM(pack.shape, jnp.float32) for pack in packs],
         limit=WHOLE,
     )(scalars, both, index, *parts)
     return outs[0], outs[1], outs[2:]
@@ -606,12 +623,12 @@
     matrix3 = gathered(own3)
     all_coupling = gathered(coupling)
     received = sum_and_copy(exchange(send, ("y0", "x", "z")), 2 * depth)
-    target2 = exchange(received, ("y0", "z"))
+    target2, half2 = lax.optimization_barrier((exchange(received, ("y0", "z")), fetched(matrix2, 2)))
     solved2, send, rest = forward(
-        target2, matrix2, received[0], places, counts[2], counts[0] + counts[1], counts[0], 4 * depth, 6, True
+        target2, (half2, matrix2), received[0], places, counts[2], counts[0] + counts[1], counts[0], 4 * depth, 6
     )
     received, matrix1 = lax.optimization_barrier((exchange(send, ("y1", "y0", "z")), fetched(matrix1)))
-    solved1, send, rest = forward(received, matrix1, rest, places, counts[1], counts[0], 0, Y, 0, False)
+    solved1, send, rest = forward(received, (matrix1,), rest, places, counts[1], counts[0], 0, Y, 0)
 
     def sum_root(copies):
         received = exchange(copies.reshape(Y * depth, -1, LANES), ALL_Y + ("z",))
@@ -620,17 +637,19 @@
     target = sum_root(send).reshape(-1, LANES)
     received = sum_root(root(target, matrix1, WIDTHS[1] + WIDTHS[0], Y)).reshape(1, -1, LANES)
     heads = scalars([y, y % 4, y % 2], windows.reshape(-1))
-    send, x0 = backward(received, matrix1, solved1, [], places, counts[1], 4 * depth, False)
-    received = exchange(send, ("y1", "y0", "z"))
-    received, chosen0 = lax.optimization_barrier((received, picked(x0, both_indices, heads, 0)))
-    send, x1 = backward(received, matrix2, solved2, [x0], places, counts[2], 2 * depth, True)
-    received = exchange(send, ("y0", "z"))
-    received, chosen1, all_coupling = lax.optimization_barrier(
-        (received, picked(x1, both_indices, heads, counts[0]), fetched(all_coupling))
+    send, x0 = backward(received, (matrix1,), solved1, [], places, counts[1], 4 * depth)
+    x0, matrix2 = lax.optimization_barrier((x0, matrix2))
+    received, chosen0, half2 = lax.optimization_barrier(
+        (exchange(send, ("y1", "y0", "z")), picked(x0, both_indices, heads, 0), fetched(matrix2, 2))
     )
-    send, x2 = backward(received, matrix3, target3, [x0, x1], places, counts[3], depth, True)
-    received = exchange(send, ("z",))
-    chosen2 = picked(x2, both_indices, heads, counts[0] + counts[1])
+    send, x1 = backward(received, (half2, matrix2), solved2, [x0], places, counts[2], 2 * depth)
+    received, chosen1, half3 = lax.optimization_barrier(
+        (exchange(send, ("y0", "z")), picked(x1, both_indices, heads, counts[0]), fetched(matrix3, 2))
+    )
+    send, x2 = backward(received, (half3, matrix3), target3, [x0, x1], places, counts[3], depth)
+    received, chosen2, all_coupling = lax.optimization_barrier(
+        (exchange(send, ("z",)), picked(x2, both_indices, heads, counts[0] + counts[1]), fetched(all_coupling))
+    )
     send = last(received, [x0, x1, x2], [chosen0, chosen1, chosen2], all_coupling, both_indices, heads)
     received = exchange(send, ("c", "x"))
     ends = scalars([z, c, (x % 2) * 2 + c])

time: 292 us -> 244 us (0.84)
  Pallas kernels: 85.4 us -> 40.3 us
  waiting for transfers between devices: 44.3 us -> 35.9 us
  local copies, waits for them, and re-layouts: 7.86 us -> 14.2 us
    pallas_call x1, Pallas kernels: 46.5 us -> 4.28 us  [first(): call(functools.partial(first_kernel, depth, [len(group) for group in grou...]
    all_to_all x7, waiting for transfers between devices: 41 us -> 32.2 us  [exchange(): return lax.all_to_all(flat, axes, 0, 0, tiled=True).reshape(operand.shape)]
    unnamed x22 -> x24, local copies, waits for them, and re-layouts: 5.66 us -> 11.9 us
    pallas_call x5, Pallas kernels: 16.9 us -> 13 us  [the longest x3 8.23 us: backward(): call(functools.partial(backward_kernel, blocks, counts, len(matrices)), (...]
  transfers between devices with their start and end apart: 12 -> 12, of which waited for: 8 -> 8; matrix products, arithmetic and copies ran while one was open for 0% -> 0% of each run, Pallas kernels for 10% -> 12%
where the time goes in v7:
time: 244 us; the launch traced here: 242 us
  blocking collectives  93.9 us (38%)
  starting transfers between devices  43.5 us (18%)
  Pallas kernels  40.3 us (17%)
  waiting for transfers between devices  35.9 us (15%)
  local copies, waits for them, and re-layouts  14.2 us (6%)
  between operations  14.1 us (6%)
    all_to_all x6, blocking collectives, exchange(): return lax.all_to_all(flat, axes, 0, 0, tiled=True).reshape(operand.shape)  83.6 us
    all_to_all x7, starting transfers between devices, exchange(): return lax.all_to_all(flat, axes, 0, 0, tiled=True).reshape(operand.shape)  41.3 us
    all_to_all x7, waiting for transfers between devices, exchange(): return lax.all_to_all(flat, axes, 0, 0, tiled=True).reshape(operand.shape)  32.2 us
    unnamed x24, local copies, waits for them, and re-layouts  11.9 us
    all_gather x1, blocking collectives, body(): lax.all_gather(own_product(subtree_values, coupling, rhs_parts), 'c', axi...  10.3 us
    pallas_call x3, Pallas kernels, backward(): call(functools.partial(backward_kernel, blocks, counts, len(matrices)), (...  8.23 us
    pallas_call x5, Pallas kernels, fetched(): call(fetch_kernel, f32(rows, width), in_specs=[HBM], out_specs=VMEM, scra...  4.92 us
  transfers between devices with their start and end apart: 12, of which 8 were waited for; matrix products, arithmetic and copies ran while one was open for 0% of the time, Pallas kernels for 12%

profile of v7, /device:TPU:1, one launch (start us, length us, event | category | flops | bytes accessed | tf_op | source)
XLA Modules:
  0.0 242.2 jit_solution(13702973727547550060)
XLA Ops:
  7.3 0.8 copy-done
  8.1 0.3 convert_reduce_fusion
  8.4 0.6 constant_dynamic-slice_fusion.index
  9.0 1.9 shard_map.173
  10.9 10.3 %all-gather = f32[32,2176]{1,0:T(8,128)} all-gather(f32[16,2176]{1,0:T(8,128)} %shard_map.173), channel_id=2, replica_groups=mesh['y2'=2,'y1'=2,'y0'=2,'x'=4,'c'=2,'z'=8] {'c'}, dimensions={0}, use_global_device_ids=true | all-gather | bytes 417792 | tf_op jit(solution)/shard_map/all_gather | solution.py:595
  21.2 0.7 concatenate.7.scalars
  21.9 4.3 %shard_map.174 = (f32[32,8,128]{2,1,0:T(8,128)}, bf16[32,2304]{1,0:T(8,128)(2,1)}, f32[16,9216]{1,0:T(8,128)}, f32[16,8192]{1,0:T(8,128)}, f32[8,10240]{1,0:T(8,128)}) custom-call(s32[80]{0:T(128)} %concatenate.7.scalars, f32[2,16,2176]{2,1,0:T(8,128)} %bitcast.21, s32[1,2304]{1,0:T(1,128)} %constant_dynamic-slice_fusion.index, f32[16,1024]{1,0:T(8,128)} %refs_0_.1, ...), custom_call_target="tpu_custom_call" | custom-call | tf_op jit(solution)/shard_map/pallas_call | solution.py:434
  26.2 0.0 all-gather.8.cloned.1.call-start
  26.2 0.7 all-gather.8.cloned.1.call-update
  26.9 2.1 collective-permute-start
  29.0 7.5 %all-to-all-start = ((f32[32,8,128]{2,1,0:T(8,128)}), f32[32,8,128]{2,1,0:T(8,128)S(1)}, u32[]{:S(2)}, u32[]{:S(2)}) async-start(f32[32,8,128]{2,1,0:T(8,128)} %get-tuple-element.47), calls=%async_computation | async-start | bytes 262144 | tf_op jit(solution)/shard_map/all_to_all | solution.py:51
  36.5 0.0 all-gather.10.cloned.1.call-start
  36.6 0.9 copy-done.8
  37.5 3.9 %shard_map.175.path = f32[64,8,128]{2,1,0:T(8,128)S(1)} custom-call(s32[80]{0:T(128)S(1)} %copy-done.11, f32[2,16,2176]{2,1,0:T(8,128)S(1)} %bitcast.22, bf16[32,2304]{1,0:T(8,128)(2,1)S(1)} %copy-done.8, s32[1,2304]{1,0:T(1,128)S(1)} %copy-done.9), custom_call_target="tpu_custom_call" | custom-call | flops 8388608 | bytes 4194304 | tf_op jit(solution)/shard_map/pallas_call | solution.py:457
  41.4 4.3 %all-to-all-done.received = f32[32,8,128]{2,1,0:T(8,128)S(1)} async-done(((f32[32,8,128]{2,1,0:T(8,128)}), f32[32,8,128]{2,1,0:T(8,128)S(1)}, u32[]{:S(2)}, u32[]{:S(2)}) %all-to-all-start) | async-done | bytes 131104 | tf_op jit(solution)/shard_map/all_to_all | solution.py:51
  45.7 9.9 %all_to_all.86.received.solved = f32[8,8,128]{2,1,0:T(8,128)S(1)} all-to-all(f32[8,8,128]{2,1,0:T(8,128)S(1)} %shard_map.176), channel_id=1, replica_groups=mesh['y2'=2,'y1'=2,'y0'=2,'x'=4,'c'=2,'z'=8] {'z'}, dimensions={0} | all-to-all | bytes 65536 | tf_op jit(solution)/shard_map/all_to_all | solution.py:51
  55.7 1.5 shard_map.177
  57.2 15.9 %all_to_all.87.received = f32[64,8,128]{2,1,0:T(8,128)S(1)} all-to-all(f32[64,8,128]{2,1,0:T(8,128)S(1)} %shard_map.177), channel_id=1, replica_groups=mesh['y2'=2,'y1'=2,'y0'=2,'x'=4,'c'=2,'z'=8] {'y0','x','z'}, dimensions={0} | all-to-all | bytes 524288 | tf_op jit(solution)/shard_map/all_to_all | solution.py:51
  73.1 0.7 shard_map.178
  73.8 3.5 %all-to-all-start.3 = ((f32[16,8,128]{2,1,0:T(8,128)}), f32[16,8,128]{2,1,0:T(8,128)S(1)}, u32[]{:S(2)}, u32[]{:S(2)}) async-start(f32[16,8,128]{2,1,0:T(8,128)} %shard_map.178), calls=%async_computation.3 | async-start | bytes 131072 | tf_op jit(solution)/shard_map/all_to_all | solution.py:51
  77.3 0.7 slice_bitcast_fusion.rest_in
  78.0 2.4 copy-done.1
  80.3 0.2 shard_map.179.refs_0_
  80.6 4.1 %all-to-all-done.3.received = f32[16,8,128]{2,1,0:T(8,128)S(1)} async-done(((f32[16,8,128]{2,1,0:T(8,128)}), f32[16,8,128]{2,1,0:T(8,128)S(1)}, u32[]{:S(2)}, u32[]{:S(2)}) %all-to-all-start.3) | async-done | bytes 65568 | tf_op jit(solution)/shard_map/all_to_all | solution.py:51
  84.6 3.3 %shard_map.180 = (f32[2,128,128]{2,1,0:T(8,128)S(1)}, f32[32,32,128]{2,1,0:T(8,128)}, f32[96,128]{1,0:T(8,128)S(1)}) custom-call(s32[80]{0:T(128)S(1)} %copy-done.11, f32[16,8,128]{2,1,0:T(8,128)S(1)} %all-to-all-done.3.received, f32[8,128]{1,0:T(8,128)S(1)} %slice_bitcast_fusion.rest_in, f32[64,8192]{1,0:T(8,128)S(1)} %shard_map.179.refs_0_, ...), custom_call_target="tpu_custom_call" | custom-call | flops 8388608 | bytes 4194304 | tf_op jit(solution)/shard_map/pallas_call | solution.py:186
  87.9 5.8 %all-to-all-start.4 = ((f32[32,32,128]{2,1,0:T(8,128)}), f32[32,32,128]{2,1,0:T(8,128)S(1)}, u32[]{:S(2)}, u32[]{:S(2)}) async-start(f32[32,32,128]{2,1,0:T(8,128)} %get-tuple-element.57), calls=%async_computation.4 | async-start | bytes 1048576 | tf_op jit(solution)/shard_map/all_to_all | solution.py:51
  93.7 0.5 all-gather.12.cloned.1.call-update
  94.3 2.4 %all-gather.8.cloned.1.call-done.matrix = f32[64,10240]{1,0:T(8,128)} async-done(((f32[8,10240]{1,0:T(8,128)}), f32[64,10240]{1,0:T(8,128)}) %all-gather.8.cloned.1.call-update) | async-done | bytes 2621456 | tf_op jit(solution)/shard_map/all_gather | solution.py:598
  96.7 1.7 copy-done.4
  98.4 0.9 shard_map.181.refs_0_.matrix
  99.3 7.0 %all-to-all-done.4.received = f32[32,32,128]{2,1,0:T(8,128)S(1)} async-done(((f32[32,32,128]{2,1,0:T(8,128)}), f32[32,32,128]{2,1,0:T(8,128)S(1)}, u32[]{:S(2)}, u32[]{:S(2)}) %all-to-all-start.4) | async-done | bytes 524320 | tf_op jit(solution)/shard_map/all_to_all | solution.py:51
  106.3 1.5 shard_map.182
  107.8 22.5 %all_to_all.88.received = f32[64,8,128]{2,1,0:T(8,128)S(1)} all-to-all(f32[64,8,128]{2,1,0:T(8,128)S(1)} %bitcast.24), channel_id=1, replica_groups=mesh['y2'=2,'y1'=2,'y0'=2,'x'=4,'c'=2,'z'=8] {'y2','y1','y0','z'}, dimensions={0} | all-to-all | bytes 524288 | tf_op jit(solution)/shard_map/all_to_all | solution.py:51
  130.4 0.1 shard_map.183
  130.4 9.5 %all_to_all.89 = f32[8,8,128]{2,1,0:T(8,128)S(1)} all-to-all(f32[8,8,128]{2,1,0:T(8,128)S(1)} %shard_map.183), channel_id=1, replica_groups=mesh['y2'=2,'y1'=2,'y0'=2,'x'=4,'c'=2,'z'=8] {'z'}, dimensions={0} | all-to-all | bytes 65536 | tf_op jit(solution)/shard_map/all_to_all | solution.py:51
  139.9 0.4 shard_map.184
  140.3 16.3 %all_to_all.90.received = f32[64,8,128]{2,1,0:T(8,128)S(1)} all-to-all(f32[64,8,128]{2,1,0:T(8,128)S(1)} %bitcast.23), channel_id=1, replica_groups=mesh['y2'=2,'y1'=2,'y0'=2,'x'=4,'c'=2,'z'=8] {'y2','y1','y0','z'}, dimensions={0} | all-to-all | bytes 524288 | tf_op jit(solution)/shard_map/all_to_all | solution.py:51
  156.6 0.1 shard_map.185
  156.7 9.5 %all_to_all.91 = f32[8,8,128]{2,1,0:T(8,128)S(1)} all-to-all(f32[8,8,128]{2,1,0:T(8,128)S(1)} %shard_map.185), channel_id=1, replica_groups=mesh['y2'=2,'y1'=2,'y0'=2,'x'=4,'c'=2,'z'=8] {'z'}, dimensions={0} | all-to-all | bytes 65536 | tf_op jit(solution)/shard_map/all_to_all | solution.py:51
  166.1 1.8 shard_map.186
  167.9 3.9 %all-to-all-start.9 = ((f32[32,32,128]{2,1,0:T(8,128)}), f32[32,32,128]{2,1,0:T(8,128)S(1)}, u32[]{:S(2)}, u32[]{:S(2)}) async-start(f32[32,32,128]{2,1,0:T(8,128)} %get-tuple-element.64), calls=%async_computation.9 | async-start | bytes 1048576 | tf_op jit(solution)/shard_map/all_to_all | solution.py:51
  171.8 0.1 reduce_sum.12
  171.9 0.1 concatenate.6.scalars
  172.0 2.2 copy-done.2
  174.2 0.2 shard_map.188.refs_0_
  174.5 2.2 shard_map.187.chosen0
  176.6 7.6 %all-to-all-done.9.received = f32[32,32,128]{2,1,0:T(8,128)S(1)} async-done(((f32[32,32,128]{2,1,0:T(8,128)}), f32[32,32,128]{2,1,0:T(8,128)S(1)}, u32[]{:S(2)}, u32[]{:S(2)}) %all-to-all-start.9) | async-done | bytes 524320 | tf_op jit(solution)/shard_map/all_to_all | solution.py:51
  184.3 3.3 %shard_map.189 = (f32[16,32,128]{2,1,0:T(8,128)}, f32[32,128]{1,0:T(8,128)S(1)}) custom-call(s32[80]{0:T(128)S(1)} %copy-done.11, f32[32,32,128]{2,1,0:T(8,128)S(1)} %all-to-all-done.9.received, f32[2,128,128]{2,1,0:T(8,128)S(1)} %get-tuple-element.69.solved, f32[64,8192]{1,0:T(8,128)S(1)} %shard_map.188.refs_0_, ...), custom_call_target="tpu_custom_call" | custom-call | flops 8388608 | bytes 4194304 | tf_op jit(solution)/shard_map/pallas_call | solution.py:288
  187.6 3.7 %all-to-all-start.10 = ((f32[16,32,128]{2,1,0:T(8,128)}), f32[16,32,128]{2,1,0:T(8,128)S(1)}, u32[]{:S(2)}, u32[]{:S(2)}) async-start(f32[16,32,128]{2,1,0:T(8,128)} %get-tuple-element.71), calls=%async_computation.10 | async-start | bytes 524288 | tf_op jit(solution)/shard_map/all_to_all | solution.py:51
  191.3 2.3 copy-done.3
  193.7 0.6 shard_map.191.refs_0_
  194.2 1.4 shard_map.190.chosen1
  195.6 3.2 %all-to-all-done.10.received = f32[16,32,128]{2,1,0:T(8,128)S(1)} async-done(((f32[16,32,128]{2,1,0:T(8,128)}), f32[16,32,128]{2,1,0:T(8,128)S(1)}, u32[]{:S(2)}, u32[]{:S(2)}) %all-to-all-start.10) | async-done | bytes 262176 | tf_op jit(solution)/shard_map/all_to_all | solution.py:51
  198.8 3.2 %shard_map.192 = (f32[8,16,128]{2,1,0:T(8,128)}, f32[32,128]{1,0:T(8,128)S(1)}) custom-call(s32[80]{0:T(128)S(1)} %copy-done.11, f32[16,32,128]{2,1,0:T(8,128)S(1)} %all-to-all-done.10.received, f32[8,8,128]{2,1,0:T(8,128)S(1)} %all_to_all.86.received.solved, f32[64,9216]{1,0:T(8,128)S(1)} %shard_map.191.refs_0_, ...), custom_call_target="tpu_custom_call" | custom-call | flops 9437184 | bytes 4718592 | tf_op jit(solution)/shard_map/pallas_call | solution.py:288
  202.0 3.4 %all-to-all-start.11 = ((f32[8,16,128]{2,1,0:T(8,128)}), f32[8,16,128]{2,1,0:T(8,128)S(1)}, u32[]{:S(2)}, u32[]{:S(2)}) async-start(f32[8,16,128]{2,1,0:T(8,128)} %get-tuple-element.76), calls=%async_computation.11 | async-start | bytes 131072 | tf_op jit(solution)/shard_map/all_to_all | solution.py:51
  205.4 1.6 copy-done.7
  207.0 3.0 %shard_map.194.coupling = f32[256,2048]{1,0:T(8,128)S(1)} custom-call(f32[256,2048]{1,0:T(8,128)S(1)} %copy-done.7), custom_call_target="tpu_custom_call" | custom-call | flops 8388608 | bytes 4194304 | tf_op jit(solution)/shard_map/pallas_call | solution.py:141
  210.0 1.4 shard_map.193.chosen2
  211.4 1.1 all-to-all-done.11.received
  212.5 3.3 %shard_map.195 = f32[8,16,128]{2,1,0:T(8,128)} custom-call(s32[152]{0:T(256)S(1)} %concatenate.6.scalars, f32[8,16,128]{2,1,0:T(8,128)S(1)} %all-to-all-done.11.received, f32[64,128]{1,0:T(8,128)S(1)} %get-tuple-element.66.x.refs_2_.x0, f32[32,128]{1,0:T(8,128)S(1)} %get-tuple-element.72.x.refs_3_.x1, f32[32,128]{1,0:T(8,128)S(1)} %get-tuple-element.77.x.x2, ...), custom_call_target="tpu_custom_call" | custom-call | tf_op jit(solution)/shard_map/pallas_call | solution.py:538
  215.8 13.5 %all-to-all-start.12 = ((f32[8,16,128]{2,1,0:T(8,128)}), f32[8,16,128]{2,1,0:T(8,128)S(1)}, u32[]{:S(2)}, u32[]{:S(2)}) async-start(f32[8,16,128]{2,1,0:T(8,128)} %shard_map.195), calls=%async_computation.12 | async-start | bytes 131072 | tf_op jit(solution)/shard_map/all_to_all | solution.py:51
  229.4 0.1 stack.35.scalars
  229.5 4.9 %all-to-all-done.12.received = f32[8,16,128]{2,1,0:T(8,128)S(1)} async-done(((f32[8,16,128]{2,1,0:T(8,128)}), f32[8,16,128]{2,1,0:T(8,128)S(1)}, u32[]{:S(2)}, u32[]{:S(2)}) %all-to-all-start.12) | async-done | bytes 65568 | tf_op jit(solution)/shard_map/all_to_all | solution.py:51
  234.3 1.3 shard_map.196
  (33 shorter events, 0.3 us)
Async XLA Ops:
  7.2 0.9 copy-start
  7.2 70.8 %all-gather.6.cloned.1.call-start = ((), (), s32[]{:S(2)}) async-start(), calls=%async_computation.13 | async-start | bytes 4718592 | tf_op jit(solution)/shard_map/all_gather | solution.py:598
  9.0 27.6 %copy-start.9 = (s32[1,2304]{1,0:T(1,128)S(1)}, s32[1,2304]{1,0:T(1,128)}, u32[]{:S(2)}) copy-start(s32[1,2304]{1,0:T(1,128)} %constant_dynamic-slice_fusion.index) | copy-start | bytes 27652
  21.2 15.4 %copy-start.5 = (f32[32,2176]{1,0:T(8,128)S(1)}, f32[32,2176]{1,0:T(8,128)}, u32[]{:S(2)}) copy-start(f32[32,2176]{1,0:T(8,128)} %all-gather) | copy-start | bytes 835588
  21.9 14.7 %copy-start.11 = (s32[80]{0:T(128)S(1)}, s32[80]{0:T(128)}, u32[]{:S(2)}) copy-start(s32[80]{0:T(128)} %concatenate.7.scalars) | copy-start | bytes 964
  26.2 29.5 %copy-start.6 = (f32[16,9216]{1,0:T(8,128)S(1)}, f32[16,9216]{1,0:T(8,128)}, u32[]{:S(2)}) copy-start(f32[16,9216]{1,0:T(8,128)} %get-tuple-element.73.own) | copy-start | bytes 1769476
  26.2 70.5 %all-gather.8.cloned.1.call-start = ((), (), s32[]{:S(2)}) async-start(), calls=%async_computation.14 | async-start | bytes 2949120 | tf_op jit(solution)/shard_map/all_gather | solution.py:598
  26.9 18.8 %collective-permute-start = (f32[16,9216]{1,0:T(8,128)}, f32[16,9216]{1,0:T(8,128)S(1)}, u32[]{:S(2)}, u32[]{:S(2)}) collective-permute-start(f32[16,9216]{1,0:T(8,128)} %get-tuple-element.73.own), channel_id=1, source_target_pairs={{0,8},{8,0},{1,9},{9,1},{2,10},{10,2},{3,11},{11,3},{4,12},{12,4},... | collective-permute-start | bytes 1769480 | tf_op jit(solution)/shard_map/ppermute | solution.py:618
  29.0 16.7 %all-to-all-start = ((f32[32,8,128]{2,1,0:T(8,128)}), f32[32,8,128]{2,1,0:T(8,128)S(1)}, u32[]{:S(2)}, u32[]{:S(2)}) async-start(f32[32,8,128]{2,1,0:T(8,128)} %get-tuple-element.47), calls=%async_computation | async-start | bytes 262144 | tf_op jit(solution)/shard_map/all_to_all | solution.py:51
  36.5 154.8 %all-gather.10.cloned.1.call-start = ((), (), s32[]{:S(2)}) async-start(), calls=%async_computation.15 | async-start | bytes 5308416 | tf_op jit(solution)/shard_map/all_gather | solution.py:598
  36.6 0.9 copy-start.8
  73.8 10.8 %all-to-all-start.3 = ((f32[16,8,128]{2,1,0:T(8,128)}), f32[16,8,128]{2,1,0:T(8,128)S(1)}, u32[]{:S(2)}, u32[]{:S(2)}) async-start(f32[16,8,128]{2,1,0:T(8,128)} %shard_map.178), calls=%async_computation.3 | async-start | bytes 131072 | tf_op jit(solution)/shard_map/all_to_all | solution.py:51
  78.0 2.4 copy-start.1
  87.9 18.4 %all-to-all-start.4 = ((f32[32,32,128]{2,1,0:T(8,128)}), f32[32,32,128]{2,1,0:T(8,128)S(1)}, u32[]{:S(2)}, u32[]{:S(2)}) async-start(f32[32,32,128]{2,1,0:T(8,128)} %get-tuple-element.57), calls=%async_computation.4 | async-start | bytes 1048576 | tf_op jit(solution)/shard_map/all_to_all | solution.py:51
  93.7 111.7 %all-gather.12.cloned.1.call-start = ((), (), s32[]{:S(2)}) async-start(), calls=%async_computation.16 | async-start | bytes 2359296 | tf_op jit(solution)/shard_map/all_gather | solution.py:598
  96.7 1.7 copy-start.4
  167.9 16.3 %all-to-all-start.9 = ((f32[32,32,128]{2,1,0:T(8,128)}), f32[32,32,128]{2,1,0:T(8,128)S(1)}, u32[]{:S(2)}, u32[]{:S(2)}) async-start(f32[32,32,128]{2,1,0:T(8,128)} %get-tuple-element.64), calls=%async_computation.9 | async-start | bytes 1048576 | tf_op jit(solution)/shard_map/all_to_all | solution.py:51
  172.0 2.2 copy-start.2
  187.6 11.3 %all-to-all-start.10 = ((f32[16,32,128]{2,1,0:T(8,128)}), f32[16,32,128]{2,1,0:T(8,128)S(1)}, u32[]{:S(2)}, u32[]{:S(2)}) async-start(f32[16,32,128]{2,1,0:T(8,128)} %get-tuple-element.71), calls=%async_computation.10 | async-start | bytes 524288 | tf_op jit(solution)/shard_map/all_to_all | solution.py:51
  191.3 2.3 copy-start.3
  202.0 10.5 %all-to-all-start.11 = ((f32[8,16,128]{2,1,0:T(8,128)}), f32[8,16,128]{2,1,0:T(8,128)S(1)}, u32[]{:S(2)}, u32[]{:S(2)}) async-start(f32[8,16,128]{2,1,0:T(8,128)} %get-tuple-element.76), calls=%async_computation.11 | async-start | bytes 131072 | tf_op jit(solution)/shard_map/all_to_all | solution.py:51
  205.4 1.6 copy-start.7
  210.0 24.3 %copy-start.10 = (f32[16,32]{1,0:T(8,128)S(1)}, f32[16,32]{1,0:T(8,128)}, u32[]{:S(2)}) copy-start(f32[16,32]{1,0:T(8,128)} %values.3) | copy-start | bytes 6148
  215.8 18.5 %all-to-all-start.12 = ((f32[8,16,128]{2,1,0:T(8,128)}), f32[8,16,128]{2,1,0:T(8,128)S(1)}, u32[]{:S(2)}, u32[]{:S(2)}) async-start(f32[8,16,128]{2,1,0:T(8,128)} %shard_map.195), calls=%async_computation.12 | async-start | bytes 131072 | tf_op jit(solution)/shard_map/all_to_all | solution.py:51
Sparse Core Ops, SparseCore 0:
  26.3 37.2 all-gather.5
  65.7 30.9 all-gather.7
  98.8 40.2 all-gather.9
  141.1 30.5 all-gather.11

commit v8 on v7

--- a/solution.py
+++ b/solution.py
@@ -136,8 +136,8 @@
         copy.wait()
 
 
-def fetched(matrix, part=1):
-    rows, width = matrix.shape[0] // part, matrix.shape[1]
+def fetched(matrix, part=1.0):
+    rows, width = int(matrix.shape[0] * part), matrix.shape[1]
     return call(
         fetch_kernel,
         f32(rows, width),
@@ -334,10 +334,10 @@
     return call(functools.partial(sum_kernel, copies), f32(copies, *received.shape[1:]))(received)
 
 
-def expand(scalars, terms, index, first_block, path):
+def expand(scalars, windows, terms, index, first_block, path):
     def one(block, carry):
-        at = pl.multiple_of(scalars[8 + first_block + block] * LANES, LANES)
-        selector = one_hot(index[0:1, pl.ds(at, 2 * LANES)], first_block + block)
+        at = pl.multiple_of(windows[scalars[2] // 2, first_block + block] * LANES, LANES)
+        selector = one_hot(index[pl.ds(scalars[7] * 2 + scalars[2] // 2, 1), pl.ds(at, 2 * LANES)], first_block + block)
         out = lax.dot_general(terms[:, pl.ds(at, 2 * LANES)], selector, NT, preferred_element_type=jnp.float32)
         path[block] = -(out[0:8] + out[8:16] + out[16:24])
         return carry
@@ -388,26 +388,25 @@
     return call(product_kernel, shape, in_specs=[VMEM] * 6, out_specs=VMEM, limit=WHOLE)(values, coupling, rhs0.T, rhs1.T, rhs2, rhs3)
 
 
-def first_kernel(depth, groups, scalars, both, index, *refs):
-    count = sum(groups)
-    parts, (send, terms, *packs), (path, ready, done, *stages) = refs[:count], refs[count : -3 - len(groups)], refs[-3 - len(groups) :]
+def stage_in(parts, stages, groups, ready):
     copies = []
-    for pack, size in zip(stages, groups):
+    for stage, size in zip(stages, groups):
         column = 0
         for part in parts[:size]:
             width = part.shape[1]
             for row in range(0, part.shape[0], 8):
-                target = pack.at[pl.ds(row, 8), pl.ds(column, width)]
-                copies.append(pltpu.make_async_copy(part.at[pl.ds(row, 8), :], target, ready.at[len(copies)]))
+                rows = pl.ds(row, 8)
+                copies.append(
+                    pltpu.make_async_copy(part.at[rows, :], stage.at[rows, pl.ds(column, width)], ready.at[len(copies)])
+                )
             column += width
         parts = parts[size:]
     for copy in copies:
         copy.start()
-    columns = both.shape[2] - LANES
-    half = pl.multiple_of(scalars[1] * 8, 8)
-    pieces = split3(both[0, pl.ds(half, 8), :columns] + both[1, pl.ds(half, 8), :columns])
-    terms[:, columns:] = jnp.zeros((32, terms.shape[1] - columns), jnp.bfloat16)
-    terms[:, :columns] = jnp.concatenate([*pieces, jnp.zeros_like(pieces[0])], axis=0)
+    return copies
+
+
+def stage_out(copies, stages, packs, done):
     for copy in copies:
         copy.wait()
     copies = []
@@ -417,7 +416,29 @@
             copies.append(pltpu.make_async_copy(stage.at[rows, :], pack.at[rows, :], done.at[len(copies)]))
     for copy in copies:
         copy.start()
-    expand(scalars, terms, index, sum(WIDTHS[:3]) // LANES, path)
+    return copies
+
+
+def pack_shapes(groups):
+    parts = [part for group in groups for part in group]
+    packs = [f32(group[0].shape[0], sum(part.shape[1] for part in group)) for group in groups]
+    scratch = [
+        pltpu.SemaphoreType.DMA((sum(part.shape[0] // 8 for part in parts),)),
+        pltpu.SemaphoreType.DMA((sum(pack.shape[0] // 8 for pack in packs),)),
+    ]
+    return parts, packs, scratch + [pltpu.VMEM(pack.shape, jnp.float32) for pack in packs]
+
+
+def first_kernel(depth, groups, scalars, windows, both, index, *refs):
+    count, number = sum(groups), len(groups)
+    parts, (send, terms, *packs), (path, ready, done, *stages) = refs[:count], refs[count : -3 - number], refs[-3 - number :]
+    copies = stage_in(parts, stages, groups, ready)
+    columns = both.shape[2] - LANES
+    half = pl.multiple_of(scalars[1] * 8, 8)
+    pieces = split3(both[0, pl.ds(half, 8), :columns] + both[1, pl.ds(half, 8), :columns])
+    terms[...] = jnp.concatenate([*pieces, jnp.zeros_like(pieces[0])], axis=0)
+    expand(scalars, windows, terms, index, sum(WIDTHS[:3]) // LANES, path)
+    copies = stage_out(copies, stages, packs, done)
     add_own(scalars, both, depth, (3,), path)
     for dest in range(X):
         for other in range(depth):
@@ -426,50 +447,50 @@
         copy.wait()
 
 
-def first(both, index, scalars, depth, groups):
+def first(both, index, scalars, windows, depth, groups):
     columns = both.shape[2] - LANES
-    parts = [part for group in groups for part in group]
-    packs = [f32(group[0].shape[0], sum(part.shape[1] for part in group)) for group in groups]
-    count = sum(part.shape[0] // 8 for part in parts)
+    parts, packs, scratch = pack_shapes(groups)
     outs = call(
         functools.partial(first_kernel, depth, [len(group) for group in groups]),
-        (f32(X * depth, 8, LANES), jax.ShapeDtypeStruct((32, columns + 2 * LANES), jnp.bfloat16), *packs),
-        in_specs=[SMEM, VMEM, VMEM] + [HBM] * len(parts),
+        (f32(X * depth, 8, LANES), jax.ShapeDtypeStruct((32, columns), jnp.bfloat16), *packs),
+        in_specs=[SMEM, SMEM, VMEM, VMEM] + [HBM] * len(parts),
         out_specs=(VMEM, VMEM) + (HBM,) * len(packs),
-        scratch_shapes=[
-            pltpu.VMEM((WIDTHS[3] // LANES, 8, LANES), jnp.float32),
-            pltpu.SemaphoreType.DMA((count,)),
-            pltpu.SemaphoreType.DMA((sum(pack.shape[0] // 8 for pack in packs),)),
-        ]
-        + [pltpu.VMEM(pack.shape, jnp.float32) for pack in packs],
+        scratch_shapes=[pltpu.VMEM((WIDTHS[3] // LANES, 8, LANES), jnp.float32)] + scratch,
         limit=WHOLE,
-    )(scalars, both, index, *parts)
+    )(scalars, windows, both, index, *parts)
     return outs[0], outs[1], outs[2:]
 
 
-def upper_kernel(depth, scalars, both, terms, index, path):
-    expand(scalars, terms, index, 0, path)
+def upper_kernel(depth, groups, scalars, windows, both, terms, index, *refs):
+    count, number = sum(groups), len(groups)
+    parts, (path, *packs), (ready, done, *stages) = refs[:count], refs[count : -2 - number], refs[-2 - number :]
+    copies = stage_out(stage_in(parts, stages, groups, ready), stages, packs, done)
+    expand(scalars, windows, terms, index, 0, path)
     add_own(scalars, both, depth, (0, 1, 2), path)
-
-
-def upper_path(both, terms, index, scalars, depth):
+    for copy in copies:
+        copy.wait()
+
+
+def upper_path(both, terms, index, scalars, windows, depth, groups):
     blocks = sum(WIDTHS[:3]) // LANES
-    return call(
-        functools.partial(upper_kernel, depth),
-        f32(blocks, 8, LANES),
-        in_specs=[SMEM, VMEM, VMEM, VMEM],
-        out_specs=VMEM,
+    parts, packs, scratch = pack_shapes(groups)
+    outs = call(
+        functools.partial(upper_kernel, depth, [len(group) for group in groups]),
+        (f32(blocks, 8, LANES), *packs),
+        in_specs=[SMEM, SMEM, VMEM, VMEM, VMEM] + [HBM] * len(parts),
+        out_specs=(VMEM,) + (HBM,) * len(packs),
+        scratch_shapes=scratch,
         cost_estimate=cost(blocks * LANES * LANES),
-    )(scalars, both, terms, index)
-
-
-def pick(scalars, index, terms, first_block, blocks, chosen):
-    total = sum(WIDTHS) // LANES
-
+        limit=STREAM,
+    )(scalars, windows, both, terms, index, *parts)
+    return outs[0], outs[1:]
+
+
+def pick(scalars, windows, index, terms, first_block, blocks, chosen):
     def one(block, carry):
         for half in range(2):
-            at = pl.multiple_of(scalars[8 + half * total + first_block + block] * LANES, LANES)
-            selector = one_hot(index[half : half + 1, pl.ds(at, 2 * LANES)], first_block + block)
+            at = pl.multiple_of(windows[half, first_block + block] * LANES, LANES)
+            selector = one_hot(index[pl.ds(scalars[7] * 2 + half, 1), pl.ds(at, 2 * LANES)], first_block + block)
             out = lax.dot_general(
                 terms[block].astype(jnp.bfloat16), selector, NN, preferred_element_type=jnp.float32
             )
@@ -485,72 +506,76 @@
     terms[...] = jnp.concatenate([*pieces, jnp.zeros_like(pieces[0])], axis=1).astype(jnp.float32)
 
 
-def pick_kernel(first_block, scalars, x, index, chosen, terms):
+def pick_kernel(first_block, scalars, windows, x, index, chosen, terms):
     store_terms(x, terms)
     chosen[...] = jnp.zeros_like(chosen)
-    pick(scalars, index, terms, first_block, x.shape[0] // PAIR, chosen)
-
-
-def picked(x, index, scalars, first_block):
+    pick(scalars, windows, index, terms, first_block, x.shape[0] // PAIR, chosen)
+
+
+def picked(x, index, scalars, windows, first_block):
     blocks = x.shape[0] // PAIR
     return call(
         functools.partial(pick_kernel, first_block),
         f32(2, 8, index.shape[1]),
-        in_specs=[SMEM, VMEM, VMEM],
+        in_specs=[SMEM, SMEM, VMEM, VMEM],
         out_specs=VMEM,
         scratch_shapes=[pltpu.VMEM((blocks, 8, LANES), jnp.float32)],
         cost_estimate=cost(blocks * 2 * LANES * LANES),
-    )(scalars, x, index)
-
-
-def last_kernel(columns, counts, scalars, received, x0, x1, x2, coupling, index, chosen0, chosen1, chosen2, send, x3, terms, chosen):
+    )(scalars, windows, x, index)
+
+
+def last_kernel(counts, scalars, windows, received, x0, x1, x2, coupling, index, chosen0, chosen1, chosen2, send, x3, terms, chosen):
     x3[...] = jnp.sum(received[...], axis=0)
     store_terms(x3, terms)
     chosen[...] = chosen0[...] + chosen1[...] + chosen2[...]
-    pick(scalars, index, terms, sum(counts[:3]), counts[3], chosen)
-    rows = coupling.shape[0] // 2
+    pick(scalars, windows, index, terms, sum(counts[:3]), counts[3], chosen)
+    rows, columns = coupling.shape[0] // 2, coupling.shape[1]
+    lane = lax.broadcasted_iota(jnp.int32, (CHUNK, LANES), 1)
     handed = []
     for half in range(2):
-        value = chosen[half, 0:2, :columns] + chosen[half, 2:4, :columns] + chosen[half, 4:6, :columns]
-        handed.append(
-            lax.dot_general(
-                value,
-                coupling[half * rows : (half + 1) * rows, :],
-                NT,
-                precision=lax.Precision.HIGHEST,
-                preferred_element_type=jnp.float32,
-            )
-        )
+        chosen[half, 0:2, :] = chosen[half, 0:2, :] + chosen[half, 2:4, :] + chosen[half, 4:6, :]
+        columns_of = []
+        for chunk in range(rows // CHUNK):
+            at = half * rows + chunk * CHUNK
+            sums = [[None, None] for _ in range(PAIR)]
+            for block in range(columns // LANES):
+                place = slice(block * LANES, (block + 1) * LANES)
+                tile = coupling[at : at + CHUNK, place]
+                for s in range(PAIR):
+                    part, old = tile * chosen[half, s : s + 1, place], sums[s][block % 2]
+                    sums[s][block % 2] = part if old is None else old + part
+            totals = [jnp.sum(value[0] + value[1], axis=1, keepdims=True) for value in sums]
+            columns_of.append(jnp.where(lane == 0, totals[0], jnp.where(lane == 1, totals[1], 0.0)))
+        handed.append(jnp.transpose(jnp.concatenate(columns_of, axis=0))[0:PAIR, :])
     send[...] = jnp.zeros_like(send)
     for dest in range(XC):
         core, x = dest // X, dest % X
         for level, ref in enumerate((x0, x1, x2, x3)):
             block = x if level < 2 else x * 2 + core
             if level < 3:
-                block = block + scalars[level] * (counts[level] // (Y // 2**level))
+                block = block + scalars[3 + level] * (counts[level] // (Y // 2**level))
             send[dest, 2 * level : 2 * level + 2, :] = ref[pl.ds(block * 2, 2), :]
         send[dest, 8:10, :] = handed[x // 2]
 
 
-def last(received, known, chosen, coupling, index, scalars):
-    columns = coupling.shape[1]
+def last(received, known, chosen, coupling, index, scalars, windows):
     counts = [width // LANES for width in WIDTHS]
     return call(
-        functools.partial(last_kernel, columns, counts),
+        functools.partial(last_kernel, counts),
         f32(XC, 16, LANES),
-        in_specs=[SMEM] + [VMEM] * 9,
+        in_specs=[SMEM, SMEM] + [VMEM] * 9,
         out_specs=VMEM,
         scratch_shapes=[
             pltpu.VMEM(received.shape[1:], jnp.float32),
             pltpu.VMEM((counts[3], 8, LANES), jnp.float32),
-            pltpu.VMEM((2, 8, columns + 2 * LANES), jnp.float32),
+            pltpu.VMEM((2, 8, coupling.shape[1]), jnp.float32),
         ],
-    )(scalars, received, *known, coupling, index, *chosen)
+    )(scalars, windows, received, *known, coupling, index, *chosen)
 
 
 def finish_kernel(scalars, received, values, out0, out1, out2, out3, handed):
     z, core = scalars[0], scalars[1]
-    offsets = (core * 64 + z * 8, core * 64 + z * 8, z * 16, z * 16, scalars[2] * values.shape[1])
+    offsets = (core * 64 + z * 8, core * 64 + z * 8, z * 16, z * 16, (lax.rem(scalars[2], 2) * 2 + core) * values.shape[1])
     for level, ref in enumerate((out0, out1, out2, out3, handed)):
         value = jnp.concatenate([received[source, 2 * level : 2 * level + 2, :] for source in range(XC)], axis=0)
         moved = pltpu.roll(value, lax.rem(LANES - offsets[level], LANES), 1)
@@ -597,33 +622,27 @@
     def gathered(whole):
         return lax.all_gather(whole, ("x", "c"), axis=0, tiled=True)
 
+    both, coupled_rows = lax.optimization_barrier((both, coupled_rows))
+    edges = jnp.arange(blocks, dtype=jnp.int32) * LANES
     both_indices = lax.dynamic_slice_in_dim(coupled_rows, y * 2, 2, 0)
-    edges = jnp.arange(blocks, dtype=jnp.int32) * LANES
     windows = jnp.sum((both_indices[:, None, :] < edges[None, :, None]).astype(jnp.int32), axis=2) // LANES
-    both_indices = jnp.pad(both_indices, ((0, 0), (0, 2 * LANES)), constant_values=-1)
-    own_windows = lax.dynamic_index_in_dim(windows, x // 2, 0, keepdims=False)
-    own_indices = lax.dynamic_slice_in_dim(both_indices, x // 2, 1, 0)
-
-    def scalars(head, *tails):
-        head = jnp.stack([jnp.asarray(value, jnp.int32) for value in head] + [jnp.int32(0)] * (8 - len(head)))
-        return jnp.concatenate([head, *tails])
-
-    places = scalars([z, c, x, y, y % 4, y % 2, (y % 2) * depth + z], own_windows)
-    groups = ((inv_level3, cross_level3), (inv_level2, cross_level2), (inv_level1, cross_level1, inv_root))
-    send, terms, (own3, pack2, pack1) = first(both, own_indices, places, depth, groups)
+    windows = jnp.minimum(windows, coupled_rows.shape[1] // LANES - 2)
+
+    places = jnp.stack([z, c, x, y, y % 4, y % 2, (y % 2) * depth + z, y])
+    send, terms, (pack2,) = first(both, coupled_rows, places, windows, depth, ((inv_level2, cross_level2),))
     matrix2 = gathered(pack2)
+    groups = ((inv_level3, cross_level3), (inv_level1, cross_level1, inv_root))
+    path, (own3, pack1) = upper_path(both, terms, coupled_rows, places, windows, depth, groups)
+    received, path, own3, pack1 = lax.optimization_barrier((exchange(send, ("x", "z")), path, own3, pack1))
+    other3 = lax.ppermute(own3, "c", [(0, 1), (1, 0)])
     matrix1 = gathered(pack1)
-    path = upper_path(both, terms, own_indices, places, depth)
-    received, other3, path = lax.optimization_barrier(
-        (exchange(send, ("x", "z")), lax.ppermute(own3, "c", [(0, 1), (1, 0)]), path)
-    )
     target3 = exchange(sum_and_copy(received, depth), ("z",))
     send = lowest(target3, own3, other3, path, counts[3], sum(counts[:3]), 2 * depth)
     send, own3, coupling = lax.optimization_barrier((send, own3, coupling))
     matrix3 = gathered(own3)
     all_coupling = gathered(coupling)
     received = sum_and_copy(exchange(send, ("y0", "x", "z")), 2 * depth)
-    target2, half2 = lax.optimization_barrier((exchange(received, ("y0", "z")), fetched(matrix2, 2)))
+    target2, half2 = lax.optimization_barrier((exchange(received, ("y0", "z")), fetched(matrix2, 0.5)))
     solved2, send, rest = forward(
         target2, (half2, matrix2), received[0], places, counts[2], counts[0] + counts[1], counts[0], 4 * depth, 6
     )
@@ -636,24 +655,22 @@
 
     target = sum_root(send).reshape(-1, LANES)
     received = sum_root(root(target, matrix1, WIDTHS[1] + WIDTHS[0], Y)).reshape(1, -1, LANES)
-    heads = scalars([y, y % 4, y % 2], windows.reshape(-1))
     send, x0 = backward(received, (matrix1,), solved1, [], places, counts[1], 4 * depth)
     x0, matrix2 = lax.optimization_barrier((x0, matrix2))
     received, chosen0, half2 = lax.optimization_barrier(
-        (exchange(send, ("y1", "y0", "z")), picked(x0, both_indices, heads, 0), fetched(matrix2, 2))
+        (exchange(send, ("y1", "y0", "z")), picked(x0, coupled_rows, places, windows, 0), fetched(matrix2, 0.5))
     )
     send, x1 = backward(received, (half2, matrix2), solved2, [x0], places, counts[2], 2 * depth)
     received, chosen1, half3 = lax.optimization_barrier(
-        (exchange(send, ("y0", "z")), picked(x1, both_indices, heads, counts[0]), fetched(matrix3, 2))
+        (exchange(send, ("y0", "z")), picked(x1, coupled_rows, places, windows, counts[0]), fetched(matrix3, 0.5))
     )
     send, x2 = backward(received, (half3, matrix3), target3, [x0, x1], places, counts[3], depth)
     received, chosen2, all_coupling = lax.optimization_barrier(
-        (exchange(send, ("z",)), picked(x2, both_indices, heads, counts[0] + counts[1]), fetched(all_coupling))
+        (exchange(send, ("z",)), picked(x2, coupled_rows, places, windows, counts[0] + counts[1]), fetched(all_coupling))
     )
-    send = last(received, [x0, x1, x2], [chosen0, chosen1, chosen2], all_coupling, both_indices, heads)
+    send = last(received, [x0, x1, x2], [chosen0, chosen1, chosen2], all_coupling, coupled_rows, places, windows)
     received = exchange(send, ("c", "x"))
-    ends = scalars([z, c, (x % 2) * 2 + c])
-    return finish(received, subtree_values, ends, [part.shape[1] for part in rhs_parts])
+    return finish(received, subtree_values, places, [part.shape[1] for part in rhs_parts])
 
 
 def solution(mesh):

time: 244 us -> 247 us (1.012)
  blocking collectives: 93.9 us -> 113 us
  starting transfers between devices: 43.5 us -> 34 us
  waiting for transfers between devices: 35.9 us -> 28.1 us
    all_to_all x6 -> x7, blocking collectives: 83.6 us -> 102 us  [exchange(): return lax.all_to_all(flat, axes, 0, 0, tiled=True).reshape(operand.shape)]
    all_to_all x7 -> x6, starting transfers between devices: 41.3 us -> 29.8 us  [exchange(): return lax.all_to_all(flat, axes, 0, 0, tiled=True).reshape(operand.shape)]
    all_to_all x7 -> x6, waiting for transfers between devices: 32.2 us -> 27.4 us  [exchange(): return lax.all_to_all(flat, axes, 0, 0, tiled=True).reshape(operand.shape)]
    unnamed x24 -> x36, local copies, waits for them, and re-layouts: 11.9 us -> 13.7 us
  transfers between devices with their start and end apart: 12 -> 11, of which waited for: 8 -> 6; matrix products, arithmetic and copies ran while one was open for 0% -> 0% of each run, Pallas kernels for 12% -> 13%
where the time goes in v8:
time: 247 us; the launch traced here: 245 us
  blocking collectives  113 us (46%)
  Pallas kernels  39.8 us (16%)
  starting transfers between devices  34 us (14%)
  waiting for transfers between devices  28.1 us (11%)
  local copies, waits for them, and re-layouts  15.9 us (6%)
  between operations  14.1 us (6%)
    all_to_all x7, blocking collectives, exchange(): return lax.all_to_all(flat, axes, 0, 0, tiled=True).reshape(operand.shape)  102 us
    all_to_all x6, starting transfers between devices, exchange(): return lax.all_to_all(flat, axes, 0, 0, tiled=True).reshape(operand.shape)  29.8 us
    all_to_all x6, waiting for transfers between devices, exchange(): return lax.all_to_all(flat, axes, 0, 0, tiled=True).reshape(operand.shape)  27.4 us
    unnamed x36, local copies, waits for them, and re-layouts  13.7 us
    all_gather x1, blocking collectives, body(): lax.all_gather(own_product(subtree_values, coupling, rhs_parts), 'c', axi...  10.3 us
    pallas_call x3, Pallas kernels, backward(): call(functools.partial(backward_kernel, blocks, counts, len(matrices)), (...  8.26 us
  transfers between devices with their start and end apart: 11, of which 6 were waited for; matrix products, arithmetic and copies ran while one was open for 0% of the time, Pallas kernels for 13%

profile of v8, /device:TPU:1, one launch (start us, length us, event | category | flops | bytes accessed | tf_op | source)
XLA Modules:
  0.0 245.4 jit_solution(10643620885044818138)
XLA Ops:
  7.2 0.0 all-gather.6.cloned.1.call-start
  7.3 2.1 shard_map.173
  9.4 10.3 %all-gather = f32[32,2176]{1,0:T(8,128)} all-gather(f32[16,2176]{1,0:T(8,128)} %shard_map.173), channel_id=2, replica_groups=mesh['y2'=2,'y1'=2,'y0'=2,'x'=4,'c'=2,'z'=8] {'c'}, dimensions={0}, use_global_device_ids=true | all-gather | bytes 417792 | tf_op jit(solution)/shard_map/all_gather | solution.py:620
  19.7 0.8 constant_dynamic-slice_fusion
  20.5 0.3 convert_reduce_fusion
  20.8 0.6 fusion.windows
  21.4 0.7 stack.32.scalars
  22.0 3.7 %shard_map.174 = (f32[32,8,128]{2,1,0:T(8,128)}, bf16[32,2048]{1,0:T(8,128)(2,1)}, f32[16,8192]{1,0:T(8,128)}) custom-call(s32[8]{0:T(128)} %stack.32.scalars, s32[2,72]{1,0:T(2,128)} %fusion.windows, f32[2,16,2176]{2,1,0:T(8,128)} %bitcast.18, s32[16,2048]{1,0:T(8,128)} %index.5, f32[16,2048]{1,0:T(8,128)} %refs_0_.2, f32[16,6144]{1,0:T(8,128)} %refs_1_.2), custom_call_target="tpu_custom_call" | custom-call | tf_op jit(solution)/shard_map/pallas_call | solution.py:453
  25.7 7.5 %all-to-all-start = ((f32[32,8,128]{2,1,0:T(8,128)}), f32[32,8,128]{2,1,0:T(8,128)S(1)}, u32[]{:S(2)}, u32[]{:S(2)}) async-start(f32[32,8,128]{2,1,0:T(8,128)} %get-tuple-element.53), calls=%async_computation | async-start | bytes 262144 | tf_op jit(solution)/shard_map/all_to_all | solution.py:51
  33.3 0.0 all-gather.8.cloned.1.call-start
  33.4 0.9 copy-done.5
  34.3 0.9 copy-done.10
  35.3 0.7 copy-done.11
  35.9 0.7 copy-done.15
  36.6 4.8 %shard_map.175 = (f32[64,8,128]{2,1,0:T(8,128)S(1)}, f32[16,9216]{1,0:T(8,128)}, f32[8,10240]{1,0:T(8,128)}) custom-call(s32[8]{0:T(128)S(1)} %copy-done.11, s32[2,72]{1,0:T(2,128)S(1)} %copy-done.15, f32[2,16,2176]{2,1,0:T(8,128)S(1)} %bitcast.19, bf16[32,2048]{1,0:T(8,128)(2,1)S(1)} %copy-done.10, s32[16,2048]{1,0:T(8,128)S(1)} %copy-done.3, ...), custom_call_target="tpu_custom_call" | custom-call | flops 8388608 | bytes 4194304 | tf_op jit(solution)/shard_map/pallas_call | solution.py:477
  41.4 1.1 all-to-all-done.received
  42.5 0.0 all-gather.10.cloned.1.call-start
  42.5 4.1 %collective-permute-start = (f32[16,9216]{1,0:T(8,128)}, f32[16,9216]{1,0:T(8,128)S(1)}, u32[]{:S(2)}, u32[]{:S(2)}) collective-permute-start(f32[16,9216]{1,0:T(8,128)} %get-tuple-element.81.own), channel_id=1, source_target_pairs={{0,8},{8,0},{1,9},{9,1},{2,10},{10,2},{3,11},{11,3},{4,12},{12,4},... | collective-permute-start | bytes 1769480 | tf_op jit(solution)/shard_map/ppermute | solution.py:637
  46.7 10.5 %all_to_all.86.received.solved = f32[8,8,128]{2,1,0:T(8,128)S(1)} all-to-all(f32[8,8,128]{2,1,0:T(8,128)S(1)} %shard_map.176), channel_id=1, replica_groups=mesh['y2'=2,'y1'=2,'y0'=2,'x'=4,'c'=2,'z'=8] {'z'}, dimensions={0} | all-to-all | bytes 65536 | tf_op jit(solution)/shard_map/all_to_all | solution.py:51
  57.2 2.3 shard_map.177
  59.6 17.1 %all_to_all.87.received = f32[64,8,128]{2,1,0:T(8,128)S(1)} all-to-all(f32[64,8,128]{2,1,0:T(8,128)S(1)} %shard_map.177), channel_id=1, replica_groups=mesh['y2'=2,'y1'=2,'y0'=2,'x'=4,'c'=2,'z'=8] {'y0','x','z'}, dimensions={0} | all-to-all | bytes 524288 | tf_op jit(solution)/shard_map/all_to_all | solution.py:51
  76.7 0.7 shard_map.178
  77.4 5.2 %all-to-all-start.3 = ((f32[16,8,128]{2,1,0:T(8,128)}), f32[16,8,128]{2,1,0:T(8,128)S(1)}, u32[]{:S(2)}, u32[]{:S(2)}) async-start(f32[16,8,128]{2,1,0:T(8,128)} %shard_map.178), calls=%async_computation.3 | async-start | bytes 131072 | tf_op jit(solution)/shard_map/all_to_all | solution.py:51
  82.6 0.7 slice_bitcast_fusion.rest_in
  83.3 2.2 copy-done
  85.5 0.2 shard_map.179.refs_0_
  85.7 4.2 %all-to-all-done.3.received = f32[16,8,128]{2,1,0:T(8,128)S(1)} async-done(((f32[16,8,128]{2,1,0:T(8,128)}), f32[16,8,128]{2,1,0:T(8,128)S(1)}, u32[]{:S(2)}, u32[]{:S(2)}) %all-to-all-start.3) | async-done | bytes 65568 | tf_op jit(solution)/shard_map/all_to_all | solution.py:51
  89.9 3.3 %shard_map.180 = (f32[2,128,128]{2,1,0:T(8,128)S(1)}, f32[32,32,128]{2,1,0:T(8,128)}, f32[96,128]{1,0:T(8,128)S(1)}) custom-call(s32[8]{0:T(128)S(1)} %copy-done.12, f32[16,8,128]{2,1,0:T(8,128)S(1)} %all-to-all-done.3.received, f32[8,128]{1,0:T(8,128)S(1)} %slice_bitcast_fusion.rest_in, f32[64,8192]{1,0:T(8,128)S(1)} %shard_map.179.refs_0_, ...), custom_call_target="tpu_custom_call" | custom-call | flops 8388608 | bytes 4194304 | tf_op jit(solution)/shard_map/pallas_call | solution.py:186
  93.3 6.0 %all-to-all-start.4 = ((f32[32,32,128]{2,1,0:T(8,128)}), f32[32,32,128]{2,1,0:T(8,128)S(1)}, u32[]{:S(2)}, u32[]{:S(2)}) async-start(f32[32,32,128]{2,1,0:T(8,128)} %get-tuple-element.65), calls=%async_computation.4 | async-start | bytes 1048576 | tf_op jit(solution)/shard_map/all_to_all | solution.py:51
  99.3 0.0 all-gather.12.cloned.1.call-start
  99.4 0.5 all-gather.12.cloned.1.call-update
  99.9 1.7 copy-done.4
  101.7 0.9 shard_map.181.refs_0_.matrix
  102.6 10.4 %all-to-all-done.4.received = f32[32,32,128]{2,1,0:T(8,128)S(1)} async-done(((f32[32,32,128]{2,1,0:T(8,128)}), f32[32,32,128]{2,1,0:T(8,128)S(1)}, u32[]{:S(2)}, u32[]{:S(2)}) %all-to-all-start.4) | async-done | bytes 524320 | tf_op jit(solution)/shard_map/all_to_all | solution.py:51
  113.0 1.5 shard_map.182
  114.5 21.8 %all_to_all.88.received = f32[64,8,128]{2,1,0:T(8,128)S(1)} all-to-all(f32[64,8,128]{2,1,0:T(8,128)S(1)} %bitcast.21), channel_id=1, replica_groups=mesh['y2'=2,'y1'=2,'y0'=2,'x'=4,'c'=2,'z'=8] {'y2','y1','y0','z'}, dimensions={0} | all-to-all | bytes 524288 | tf_op jit(solution)/shard_map/all_to_all | solution.py:51
  136.3 0.1 shard_map.183
  136.4 9.5 %all_to_all.89 = f32[8,8,128]{2,1,0:T(8,128)S(1)} all-to-all(f32[8,8,128]{2,1,0:T(8,128)S(1)} %shard_map.183), channel_id=1, replica_groups=mesh['y2'=2,'y1'=2,'y0'=2,'x'=4,'c'=2,'z'=8] {'z'}, dimensions={0} | all-to-all | bytes 65536 | tf_op jit(solution)/shard_map/all_to_all | solution.py:51
  145.8 0.4 shard_map.184
  146.2 16.4 %all_to_all.90.received = f32[64,8,128]{2,1,0:T(8,128)S(1)} all-to-all(f32[64,8,128]{2,1,0:T(8,128)S(1)} %bitcast.20), channel_id=1, replica_groups=mesh['y2'=2,'y1'=2,'y0'=2,'x'=4,'c'=2,'z'=8] {'y2','y1','y0','z'}, dimensions={0} | all-to-all | bytes 524288 | tf_op jit(solution)/shard_map/all_to_all | solution.py:51
  162.6 0.1 shard_map.185
  162.7 9.4 %all_to_all.91 = f32[8,8,128]{2,1,0:T(8,128)S(1)} all-to-all(f32[8,8,128]{2,1,0:T(8,128)S(1)} %shard_map.185), channel_id=1, replica_groups=mesh['y2'=2,'y1'=2,'y0'=2,'x'=4,'c'=2,'z'=8] {'z'}, dimensions={0} | all-to-all | bytes 65536 | tf_op jit(solution)/shard_map/all_to_all | solution.py:51
  172.1 1.8 shard_map.186
  173.9 3.9 %all-to-all-start.9 = ((f32[32,32,128]{2,1,0:T(8,128)}), f32[32,32,128]{2,1,0:T(8,128)S(1)}, u32[]{:S(2)}, u32[]{:S(2)}) async-start(f32[32,32,128]{2,1,0:T(8,128)} %get-tuple-element.72), calls=%async_computation.9 | async-start | bytes 1048576 | tf_op jit(solution)/shard_map/all_to_all | solution.py:51
  177.8 2.2 copy-done.1
  180.0 0.2 shard_map.188.refs_0_
  180.2 0.4 copy-done.16
  180.6 2.2 shard_map.187.chosen0
  182.8 7.4 %all-to-all-done.9.received = f32[32,32,128]{2,1,0:T(8,128)S(1)} async-done(((f32[32,32,128]{2,1,0:T(8,128)}), f32[32,32,128]{2,1,0:T(8,128)S(1)}, u32[]{:S(2)}, u32[]{:S(2)}) %all-to-all-start.9) | async-done | bytes 524320 | tf_op jit(solution)/shard_map/all_to_all | solution.py:51
  190.2 3.3 %shard_map.189 = (f32[16,32,128]{2,1,0:T(8,128)}, f32[32,128]{1,0:T(8,128)S(1)}) custom-call(s32[8]{0:T(128)S(1)} %copy-done.12, f32[32,32,128]{2,1,0:T(8,128)S(1)} %all-to-all-done.9.received, f32[2,128,128]{2,1,0:T(8,128)S(1)} %get-tuple-element.77.solved, f32[64,8192]{1,0:T(8,128)S(1)} %shard_map.188.refs_0_, ...), custom_call_target="tpu_custom_call" | custom-call | flops 8388608 | bytes 4194304 | tf_op jit(solution)/shard_map/pallas_call | solution.py:288
  193.5 3.7 %all-to-all-start.10 = ((f32[16,32,128]{2,1,0:T(8,128)}), f32[16,32,128]{2,1,0:T(8,128)S(1)}, u32[]{:S(2)}, u32[]{:S(2)}) async-start(f32[16,32,128]{2,1,0:T(8,128)} %get-tuple-element.79), calls=%async_computation.10 | async-start | bytes 524288 | tf_op jit(solution)/shard_map/all_to_all | solution.py:51
  197.3 2.3 copy-done.2
  199.6 0.6 shard_map.191.refs_0_
  200.2 1.4 shard_map.190.chosen1
  201.6 3.2 %all-to-all-done.10.received = f32[16,32,128]{2,1,0:T(8,128)S(1)} async-done(((f32[16,32,128]{2,1,0:T(8,128)}), f32[16,32,128]{2,1,0:T(8,128)S(1)}, u32[]{:S(2)}, u32[]{:S(2)}) %all-to-all-start.10) | async-done | bytes 262176 | tf_op jit(solution)/shard_map/all_to_all | solution.py:51
  204.8 3.2 %shard_map.192 = (f32[8,16,128]{2,1,0:T(8,128)}, f32[32,128]{1,0:T(8,128)S(1)}) custom-call(s32[8]{0:T(128)S(1)} %copy-done.12, f32[16,32,128]{2,1,0:T(8,128)S(1)} %all-to-all-done.10.received, f32[8,8,128]{2,1,0:T(8,128)S(1)} %all_to_all.86.received.solved, f32[64,9216]{1,0:T(8,128)S(1)} %shard_map.191.refs_0_, ...), custom_call_target="tpu_custom_call" | custom-call | flops 9437184 | bytes 4718592 | tf_op jit(solution)/shard_map/pallas_call | solution.py:288
  208.0 3.4 %all-to-all-start.11 = ((f32[8,16,128]{2,1,0:T(8,128)}), f32[8,16,128]{2,1,0:T(8,128)S(1)}, u32[]{:S(2)}, u32[]{:S(2)}) async-start(f32[8,16,128]{2,1,0:T(8,128)} %get-tuple-element.84), calls=%async_computation.11 | async-start | bytes 131072 | tf_op jit(solution)/shard_map/all_to_all | solution.py:51
  211.4 1.6 copy-done.6
  213.0 3.0 %shard_map.194.coupling = f32[256,2048]{1,0:T(8,128)S(1)} custom-call(f32[256,2048]{1,0:T(8,128)S(1)} %copy-done.6), custom_call_target="tpu_custom_call" | custom-call | flops 8388608 | bytes 4194304 | tf_op jit(solution)/shard_map/pallas_call | solution.py:141
  216.0 1.4 shard_map.193.chosen2
  217.4 1.1 all-to-all-done.11.received
  218.5 1.5 shard_map.195
  220.0 17.6 %all_to_all.92.received = f32[8,16,128]{2,1,0:T(8,128)S(1)} all-to-all(f32[8,16,128]{2,1,0:T(8,128)S(1)} %shard_map.195), channel_id=1, replica_groups=mesh['y2'=2,'y1'=2,'y0'=2,'x'=4,'c'=2,'z'=8] {'c','x'}, dimensions={0} | all-to-all | bytes 131072 | tf_op jit(solution)/shard_map/all_to_all | solution.py:51
  237.5 1.3 shard_map.196
  (36 shorter events, 0.2 us)
Async XLA Ops:
  7.2 26.2 %copy-start.3 = (s32[16,2048]{1,0:T(8,128)S(1)}, s32[16,2048]{1,0:T(8,128)}, u32[]{:S(2)}) copy-start(s32[16,2048]{1,0:T(8,128)} %index.5) | copy-start | bytes 393220
  7.2 26.2 %copy-start.9 = (f32[8,4096]{1,0:T(8,128)S(1)}, f32[8,4096]{1,0:T(8,128)}, u32[]{:S(2)}) copy-start(f32[8,4096]{1,0:T(8,128)} %refs_4_.1) | copy-start | bytes 393220
  7.2 26.2 %copy-start.14 = (f32[8,2048]{1,0:T(8,128)S(1)}, f32[8,2048]{1,0:T(8,128)}, u32[]{:S(2)}) copy-start(f32[8,2048]{1,0:T(8,128)} %refs_2_.1) | copy-start | bytes 196612
  7.2 26.2 %copy-start.13 = (f32[16,1024]{1,0:T(8,128)S(1)}, f32[16,1024]{1,0:T(8,128)}, u32[]{:S(2)}) copy-start(f32[16,1024]{1,0:T(8,128)} %refs_0_.3) | copy-start | bytes 196612
  7.2 26.2 %copy-start.8 = (f32[8,4096]{1,0:T(8,128)S(1)}, f32[8,4096]{1,0:T(8,128)}, u32[]{:S(2)}) copy-start(f32[8,4096]{1,0:T(8,128)} %refs_3_.1) | copy-start | bytes 393220
  7.2 26.2 %copy-start.7 = (f32[16,8192]{1,0:T(8,128)S(1)}, f32[16,8192]{1,0:T(8,128)}, u32[]{:S(2)}) copy-start(f32[16,8192]{1,0:T(8,128)} %refs_1_.3) | copy-start | bytes 1572868
  7.2 76.0 %all-gather.6.cloned.1.call-start = ((), (), s32[]{:S(2)}) async-start(), calls=%async_computation.13 | async-start | bytes 4718592 | tf_op jit(solution)/shard_map/all_gather | solution.py:623
  25.7 16.7 %all-to-all-start = ((f32[32,8,128]{2,1,0:T(8,128)}), f32[32,8,128]{2,1,0:T(8,128)S(1)}, u32[]{:S(2)}, u32[]{:S(2)}) async-start(f32[32,8,128]{2,1,0:T(8,128)} %get-tuple-element.53), calls=%async_computation | async-start | bytes 262144 | tf_op jit(solution)/shard_map/all_to_all | solution.py:51
  33.3 66.6 %all-gather.8.cloned.1.call-start = ((), (), s32[]{:S(2)}) async-start(), calls=%async_computation.14 | async-start | bytes 2949120 | tf_op jit(solution)/shard_map/all_gather | solution.py:623
  33.4 1.0 copy-start.5
  34.3 0.9 copy-start.10
  35.3 0.7 copy-start.11
  35.9 0.7 copy-start.15
  42.5 154.8 %all-gather.10.cloned.1.call-start = ((), (), s32[]{:S(2)}) async-start(), calls=%async_computation.15 | async-start | bytes 5308416 | tf_op jit(solution)/shard_map/all_gather | solution.py:623
  42.5 14.7 %collective-permute-start = (f32[16,9216]{1,0:T(8,128)}, f32[16,9216]{1,0:T(8,128)S(1)}, u32[]{:S(2)}, u32[]{:S(2)}) collective-permute-start(f32[16,9216]{1,0:T(8,128)} %get-tuple-element.81.own), channel_id=1, source_target_pairs={{0,8},{8,0},{1,9},{9,1},{2,10},{10,2},{3,11},{11,3},{4,12},{12,4},... | collective-permute-start | bytes 1769480 | tf_op jit(solution)/shard_map/ppermute | solution.py:637
  77.4 12.6 %all-to-all-start.3 = ((f32[16,8,128]{2,1,0:T(8,128)}), f32[16,8,128]{2,1,0:T(8,128)S(1)}, u32[]{:S(2)}, u32[]{:S(2)}) async-start(f32[16,8,128]{2,1,0:T(8,128)} %shard_map.178), calls=%async_computation.3 | async-start | bytes 131072 | tf_op jit(solution)/shard_map/all_to_all | solution.py:51
  83.3 2.2 copy-start
  85.5 4.5 %copy-start.12 = (s32[8]{0:T(128)S(1)}, s32[8]{0:T(128)}, u32[]{:S(2)}) copy-start(s32[8]{0:T(128)} %stack.32.scalars) | copy-start | bytes 100
  93.3 19.7 %all-to-all-start.4 = ((f32[32,32,128]{2,1,0:T(8,128)}), f32[32,32,128]{2,1,0:T(8,128)S(1)}, u32[]{:S(2)}, u32[]{:S(2)}) async-start(f32[32,32,128]{2,1,0:T(8,128)} %get-tuple-element.65), calls=%async_computation.4 | async-start | bytes 1048576 | tf_op jit(solution)/shard_map/all_to_all | solution.py:51
  99.3 112.0 %all-gather.12.cloned.1.call-start = ((), (), s32[]{:S(2)}) async-start(), calls=%async_computation.16 | async-start | bytes 2359296 | tf_op jit(solution)/shard_map/all_gather | solution.py:623
  99.9 1.7 copy-start.4
  173.9 16.3 %all-to-all-start.9 = ((f32[32,32,128]{2,1,0:T(8,128)}), f32[32,32,128]{2,1,0:T(8,128)S(1)}, u32[]{:S(2)}, u32[]{:S(2)}) async-start(f32[32,32,128]{2,1,0:T(8,128)} %get-tuple-element.72), calls=%async_computation.9 | async-start | bytes 1048576 | tf_op jit(solution)/shard_map/all_to_all | solution.py:51
  177.8 2.2 copy-start.1
  180.0 0.7 copy-start.16
  193.5 11.3 %all-to-all-start.10 = ((f32[16,32,128]{2,1,0:T(8,128)}), f32[16,32,128]{2,1,0:T(8,128)S(1)}, u32[]{:S(2)}, u32[]{:S(2)}) async-start(f32[16,32,128]{2,1,0:T(8,128)} %get-tuple-element.79), calls=%async_computation.10 | async-start | bytes 524288 | tf_op jit(solution)/shard_map/all_to_all | solution.py:51
  197.3 2.3 copy-start.2
  208.0 10.5 %all-to-all-start.11 = ((f32[8,16,128]{2,1,0:T(8,128)}), f32[8,16,128]{2,1,0:T(8,128)S(1)}, u32[]{:S(2)}, u32[]{:S(2)}) async-start(f32[8,16,128]{2,1,0:T(8,128)} %get-tuple-element.84), calls=%async_computation.11 | async-start | bytes 131072 | tf_op jit(solution)/shard_map/all_to_all | solution.py:51
  211.4 1.6 copy-start.6
  216.0 21.5 %copy-start.17 = (f32[16,32]{1,0:T(8,128)S(1)}, f32[16,32]{1,0:T(8,128)}, u32[]{:S(2)}) copy-start(f32[16,32]{1,0:T(8,128)} %values.3) | copy-start | bytes 6148
Sparse Core Ops, SparseCore 0:
  25.9 36.7 all-gather.5
  64.8 31.3 all-gather.7
  98.4 40.2 all-gather.9
  140.6 30.5 all-gather.11

commit v9 on v8

--- a/solution.py
+++ b/solution.py
@@ -42,6 +42,22 @@
     return pl.CostEstimate(flops=8 * elements, bytes_accessed=4 * elements, transcendentals=0)
 
 
+def position(name):
+    if name == "y":
+        return (lax.axis_index("y2") * 2 + lax.axis_index("y1")) * 2 + lax.axis_index("y0")
+    if name == "y1":
+        return lax.axis_index("y1") * 2 + lax.axis_index("y0")
+    return lax.axis_index(name)
+
+
+def own_subtree():
+    return position("y") * 2 + position("x") // 2
+
+
+def window(counts, subtree, block, columns):
+    return pl.multiple_of(jnp.minimum(counts[subtree, block] // LANES, columns // LANES - 2) * LANES, LANES)
+
+
 def f32(*shape):
     return jax.ShapeDtypeStruct(shape, jnp.float32)
 
@@ -148,7 +164,7 @@
     )(matrix)
 
 
-def forward_kernel(blocks, upper, keep, extra, count, scalars, received, rest_in, *refs):
+def forward_kernel(blocks, upper, keep, extra, count, received, rest_in, *refs):
     matrices, (solved, send, rest, vector, total, *stream) = refs[:count], refs[count:]
     matrices, copies = begin(matrices, stream)
     if extra:
@@ -168,8 +184,9 @@
     whole = -jnp.sum(total[...], axis=1)
     if extra:
         rest[...] = whole
+        place = position("y0") * (blocks // 2) + position("z")
         for row in range(extra):
-            at = pl.ds(scalars[6] * extra + row, 1)
+            at = pl.ds(place * extra + row, 1)
             rest[at, :] = rest[at, :] + rest_in[2 + row : 3 + row, :]
         whole = rest[...]
     else:
@@ -179,20 +196,20 @@
         send[copy] = whole[2 * keep :, :]
 
 
-def forward(received, matrices, rest_in, scalars, blocks, upper, keep, copies, extra):
+def forward(received, matrices, rest_in, blocks, upper, keep, copies, extra):
     rows = matrices[-1].shape[0]
     streamed = len(matrices) > 1
     width = upper * LANES + blocks * LANES
     return call(
         functools.partial(forward_kernel, blocks, upper, keep, extra, len(matrices)),
         (f32(PAIR, rows, LANES), f32(copies, 2 * (upper - keep), LANES), f32(2 * upper, LANES)),
-        in_specs=[SMEM, VMEM, VMEM] + ([VMEM, HBM] if streamed else [VMEM]),
+        in_specs=[VMEM, VMEM] + ([VMEM, HBM] if streamed else [VMEM]),
         out_specs=(VMEM,) * 3,
         scratch_shapes=[pltpu.VMEM((2 * blocks, LANES), jnp.float32), pltpu.VMEM((2 * upper, 8, LANES), jnp.float32)]
         + stream_buffers(matrices, width),
         limit=STREAM if streamed else LIMIT,
         cost_estimate=cost(rows * width),
-    )(scalars, received, rest_in, *matrices)
+    )(received, rest_in, *matrices)
 
 
 def lowest_kernel(blocks, upper, received, own, other, path, send, total, buffer, ready):
@@ -251,7 +268,7 @@
     )(received, own, other, path)
 
 
-def backward_kernel(blocks, known_blocks, number, scalars, received, solved, *refs):
+def backward_kernel(blocks, known_blocks, number, received, solved, *refs):
     matrices, refs = refs[:number], refs[number:]
     known, (send, newest, total, vector, *stream) = refs[: len(known_blocks) - 1], refs[len(known_blocks) - 1 :]
     matrices, copies = begin(matrices, stream)
@@ -260,7 +277,7 @@
     again = solved.shape[2] == LANES and solved.shape[0] == blocks
     if again:
         for block in range(blocks):
-            vector[2 * block : 2 * block + 2, :] = solved[block, pl.ds(scalars[2] * 2, 2), :]
+            vector[2 * block : 2 * block + 2, :] = solved[block, pl.ds(position("x") * 2, 2), :]
 
     def step(matrix, rows, place):
         if again:
@@ -280,7 +297,7 @@
         send[copy] = whole
 
 
-def backward(received, matrices, solved, known, scalars, blocks, copies):
+def backward(received, matrices, solved, known, blocks, copies):
     rows = matrices[-1].shape[0]
     streamed = len(matrices) > 1
     counts = [array.shape[0] // PAIR for array in known] + [received.shape[1] // PAIR]
@@ -288,13 +305,13 @@
     return call(
         functools.partial(backward_kernel, blocks, counts, len(matrices)),
         (f32(copies, 2 * blocks, LANES), f32(*received.shape[1:])),
-        in_specs=[SMEM, VMEM, VMEM] + ([VMEM, HBM] if streamed else [VMEM]) + [VMEM] * len(known),
+        in_specs=[VMEM, VMEM] + ([VMEM, HBM] if streamed else [VMEM]) + [VMEM] * len(known),
         out_specs=(VMEM,) * 2,
         scratch_shapes=[pltpu.VMEM((2 * blocks, 8, LANES), jnp.float32), pltpu.VMEM((2 * blocks, LANES), jnp.float32)]
         + stream_buffers(matrices, width),
         limit=STREAM if streamed else LIMIT,
         cost_estimate=cost(rows * width),
-    )(scalars, received, solved, *matrices, *known)
+    )(received, solved, *matrices, *known)
 
 
 def root_kernel(column, blocks, vector, matrix, send, total):
@@ -334,10 +351,12 @@
     return call(functools.partial(sum_kernel, copies), f32(copies, *received.shape[1:]))(received)
 
 
-def expand(scalars, windows, terms, index, first_block, path):
+def expand(counts, terms, index, first_block, path):
+    subtree = own_subtree()
+
     def one(block, carry):
-        at = pl.multiple_of(windows[scalars[2] // 2, first_block + block] * LANES, LANES)
-        selector = one_hot(index[pl.ds(scalars[7] * 2 + scalars[2] // 2, 1), pl.ds(at, 2 * LANES)], first_block + block)
+        at = window(counts, subtree, first_block + block, index.shape[1])
+        selector = one_hot(index[pl.ds(subtree, 1), pl.ds(at, 2 * LANES)], first_block + block)
         out = lax.dot_general(terms[:, pl.ds(at, 2 * LANES)], selector, NT, preferred_element_type=jnp.float32)
         path[block] = -(out[0:8] + out[8:16] + out[16:24])
         return carry
@@ -345,8 +364,8 @@
     lax.fori_loop(0, path.shape[0], one, 0, unroll=4)
 
 
-def add_own(scalars, both, depth, heights, path):
-    z, core, x = scalars[0], scalars[1], scalars[2]
+def add_own(both, depth, heights, path):
+    z, core, x = position("z"), position("c"), position("x")
     half = pl.multiple_of(core * 8, 8)
     lane = lax.broadcasted_iota(jnp.int32, (8, LANES), 1)
     start = source = 0
@@ -358,7 +377,7 @@
             offset = z * width
             block = start
             if height < 3:
-                block = block + scalars[3 + height] * (XC * depth * width // LANES)
+                block = block + position(("y", "y1", "y0")[height]) * (XC * depth * width // LANES)
             if width == 8:
                 offset = offset + other * 64
                 block = block + x
@@ -429,17 +448,17 @@
     return parts, packs, scratch + [pltpu.VMEM(pack.shape, jnp.float32) for pack in packs]
 
 
-def first_kernel(depth, groups, scalars, windows, both, index, *refs):
+def first_kernel(depth, groups, counts, both, index, *refs):
     count, number = sum(groups), len(groups)
     parts, (send, terms, *packs), (path, ready, done, *stages) = refs[:count], refs[count : -3 - number], refs[-3 - number :]
     copies = stage_in(parts, stages, groups, ready)
     columns = both.shape[2] - LANES
-    half = pl.multiple_of(scalars[1] * 8, 8)
+    half = pl.multiple_of(position("c") * 8, 8)
     pieces = split3(both[0, pl.ds(half, 8), :columns] + both[1, pl.ds(half, 8), :columns])
     terms[...] = jnp.concatenate([*pieces, jnp.zeros_like(pieces[0])], axis=0)
-    expand(scalars, windows, terms, index, sum(WIDTHS[:3]) // LANES, path)
+    expand(counts, terms, index, sum(WIDTHS[:3]) // LANES, path)
     copies = stage_out(copies, stages, packs, done)
-    add_own(scalars, both, depth, (3,), path)
+    add_own(both, depth, (3,), path)
     for dest in range(X):
         for other in range(depth):
             send[dest * depth + other] = path[other]
@@ -447,50 +466,41 @@
         copy.wait()
 
 
-def first(both, index, scalars, windows, depth, groups):
+def first(both, index, counts, depth, groups):
     columns = both.shape[2] - LANES
     parts, packs, scratch = pack_shapes(groups)
     outs = call(
         functools.partial(first_kernel, depth, [len(group) for group in groups]),
         (f32(X * depth, 8, LANES), jax.ShapeDtypeStruct((32, columns), jnp.bfloat16), *packs),
-        in_specs=[SMEM, SMEM, VMEM, VMEM] + [HBM] * len(parts),
+        in_specs=[SMEM, VMEM, VMEM] + [HBM] * len(parts),
         out_specs=(VMEM, VMEM) + (HBM,) * len(packs),
         scratch_shapes=[pltpu.VMEM((WIDTHS[3] // LANES, 8, LANES), jnp.float32)] + scratch,
         limit=WHOLE,
-    )(scalars, windows, both, index, *parts)
+    )(counts, both, index, *parts)
     return outs[0], outs[1], outs[2:]
 
 
-def upper_kernel(depth, groups, scalars, windows, both, terms, index, *refs):
-    count, number = sum(groups), len(groups)
-    parts, (path, *packs), (ready, done, *stages) = refs[:count], refs[count : -2 - number], refs[-2 - number :]
-    copies = stage_out(stage_in(parts, stages, groups, ready), stages, packs, done)
-    expand(scalars, windows, terms, index, 0, path)
-    add_own(scalars, both, depth, (0, 1, 2), path)
-    for copy in copies:
-        copy.wait()
-
-
-def upper_path(both, terms, index, scalars, windows, depth, groups):
+def upper_kernel(depth, counts, both, terms, index, path):
+    expand(counts, terms, index, 0, path)
+    add_own(both, depth, (0, 1, 2), path)
+
+
+def upper_path(both, terms, index, counts, depth):
     blocks = sum(WIDTHS[:3]) // LANES
-    parts, packs, scratch = pack_shapes(groups)
-    outs = call(
-        functools.partial(upper_kernel, depth, [len(group) for group in groups]),
-        (f32(blocks, 8, LANES), *packs),
-        in_specs=[SMEM, SMEM, VMEM, VMEM, VMEM] + [HBM] * len(parts),
-        out_specs=(VMEM,) + (HBM,) * len(packs),
-        scratch_shapes=scratch,
+    return call(
+        functools.partial(upper_kernel, depth),
+        f32(blocks, 8, LANES),
+        in_specs=[SMEM, VMEM, VMEM, VMEM],
+        out_specs=VMEM,
         cost_estimate=cost(blocks * LANES * LANES),
-        limit=STREAM,
-    )(scalars, windows, both, terms, index, *parts)
-    return outs[0], outs[1:]
-
-
-def pick(scalars, windows, index, terms, first_block, blocks, chosen):
+    )(counts, both, terms, index)
+
+
+def pick(counts, index, terms, first_block, blocks, chosen):
     def one(block, carry):
         for half in range(2):
-            at = pl.multiple_of(windows[half, first_block + block] * LANES, LANES)
-            selector = one_hot(index[pl.ds(scalars[7] * 2 + half, 1), pl.ds(at, 2 * LANES)], first_block + block)
+            at = window(counts, position("y") * 2 + half, first_block + block, index.shape[1])
+            selector = one_hot(index[pl.ds(position("y") * 2 + half, 1), pl.ds(at, 2 * LANES)], first_block + block)
             out = lax.dot_general(
                 terms[block].astype(jnp.bfloat16), selector, NN, preferred_element_type=jnp.float32
             )
@@ -506,29 +516,29 @@
     terms[...] = jnp.concatenate([*pieces, jnp.zeros_like(pieces[0])], axis=1).astype(jnp.float32)
 
 
-def pick_kernel(first_block, scalars, windows, x, index, chosen, terms):
+def pick_kernel(first_block, counts, x, index, chosen, terms):
     store_terms(x, terms)
     chosen[...] = jnp.zeros_like(chosen)
-    pick(scalars, windows, index, terms, first_block, x.shape[0] // PAIR, chosen)
-
-
-def picked(x, index, scalars, windows, first_block):
+    pick(counts, index, terms, first_block, x.shape[0] // PAIR, chosen)
+
+
+def picked(x, index, counts, first_block):
     blocks = x.shape[0] // PAIR
     return call(
         functools.partial(pick_kernel, first_block),
         f32(2, 8, index.shape[1]),
-        in_specs=[SMEM, SMEM, VMEM, VMEM],
+        in_specs=[SMEM, VMEM, VMEM],
         out_specs=VMEM,
         scratch_shapes=[pltpu.VMEM((blocks, 8, LANES), jnp.float32)],
         cost_estimate=cost(blocks * 2 * LANES * LANES),
-    )(scalars, windows, x, index)
-
-
-def last_kernel(counts, scalars, windows, received, x0, x1, x2, coupling, index, chosen0, chosen1, chosen2, send, x3, terms, chosen):
+    )(counts, x, index)
+
+
+def last_kernel(widths, counts, received, x0, x1, x2, coupling, index, chosen0, chosen1, chosen2, send, x3, terms, chosen):
     x3[...] = jnp.sum(received[...], axis=0)
     store_terms(x3, terms)
     chosen[...] = chosen0[...] + chosen1[...] + chosen2[...]
-    pick(scalars, windows, index, terms, sum(counts[:3]), counts[3], chosen)
+    pick(counts, index, terms, sum(widths[:3]), widths[3], chosen)
     rows, columns = coupling.shape[0] // 2, coupling.shape[1]
     lane = lax.broadcasted_iota(jnp.int32, (CHUNK, LANES), 1)
     handed = []
@@ -553,29 +563,29 @@
         for level, ref in enumerate((x0, x1, x2, x3)):
             block = x if level < 2 else x * 2 + core
             if level < 3:
-                block = block + scalars[3 + level] * (counts[level] // (Y // 2**level))
+                block = block + position(("y", "y1", "y0")[level]) * (widths[level] // (Y // 2**level))
             send[dest, 2 * level : 2 * level + 2, :] = ref[pl.ds(block * 2, 2), :]
         send[dest, 8:10, :] = handed[x // 2]
 
 
-def last(received, known, chosen, coupling, index, scalars, windows):
-    counts = [width // LANES for width in WIDTHS]
-    return call(
-        functools.partial(last_kernel, counts),
+def last(received, known, chosen, coupling, index, counts):
+    widths = [width // LANES for width in WIDTHS]
+    return call(
+        functools.partial(last_kernel, widths),
         f32(XC, 16, LANES),
-        in_specs=[SMEM, SMEM] + [VMEM] * 9,
+        in_specs=[SMEM] + [VMEM] * 9,
         out_specs=VMEM,
         scratch_shapes=[
             pltpu.VMEM(received.shape[1:], jnp.float32),
-            pltpu.VMEM((counts[3], 8, LANES), jnp.float32),
+            pltpu.VMEM((widths[3], 8, LANES), jnp.float32),
             pltpu.VMEM((2, 8, coupling.shape[1]), jnp.float32),
         ],
-    )(scalars, windows, received, *known, coupling, index, *chosen)
-
-
-def finish_kernel(scalars, received, values, out0, out1, out2, out3, handed):
-    z, core = scalars[0], scalars[1]
-    offsets = (core * 64 + z * 8, core * 64 + z * 8, z * 16, z * 16, (lax.rem(scalars[2], 2) * 2 + core) * values.shape[1])
+    )(counts, received, *known, coupling, index, *chosen)
+
+
+def finish_kernel(received, values, out0, out1, out2, out3, handed):
+    z, core = position("z"), position("c")
+    offsets = (core * 64 + z * 8, core * 64 + z * 8, z * 16, z * 16, (lax.rem(position("x"), 2) * 2 + core) * values.shape[1])
     for level, ref in enumerate((out0, out1, out2, out3, handed)):
         value = jnp.concatenate([received[source, 2 * level : 2 * level + 2, :] for source in range(XC)], axis=0)
         moved = pltpu.roll(value, lax.rem(LANES - offsets[level], LANES), 1)
@@ -587,10 +597,10 @@
             ref[...] = values[...] - moved[:, : ref.shape[1]]
 
 
-def finish(received, values, scalars, widths):
+def finish(received, values, widths):
     samples = XC * PAIR
     shapes = [f32(width, samples) for width in widths[:2]] + [f32(samples, width) for width in widths[2:]]
-    outs = call(finish_kernel, (*shapes, f32(*values.shape)), in_specs=[SMEM, VMEM, VMEM])(scalars, received, values)
+    outs = call(finish_kernel, (*shapes, f32(*values.shape)), in_specs=[VMEM, VMEM])(received, values)
     return outs[0].T, outs[1].T, *outs[2:]
 
 
@@ -611,8 +621,6 @@
     coupled_rows,
 ):
     depth = lax.axis_size("z")
-    y = (lax.axis_index("y2") * 2 + lax.axis_index("y1")) * 2 + lax.axis_index("y0")
-    x, c, z = lax.axis_index("x"), lax.axis_index("c"), lax.axis_index("z")
     counts = [width // LANES for width in WIDTHS]
     blocks = sum(counts)
 
@@ -624,18 +632,16 @@
 
     both, coupled_rows = lax.optimization_barrier((both, coupled_rows))
     edges = jnp.arange(blocks, dtype=jnp.int32) * LANES
-    both_indices = lax.dynamic_slice_in_dim(coupled_rows, y * 2, 2, 0)
-    windows = jnp.sum((both_indices[:, None, :] < edges[None, :, None]).astype(jnp.int32), axis=2) // LANES
-    windows = jnp.minimum(windows, coupled_rows.shape[1] // LANES - 2)
-
-    places = jnp.stack([z, c, x, y, y % 4, y % 2, (y % 2) * depth + z, y])
-    send, terms, (pack2,) = first(both, coupled_rows, places, windows, depth, ((inv_level2, cross_level2),))
+    ahead = jnp.sum((coupled_rows[:, None, :] < edges[None, :, None]).astype(jnp.int32), axis=2)
+
+    groups = ((inv_level3, cross_level3), (inv_level2, cross_level2), (inv_level1, cross_level1, inv_root))
+    send, terms, (own3, pack2, pack1) = first(both, coupled_rows, ahead, depth, groups)
     matrix2 = gathered(pack2)
-    groups = ((inv_level3, cross_level3), (inv_level1, cross_level1, inv_root))
-    path, (own3, pack1) = upper_path(both, terms, coupled_rows, places, windows, depth, groups)
-    received, path, own3, pack1 = lax.optimization_barrier((exchange(send, ("x", "z")), path, own3, pack1))
-    other3 = lax.ppermute(own3, "c", [(0, 1), (1, 0)])
     matrix1 = gathered(pack1)
+    path = upper_path(both, terms, coupled_rows, ahead, depth)
+    received, other3, path = lax.optimization_barrier(
+        (exchange(send, ("x", "z")), lax.ppermute(own3, "c", [(0, 1), (1, 0)]), path)
+    )
     target3 = exchange(sum_and_copy(received, depth), ("z",))
     send = lowest(target3, own3, other3, path, counts[3], sum(counts[:3]), 2 * depth)
     send, own3, coupling = lax.optimization_barrier((send, own3, coupling))
@@ -644,10 +650,10 @@
     received = sum_and_copy(exchange(send, ("y0", "x", "z")), 2 * depth)
     target2, half2 = lax.optimization_barrier((exchange(received, ("y0", "z")), fetched(matrix2, 0.5)))
     solved2, send, rest = forward(
-        target2, (half2, matrix2), received[0], places, counts[2], counts[0] + counts[1], counts[0], 4 * depth, 6
+        target2, (half2, matrix2), received[0], counts[2], counts[0] + counts[1], counts[0], 4 * depth, 6
     )
     received, matrix1 = lax.optimization_barrier((exchange(send, ("y1", "y0", "z")), fetched(matrix1)))
-    solved1, send, rest = forward(received, (matrix1,), rest, places, counts[1], counts[0], 0, Y, 0)
+    solved1, send, rest = forward(received, (matrix1,), rest, counts[1], counts[0], 0, Y, 0)
 
     def sum_root(copies):
         received = exchange(copies.reshape(Y * depth, -1, LANES), ALL_Y + ("z",))
@@ -655,22 +661,22 @@
 
     target = sum_root(send).reshape(-1, LANES)
     received = sum_root(root(target, matrix1, WIDTHS[1] + WIDTHS[0], Y)).reshape(1, -1, LANES)
-    send, x0 = backward(received, (matrix1,), solved1, [], places, counts[1], 4 * depth)
+    send, x0 = backward(received, (matrix1,), solved1, [], counts[1], 4 * depth)
     x0, matrix2 = lax.optimization_barrier((x0, matrix2))
     received, chosen0, half2 = lax.optimization_barrier(
-        (exchange(send, ("y1", "y0", "z")), picked(x0, coupled_rows, places, windows, 0), fetched(matrix2, 0.5))
+        (exchange(send, ("y1", "y0", "z")), picked(x0, coupled_rows, ahead, 0), fetched(matrix2, 0.5))
     )
-    send, x1 = backward(received, (half2, matrix2), solved2, [x0], places, counts[2], 2 * depth)
+    send, x1 = backward(received, (half2, matrix2), solved2, [x0], counts[2], 2 * depth)
     received, chosen1, half3 = lax.optimization_barrier(
-        (exchange(send, ("y0", "z")), picked(x1, coupled_rows, places, windows, counts[0]), fetched(matrix3, 0.5))
+        (exchange(send, ("y0", "z")), picked(x1, coupled_rows, ahead, counts[0]), fetched(matrix3, 0.5))
     )
-    send, x2 = backward(received, (half3, matrix3), target3, [x0, x1], places, counts[3], depth)
+    send, x2 = backward(received, (half3, matrix3), target3, [x0, x1], counts[3], depth)
     received, chosen2, all_coupling = lax.optimization_barrier(
-        (exchange(send, ("z",)), picked(x2, coupled_rows, places, windows, counts[0] + counts[1]), fetched(all_coupling))
+        (exchange(send, ("z",)), picked(x2, coupled_rows, ahead, counts[0] + counts[1]), fetched(all_coupling))
     )
-    send = last(received, [x0, x1, x2], [chosen0, chosen1, chosen2], all_coupling, coupled_rows, places, windows)
+    send = last(received, [x0, x1, x2], [chosen0, chosen1, chosen2], all_coupling, coupled_rows, ahead)
     received = exchange(send, ("c", "x"))
-    return finish(received, subtree_values, places, [part.shape[1] for part in rhs_parts])
+    return finish(received, subtree_values, [part.shape[1] for part in rhs_parts])
 
 
 def solution(mesh):

time: 247 us -> 240 us (0.972)
  starting transfers between devices: 34 us -> 30 us
  Pallas kernels: 39.8 us -> 36.6 us
  local copies, waits for them, and re-layouts: 15.9 us -> 13 us
    unnamed x36 -> x22, local copies, waits for them, and re-layouts: 13.7 us -> 12.3 us
  transfers between devices with their start and end apart: 11 -> 11, of which waited for: 6 -> 7; matrix products, arithmetic and copies ran while one was open for 0% -> 0% of each run, Pallas kernels for 13% -> 12%
where the time goes in v9:
time: 240 us; the launch traced here: 238 us
  blocking collectives  112 us (47%)
  Pallas kernels  36.6 us (15%)
  starting transfers between devices  30 us (12%)
  waiting for transfers between devices  30 us (12%)
  between operations  14 us (6%)
  local copies, waits for them, and re-layouts  13 us (5%)
  other arithmetic  2.65 us (1%)
    all_to_all x7, blocking collectives, exchange(): return lax.all_to_all(flat, axes, 0, 0, tiled=True).reshape(operand.shape)  102 us
    all_to_all x6, starting transfers between devices, exchange(): return lax.all_to_all(flat, axes, 0, 0, tiled=True).reshape(operand.shape)  27.8 us
    all_to_all x6, waiting for transfers between devices, exchange(): return lax.all_to_all(flat, axes, 0, 0, tiled=True).reshape(operand.shape)  27.1 us
    unnamed x22, local copies, waits for them, and re-layouts  12.3 us
    all_gather x1, blocking collectives, body(): lax.all_gather(own_product(subtree_values, coupling, rhs_parts), 'c', axi...  10.3 us
    pallas_call x3, Pallas kernels, backward(): call(functools.partial(backward_kernel, blocks, counts, len(matrices)), (...  6.76 us
    pallas_call x3, Pallas kernels, picked(): call(functools.partial(pick_kernel, first_block), f32(2, 8, index.shape[1...  5.59 us
    pallas_call x5, Pallas kernels, fetched(): call(fetch_kernel, f32(rows, width), in_specs=[HBM], out_specs=VMEM, scra...  4.92 us
  transfers between devices with their start and end apart: 11, of which 7 were waited for; matrix products, arithmetic and copies ran while one was open for 0% of the time, Pallas kernels for 12%

profile of v9, /device:TPU:1, one launch (start us, length us, event | category | flops | bytes accessed | tf_op | source)
XLA Modules:
  0.0 238.3 jit_solution(5898735994106202744)
XLA Ops:
  7.2 0.0 all-gather.6.cloned.1.call-start
  7.2 1.9 shard_map.173
  9.1 10.3 %all-gather = f32[32,2176]{1,0:T(8,128)} all-gather(f32[16,2176]{1,0:T(8,128)} %shard_map.173), channel_id=2, replica_groups=mesh['y2'=2,'y1'=2,'y0'=2,'x'=4,'c'=2,'z'=8] {'c'}, dimensions={0}, use_global_device_ids=true | all-gather | bytes 417792 | tf_op jit(solution)/shard_map/all_gather | solution.py:628
  19.4 2.6 %convert_reduce_fusion.counts = s32[16,72]{1,0:T(8,128)} fusion(s32[16,2048]{1,0:T(8,128)} %index.5, s32[72]{0:T(128)S(1)} %iota_multiply_fusion), kind=kLoop, calls=%fused_computation | loop fusion | flops 7076736 | bytes 135968 | tf_op jit(solution)/shard_map/reduce_sum | solution.py:635
  22.1 4.3 %shard_map.174 = (f32[32,8,128]{2,1,0:T(8,128)}, bf16[32,2048]{1,0:T(8,128)(2,1)}, f32[16,9216]{1,0:T(8,128)}, f32[16,8192]{1,0:T(8,128)}, f32[8,10240]{1,0:T(8,128)}) custom-call(s32[16,72]{1,0:T(8,128)} %convert_reduce_fusion.counts, f32[2,16,2176]{2,1,0:T(8,128)} %bitcast.11, s32[16,2048]{1,0:T(8,128)} %index.5, f32[16,1024]{1,0:T(8,128)} %refs_0_.1, ...), custom_call_target="tpu_custom_call" | custom-call | tf_op jit(solution)/shard_map/pallas_call | solution.py:472
  26.4 0.0 all-gather.6.cloned.1.call-update
  26.4 0.0 all-gather.8.cloned.1.call-start
  26.5 0.7 all-gather.8.cloned.1.call-update
  27.2 2.1 collective-permute-start
  29.2 7.5 %all-to-all-start = ((f32[32,8,128]{2,1,0:T(8,128)}), f32[32,8,128]{2,1,0:T(8,128)S(1)}, u32[]{:S(2)}, u32[]{:S(2)}) async-start(f32[32,8,128]{2,1,0:T(8,128)} %get-tuple-element.51), calls=%async_computation | async-start | bytes 262144 | tf_op jit(solution)/shard_map/all_to_all | solution.py:67
  36.7 0.0 all-gather.10.cloned.1.call-start
  36.8 0.9 copy-done.9
  37.7 4.1 %shard_map.175.path = f32[64,8,128]{2,1,0:T(8,128)S(1)} custom-call(s32[16,72]{1,0:T(8,128)S(1)} %copy-done.8, f32[2,16,2176]{2,1,0:T(8,128)S(1)} %bitcast.12, bf16[32,2048]{1,0:T(8,128)(2,1)S(1)} %copy-done.9, s32[16,2048]{1,0:T(8,128)S(1)} %copy-done.3), custom_call_target="tpu_custom_call" | custom-call | flops 8388608 | bytes 4194304 | tf_op jit(solution)/shard_map/pallas_call | solution.py:490
  41.9 4.0 %all-to-all-done.received = f32[32,8,128]{2,1,0:T(8,128)S(1)} async-done(((f32[32,8,128]{2,1,0:T(8,128)}), f32[32,8,128]{2,1,0:T(8,128)S(1)}, u32[]{:S(2)}, u32[]{:S(2)}) %all-to-all-start) | async-done | bytes 131104 | tf_op jit(solution)/shard_map/all_to_all | solution.py:67
  45.9 9.9 %all_to_all.86.received.solved = f32[8,8,128]{2,1,0:T(8,128)S(1)} all-to-all(f32[8,8,128]{2,1,0:T(8,128)S(1)} %shard_map.176), channel_id=1, replica_groups=mesh['y2'=2,'y1'=2,'y0'=2,'x'=4,'c'=2,'z'=8] {'z'}, dimensions={0} | all-to-all | bytes 65536 | tf_op jit(solution)/shard_map/all_to_all | solution.py:67
  55.9 1.1 copy-done.6
  56.9 1.6 shard_map.177
  58.5 0.0 all-gather.10.cloned.1.call-update
  58.5 16.1 %all_to_all.87.received = f32[64,8,128]{2,1,0:T(8,128)S(1)} all-to-all(f32[64,8,128]{2,1,0:T(8,128)S(1)} %shard_map.177), channel_id=1, replica_groups=mesh['y2'=2,'y1'=2,'y0'=2,'x'=4,'c'=2,'z'=8] {'y0','x','z'}, dimensions={0} | all-to-all | bytes 524288 | tf_op jit(solution)/shard_map/all_to_all | solution.py:67
  74.6 0.7 shard_map.178
  75.3 3.5 %all-to-all-start.3 = ((f32[16,8,128]{2,1,0:T(8,128)}), f32[16,8,128]{2,1,0:T(8,128)S(1)}, u32[]{:S(2)}, u32[]{:S(2)}) async-start(f32[16,8,128]{2,1,0:T(8,128)} %shard_map.178), calls=%async_computation.3 | async-start | bytes 131072 | tf_op jit(solution)/shard_map/all_to_all | solution.py:67
  78.8 0.7 slice_bitcast_fusion.rest_in
  79.5 2.5 %copy-done = f32[128,8192]{1,0:T(8,128)S(1)} copy-done((f32[128,8192]{1,0:T(8,128)S(1)}, f32[128,8192]{1,0:T(8,128)}, u32[]{:S(2)}) %copy-start) | copy-done | bytes 4194328
  82.0 0.2 shard_map.179.refs_0_
  82.2 3.9 %all-to-all-done.3.received = f32[16,8,128]{2,1,0:T(8,128)S(1)} async-done(((f32[16,8,128]{2,1,0:T(8,128)}), f32[16,8,128]{2,1,0:T(8,128)S(1)}, u32[]{:S(2)}, u32[]{:S(2)}) %all-to-all-start.3) | async-done | bytes 65568 | tf_op jit(solution)/shard_map/all_to_all | solution.py:67
  86.2 2.8 %shard_map.180 = (f32[2,128,128]{2,1,0:T(8,128)S(1)}, f32[32,32,128]{2,1,0:T(8,128)}, f32[96,128]{1,0:T(8,128)S(1)}) custom-call(f32[16,8,128]{2,1,0:T(8,128)S(1)} %all-to-all-done.3.received, f32[8,128]{1,0:T(8,128)S(1)} %slice_bitcast_fusion.rest_in, f32[64,8192]{1,0:T(8,128)S(1)} %shard_map.179.refs_0_, ...), custom_call_target="tpu_custom_call" | custom-call | flops 8388608 | bytes 4194304 | tf_op jit(solution)/shard_map/pallas_call | solution.py:203
  88.9 5.8 %all-to-all-start.4 = ((f32[32,32,128]{2,1,0:T(8,128)}), f32[32,32,128]{2,1,0:T(8,128)S(1)}, u32[]{:S(2)}, u32[]{:S(2)}) async-start(f32[32,32,128]{2,1,0:T(8,128)} %get-tuple-element.61), calls=%async_computation.4 | async-start | bytes 1048576 | tf_op jit(solution)/shard_map/all_to_all | solution.py:67
  94.7 0.0 all-gather.12.cloned.1.call-start
  94.8 0.5 all-gather.12.cloned.1.call-update
  95.3 1.6 all-gather.8.cloned.1.call-done.matrix
  96.9 1.7 copy-done.4
  98.6 0.9 shard_map.181.refs_0_.matrix
  99.5 7.8 %all-to-all-done.4.received = f32[32,32,128]{2,1,0:T(8,128)S(1)} async-done(((f32[32,32,128]{2,1,0:T(8,128)}), f32[32,32,128]{2,1,0:T(8,128)S(1)}, u32[]{:S(2)}, u32[]{:S(2)}) %all-to-all-start.4) | async-done | bytes 524320 | tf_op jit(solution)/shard_map/all_to_all | solution.py:67
  107.3 1.0 shard_map.182
  108.3 22.5 %all_to_all.88.received = f32[64,8,128]{2,1,0:T(8,128)S(1)} all-to-all(f32[64,8,128]{2,1,0:T(8,128)S(1)} %bitcast.14), channel_id=1, replica_groups=mesh['y2'=2,'y1'=2,'y0'=2,'x'=4,'c'=2,'z'=8] {'y2','y1','y0','z'}, dimensions={0} | all-to-all | bytes 524288 | tf_op jit(solution)/shard_map/all_to_all | solution.py:67
  130.8 0.1 shard_map.183
  130.9 9.5 %all_to_all.89 = f32[8,8,128]{2,1,0:T(8,128)S(1)} all-to-all(f32[8,8,128]{2,1,0:T(8,128)S(1)} %shard_map.183), channel_id=1, replica_groups=mesh['y2'=2,'y1'=2,'y0'=2,'x'=4,'c'=2,'z'=8] {'z'}, dimensions={0} | all-to-all | bytes 65536 | tf_op jit(solution)/shard_map/all_to_all | solution.py:67
  140.4 0.4 shard_map.184
  140.8 16.4 %all_to_all.90.received = f32[64,8,128]{2,1,0:T(8,128)S(1)} all-to-all(f32[64,8,128]{2,1,0:T(8,128)S(1)} %bitcast.13), channel_id=1, replica_groups=mesh['y2'=2,'y1'=2,'y0'=2,'x'=4,'c'=2,'z'=8] {'y2','y1','y0','z'}, dimensions={0} | all-to-all | bytes 524288 | tf_op jit(solution)/shard_map/all_to_all | solution.py:67
  157.2 0.1 shard_map.185
  157.3 9.4 %all_to_all.91 = f32[8,8,128]{2,1,0:T(8,128)S(1)} all-to-all(f32[8,8,128]{2,1,0:T(8,128)S(1)} %shard_map.185), channel_id=1, replica_groups=mesh['y2'=2,'y1'=2,'y0'=2,'x'=4,'c'=2,'z'=8] {'z'}, dimensions={0} | all-to-all | bytes 65536 | tf_op jit(solution)/shard_map/all_to_all | solution.py:67
  166.6 1.2 shard_map.186
  167.9 3.9 %all-to-all-start.9 = ((f32[32,32,128]{2,1,0:T(8,128)}), f32[32,32,128]{2,1,0:T(8,128)S(1)}, u32[]{:S(2)}, u32[]{:S(2)}) async-start(f32[32,32,128]{2,1,0:T(8,128)} %get-tuple-element.68), calls=%async_computation.9 | async-start | bytes 1048576 | tf_op jit(solution)/shard_map/all_to_all | solution.py:67
  171.8 2.2 copy-done.1
  174.0 0.2 shard_map.188.refs_0_
  174.2 2.4 %shard_map.187.chosen0 = f32[2,8,2048]{2,1,0:T(8,128)S(1)} custom-call(s32[16,72]{1,0:T(8,128)S(1)} %copy-done.8, f32[64,128]{1,0:T(8,128)S(1)} %get-tuple-element.70.x.refs_2_.x0, s32[16,2048]{1,0:T(8,128)S(1)} %copy-done.3), custom_call_target="tpu_custom_call" | custom-call | flops 8388608 | bytes 4194304 | tf_op jit(solution)/shard_map/pallas_call | solution.py:527
  176.7 7.4 %all-to-all-done.9.received = f32[32,32,128]{2,1,0:T(8,128)S(1)} async-done(((f32[32,32,128]{2,1,0:T(8,128)}), f32[32,32,128]{2,1,0:T(8,128)S(1)}, u32[]{:S(2)}, u32[]{:S(2)}) %all-to-all-start.9) | async-done | bytes 524320 | tf_op jit(solution)/shard_map/all_to_all | solution.py:67
  184.1 2.8 %shard_map.189 = (f32[16,32,128]{2,1,0:T(8,128)}, f32[32,128]{1,0:T(8,128)S(1)}) custom-call(f32[32,32,128]{2,1,0:T(8,128)S(1)} %all-to-all-done.9.received, f32[2,128,128]{2,1,0:T(8,128)S(1)} %get-tuple-element.73.solved, f32[64,8192]{1,0:T(8,128)S(1)} %shard_map.188.refs_0_, f32[128,8192]{1,0:T(8,128)} %all-gather.6.cloned.1.call-done.matrix.refs_1_, ...), custom_call_target="tpu_custom_call" | custom-call | flops 8388608 | bytes 4194304 | tf_op jit(solution)/shard_map/pallas_call | solution.py:305
  186.8 3.7 %all-to-all-start.10 = ((f32[16,32,128]{2,1,0:T(8,128)}), f32[16,32,128]{2,1,0:T(8,128)S(1)}, u32[]{:S(2)}, u32[]{:S(2)}) async-start(f32[16,32,128]{2,1,0:T(8,128)} %get-tuple-element.75), calls=%async_computation.10 | async-start | bytes 524288 | tf_op jit(solution)/shard_map/all_to_all | solution.py:67
  190.6 0.0 all-gather.10.cloned.1.call-done.matrix.refs_1_
  190.6 2.3 copy-done.2
  192.9 0.6 shard_map.191.refs_0_
  193.5 1.6 shard_map.190.chosen1
  195.1 3.0 %all-to-all-done.10.received = f32[16,32,128]{2,1,0:T(8,128)S(1)} async-done(((f32[16,32,128]{2,1,0:T(8,128)}), f32[16,32,128]{2,1,0:T(8,128)S(1)}, u32[]{:S(2)}, u32[]{:S(2)}) %all-to-all-start.10) | async-done | bytes 262176 | tf_op jit(solution)/shard_map/all_to_all | solution.py:67
  198.1 2.8 %shard_map.192 = (f32[8,16,128]{2,1,0:T(8,128)}, f32[32,128]{1,0:T(8,128)S(1)}) custom-call(f32[16,32,128]{2,1,0:T(8,128)S(1)} %all-to-all-done.10.received, f32[8,8,128]{2,1,0:T(8,128)S(1)} %all_to_all.86.received.solved, f32[64,9216]{1,0:T(8,128)S(1)} %shard_map.191.refs_0_, f32[128,9216]{1,0:T(8,128)} %all-gather.10.cloned.1.call-done.matrix.refs_1_, ...), custom_call_target="tpu_custom_call" | custom-call | flops 9437184 | bytes 4718592 | tf_op jit(solution)/shard_map/pallas_call | solution.py:305
  200.9 3.4 %all-to-all-start.11 = ((f32[8,16,128]{2,1,0:T(8,128)}), f32[8,16,128]{2,1,0:T(8,128)S(1)}, u32[]{:S(2)}, u32[]{:S(2)}) async-start(f32[8,16,128]{2,1,0:T(8,128)} %get-tuple-element.80), calls=%async_computation.11 | async-start | bytes 131072 | tf_op jit(solution)/shard_map/all_to_all | solution.py:67
  204.2 0.0 all-gather.12.cloned.1.call-done.matrix
  204.3 1.6 copy-done.7
  205.9 3.0 %shard_map.194.coupling = f32[256,2048]{1,0:T(8,128)S(1)} custom-call(f32[256,2048]{1,0:T(8,128)S(1)} %copy-done.7), custom_call_target="tpu_custom_call" | custom-call | flops 8388608 | bytes 4194304 | tf_op jit(solution)/shard_map/pallas_call | solution.py:157
  208.9 1.6 shard_map.193.chosen2
  210.5 0.9 all-to-all-done.11.received
  211.4 1.7 shard_map.195
  213.0 17.9 %all_to_all.92.received = f32[8,16,128]{2,1,0:T(8,128)S(1)} all-to-all(f32[8,16,128]{2,1,0:T(8,128)S(1)} %shard_map.195), channel_id=1, replica_groups=mesh['y2'=2,'y1'=2,'y0'=2,'x'=4,'c'=2,'z'=8] {'c','x'}, dimensions={0} | all-to-all | bytes 131072 | tf_op jit(solution)/shard_map/all_to_all | solution.py:67
  231.0 0.8 shard_map.196
  (19 shorter events, 0.1 us)
Async XLA Ops:
  7.2 29.6 %copy-start.3 = (s32[16,2048]{1,0:T(8,128)S(1)}, s32[16,2048]{1,0:T(8,128)}, u32[]{:S(2)}) copy-start(s32[16,2048]{1,0:T(8,128)} %index.5) | copy-start | bytes 393220
  7.2 72.3 %all-gather.6.cloned.1.call-start = ((), (), s32[]{:S(2)}) async-start(), calls=%async_computation.13 | async-start | bytes 4718592 | tf_op jit(solution)/shard_map/all_gather | solution.py:631
  19.4 17.4 %copy-start.5 = (f32[32,2176]{1,0:T(8,128)S(1)}, f32[32,2176]{1,0:T(8,128)}, u32[]{:S(2)}) copy-start(f32[32,2176]{1,0:T(8,128)} %all-gather) | copy-start | bytes 835588
  22.1 14.7 %copy-start.8 = (s32[16,72]{1,0:T(8,128)S(1)}, s32[16,72]{1,0:T(8,128)}, u32[]{:S(2)}) copy-start(s32[16,72]{1,0:T(8,128)} %convert_reduce_fusion.counts) | copy-start | bytes 13828
  26.4 70.5 %all-gather.8.cloned.1.call-start = ((), (), s32[]{:S(2)}) async-start(), calls=%async_computation.14 | async-start | bytes 2949120 | tf_op jit(solution)/shard_map/all_gather | solution.py:631
  27.2 18.7 %collective-permute-start = (f32[16,9216]{1,0:T(8,128)}, f32[16,9216]{1,0:T(8,128)S(1)}, u32[]{:S(2)}, u32[]{:S(2)}) collective-permute-start(f32[16,9216]{1,0:T(8,128)} %get-tuple-element.77.own), channel_id=1, source_target_pairs={{0,8},{8,0},{1,9},{9,1},{2,10},{10,2},{3,11},{11,3},{4,12},{12,4},... | collective-permute-start | bytes 1769480 | tf_op jit(solution)/shard_map/ppermute | solution.py:643
  29.2 16.7 %all-to-all-start = ((f32[32,8,128]{2,1,0:T(8,128)}), f32[32,8,128]{2,1,0:T(8,128)S(1)}, u32[]{:S(2)}, u32[]{:S(2)}) async-start(f32[32,8,128]{2,1,0:T(8,128)} %get-tuple-element.51), calls=%async_computation | async-start | bytes 262144 | tf_op jit(solution)/shard_map/all_to_all | solution.py:67
  36.7 153.8 %all-gather.10.cloned.1.call-start = ((), (), s32[]{:S(2)}) async-start(), calls=%async_computation.15 | async-start | bytes 5308416 | tf_op jit(solution)/shard_map/all_gather | solution.py:631
  36.8 0.9 copy-start.9
  55.9 1.1 copy-start.6
  75.3 10.8 %all-to-all-start.3 = ((f32[16,8,128]{2,1,0:T(8,128)}), f32[16,8,128]{2,1,0:T(8,128)S(1)}, u32[]{:S(2)}, u32[]{:S(2)}) async-start(f32[16,8,128]{2,1,0:T(8,128)} %shard_map.178), calls=%async_computation.3 | async-start | bytes 131072 | tf_op jit(solution)/shard_map/all_to_all | solution.py:67
  79.5 2.5 %copy-start = (f32[128,8192]{1,0:T(8,128)S(1)}, f32[128,8192]{1,0:T(8,128)}, u32[]{:S(2)}) copy-start(f32[128,8192]{1,0:T(8,128)} %all-gather.6.cloned.1.call-done.matrix.refs_1_) | copy-start | bytes 12582916
  88.9 18.4 %all-to-all-start.4 = ((f32[32,32,128]{2,1,0:T(8,128)}), f32[32,32,128]{2,1,0:T(8,128)S(1)}, u32[]{:S(2)}, u32[]{:S(2)}) async-start(f32[32,32,128]{2,1,0:T(8,128)} %get-tuple-element.61), calls=%async_computation.4 | async-start | bytes 1048576 | tf_op jit(solution)/shard_map/all_to_all | solution.py:67
  94.7 109.5 %all-gather.12.cloned.1.call-start = ((), (), s32[]{:S(2)}) async-start(), calls=%async_computation.16 | async-start | bytes 2359296 | tf_op jit(solution)/shard_map/all_gather | solution.py:631
  96.9 1.7 copy-start.4
  167.9 16.2 %all-to-all-start.9 = ((f32[32,32,128]{2,1,0:T(8,128)}), f32[32,32,128]{2,1,0:T(8,128)S(1)}, u32[]{:S(2)}, u32[]{:S(2)}) async-start(f32[32,32,128]{2,1,0:T(8,128)} %get-tuple-element.68), calls=%async_computation.9 | async-start | bytes 1048576 | tf_op jit(solution)/shard_map/all_to_all | solution.py:67
  171.8 2.2 copy-start.1
  186.8 11.3 %all-to-all-start.10 = ((f32[16,32,128]{2,1,0:T(8,128)}), f32[16,32,128]{2,1,0:T(8,128)S(1)}, u32[]{:S(2)}, u32[]{:S(2)}) async-start(f32[16,32,128]{2,1,0:T(8,128)} %get-tuple-element.75), calls=%async_computation.10 | async-start | bytes 524288 | tf_op jit(solution)/shard_map/all_to_all | solution.py:67
  190.6 2.3 copy-start.2
  200.9 10.5 %all-to-all-start.11 = ((f32[8,16,128]{2,1,0:T(8,128)}), f32[8,16,128]{2,1,0:T(8,128)S(1)}, u32[]{:S(2)}, u32[]{:S(2)}) async-start(f32[8,16,128]{2,1,0:T(8,128)} %get-tuple-element.80), calls=%async_computation.11 | async-start | bytes 131072 | tf_op jit(solution)/shard_map/all_to_all | solution.py:67
  204.3 1.6 copy-start.7
  208.9 22.1 %copy-start.10 = (f32[16,32]{1,0:T(8,128)S(1)}, f32[16,32]{1,0:T(8,128)}, u32[]{:S(2)}) copy-start(f32[16,32]{1,0:T(8,128)} %values.3) | copy-start | bytes 6148
Sparse Core Ops, SparseCore 0:
  26.5 37.2 all-gather.5
  66.0 30.8 all-gather.7
  99.0 40.2 all-gather.9
  141.3 30.5 all-gather.11

commit v10 on v9

--- a/solution.py
+++ b/solution.py
@@ -54,8 +54,8 @@
     return position("y") * 2 + position("x") // 2
 
 
-def window(counts, subtree, block, columns):
-    return pl.multiple_of(jnp.minimum(counts[subtree, block] // LANES, columns // LANES - 2) * LANES, LANES)
+def window(counts, half, block, columns):
+    return pl.multiple_of(jnp.minimum(counts[half, block] // LANES, columns // LANES - 2) * LANES, LANES)
 
 
 def f32(*shape):
@@ -355,7 +355,7 @@
     subtree = own_subtree()
 
     def one(block, carry):
-        at = window(counts, subtree, first_block + block, index.shape[1])
+        at = window(counts, position("x") // 2, first_block + block, index.shape[1])
         selector = one_hot(index[pl.ds(subtree, 1), pl.ds(at, 2 * LANES)], first_block + block)
         out = lax.dot_general(terms[:, pl.ds(at, 2 * LANES)], selector, NT, preferred_element_type=jnp.float32)
         path[block] = -(out[0:8] + out[8:16] + out[16:24])
@@ -390,7 +390,7 @@
         source += width
 
 
-def product_kernel(values, coupling, rhs0, rhs1, rhs2, rhs3, out):
+def product_kernel(values, coupling, rhs0, rhs1, rhs2, rhs3, index, out, ahead):
     columns = coupling.shape[1]
     out[:, :columns] = lax.dot_general(
         values[...], coupling[...], NN, precision=lax.Precision.HIGHEST, preferred_element_type=jnp.float32
@@ -399,12 +399,24 @@
     filled = sum(part.shape[1] for part in parts)
     parts.append(jnp.zeros((out.shape[0], LANES - filled), jnp.float32))
     out[:, columns:] = jnp.concatenate(parts, axis=1)
-
-
-def own_product(values, coupling, rhs_parts):
+    edges = lax.broadcasted_iota(jnp.int32, (LANES, 2 * LANES), 0) * LANES
+    for half in range(2):
+        def compare(block, total):
+            at = pl.multiple_of(block * 2 * LANES, LANES)
+            row = index[pl.ds(position("y") * 2 + half, 1), pl.ds(at, 2 * LANES)]
+            return total + jnp.where(row < edges, 1.0, 0.0)
+
+        total = lax.fori_loop(0, columns // (2 * LANES), compare, jnp.zeros((LANES, 2 * LANES), jnp.float32), unroll=2)
+        total = jnp.broadcast_to(jnp.sum(total, axis=1, keepdims=True), (LANES, LANES))
+        ahead[half : half + 1, :] = jnp.transpose(total)[0:1, :].astype(jnp.int32)
+
+
+def own_product(values, coupling, rhs_parts, index):
     rhs0, rhs1, rhs2, rhs3 = rhs_parts
-    shape = f32(values.shape[0], coupling.shape[1] + LANES)
-    return call(product_kernel, shape, in_specs=[VMEM] * 6, out_specs=VMEM, limit=WHOLE)(values, coupling, rhs0.T, rhs1.T, rhs2, rhs3)
+    shapes = (f32(values.shape[0], coupling.shape[1] + LANES), jax.ShapeDtypeStruct((2, LANES), jnp.int32))
+    return call(product_kernel, shapes, in_specs=[VMEM] * 7, out_specs=(VMEM, VMEM), limit=WHOLE)(
+        values, coupling, rhs0.T, rhs1.T, rhs2, rhs3, index
+    )
 
 
 def stage_in(parts, stages, groups, ready):
@@ -499,7 +511,7 @@
 def pick(counts, index, terms, first_block, blocks, chosen):
     def one(block, carry):
         for half in range(2):
-            at = window(counts, position("y") * 2 + half, first_block + block, index.shape[1])
+            at = window(counts, half, first_block + block, index.shape[1])
             selector = one_hot(index[pl.ds(position("y") * 2 + half, 1), pl.ds(at, 2 * LANES)], first_block + block)
             out = lax.dot_general(
                 terms[block].astype(jnp.bfloat16), selector, NN, preferred_element_type=jnp.float32
@@ -622,26 +634,22 @@
 ):
     depth = lax.axis_size("z")
     counts = [width // LANES for width in WIDTHS]
-    blocks = sum(counts)
 
     rhs_parts = [rhs_root, rhs_level1, rhs_level2, rhs_level3]
-    both = lax.all_gather(own_product(subtree_values, coupling, rhs_parts), "c", axis=0, tiled=False)
+    product, ahead = own_product(subtree_values, coupling, rhs_parts, coupled_rows)
+    both = lax.all_gather(product, "c", axis=0, tiled=False)
 
     def gathered(whole):
         return lax.all_gather(whole, ("x", "c"), axis=0, tiled=True)
-
-    both, coupled_rows = lax.optimization_barrier((both, coupled_rows))
-    edges = jnp.arange(blocks, dtype=jnp.int32) * LANES
-    ahead = jnp.sum((coupled_rows[:, None, :] < edges[None, :, None]).astype(jnp.int32), axis=2)
 
     groups = ((inv_level3, cross_level3), (inv_level2, cross_level2), (inv_level1, cross_level1, inv_root))
     send, terms, (own3, pack2, pack1) = first(both, coupled_rows, ahead, depth, groups)
     matrix2 = gathered(pack2)
+    path = upper_path(both, terms, coupled_rows, ahead, depth)
+    received, other3, path, pack1 = lax.optimization_barrier(
+        (exchange(send, ("x", "z")), lax.ppermute(own3, "c", [(0, 1), (1, 0)]), path, pack1)
+    )
     matrix1 = gathered(pack1)
-    path = upper_path(both, terms, coupled_rows, ahead, depth)
-    received, other3, path = lax.optimization_barrier(
-        (exchange(send, ("x", "z")), lax.ppermute(own3, "c", [(0, 1), (1, 0)]), path)
-    )
     target3 = exchange(sum_and_copy(received, depth), ("z",))
     send = lowest(target3, own3, other3, path, counts[3], sum(counts[:3]), 2 * depth)
     send, own3, coupling = lax.optimization_barrier((send, own3, coupling))

time: 240 us -> 236 us (0.983)
  other arithmetic: 2.65 us -> 0 us
    reduce_sum x1 -> x0, other arithmetic: 2.64 us -> none  [body(): jnp.sum((coupled_rows[:, None, :] < edges[None, :, None]).astype(jnp.int3...]
    unnamed x22 -> x24, local copies, waits for them, and re-layouts: 12.3 us -> 11.5 us
where the time goes in v10:
time: 236 us; the launch traced here: 235 us
  blocking collectives  112 us (47%)
  Pallas kernels  36.8 us (16%)
  starting transfers between devices  30.1 us (13%)
  waiting for transfers between devices  29.5 us (12%)
  between operations  14 us (6%)
  local copies, waits for them, and re-layouts  12.2 us (5%)
    all_to_all x7, blocking collectives, exchange(): return lax.all_to_all(flat, axes, 0, 0, tiled=True).reshape(operand.shape)  102 us
    all_to_all x6, starting transfers between devices, exchange(): return lax.all_to_all(flat, axes, 0, 0, tiled=True).reshape(operand.shape)  27.7 us
    all_to_all x6, waiting for transfers between devices, exchange(): return lax.all_to_all(flat, axes, 0, 0, tiled=True).reshape(operand.shape)  25.5 us
    unnamed x24, local copies, waits for them, and re-layouts  11.5 us
    all_gather x1, blocking collectives, body(): both = lax.all_gather(product, 'c', axis=0, tiled=False)  10.4 us
    pallas_call x3, Pallas kernels, backward(): call(functools.partial(backward_kernel, blocks, counts, len(matrices)), (...  6.75 us
    pallas_call x3, Pallas kernels, picked(): call(functools.partial(pick_kernel, first_block), f32(2, 8, index.shape[1...  5.34 us
    pallas_call x5, Pallas kernels, fetched(): call(fetch_kernel, f32(rows, width), in_specs=[HBM], out_specs=VMEM, scra...  4.92 us
  transfers between devices with their start and end apart: 11, of which 7 were waited for; matrix products, arithmetic and copies ran while one was open for 0% of the time, Pallas kernels for 12%

profile of v10, /device:TPU:1, one launch (start us, length us, event | category | flops | bytes accessed | tf_op | source)
XLA Modules:
  0.0 234.6 jit_solution(10901435151835930778)
XLA Ops:
  7.2 0.0 copy-start.3
  7.2 0.0 all-gather.6.cloned.1.call-start
  7.2 2.6 %shard_map.173 = (f32[16,2176]{1,0:T(8,128)}, s32[2,128]{1,0:T(2,128)}) custom-call(f32[16,32]{1,0:T(8,128)} %values.3, f32[32,2048]{1,0:T(8,128)} %coupling.1, f32[8,16]{1,0:T(8,128)} %bitcast.17, f32[8,16]{1,0:T(8,128)} %bitcast.18, f32[16,16]{1,0:T(8,128)} %rhs2.1, f32[16,16]{1,0:T(8,128)} %rhs3.1, s32[16,2048]{1,0:T(8,128)} %index.13), custom_call_target="tpu_custom_call" | custom-call | tf_op jit(solution)/shard_map/pallas_call | solution.py:417
  9.8 10.4 %all-gather = f32[32,2176]{1,0:T(8,128)} all-gather(f32[16,2176]{1,0:T(8,128)} %get-tuple-element.51), channel_id=2, replica_groups=mesh['y2'=2,'y1'=2,'y0'=2,'x'=4,'c'=2,'z'=8] {'c'}, dimensions={0}, use_global_device_ids=true | all-gather | bytes 417792 | tf_op jit(solution)/shard_map/all_gather | solution.py:640
  20.3 4.4 %shard_map.174 = (f32[32,8,128]{2,1,0:T(8,128)}, bf16[32,2048]{1,0:T(8,128)(2,1)}, f32[16,9216]{1,0:T(8,128)}, f32[16,8192]{1,0:T(8,128)}, f32[8,10240]{1,0:T(8,128)}) custom-call(s32[2,128]{1,0:T(2,128)} %get-tuple-element.50.counts, f32[2,16,2176]{2,1,0:T(8,128)} %bitcast.11, s32[16,2048]{1,0:T(8,128)} %index.13, f32[16,1024]{1,0:T(8,128)} %refs_0_.1, ...), custom_call_target="tpu_custom_call" | custom-call | tf_op jit(solution)/shard_map/pallas_call | solution.py:484
  24.6 0.0 all-gather.6.cloned.1.call-update
  24.7 2.2 collective-permute-start
  26.9 7.5 %all-to-all-start = ((f32[32,8,128]{2,1,0:T(8,128)}), f32[32,8,128]{2,1,0:T(8,128)S(1)}, u32[]{:S(2)}, u32[]{:S(2)}) async-start(f32[32,8,128]{2,1,0:T(8,128)} %get-tuple-element.52), calls=%async_computation | async-start | bytes 262144 | tf_op jit(solution)/shard_map/all_to_all | solution.py:67
  34.4 0.0 all-gather.8.cloned.1.call-start
  34.5 0.9 copy-done.8
  35.4 4.0 %shard_map.175.path = f32[64,8,128]{2,1,0:T(8,128)S(1)} custom-call(s32[2,128]{1,0:T(2,128)S(1)} %copy-done.9, f32[2,16,2176]{2,1,0:T(8,128)S(1)} %bitcast.12, bf16[32,2048]{1,0:T(8,128)(2,1)S(1)} %copy-done.8, s32[16,2048]{1,0:T(8,128)S(1)} %copy-done.3), custom_call_target="tpu_custom_call" | custom-call | flops 8388608 | bytes 4194304 | tf_op jit(solution)/shard_map/pallas_call | solution.py:502
  39.4 4.1 %all-to-all-done.received = f32[32,8,128]{2,1,0:T(8,128)S(1)} async-done(((f32[32,8,128]{2,1,0:T(8,128)}), f32[32,8,128]{2,1,0:T(8,128)S(1)}, u32[]{:S(2)}, u32[]{:S(2)}) %all-to-all-start) | async-done | bytes 131104 | tf_op jit(solution)/shard_map/all_to_all | solution.py:67
  43.6 0.0 all-gather.8.cloned.1.call-update
  43.6 0.0 all-gather.10.cloned.1.call-start
  43.7 9.9 %all_to_all.86.received.solved = f32[8,8,128]{2,1,0:T(8,128)S(1)} all-to-all(f32[8,8,128]{2,1,0:T(8,128)S(1)} %shard_map.176), channel_id=1, replica_groups=mesh['y2'=2,'y1'=2,'y0'=2,'x'=4,'c'=2,'z'=8] {'z'}, dimensions={0} | all-to-all | bytes 65536 | tf_op jit(solution)/shard_map/all_to_all | solution.py:67
  53.6 1.5 shard_map.177
  55.1 0.0 all-gather.10.cloned.1.call-update
  55.2 16.0 %all_to_all.87.received = f32[64,8,128]{2,1,0:T(8,128)S(1)} all-to-all(f32[64,8,128]{2,1,0:T(8,128)S(1)} %shard_map.177), channel_id=1, replica_groups=mesh['y2'=2,'y1'=2,'y0'=2,'x'=4,'c'=2,'z'=8] {'y0','x','z'}, dimensions={0} | all-to-all | bytes 524288 | tf_op jit(solution)/shard_map/all_to_all | solution.py:67
  71.1 0.7 shard_map.178
  71.8 3.5 %all-to-all-start.3 = ((f32[16,8,128]{2,1,0:T(8,128)}), f32[16,8,128]{2,1,0:T(8,128)S(1)}, u32[]{:S(2)}, u32[]{:S(2)}) async-start(f32[16,8,128]{2,1,0:T(8,128)} %shard_map.178), calls=%async_computation.3 | async-start | bytes 131072 | tf_op jit(solution)/shard_map/all_to_all | solution.py:67
  75.3 0.7 slice_bitcast_fusion.rest_in
  76.0 2.3 copy-done
  78.3 0.2 shard_map.179.refs_0_
  78.6 4.1 %all-to-all-done.3.received = f32[16,8,128]{2,1,0:T(8,128)S(1)} async-done(((f32[16,8,128]{2,1,0:T(8,128)}), f32[16,8,128]{2,1,0:T(8,128)S(1)}, u32[]{:S(2)}, u32[]{:S(2)}) %all-to-all-start.3) | async-done | bytes 65568 | tf_op jit(solution)/shard_map/all_to_all | solution.py:67
  82.7 2.8 %shard_map.180 = (f32[2,128,128]{2,1,0:T(8,128)S(1)}, f32[32,32,128]{2,1,0:T(8,128)}, f32[96,128]{1,0:T(8,128)S(1)}) custom-call(f32[16,8,128]{2,1,0:T(8,128)S(1)} %all-to-all-done.3.received, f32[8,128]{1,0:T(8,128)S(1)} %slice_bitcast_fusion.rest_in, f32[64,8192]{1,0:T(8,128)S(1)} %shard_map.179.refs_0_, ...), custom_call_target="tpu_custom_call" | custom-call | flops 8388608 | bytes 4194304 | tf_op jit(solution)/shard_map/pallas_call | solution.py:203
  85.4 5.7 %all-to-all-start.4 = ((f32[32,32,128]{2,1,0:T(8,128)}), f32[32,32,128]{2,1,0:T(8,128)S(1)}, u32[]{:S(2)}, u32[]{:S(2)}) async-start(f32[32,32,128]{2,1,0:T(8,128)} %get-tuple-element.63), calls=%async_computation.4 | async-start | bytes 1048576 | tf_op jit(solution)/shard_map/all_to_all | solution.py:67
  91.2 0.0 all-gather.12.cloned.1.call-start
  91.2 0.5 all-gather.12.cloned.1.call-update
  91.8 3.3 %all-gather.8.cloned.1.call-done.matrix = f32[64,10240]{1,0:T(8,128)} async-done(((f32[8,10240]{1,0:T(8,128)}), f32[64,10240]{1,0:T(8,128)}) %all-gather.8.cloned.1.call-update) | async-done | bytes 2621456 | tf_op jit(solution)/shard_map/all_gather | solution.py:643
  95.1 1.7 copy-done.4
  96.8 0.9 shard_map.181.refs_0_.matrix
  97.7 6.1 %all-to-all-done.4.received = f32[32,32,128]{2,1,0:T(8,128)S(1)} async-done(((f32[32,32,128]{2,1,0:T(8,128)}), f32[32,32,128]{2,1,0:T(8,128)S(1)}, u32[]{:S(2)}, u32[]{:S(2)}) %all-to-all-start.4) | async-done | bytes 524320 | tf_op jit(solution)/shard_map/all_to_all | solution.py:67
  103.9 1.0 shard_map.182
  104.8 22.5 %all_to_all.88.received = f32[64,8,128]{2,1,0:T(8,128)S(1)} all-to-all(f32[64,8,128]{2,1,0:T(8,128)S(1)} %bitcast.14), channel_id=1, replica_groups=mesh['y2'=2,'y1'=2,'y0'=2,'x'=4,'c'=2,'z'=8] {'y2','y1','y0','z'}, dimensions={0} | all-to-all | bytes 524288 | tf_op jit(solution)/shard_map/all_to_all | solution.py:67
  127.3 0.1 shard_map.183
  127.4 9.5 %all_to_all.89 = f32[8,8,128]{2,1,0:T(8,128)S(1)} all-to-all(f32[8,8,128]{2,1,0:T(8,128)S(1)} %shard_map.183), channel_id=1, replica_groups=mesh['y2'=2,'y1'=2,'y0'=2,'x'=4,'c'=2,'z'=8] {'z'}, dimensions={0} | all-to-all | bytes 65536 | tf_op jit(solution)/shard_map/all_to_all | solution.py:67
  136.9 0.4 shard_map.184
  137.2 16.3 %all_to_all.90.received = f32[64,8,128]{2,1,0:T(8,128)S(1)} all-to-all(f32[64,8,128]{2,1,0:T(8,128)S(1)} %bitcast.13), channel_id=1, replica_groups=mesh['y2'=2,'y1'=2,'y0'=2,'x'=4,'c'=2,'z'=8] {'y2','y1','y0','z'}, dimensions={0} | all-to-all | bytes 524288 | tf_op jit(solution)/shard_map/all_to_all | solution.py:67
  153.5 0.1 shard_map.185
  153.6 9.5 %all_to_all.91 = f32[8,8,128]{2,1,0:T(8,128)S(1)} all-to-all(f32[8,8,128]{2,1,0:T(8,128)S(1)} %shard_map.185), channel_id=1, replica_groups=mesh['y2'=2,'y1'=2,'y0'=2,'x'=4,'c'=2,'z'=8] {'z'}, dimensions={0} | all-to-all | bytes 65536 | tf_op jit(solution)/shard_map/all_to_all | solution.py:67
  163.1 1.2 shard_map.186
  164.3 3.9 %all-to-all-start.9 = ((f32[32,32,128]{2,1,0:T(8,128)}), f32[32,32,128]{2,1,0:T(8,128)S(1)}, u32[]{:S(2)}, u32[]{:S(2)}) async-start(f32[32,32,128]{2,1,0:T(8,128)} %get-tuple-element.70), calls=%async_computation.9 | async-start | bytes 1048576 | tf_op jit(solution)/shard_map/all_to_all | solution.py:67
  168.2 2.2 copy-done.1
  170.4 0.2 shard_map.188.refs_0_
  170.6 0.4 copy-done.10
  171.1 2.3 shard_map.187.chosen0
  173.4 7.1 %all-to-all-done.9.received = f32[32,32,128]{2,1,0:T(8,128)S(1)} async-done(((f32[32,32,128]{2,1,0:T(8,128)}), f32[32,32,128]{2,1,0:T(8,128)S(1)}, u32[]{:S(2)}, u32[]{:S(2)}) %all-to-all-start.9) | async-done | bytes 524320 | tf_op jit(solution)/shard_map/all_to_all | solution.py:67
  180.5 2.8 %shard_map.189 = (f32[16,32,128]{2,1,0:T(8,128)}, f32[32,128]{1,0:T(8,128)S(1)}) custom-call(f32[32,32,128]{2,1,0:T(8,128)S(1)} %all-to-all-done.9.received, f32[2,128,128]{2,1,0:T(8,128)S(1)} %get-tuple-element.75.solved, f32[64,8192]{1,0:T(8,128)S(1)} %shard_map.188.refs_0_, f32[128,8192]{1,0:T(8,128)} %all-gather.6.cloned.1.call-done.matrix.refs_1_, ...), custom_call_target="tpu_custom_call" | custom-call | flops 8388608 | bytes 4194304 | tf_op jit(solution)/shard_map/pallas_call | solution.py:305
  183.2 3.7 %all-to-all-start.10 = ((f32[16,32,128]{2,1,0:T(8,128)}), f32[16,32,128]{2,1,0:T(8,128)S(1)}, u32[]{:S(2)}, u32[]{:S(2)}) async-start(f32[16,32,128]{2,1,0:T(8,128)} %get-tuple-element.77), calls=%async_computation.10 | async-start | bytes 524288 | tf_op jit(solution)/shard_map/all_to_all | solution.py:67
  187.0 0.0 all-gather.10.cloned.1.call-done.matrix.refs_1_
  187.0 2.3 copy-done.2
  189.3 0.6 shard_map.191.refs_0_
  189.9 1.5 shard_map.190.chosen1
  191.4 3.1 %all-to-all-done.10.received = f32[16,32,128]{2,1,0:T(8,128)S(1)} async-done(((f32[16,32,128]{2,1,0:T(8,128)}), f32[16,32,128]{2,1,0:T(8,128)S(1)}, u32[]{:S(2)}, u32[]{:S(2)}) %all-to-all-start.10) | async-done | bytes 262176 | tf_op jit(solution)/shard_map/all_to_all | solution.py:67
  194.5 2.8 %shard_map.192 = (f32[8,16,128]{2,1,0:T(8,128)}, f32[32,128]{1,0:T(8,128)S(1)}) custom-call(f32[16,32,128]{2,1,0:T(8,128)S(1)} %all-to-all-done.10.received, f32[8,8,128]{2,1,0:T(8,128)S(1)} %all_to_all.86.received.solved, f32[64,9216]{1,0:T(8,128)S(1)} %shard_map.191.refs_0_, f32[128,9216]{1,0:T(8,128)} %all-gather.10.cloned.1.call-done.matrix.refs_1_, ...), custom_call_target="tpu_custom_call" | custom-call | flops 9437184 | bytes 4718592 | tf_op jit(solution)/shard_map/pallas_call | solution.py:305
  197.3 3.4 %all-to-all-start.11 = ((f32[8,16,128]{2,1,0:T(8,128)}), f32[8,16,128]{2,1,0:T(8,128)S(1)}, u32[]{:S(2)}, u32[]{:S(2)}) async-start(f32[8,16,128]{2,1,0:T(8,128)} %get-tuple-element.82), calls=%async_computation.11 | async-start | bytes 131072 | tf_op jit(solution)/shard_map/all_to_all | solution.py:67
  200.6 0.0 all-gather.12.cloned.1.call-done.matrix
  200.7 1.6 copy-done.7
  202.3 3.0 %shard_map.194.coupling = f32[256,2048]{1,0:T(8,128)S(1)} custom-call(f32[256,2048]{1,0:T(8,128)S(1)} %copy-done.7), custom_call_target="tpu_custom_call" | custom-call | flops 8388608 | bytes 4194304 | tf_op jit(solution)/shard_map/pallas_call | solution.py:157
  205.3 1.5 shard_map.193.chosen2
  206.8 1.0 all-to-all-done.11.received
  207.8 1.6 shard_map.195
  209.3 18.0 %all_to_all.92.received = f32[8,16,128]{2,1,0:T(8,128)S(1)} all-to-all(f32[8,16,128]{2,1,0:T(8,128)S(1)} %shard_map.195), channel_id=1, replica_groups=mesh['y2'=2,'y1'=2,'y0'=2,'x'=4,'c'=2,'z'=8] {'c','x'}, dimensions={0} | all-to-all | bytes 131072 | tf_op jit(solution)/shard_map/all_to_all | solution.py:67
  227.3 0.8 shard_map.196
  (19 shorter events, 0.1 us)
Async XLA Ops:
  7.2 27.3 %copy-start.3 = (s32[16,2048]{1,0:T(8,128)S(1)}, s32[16,2048]{1,0:T(8,128)}, u32[]{:S(2)}) copy-start(s32[16,2048]{1,0:T(8,128)} %index.13) | copy-start | bytes 393220
  7.2 68.8 %all-gather.6.cloned.1.call-start = ((), (), s32[]{:S(2)}) async-start(), calls=%async_computation.13 | async-start | bytes 4718592 | tf_op jit(solution)/shard_map/all_gather | solution.py:643
  9.8 24.6 %copy-start.9 = (s32[2,128]{1,0:T(2,128)S(1)}, s32[2,128]{1,0:T(2,128)}, u32[]{:S(2)}) copy-start(s32[2,128]{1,0:T(2,128)} %get-tuple-element.50.counts) | copy-start | bytes 3076
  20.3 14.2 %copy-start.5 = (f32[32,2176]{1,0:T(8,128)S(1)}, f32[32,2176]{1,0:T(8,128)}, u32[]{:S(2)}) copy-start(f32[32,2176]{1,0:T(8,128)} %all-gather) | copy-start | bytes 835588
  24.6 29.0 %copy-start.6 = (f32[16,9216]{1,0:T(8,128)S(1)}, f32[16,9216]{1,0:T(8,128)}, u32[]{:S(2)}) copy-start(f32[16,9216]{1,0:T(8,128)} %get-tuple-element.79.own) | copy-start | bytes 1769476
  24.7 18.9 %collective-permute-start = (f32[16,9216]{1,0:T(8,128)}, f32[16,9216]{1,0:T(8,128)S(1)}, u32[]{:S(2)}, u32[]{:S(2)}) collective-permute-start(f32[16,9216]{1,0:T(8,128)} %get-tuple-element.79.own), channel_id=1, source_target_pairs={{0,8},{8,0},{1,9},{9,1},{2,10},{10,2},{3,11},{11,3},{4,12},{12,4},... | collective-permute-start | bytes 1769480 | tf_op jit(solution)/shard_map/ppermute | solution.py:650
  26.9 16.7 %all-to-all-start = ((f32[32,8,128]{2,1,0:T(8,128)}), f32[32,8,128]{2,1,0:T(8,128)S(1)}, u32[]{:S(2)}, u32[]{:S(2)}) async-start(f32[32,8,128]{2,1,0:T(8,128)} %get-tuple-element.52), calls=%async_computation | async-start | bytes 262144 | tf_op jit(solution)/shard_map/all_to_all | solution.py:67
  34.4 60.7 %all-gather.8.cloned.1.call-start = ((), (), s32[]{:S(2)}) async-start(), calls=%async_computation.14 | async-start | bytes 2949120 | tf_op jit(solution)/shard_map/all_gather | solution.py:643
  34.5 0.9 copy-start.8
  43.6 143.4 %all-gather.10.cloned.1.call-start = ((), (), s32[]{:S(2)}) async-start(), calls=%async_computation.15 | async-start | bytes 5308416 | tf_op jit(solution)/shard_map/all_gather | solution.py:643
  71.8 10.8 %all-to-all-start.3 = ((f32[16,8,128]{2,1,0:T(8,128)}), f32[16,8,128]{2,1,0:T(8,128)S(1)}, u32[]{:S(2)}, u32[]{:S(2)}) async-start(f32[16,8,128]{2,1,0:T(8,128)} %shard_map.178), calls=%async_computation.3 | async-start | bytes 131072 | tf_op jit(solution)/shard_map/all_to_all | solution.py:67
  76.0 2.3 copy-start
  85.4 18.4 %all-to-all-start.4 = ((f32[32,32,128]{2,1,0:T(8,128)}), f32[32,32,128]{2,1,0:T(8,128)S(1)}, u32[]{:S(2)}, u32[]{:S(2)}) async-start(f32[32,32,128]{2,1,0:T(8,128)} %get-tuple-element.63), calls=%async_computation.4 | async-start | bytes 1048576 | tf_op jit(solution)/shard_map/all_to_all | solution.py:67
  91.2 109.5 %all-gather.12.cloned.1.call-start = ((), (), s32[]{:S(2)}) async-start(), calls=%async_computation.16 | async-start | bytes 2359296 | tf_op jit(solution)/shard_map/all_gather | solution.py:643
  95.1 1.7 copy-start.4
  164.3 16.2 %all-to-all-start.9 = ((f32[32,32,128]{2,1,0:T(8,128)}), f32[32,32,128]{2,1,0:T(8,128)S(1)}, u32[]{:S(2)}, u32[]{:S(2)}) async-start(f32[32,32,128]{2,1,0:T(8,128)} %get-tuple-element.70), calls=%async_computation.9 | async-start | bytes 1048576 | tf_op jit(solution)/shard_map/all_to_all | solution.py:67
  168.2 2.2 copy-start.1
  170.4 0.7 copy-start.10
  183.2 11.3 %all-to-all-start.10 = ((f32[16,32,128]{2,1,0:T(8,128)}), f32[16,32,128]{2,1,0:T(8,128)S(1)}, u32[]{:S(2)}, u32[]{:S(2)}) async-start(f32[16,32,128]{2,1,0:T(8,128)} %get-tuple-element.77), calls=%async_computation.10 | async-start | bytes 524288 | tf_op jit(solution)/shard_map/all_to_all | solution.py:67
  187.0 2.3 copy-start.2
  197.3 10.5 %all-to-all-start.11 = ((f32[8,16,128]{2,1,0:T(8,128)}), f32[8,16,128]{2,1,0:T(8,128)S(1)}, u32[]{:S(2)}, u32[]{:S(2)}) async-start(f32[8,16,128]{2,1,0:T(8,128)} %get-tuple-element.82), calls=%async_computation.11 | async-start | bytes 131072 | tf_op jit(solution)/shard_map/all_to_all | solution.py:67
  200.7 1.6 copy-start.7
  205.3 22.1 %copy-start.11 = (f32[16,32]{1,0:T(8,128)S(1)}, f32[16,32]{1,0:T(8,128)}, u32[]{:S(2)}) copy-start(f32[16,32]{1,0:T(8,128)} %values.3) | copy-start | bytes 6148
Sparse Core Ops, SparseCore 0:
  24.8 37.0 all-gather.5
  64.0 31.0 all-gather.7
  97.2 40.2 all-gather.9
  139.5 30.5 all-gather.11

commit v11 on v10

--- a/solution.py
+++ b/solution.py
@@ -390,35 +390,6 @@
         source += width
 
 
-def product_kernel(values, coupling, rhs0, rhs1, rhs2, rhs3, index, out, ahead):
-    columns = coupling.shape[1]
-    out[:, :columns] = lax.dot_general(
-        values[...], coupling[...], NN, precision=lax.Precision.HIGHEST, preferred_element_type=jnp.float32
-    )
-    parts = [jnp.transpose(rhs0[...]), jnp.transpose(rhs1[...]), rhs2[...], rhs3[...]]
-    filled = sum(part.shape[1] for part in parts)
-    parts.append(jnp.zeros((out.shape[0], LANES - filled), jnp.float32))
-    out[:, columns:] = jnp.concatenate(parts, axis=1)
-    edges = lax.broadcasted_iota(jnp.int32, (LANES, 2 * LANES), 0) * LANES
-    for half in range(2):
-        def compare(block, total):
-            at = pl.multiple_of(block * 2 * LANES, LANES)
-            row = index[pl.ds(position("y") * 2 + half, 1), pl.ds(at, 2 * LANES)]
-            return total + jnp.where(row < edges, 1.0, 0.0)
-
-        total = lax.fori_loop(0, columns // (2 * LANES), compare, jnp.zeros((LANES, 2 * LANES), jnp.float32), unroll=2)
-        total = jnp.broadcast_to(jnp.sum(total, axis=1, keepdims=True), (LANES, LANES))
-        ahead[half : half + 1, :] = jnp.transpose(total)[0:1, :].astype(jnp.int32)
-
-
-def own_product(values, coupling, rhs_parts, index):
-    rhs0, rhs1, rhs2, rhs3 = rhs_parts
-    shapes = (f32(values.shape[0], coupling.shape[1] + LANES), jax.ShapeDtypeStruct((2, LANES), jnp.int32))
-    return call(product_kernel, shapes, in_specs=[VMEM] * 7, out_specs=(VMEM, VMEM), limit=WHOLE)(
-        values, coupling, rhs0.T, rhs1.T, rhs2, rhs3, index
-    )
-
-
 def stage_in(parts, stages, groups, ready):
     copies = []
     for stage, size in zip(stages, groups):
@@ -460,36 +431,69 @@
     return parts, packs, scratch + [pltpu.VMEM(pack.shape, jnp.float32) for pack in packs]
 
 
-def first_kernel(depth, groups, counts, both, index, *refs):
+def product_kernel(groups, values, coupling, rhs0, rhs1, rhs2, rhs3, index, *refs):
     count, number = sum(groups), len(groups)
-    parts, (send, terms, *packs), (path, ready, done, *stages) = refs[:count], refs[count : -3 - number], refs[-3 - number :]
+    parts, (out, ahead, *packs), (ready, done, *stages) = refs[:count], refs[count : -2 - number], refs[-2 - number :]
     copies = stage_in(parts, stages, groups, ready)
+    columns = coupling.shape[1]
+    out[:, :columns] = lax.dot_general(
+        values[...], coupling[...], NN, precision=lax.Precision.HIGHEST, preferred_element_type=jnp.float32
+    )
+    copies = stage_out(copies, stages, packs, done)
+    sides = [jnp.transpose(rhs0[...]), jnp.transpose(rhs1[...]), rhs2[...], rhs3[...]]
+    filled = sum(side.shape[1] for side in sides)
+    sides.append(jnp.zeros((out.shape[0], LANES - filled), jnp.float32))
+    out[:, columns:] = jnp.concatenate(sides, axis=1)
+    edges = lax.broadcasted_iota(jnp.int32, (LANES, 2 * LANES), 0) * LANES
+    for half in range(2):
+        def compare(block, total):
+            at = pl.multiple_of(block * 2 * LANES, LANES)
+            row = index[pl.ds(position("y") * 2 + half, 1), pl.ds(at, 2 * LANES)]
+            return total + jnp.where(row < edges, 1.0, 0.0)
+
+        total = lax.fori_loop(0, columns // (2 * LANES), compare, jnp.zeros((LANES, 2 * LANES), jnp.float32), unroll=2)
+        total = jnp.broadcast_to(jnp.sum(total, axis=1, keepdims=True), (LANES, LANES))
+        ahead[half : half + 1, :] = jnp.transpose(total)[0:1, :].astype(jnp.int32)
+    for copy in copies:
+        copy.wait()
+
+
+def own_product(values, coupling, rhs_parts, index, groups):
+    rhs0, rhs1, rhs2, rhs3 = rhs_parts
+    parts, packs, scratch = pack_shapes(groups)
+    shapes = (f32(values.shape[0], coupling.shape[1] + LANES), jax.ShapeDtypeStruct((2, LANES), jnp.int32))
+    outs = call(
+        functools.partial(product_kernel, [len(group) for group in groups]),
+        (*shapes, *packs),
+        in_specs=[VMEM] * 7 + [HBM] * len(parts),
+        out_specs=(VMEM, VMEM) + (HBM,) * len(packs),
+        scratch_shapes=scratch,
+        limit=WHOLE,
+    )(values, coupling, rhs0.T, rhs1.T, rhs2, rhs3, index, *parts)
+    return outs[0], outs[1], outs[2:]
+
+
+def first_kernel(depth, counts, both, index, send, terms, path):
     columns = both.shape[2] - LANES
     half = pl.multiple_of(position("c") * 8, 8)
     pieces = split3(both[0, pl.ds(half, 8), :columns] + both[1, pl.ds(half, 8), :columns])
     terms[...] = jnp.concatenate([*pieces, jnp.zeros_like(pieces[0])], axis=0)
     expand(counts, terms, index, sum(WIDTHS[:3]) // LANES, path)
-    copies = stage_out(copies, stages, packs, done)
     add_own(both, depth, (3,), path)
     for dest in range(X):
         for other in range(depth):
             send[dest * depth + other] = path[other]
-    for copy in copies:
-        copy.wait()
-
-
-def first(both, index, counts, depth, groups):
+
+
+def first(both, index, counts, depth):
     columns = both.shape[2] - LANES
-    parts, packs, scratch = pack_shapes(groups)
-    outs = call(
-        functools.partial(first_kernel, depth, [len(group) for group in groups]),
-        (f32(X * depth, 8, LANES), jax.ShapeDtypeStruct((32, columns), jnp.bfloat16), *packs),
-        in_specs=[SMEM, VMEM, VMEM] + [HBM] * len(parts),
-        out_specs=(VMEM, VMEM) + (HBM,) * len(packs),
-        scratch_shapes=[pltpu.VMEM((WIDTHS[3] // LANES, 8, LANES), jnp.float32)] + scratch,
-        limit=WHOLE,
-    )(counts, both, index, *parts)
-    return outs[0], outs[1], outs[2:]
+    return call(
+        functools.partial(first_kernel, depth),
+        (f32(X * depth, 8, LANES), jax.ShapeDtypeStruct((32, columns), jnp.bfloat16)),
+        in_specs=[SMEM, VMEM, VMEM],
+        out_specs=(VMEM, VMEM),
+        scratch_shapes=[pltpu.VMEM((WIDTHS[3] // LANES, 8, LANES), jnp.float32)],
+    )(counts, both, index)
 
 
 def upper_kernel(depth, counts, both, terms, index, path):
@@ -636,14 +640,14 @@
     counts = [width // LANES for width in WIDTHS]
 
     rhs_parts = [rhs_root, rhs_level1, rhs_level2, rhs_level3]
-    product, ahead = own_product(subtree_values, coupling, rhs_parts, coupled_rows)
+    groups = ((inv_level3, cross_level3), (inv_level2, cross_level2), (inv_level1, cross_level1, inv_root))
+    product, ahead, (own3, pack2, pack1) = own_product(subtree_values, coupling, rhs_parts, coupled_rows, groups)
     both = lax.all_gather(product, "c", axis=0, tiled=False)
 
     def gathered(whole):
         return lax.all_gather(whole, ("x", "c"), axis=0, tiled=True)
 
-    groups = ((inv_level3, cross_level3), (inv_level2, cross_level2), (inv_level1, cross_level1, inv_root))
-    send, terms, (own3, pack2, pack1) = first(both, coupled_rows, ahead, depth, groups)
+    send, terms = first(both, coupled_rows, ahead, depth)
     matrix2 = gathered(pack2)
     path = upper_path(both, terms, coupled_rows, ahead, depth)
     received, other3, path, pack1 = lax.optimization_barrier(

time: 236 us -> 235 us (level)
  blocking collectives: 112 us -> 103 us
  starting transfers between devices: 30.1 us -> 37.2 us
    all_gather x1, blocking collectives: 10.4 us -> 2.22 us  [body(): both = lax.all_gather(product, 'c', axis=0, tiled=False)]
    ppermute x1, starting transfers between devices: 2.19 us -> 8.92 us  [body(): lax.ppermute(own3, 'c', [(0, 1), (1, 0)])]
    all_to_all x6, waiting for transfers between devices: 25.5 us -> 29.7 us  [exchange(): return lax.all_to_all(flat, axes, 0, 0, tiled=True).reshape(operand.shape)]
    all_gather x4, waiting for transfers between devices: 3.35 us -> 0.06 us  [gathered(): return lax.all_gather(whole, ('x', 'c'), axis=0, tiled=True)]
    unnamed x24 -> x22, local copies, waits for them, and re-layouts: 11.5 us -> 11.8 us
  transfers between devices with their start and end apart: 11 -> 11, of which waited for: 7 -> 6; matrix products, arithmetic and copies ran while one was open for 0% -> 0% of each run, Pallas kernels for 12% -> 13%
where the time goes in v11:
time: 235 us; the launch traced here: 233 us
  blocking collectives  103 us (44%)
  starting transfers between devices  37.2 us (16%)
  Pallas kernels  35.8 us (15%)
  waiting for transfers between devices  30.3 us (13%)
  between operations  14 us (6%)
  local copies, waits for them, and re-layouts  12.5 us (5%)
    all_to_all x7, blocking collectives, exchange(): return lax.all_to_all(flat, axes, 0, 0, tiled=True).reshape(operand.shape)  101 us
    all_to_all x6, waiting for transfers between devices, exchange(): return lax.all_to_all(flat, axes, 0, 0, tiled=True).reshape(operand.shape)  29.7 us
    all_to_all x6, starting transfers between devices, exchange(): return lax.all_to_all(flat, axes, 0, 0, tiled=True).reshape(operand.shape)  28.1 us
    unnamed x22, local copies, waits for them, and re-layouts  11.8 us
    ppermute x1, starting transfers between devices, body(): lax.ppermute(own3, 'c', [(0, 1), (1, 0)])  8.92 us
    pallas_call x3, Pallas kernels, backward(): call(functools.partial(backward_kernel, blocks, counts, len(matrices)), (...  6.67 us
    pallas_call x3, Pallas kernels, picked(): call(functools.partial(pick_kernel, first_block), f32(2, 8, index.shape[1...  5.34 us
    pallas_call x5, Pallas kernels, fetched(): call(fetch_kernel, f32(rows, width), in_specs=[HBM], out_specs=VMEM, scra...  4.92 us
  transfers between devices with their start and end apart: 11, of which 6 were waited for; matrix products, arithmetic and copies ran while one was open for 0% of the time, Pallas kernels for 13%

profile of v11, /device:TPU:1, one launch (start us, length us, event | category | flops | bytes accessed | tf_op | source)
XLA Modules:
  0.0 233.2 jit_solution(13442952213934926481)
XLA Ops:
  7.2 0.0 all-gather.6.cloned.1.call-start
  7.2 4.3 %shard_map.173 = (f32[16,2176]{1,0:T(8,128)}, s32[2,128]{1,0:T(2,128)}, f32[16,9216]{1,0:T(8,128)}, f32[16,8192]{1,0:T(8,128)}, f32[8,10240]{1,0:T(8,128)}) custom-call(f32[16,32]{1,0:T(8,128)} %values.3, f32[32,2048]{1,0:T(8,128)} %coupling.1, f32[8,16]{1,0:T(8,128)} %bitcast.17, f32[8,16]{1,0:T(8,128)} %bitcast.18, f32[16,16]{1,0:T(8,128)} %rhs2.1, ...), custom_call_target="tpu_custom_call" | custom-call | tf_op jit(solution)/shard_map/pallas_call | solution.py:465
  11.6 0.0 all-gather.6.cloned.1.call-update
  11.6 8.9 %collective-permute-start = (f32[16,9216]{1,0:T(8,128)}, f32[16,9216]{1,0:T(8,128)S(1)}, u32[]{:S(2)}, u32[]{:S(2)}) collective-permute-start(f32[16,9216]{1,0:T(8,128)} %get-tuple-element.79.own), channel_id=1, source_target_pairs={{0,8},{8,0},{1,9},{9,1},{2,10},{10,2},{3,11},{11,3},{4,12},{12,4},... | collective-permute-start | bytes 1769480 | tf_op jit(solution)/shard_map/ppermute | solution.py:654
  20.5 2.2 all-gather
  22.7 0.7 copy-done.7
  23.4 1.8 shard_map.174
  25.2 7.5 %all-to-all-start = ((f32[32,8,128]{2,1,0:T(8,128)}), f32[32,8,128]{2,1,0:T(8,128)S(1)}, u32[]{:S(2)}, u32[]{:S(2)}) async-start(f32[32,8,128]{2,1,0:T(8,128)} %get-tuple-element.52), calls=%async_computation | async-start | bytes 262144 | tf_op jit(solution)/shard_map/all_to_all | solution.py:67
  32.7 0.0 all-gather.8.cloned.1.call-start
  32.8 0.7 copy-done.8
  33.4 4.0 %shard_map.175.path = f32[64,8,128]{2,1,0:T(8,128)S(1)} custom-call(s32[2,128]{1,0:T(2,128)S(1)} %copy-done.8, f32[2,16,2176]{2,1,0:T(8,128)S(1)} %bitcast.12, bf16[32,2048]{1,0:T(8,128)(2,1)S(1)} %get-tuple-element.54.terms, s32[16,2048]{1,0:T(8,128)S(1)} %copy-done.3), custom_call_target="tpu_custom_call" | custom-call | flops 8388608 | bytes 4194304 | tf_op jit(solution)/shard_map/pallas_call | solution.py:506
  37.5 4.4 %all-to-all-done.received = f32[32,8,128]{2,1,0:T(8,128)S(1)} async-done(((f32[32,8,128]{2,1,0:T(8,128)}), f32[32,8,128]{2,1,0:T(8,128)S(1)}, u32[]{:S(2)}, u32[]{:S(2)}) %all-to-all-start) | async-done | bytes 131104 | tf_op jit(solution)/shard_map/all_to_all | solution.py:67
  41.9 0.0 all-gather.8.cloned.1.call-update
  41.9 0.0 all-gather.10.cloned.1.call-start
  42.0 10.0 %all_to_all.86.received.solved = f32[8,8,128]{2,1,0:T(8,128)S(1)} all-to-all(f32[8,8,128]{2,1,0:T(8,128)S(1)} %shard_map.176), channel_id=1, replica_groups=mesh['y2'=2,'y1'=2,'y0'=2,'x'=4,'c'=2,'z'=8] {'z'}, dimensions={0} | all-to-all | bytes 65536 | tf_op jit(solution)/shard_map/all_to_all | solution.py:67
  52.0 1.5 shard_map.177
  53.5 0.0 all-gather.10.cloned.1.call-update
  53.5 15.7 %all_to_all.87.received = f32[64,8,128]{2,1,0:T(8,128)S(1)} all-to-all(f32[64,8,128]{2,1,0:T(8,128)S(1)} %shard_map.177), channel_id=1, replica_groups=mesh['y2'=2,'y1'=2,'y0'=2,'x'=4,'c'=2,'z'=8] {'y0','x','z'}, dimensions={0} | all-to-all | bytes 524288 | tf_op jit(solution)/shard_map/all_to_all | solution.py:67
  69.2 0.7 shard_map.178
  69.9 4.0 %all-to-all-start.3 = ((f32[16,8,128]{2,1,0:T(8,128)}), f32[16,8,128]{2,1,0:T(8,128)S(1)}, u32[]{:S(2)}, u32[]{:S(2)}) async-start(f32[16,8,128]{2,1,0:T(8,128)} %shard_map.178), calls=%async_computation.3 | async-start | bytes 131072 | tf_op jit(solution)/shard_map/all_to_all | solution.py:67
  74.0 0.7 slice_bitcast_fusion.rest_in
  74.6 2.2 copy-done
  76.8 0.2 shard_map.179.refs_0_
  77.1 4.3 %all-to-all-done.3.received = f32[16,8,128]{2,1,0:T(8,128)S(1)} async-done(((f32[16,8,128]{2,1,0:T(8,128)}), f32[16,8,128]{2,1,0:T(8,128)S(1)}, u32[]{:S(2)}, u32[]{:S(2)}) %all-to-all-start.3) | async-done | bytes 65568 | tf_op jit(solution)/shard_map/all_to_all | solution.py:67
  81.3 2.8 %shard_map.180 = (f32[2,128,128]{2,1,0:T(8,128)S(1)}, f32[32,32,128]{2,1,0:T(8,128)}, f32[96,128]{1,0:T(8,128)S(1)}) custom-call(f32[16,8,128]{2,1,0:T(8,128)S(1)} %all-to-all-done.3.received, f32[8,128]{1,0:T(8,128)S(1)} %slice_bitcast_fusion.rest_in, f32[64,8192]{1,0:T(8,128)S(1)} %shard_map.179.refs_0_, ...), custom_call_target="tpu_custom_call" | custom-call | flops 8388608 | bytes 4194304 | tf_op jit(solution)/shard_map/pallas_call | solution.py:203
  84.1 5.6 %all-to-all-start.4 = ((f32[32,32,128]{2,1,0:T(8,128)}), f32[32,32,128]{2,1,0:T(8,128)S(1)}, u32[]{:S(2)}, u32[]{:S(2)}) async-start(f32[32,32,128]{2,1,0:T(8,128)} %get-tuple-element.63), calls=%async_computation.4 | async-start | bytes 1048576 | tf_op jit(solution)/shard_map/all_to_all | solution.py:67
  89.7 0.0 all-gather.12.cloned.1.call-start
  89.8 0.5 all-gather.12.cloned.1.call-update
  90.3 0.0 all-gather.8.cloned.1.call-done.matrix
  90.3 1.7 copy-done.4
  92.1 0.9 shard_map.181.refs_0_.matrix
  93.0 9.6 %all-to-all-done.4.received = f32[32,32,128]{2,1,0:T(8,128)S(1)} async-done(((f32[32,32,128]{2,1,0:T(8,128)}), f32[32,32,128]{2,1,0:T(8,128)S(1)}, u32[]{:S(2)}, u32[]{:S(2)}) %all-to-all-start.4) | async-done | bytes 524320 | tf_op jit(solution)/shard_map/all_to_all | solution.py:67
  102.6 0.9 shard_map.182
  103.5 22.3 %all_to_all.88.received = f32[64,8,128]{2,1,0:T(8,128)S(1)} all-to-all(f32[64,8,128]{2,1,0:T(8,128)S(1)} %bitcast.14), channel_id=1, replica_groups=mesh['y2'=2,'y1'=2,'y0'=2,'x'=4,'c'=2,'z'=8] {'y2','y1','y0','z'}, dimensions={0} | all-to-all | bytes 524288 | tf_op jit(solution)/shard_map/all_to_all | solution.py:67
  125.8 0.1 shard_map.183
  125.9 9.6 %all_to_all.89 = f32[8,8,128]{2,1,0:T(8,128)S(1)} all-to-all(f32[8,8,128]{2,1,0:T(8,128)S(1)} %shard_map.183), channel_id=1, replica_groups=mesh['y2'=2,'y1'=2,'y0'=2,'x'=4,'c'=2,'z'=8] {'z'}, dimensions={0} | all-to-all | bytes 65536 | tf_op jit(solution)/shard_map/all_to_all | solution.py:67
  135.5 0.4 shard_map.184
  135.8 16.4 %all_to_all.90.received = f32[64,8,128]{2,1,0:T(8,128)S(1)} all-to-all(f32[64,8,128]{2,1,0:T(8,128)S(1)} %bitcast.13), channel_id=1, replica_groups=mesh['y2'=2,'y1'=2,'y0'=2,'x'=4,'c'=2,'z'=8] {'y2','y1','y0','z'}, dimensions={0} | all-to-all | bytes 524288 | tf_op jit(solution)/shard_map/all_to_all | solution.py:67
  152.3 0.1 shard_map.185
  152.3 9.5 %all_to_all.91 = f32[8,8,128]{2,1,0:T(8,128)S(1)} all-to-all(f32[8,8,128]{2,1,0:T(8,128)S(1)} %shard_map.185), channel_id=1, replica_groups=mesh['y2'=2,'y1'=2,'y0'=2,'x'=4,'c'=2,'z'=8] {'z'}, dimensions={0} | all-to-all | bytes 65536 | tf_op jit(solution)/shard_map/all_to_all | solution.py:67
  161.8 1.2 shard_map.186
  163.0 3.9 %all-to-all-start.9 = ((f32[32,32,128]{2,1,0:T(8,128)}), f32[32,32,128]{2,1,0:T(8,128)S(1)}, u32[]{:S(2)}, u32[]{:S(2)}) async-start(f32[32,32,128]{2,1,0:T(8,128)} %get-tuple-element.70), calls=%async_computation.9 | async-start | bytes 1048576 | tf_op jit(solution)/shard_map/all_to_all | solution.py:67
  166.9 2.2 copy-done.1
  169.1 0.2 shard_map.188.refs_0_
  169.3 0.4 copy-done.9
  169.8 2.3 shard_map.187.chosen0
  172.1 7.4 %all-to-all-done.9.received = f32[32,32,128]{2,1,0:T(8,128)S(1)} async-done(((f32[32,32,128]{2,1,0:T(8,128)}), f32[32,32,128]{2,1,0:T(8,128)S(1)}, u32[]{:S(2)}, u32[]{:S(2)}) %all-to-all-start.9) | async-done | bytes 524320 | tf_op jit(solution)/shard_map/all_to_all | solution.py:67
  179.4 2.7 %shard_map.189 = (f32[16,32,128]{2,1,0:T(8,128)}, f32[32,128]{1,0:T(8,128)S(1)}) custom-call(f32[32,32,128]{2,1,0:T(8,128)S(1)} %all-to-all-done.9.received, f32[2,128,128]{2,1,0:T(8,128)S(1)} %get-tuple-element.75.solved, f32[64,8192]{1,0:T(8,128)S(1)} %shard_map.188.refs_0_, f32[128,8192]{1,0:T(8,128)} %all-gather.6.cloned.1.call-done.matrix.refs_1_, ...), custom_call_target="tpu_custom_call" | custom-call | flops 8388608 | bytes 4194304 | tf_op jit(solution)/shard_map/pallas_call | solution.py:305
  182.2 3.7 %all-to-all-start.10 = ((f32[16,32,128]{2,1,0:T(8,128)}), f32[16,32,128]{2,1,0:T(8,128)S(1)}, u32[]{:S(2)}, u32[]{:S(2)}) async-start(f32[16,32,128]{2,1,0:T(8,128)} %get-tuple-element.77), calls=%async_computation.10 | async-start | bytes 524288 | tf_op jit(solution)/shard_map/all_to_all | solution.py:67
  185.9 0.0 all-gather.10.cloned.1.call-done.matrix.refs_1_
  186.0 2.3 copy-done.2
  188.3 0.6 shard_map.191.refs_0_
  188.8 1.5 shard_map.190.chosen1
  190.4 3.1 %all-to-all-done.10.received = f32[16,32,128]{2,1,0:T(8,128)S(1)} async-done(((f32[16,32,128]{2,1,0:T(8,128)}), f32[16,32,128]{2,1,0:T(8,128)S(1)}, u32[]{:S(2)}, u32[]{:S(2)}) %all-to-all-start.10) | async-done | bytes 262176 | tf_op jit(solution)/shard_map/all_to_all | solution.py:67
  193.5 2.7 %shard_map.192 = (f32[8,16,128]{2,1,0:T(8,128)}, f32[32,128]{1,0:T(8,128)S(1)}) custom-call(f32[16,32,128]{2,1,0:T(8,128)S(1)} %all-to-all-done.10.received, f32[8,8,128]{2,1,0:T(8,128)S(1)} %all_to_all.86.received.solved, f32[64,9216]{1,0:T(8,128)S(1)} %shard_map.191.refs_0_, f32[128,9216]{1,0:T(8,128)} %all-gather.10.cloned.1.call-done.matrix.refs_1_, ...), custom_call_target="tpu_custom_call" | custom-call | flops 9437184 | bytes 4718592 | tf_op jit(solution)/shard_map/pallas_call | solution.py:305
  196.2 3.4 %all-to-all-start.11 = ((f32[8,16,128]{2,1,0:T(8,128)}), f32[8,16,128]{2,1,0:T(8,128)S(1)}, u32[]{:S(2)}, u32[]{:S(2)}) async-start(f32[8,16,128]{2,1,0:T(8,128)} %get-tuple-element.82), calls=%async_computation.11 | async-start | bytes 131072 | tf_op jit(solution)/shard_map/all_to_all | solution.py:67
  199.5 0.0 all-gather.12.cloned.1.call-done.matrix
  199.6 1.6 copy-done.6
  201.2 3.0 %shard_map.194.coupling = f32[256,2048]{1,0:T(8,128)S(1)} custom-call(f32[256,2048]{1,0:T(8,128)S(1)} %copy-done.6), custom_call_target="tpu_custom_call" | custom-call | flops 8388608 | bytes 4194304 | tf_op jit(solution)/shard_map/pallas_call | solution.py:157
  204.2 1.5 shard_map.193.chosen2
  205.7 1.0 all-to-all-done.11.received
  206.7 1.5 shard_map.195
  208.2 17.8 %all_to_all.92.received = f32[8,16,128]{2,1,0:T(8,128)S(1)} all-to-all(f32[8,16,128]{2,1,0:T(8,128)S(1)} %shard_map.195), channel_id=1, replica_groups=mesh['y2'=2,'y1'=2,'y0'=2,'x'=4,'c'=2,'z'=8] {'c','x'}, dimensions={0} | all-to-all | bytes 131072 | tf_op jit(solution)/shard_map/all_to_all | solution.py:67
  226.0 0.8 shard_map.196
  (17 shorter events, 0.1 us)
Async XLA Ops:
  7.2 15.6 %copy-start.3 = (s32[16,2048]{1,0:T(8,128)S(1)}, s32[16,2048]{1,0:T(8,128)}, u32[]{:S(2)}) copy-start(s32[16,2048]{1,0:T(8,128)} %index.13) | copy-start | bytes 393220
  7.2 67.4 %all-gather.6.cloned.1.call-start = ((), (), s32[]{:S(2)}) async-start(), calls=%async_computation.13 | async-start | bytes 4718592 | tf_op jit(solution)/shard_map/all_gather | solution.py:648
  11.5 40.4 %copy-start.5 = (f32[16,9216]{1,0:T(8,128)S(1)}, f32[16,9216]{1,0:T(8,128)}, u32[]{:S(2)}) copy-start(f32[16,9216]{1,0:T(8,128)} %get-tuple-element.79.own) | copy-start | bytes 1769476
  11.6 30.3 %collective-permute-start = (f32[16,9216]{1,0:T(8,128)}, f32[16,9216]{1,0:T(8,128)S(1)}, u32[]{:S(2)}, u32[]{:S(2)}) collective-permute-start(f32[16,9216]{1,0:T(8,128)} %get-tuple-element.79.own), channel_id=1, source_target_pairs={{0,8},{8,0},{1,9},{9,1},{2,10},{10,2},{3,11},{11,3},{4,12},{12,4},... | collective-permute-start | bytes 1769480 | tf_op jit(solution)/shard_map/ppermute | solution.py:654
  22.7 0.7 copy-start.7
  25.2 16.7 %all-to-all-start = ((f32[32,8,128]{2,1,0:T(8,128)}), f32[32,8,128]{2,1,0:T(8,128)S(1)}, u32[]{:S(2)}, u32[]{:S(2)}) async-start(f32[32,8,128]{2,1,0:T(8,128)} %get-tuple-element.52), calls=%async_computation | async-start | bytes 262144 | tf_op jit(solution)/shard_map/all_to_all | solution.py:67
  32.7 57.6 %all-gather.8.cloned.1.call-start = ((), (), s32[]{:S(2)}) async-start(), calls=%async_computation.14 | async-start | bytes 2949120 | tf_op jit(solution)/shard_map/all_gather | solution.py:648
  32.8 0.7 copy-start.8
  41.9 144.1 %all-gather.10.cloned.1.call-start = ((), (), s32[]{:S(2)}) async-start(), calls=%async_computation.15 | async-start | bytes 5308416 | tf_op jit(solution)/shard_map/all_gather | solution.py:648
  69.9 11.4 %all-to-all-start.3 = ((f32[16,8,128]{2,1,0:T(8,128)}), f32[16,8,128]{2,1,0:T(8,128)S(1)}, u32[]{:S(2)}, u32[]{:S(2)}) async-start(f32[16,8,128]{2,1,0:T(8,128)} %shard_map.178), calls=%async_computation.3 | async-start | bytes 131072 | tf_op jit(solution)/shard_map/all_to_all | solution.py:67
  74.6 2.2 copy-start
  84.1 18.5 %all-to-all-start.4 = ((f32[32,32,128]{2,1,0:T(8,128)}), f32[32,32,128]{2,1,0:T(8,128)S(1)}, u32[]{:S(2)}, u32[]{:S(2)}) async-start(f32[32,32,128]{2,1,0:T(8,128)} %get-tuple-element.63), calls=%async_computation.4 | async-start | bytes 1048576 | tf_op jit(solution)/shard_map/all_to_all | solution.py:67
  89.7 109.8 %all-gather.12.cloned.1.call-start = ((), (), s32[]{:S(2)}) async-start(), calls=%async_computation.16 | async-start | bytes 2359296 | tf_op jit(solution)/shard_map/all_gather | solution.py:648
  90.3 1.7 copy-start.4
  163.0 16.4 %all-to-all-start.9 = ((f32[32,32,128]{2,1,0:T(8,128)}), f32[32,32,128]{2,1,0:T(8,128)S(1)}, u32[]{:S(2)}, u32[]{:S(2)}) async-start(f32[32,32,128]{2,1,0:T(8,128)} %get-tuple-element.70), calls=%async_computation.9 | async-start | bytes 1048576 | tf_op jit(solution)/shard_map/all_to_all | solution.py:67
  166.9 2.2 copy-start.1
  169.1 0.7 copy-start.9
  182.2 11.3 %all-to-all-start.10 = ((f32[16,32,128]{2,1,0:T(8,128)}), f32[16,32,128]{2,1,0:T(8,128)S(1)}, u32[]{:S(2)}, u32[]{:S(2)}) async-start(f32[16,32,128]{2,1,0:T(8,128)} %get-tuple-element.77), calls=%async_computation.10 | async-start | bytes 524288 | tf_op jit(solution)/shard_map/all_to_all | solution.py:67
  185.9 2.3 %copy-start.2 = (f32[128,9216]{1,0:T(8,128)S(1)}, f32[128,9216]{1,0:T(8,128)}, u32[]{:S(2)}) copy-start(f32[128,9216]{1,0:T(8,128)} %all-gather.10.cloned.1.call-done.matrix.refs_1_) | copy-start | bytes 14155780
  196.2 10.5 %all-to-all-start.11 = ((f32[8,16,128]{2,1,0:T(8,128)}), f32[8,16,128]{2,1,0:T(8,128)S(1)}, u32[]{:S(2)}, u32[]{:S(2)}) async-start(f32[8,16,128]{2,1,0:T(8,128)} %get-tuple-element.82), calls=%async_computation.11 | async-start | bytes 131072 | tf_op jit(solution)/shard_map/all_to_all | solution.py:67
  199.6 1.6 copy-start.6
  204.2 21.8 %copy-start.10 = (f32[16,32]{1,0:T(8,128)S(1)}, f32[16,32]{1,0:T(8,128)}, u32[]{:S(2)}) copy-start(f32[16,32]{1,0:T(8,128)} %values.3) | copy-start | bytes 6148
Sparse Core Ops, SparseCore 0:
  11.7 44.7 all-gather.5
  58.6 31.1 all-gather.7
  91.9 40.2 all-gather.9
  134.1 30.5 all-gather.11
